TPU v7x, 512 devices: a whole 4x4x16 slice. The times are simulated.
512 devices in a mesh: liq: 32 (over y, x, core), ill: 16 (over z).
Axes of the slice: x: 4, y: 4, z: 16, core: 2. Of those that a mesh axis runs over, the one named last changes fastest.
Arguments:
- right_side: float32 [256, 128, 512], P('liq', 'ill'), may hold values from -6 to 6
- value_guess: float32 [256, 128, 512], P('liq', 'ill'), may hold values from -6 to 6
- speed_liq: float32 [256, 128, 512], P('liq', 'ill'), may hold values from 200 to 2000
- speed_ill: float32 [256, 128, 512], P('liq', 'ill'), may hold values from 0.5 to 5
- flag_liq: int32 [256, 128, 512], P('liq', 'ill'), may hold values 0 or 1
- flag_ill: int32 [256, 128, 512], P('liq', 'ill'), may hold values 0 or 1
- jump_rates: float32 [512, 512], replicated, as said below
Outputs:
- policy_value: float32 [256, 128, 512], P('liq', 'ill')
Inputs may be any that keep to these rules, and one draw needn't show every extreme that they name: `flag_liq`: one marks a drift toward higher liquid assets, zero toward lower. `flag_ill`: one marks a drift toward higher illiquid assets, zero toward lower. jump_rates[j, i] is the rate of a jump from income state i to state j; the diagonal is zero and no entry is negative.
All inputs are finite; a program needn't handle non-finite values. No bound on the sum of `flag_liq` or of `flag_ill` on one device may be relied on, other than what follows from the above.
Results may differ from a plain program's by a relative error of at most 0.00026.
Values sent between devices are 32-bit elements; how exact they have to be, the bound alone decides.
No kernel may reach another device: no remote copies, remote signals or barrier semaphores. Data moves between devices by JAX's collectives and lax.ppermute only.
A program may use at most 64 MiB of HBM per device.

v0:
```python
import jax
import jax.numpy as jnp
from jax import lax
from jax.sharding import PartitionSpec as P

SWEEPS = 4


OMEGA = 0.8
DISCOUNT = 0.05
HIGH = lax.Precision.HIGHEST


def extended(cells, sides, width):
    for axis, dim in sides:
        count = lax.axis_size(axis)
        ends = count - 1
        head = lax.slice_in_dim(cells, 0, width, axis=dim)
        tail = lax.slice_in_dim(cells, cells.shape[dim] - width, cells.shape[dim], axis=dim)
        cells = jnp.concatenate(
            [
                lax.ppermute(tail, axis, [(i, (i + 1) % count) for i in range(ends)]),
                cells,
                lax.ppermute(head, axis, [((i + 1) % count, i) for i in range(ends)]),
            ],
            axis=dim,
        )
    return cells


def income_part(field, jump_rates):
    rows = field.reshape(-1, field.shape[2])
    return jnp.dot(rows, jump_rates, precision=HIGH).reshape(field.shape)


def diagonal_of(fwd_a, bwd_a, fwd_b, bwd_b, outflow):
    return DISCOUNT + fwd_a + bwd_a + fwd_b + bwd_b + outflow[None, None, :]


def residual_of(padded, rhs, coefs, jump_rates):
    fwd_a, bwd_a, fwd_b, bwd_b, diag = coefs
    center = padded[1:-1, 1:-1]
    applied = diag * center - fwd_a * padded[2:, 1:-1] - bwd_a * padded[:-2, 1:-1]
    applied = applied - fwd_b * padded[1:-1, 2:] - bwd_b * padded[1:-1, :-2]
    applied = applied - income_part(center, jump_rates)
    return rhs - applied


def relax(padded, rhs, coefs, jump_rates):
    return padded[1:-1, 1:-1] + OMEGA * residual_of(padded, rhs, coefs, jump_rates) / coefs[4]


def restrict(field):
    size_a, size_b, size_z = field.shape
    return field.reshape(size_a // 2, 2, size_b // 2, 2, size_z).mean(axis=(1, 3))


def prolong(field):
    size_a, size_b, size_z = field.shape
    wide = jnp.broadcast_to(field[:, None, :, None, :], (size_a, 2, size_b, 2, size_z))
    return wide.reshape(2 * size_a, 2 * size_b, size_z)


def coarser(coefs):
    return tuple((0.5 * restrict(entry) for entry in coefs))


def line_solve(rhs, coefs):
    fwd_a, bwd_a, fwd_b, bwd_b, diag = coefs
    lower = jnp.transpose(-bwd_a, (1, 2, 0))
    upper = jnp.transpose(-fwd_a, (1, 2, 0))
    middle = jnp.transpose(diag, (1, 2, 0))
    length = lower.shape[2]
    place = lax.broadcasted_iota(jnp.int32, lower.shape, 2)
    lower = jnp.where(place == 0, jnp.zeros_like(lower), lower)
    upper = jnp.where(place == length - 1, jnp.zeros_like(upper), upper)
    target = jnp.transpose(rhs, (1, 2, 0))[..., None]
    solved = lax.linalg.tridiagonal_solve(lower, middle, upper, target)[..., 0]
    return jnp.transpose(solved, (2, 0, 1))


def fine_pad(field):
    return extended(field, (("liq", 0), ("ill", 1)), 1)


def mid_pad(field):
    return extended(field, (("liq", 0), ("ill", 1)), 1)


def coarse_solve(rhs_line, line, jump_rates):
    error_line = line_solve(rhs_line, line)
    for step in range(SWEEPS - 1):
        padded = extended(error_line, (("ill", 1),), 1)
        target = rhs_line + line[2] * padded[:, 2:] + line[3] * padded[:, :-2]
        target = target + income_part(error_line, jump_rates)
        error_line = line_solve(target, line)
    return error_line


def body(right_side, value_guess, speed_liq, speed_ill, flag_liq, flag_ill, jump_rates):
    outflow = jnp.sum(jump_rates, axis=0)
    up_liq = flag_liq.astype(jnp.float32)
    up_ill = flag_ill.astype(jnp.float32)
    fine4 = (
        speed_liq * up_liq,
        speed_liq * (1.0 - up_liq),
        speed_ill * up_ill,
        speed_ill * (1.0 - up_ill),
    )
    fine = fine4 + (diagonal_of(*fine4, outflow),)
    mid4 = coarser(fine4)
    mid = mid4 + (diagonal_of(*mid4, outflow),)
    low4 = coarser(mid4)

    def fine_pair(field):
        for step in range(2):
            field = relax(fine_pad(field), right_side, fine, jump_rates)
        return field

    value = fine_pair(value_guess)
    rhs_mid = restrict(residual_of(fine_pad(value), right_side, fine, jump_rates))
    error_mid = OMEGA * rhs_mid / mid[4]
    error_mid = relax(mid_pad(error_mid), rhs_mid, mid, jump_rates)
    rhs_low = restrict(residual_of(mid_pad(error_mid), rhs_mid, mid, jump_rates))
    gathered = (
        lax.all_gather(rhs_low, "liq", axis=0, tiled=True),
        lax.all_gather(low4[0], "liq", axis=0, tiled=True),
        lax.all_gather(low4[1], "liq", axis=0, tiled=True),
        lax.all_gather(low4[2], "liq", axis=0, tiled=True),
        lax.all_gather(low4[3], "liq", axis=0, tiled=True),
    )
    rhs_line = gathered[0]
    line4 = (gathered[1], gathered[2], gathered[3], gathered[4])
    line = line4 + (diagonal_of(*line4, outflow),)
    error_line = coarse_solve(rhs_line, line, jump_rates)
    width = rhs_low.shape[0]
    error_low = lax.dynamic_slice_in_dim(error_line, lax.axis_index("liq") * width, width, 0)
    field = error_mid + prolong(error_low)
    for step in range(2):
        field = relax(mid_pad(field), rhs_mid, mid, jump_rates)
    error_mid = field
    value = fine_pair(value + prolong(error_mid))
    return value


def solution(mesh):
    in_specs = (
        P("liq", "ill", None),
        P("liq", "ill", None),
        P("liq", "ill", None),
        P("liq", "ill", None),
        P("liq", "ill", None),
        P("liq", "ill", None),
        P(),
    )
    out_specs = P("liq", "ill", None)
    return jax.shard_map(body, mesh=mesh, in_specs=in_specs, out_specs=out_specs, check_vma=False)
```

profile of v0, /device:TPU:400, one launch (start us, length us, event | category | flops | bytes accessed | tf_op | source)
XLA Modules:
  0.0 351.1 jit_solution(5555081220845657260)
XLA Ops:
  2.7 5.8 %collective-permute-start = (f32[1,8,512]{2,1,0:T(8,128)S(1)}, f32[1,8,512]{2,1,0:T(8,128)S(1)}, u32[]{:S(2)}, u32[]{:S(2)}) collective-permute-start(f32[1,8,512]{2,1,0:T(8,128)S(1)} %get-tuple-element.777), channel_id=1, source_target_pairs={{16,0},{32,16},{48,32},{64,48},{80,64},{96,80},{112,96},{128,112},... | collective-permute-start | bytes 49160 | tf_op jit(solution)/shard_map/ppermute | solution.py:24
  10.0 4.1 %collective-permute-start.2 = (f32[10,1,512]{2,1,0:T(1,128)S(1)}, f32[10,1,512]{2,1,0:T(1,128)S(1)}, u32[]{:S(2)}, u32[]{:S(2)}) collective-permute-start(f32[10,1,512]{2,1,0:T(1,128)S(1)} %get-tuple-element.767), channel_id=1, source_target_pairs={{1,0},{2,1},{3,2},{4,3},{5,4},{6,5},{7,6},{8,7},{9,8},{10,9},{11,1... | collective-permute-start | bytes 61448 | tf_op jit(solution)/shard_map/ppermute | solution.py:24
  14.1 2.1 collective-permute-start.3
  17.5 3.6 %collective-permute-done.3 = f32[10,1,512]{2,1,0:T(1,128)S(1)} collective-permute-done((f32[10,1,512]{2,1,0:T(1,128)S(1)}, f32[10,1,512]{2,1,0:T(1,128)S(1)}, u32[]{:S(2)}, u32[]{:S(2)}) %collective-permute-start.3) | collective-permute-done | bytes 20512 | tf_op jit(solution)/shard_map/ppermute | solution.py:22
  23.1 4.3 %collective-permute-start.4 = (f32[1,8,512]{2,1,0:T(8,128)S(1)}, f32[1,8,512]{2,1,0:T(8,128)S(1)}, u32[]{:S(2)}, u32[]{:S(2)}) collective-permute-start(f32[1,8,512]{2,1,0:T(8,128)S(1)} %get-tuple-element.776), channel_id=1, source_target_pairs={{16,0},{32,16},{48,32},{64,48},{80,64},{96,80},{112,96},{128,112},... | collective-permute-start | bytes 49160 | tf_op jit(solution)/shard_map/ppermute | solution.py:24
  27.4 1.9 collective-permute-start.5
  29.3 5.2 %collective-permute-done.5 = f32[1,8,512]{2,1,0:T(8,128)S(1)} collective-permute-done((f32[1,8,512]{2,1,0:T(8,128)S(1)}, f32[1,8,512]{2,1,0:T(8,128)S(1)}, u32[]{:S(2)}, u32[]{:S(2)}) %collective-permute-start.5) | collective-permute-done | bytes 16416 | tf_op jit(solution)/shard_map/ppermute | solution.py:22
  34.6 2.4 collective-permute-start.6
  37.0 3.4 collective-permute-start.7
  40.4 3.4 collective-permute-done.7
  44.7 1.9 collective-permute-start.8
  46.7 2.4 collective-permute-start.9
  49.1 4.7 %collective-permute-done.9 = f32[1,8,512]{2,1,0:T(8,128)S(1)} collective-permute-done((f32[1,8,512]{2,1,0:T(8,128)S(1)}, f32[1,8,512]{2,1,0:T(8,128)S(1)}, u32[]{:S(2)}, u32[]{:S(2)}) %collective-permute-start.9) | collective-permute-done | bytes 16416 | tf_op jit(solution)/shard_map/ppermute | solution.py:22
  53.8 1.9 collective-permute-start.10
  55.8 3.9 %collective-permute-start.11 = (f32[10,1,512]{2,1,0:T(1,128)S(1)}, f32[10,1,512]{2,1,0:T(1,128)S(1)}, u32[]{:S(2)}, u32[]{:S(2)}) collective-permute-start(f32[10,1,512]{2,1,0:T(1,128)S(1)} %get-tuple-element.764), channel_id=1, source_target_pairs={{0,1},{1,2},{2,3},{3,4},{4,5},{5,6},{6,7},{7,8},{8,9},{9,10},{10,1... | collective-permute-start | bytes 61448 | tf_op jit(solution)/shard_map/ppermute | solution.py:22
  66.2 2.4 collective-permute-start.13
  68.7 23.0 %all_gather.16 = f32[64,2,512]{2,1,0:T(2,128)S(1)} all-gather(f32[2,2,512]{2,1,0:T(2,128)S(1)} %broadcast_multiply_fusion.7), channel_id=1, replica_groups=mesh['liq'=32,'ill'=16] {'liq'}, dimensions={0}, use_global_device_ids=true | all-gather | bytes 270336 | tf_op jit(solution)/shard_map/all_gather | solution.py:129
  91.8 23.9 %all_gather.17 = f32[64,2,512]{2,1,0:T(2,128)S(1)} all-gather(f32[2,2,512]{2,1,0:T(2,128)S(1)} %broadcast_multiply_fusion.6), channel_id=1, replica_groups=mesh['liq'=32,'ill'=16] {'liq'}, dimensions={0}, use_global_device_ids=true | all-gather | bytes 270336 | tf_op jit(solution)/shard_map/all_gather | solution.py:127
  115.8 22.8 %all_gather.18 = f32[64,2,512]{2,1,0:T(2,128)S(1)} all-gather(f32[2,2,512]{2,1,0:T(2,128)S(1)} %broadcast_multiply_fusion.5), channel_id=1, replica_groups=mesh['liq'=32,'ill'=16] {'liq'}, dimensions={0}, use_global_device_ids=true | all-gather | bytes 270336 | tf_op jit(solution)/shard_map/all_gather | solution.py:128
  138.7 23.7 %all_gather.19 = f32[64,2,512]{2,1,0:T(2,128)S(1)} all-gather(f32[2,2,512]{2,1,0:T(2,128)S(1)} %broadcast_multiply_fusion.4), channel_id=1, replica_groups=mesh['liq'=32,'ill'=16] {'liq'}, dimensions={0}, use_global_device_ids=true | all-gather | bytes 270336 | tf_op jit(solution)/shard_map/all_gather | solution.py:130
  163.0 1.9 collective-permute-start.14
  164.9 4.1 %collective-permute-start.15 = (f32[6,1,512]{2,1,0:T(1,128)S(1)}, f32[6,1,512]{2,1,0:T(1,128)S(1)}, u32[]{:S(2)}, u32[]{:S(2)}) collective-permute-start(f32[6,1,512]{2,1,0:T(1,128)S(1)} %get-tuple-element.786), channel_id=1, source_target_pairs={{0,1},{1,2},{2,3},{3,4},{4,5},{5,6},{6,7},{7,8},{8,9},{9,10},{10,1... | collective-permute-start | bytes 36872 | tf_op jit(solution)/shard_map/ppermute | solution.py:22
  169.1 2.6 collective-permute-done.15
  172.4 2.2 collective-permute-start.16
  174.6 2.1 collective-permute-start.17
  176.7 4.9 %collective-permute-done.17 = f32[1,4,512]{2,1,0:T(4,128)S(1)} collective-permute-done((f32[1,4,512]{2,1,0:T(4,128)S(1)}, f32[1,4,512]{2,1,0:T(4,128)S(1)}, u32[]{:S(2)}, u32[]{:S(2)}) %collective-permute-start.17) | collective-permute-done | bytes 8224 | tf_op jit(solution)/shard_map/ppermute | solution.py:22
  181.7 1.9 collective-permute-start.18
  183.6 3.9 %collective-permute-start.19 = (f32[6,1,512]{2,1,0:T(1,128)S(1)}, f32[6,1,512]{2,1,0:T(1,128)S(1)}, u32[]{:S(2)}, u32[]{:S(2)}) collective-permute-start(f32[6,1,512]{2,1,0:T(1,128)S(1)} %get-tuple-element.784), channel_id=1, source_target_pairs={{0,1},{1,2},{2,3},{3,4},{4,5},{5,6},{6,7},{7,8},{8,9},{9,10},{10,1... | collective-permute-start | bytes 36872 | tf_op jit(solution)/shard_map/ppermute | solution.py:22
  188.3 2.1 collective-permute-done.19
  191.2 23.5 %all_gather.15 = f32[64,2,512]{2,1,0:T(2,128)S(1)} all-gather(f32[2,2,512]{2,1,0:T(2,128)S(1)} %broadcast_multiply_fusion.8), channel_id=1, replica_groups=mesh['liq'=32,'ill'=16] {'liq'}, dimensions={0}, use_global_device_ids=true | all-gather | bytes 270336 | tf_op jit(solution)/shard_map/all_gather | solution.py:126
  223.5 1.9 collective-permute-start.20
  225.4 3.9 %collective-permute-start.21 = (f32[64,1,512]{2,0,1:T(8,128)}, f32[64,1,512]{2,0,1:T(8,128)}, u32[]{:S(2)}, u32[]{:S(2)}) collective-permute-start(f32[64,1,512]{2,0,1:T(8,128)} %get-tuple-element.755), channel_id=1, source_target_pairs={{0,1},{1,2},{2,3},{3,4},{4,5},{5,6},{6,7},{7,8},{8,9},{9,10},{10,1... | collective-permute-start | bytes 393224 | tf_op jit(solution)/shard_map/ppermute | solution.py:22
  229.4 2.1 collective-permute-done.20
  231.5 3.1 collective-permute-done.21
  244.4 1.9 collective-permute-start.22
  246.3 4.1 %collective-permute-start.23 = (f32[64,1,512]{2,1,0:T(1,128)S(1)}, f32[64,1,512]{2,1,0:T(1,128)S(1)}, u32[]{:S(2)}, u32[]{:S(2)}) collective-permute-start(f32[64,1,512]{2,1,0:T(1,128)S(1)} %get-tuple-element.691), channel_id=1, source_target_pairs={{0,1},{1,2},{2,3},{3,4},{4,5},{5,6},{6,7},{7,8},{8,9},{9,10},{10,1... | collective-permute-start | bytes 393224 | tf_op jit(solution)/shard_map/ppermute | solution.py:22
  251.2 3.1 collective-permute-done.23
  260.3 1.9 collective-permute-start.24
  262.2 3.9 %collective-permute-start.25 = (f32[64,1,512]{2,1,0:T(1,128)S(1)}, f32[64,1,512]{2,1,0:T(1,128)S(1)}, u32[]{:S(2)}, u32[]{:S(2)}) collective-permute-start(f32[64,1,512]{2,1,0:T(1,128)S(1)} %get-tuple-element.687), channel_id=1, source_target_pairs={{0,1},{1,2},{2,3},{3,4},{4,5},{5,6},{6,7},{7,8},{8,9},{9,10},{10,1... | collective-permute-start | bytes 393224 | tf_op jit(solution)/shard_map/ppermute | solution.py:22
  267.2 3.1 collective-permute-done.25
  275.8 1.9 collective-permute-start.26
  277.8 2.4 collective-permute-start.27
  280.2 4.7 %collective-permute-done.27 = f32[1,4,512]{2,1,0:T(4,128)S(1)} collective-permute-done((f32[1,4,512]{2,1,0:T(4,128)S(1)}, f32[1,4,512]{2,1,0:T(4,128)S(1)}, u32[]{:S(2)}, u32[]{:S(2)}) %collective-permute-start.27) | collective-permute-done | bytes 8224 | tf_op jit(solution)/shard_map/ppermute | solution.py:22
  284.9 1.9 collective-permute-start.28
  286.8 3.9 %collective-permute-start.29 = (f32[6,1,512]{2,1,0:T(1,128)S(1)}, f32[6,1,512]{2,1,0:T(1,128)S(1)}, u32[]{:S(2)}, u32[]{:S(2)}) collective-permute-start(f32[6,1,512]{2,1,0:T(1,128)S(1)} %get-tuple-element.782), channel_id=1, source_target_pairs={{0,1},{1,2},{2,3},{3,4},{4,5},{5,6},{6,7},{7,8},{8,9},{9,10},{10,1... | collective-permute-start | bytes 36872 | tf_op jit(solution)/shard_map/ppermute | solution.py:22
  290.7 2.9 collective-permute-done.29
  294.3 1.9 collective-permute-start.30
  296.2 2.4 collective-permute-start.31
  298.6 4.7 %collective-permute-done.31 = f32[1,4,512]{2,1,0:T(4,128)S(1)} collective-permute-done((f32[1,4,512]{2,1,0:T(4,128)S(1)}, f32[1,4,512]{2,1,0:T(4,128)S(1)}, u32[]{:S(2)}, u32[]{:S(2)}) %collective-permute-start.31) | collective-permute-done | bytes 8224 | tf_op jit(solution)/shard_map/ppermute | solution.py:22
  303.3 1.9 collective-permute-start.32
  305.2 3.9 %collective-permute-start.33 = (f32[6,1,512]{2,1,0:T(1,128)S(1)}, f32[6,1,512]{2,1,0:T(1,128)S(1)}, u32[]{:S(2)}, u32[]{:S(2)}) collective-permute-start(f32[6,1,512]{2,1,0:T(1,128)S(1)} %get-tuple-element.780), channel_id=1, source_target_pairs={{0,1},{1,2},{2,3},{3,4},{4,5},{5,6},{6,7},{7,8},{8,9},{9,10},{10,1... | collective-permute-start | bytes 36872 | tf_op jit(solution)/shard_map/ppermute | solution.py:22
  309.2 2.9 collective-permute-done.33
  313.0 1.9 collective-permute-start.34
  314.9 2.4 collective-permute-start.35
  317.3 4.7 %collective-permute-done.35 = f32[1,8,512]{2,1,0:T(8,128)S(1)} collective-permute-done((f32[1,8,512]{2,1,0:T(8,128)S(1)}, f32[1,8,512]{2,1,0:T(8,128)S(1)}, u32[]{:S(2)}, u32[]{:S(2)}) %collective-permute-start.35) | collective-permute-done | bytes 16416 | tf_op jit(solution)/shard_map/ppermute | solution.py:22
  322.1 1.9 collective-permute-start.36
  324.0 3.9 %collective-permute-start.37 = (f32[10,1,512]{2,1,0:T(1,128)S(1)}, f32[10,1,512]{2,1,0:T(1,128)S(1)}, u32[]{:S(2)}, u32[]{:S(2)}) collective-permute-start(f32[10,1,512]{2,1,0:T(1,128)S(1)} %get-tuple-element.762), channel_id=1, source_target_pairs={{0,1},{1,2},{2,3},{3,4},{4,5},{5,6},{6,7},{7,8},{8,9},{9,10},{10,1... | collective-permute-start | bytes 61448 | tf_op jit(solution)/shard_map/ppermute | solution.py:22
  328.0 2.9 collective-permute-done.37
  331.7 1.9 collective-permute-start.38
  333.7 2.4 collective-permute-start.39
  336.1 4.7 %collective-permute-done.39 = f32[1,8,512]{2,1,0:T(8,128)S(1)} collective-permute-done((f32[1,8,512]{2,1,0:T(8,128)S(1)}, f32[1,8,512]{2,1,0:T(8,128)S(1)}, u32[]{:S(2)}, u32[]{:S(2)}) %collective-permute-start.39) | collective-permute-done | bytes 16416 | tf_op jit(solution)/shard_map/ppermute | solution.py:22
  340.9 1.9 collective-permute-start.40
  342.8 3.9 %collective-permute-start.41 = (f32[10,1,512]{2,1,0:T(1,128)S(1)}, f32[10,1,512]{2,1,0:T(1,128)S(1)}, u32[]{:S(2)}, u32[]{:S(2)}) collective-permute-start(f32[10,1,512]{2,1,0:T(1,128)S(1)} %get-tuple-element.760), channel_id=1, source_target_pairs={{0,1},{1,2},{2,3},{3,4},{4,5},{5,6},{6,7},{7,8},{8,9},{9,10},{10,1... | collective-permute-start | bytes 61448 | tf_op jit(solution)/shard_map/ppermute | solution.py:22
  346.7 2.9 collective-permute-done.41
  (790 shorter events, 50.4 us)
Async XLA Ops:
  0.0 21.1 %copy-start = (f32[512,512]{1,0:T(8,128)S(1)}, f32[512,512]{1,0:T(8,128)}, u32[]{:S(2)}) copy-start(f32[512,512]{1,0:T(8,128)} %param.13) | copy-start | bytes 3145732
  0.8 7.7 %collective-permute-start.1 = (f32[1,8,512]{2,1,0:T(8,128)S(1)}, f32[1,8,512]{2,1,0:T(8,128)S(1)}, u32[]{:S(2)}, u32[]{:S(2)}) collective-permute-start(f32[1,8,512]{2,1,0:T(8,128)S(1)} %get-tuple-element.778), channel_id=1, source_target_pairs={{0,16},{16,32},{32,48},{48,64},{64,80},{80,96},{96,112},{112,128},... | collective-permute-start | bytes 49160 | tf_op jit(solution)/shard_map/ppermute | solution.py:22
  2.7 7.2 %collective-permute-start = (f32[1,8,512]{2,1,0:T(8,128)S(1)}, f32[1,8,512]{2,1,0:T(8,128)S(1)}, u32[]{:S(2)}, u32[]{:S(2)}) collective-permute-start(f32[1,8,512]{2,1,0:T(8,128)S(1)} %get-tuple-element.777), channel_id=1, source_target_pairs={{16,0},{32,16},{48,32},{64,48},{80,64},{96,80},{112,96},{128,112},... | collective-permute-start | bytes 49160 | tf_op jit(solution)/shard_map/ppermute | solution.py:24
  10.0 7.6 %collective-permute-start.2 = (f32[10,1,512]{2,1,0:T(1,128)S(1)}, f32[10,1,512]{2,1,0:T(1,128)S(1)}, u32[]{:S(2)}, u32[]{:S(2)}) collective-permute-start(f32[10,1,512]{2,1,0:T(1,128)S(1)} %get-tuple-element.767), channel_id=1, source_target_pairs={{1,0},{2,1},{3,2},{4,3},{5,4},{6,5},{7,6},{8,7},{9,8},{10,9},{11,1... | collective-permute-start | bytes 61448 | tf_op jit(solution)/shard_map/ppermute | solution.py:24
  14.1 7.1 %copy-start.1 = (f32[8,8,512]{2,1,0:T(8,128)S(1)}, f32[8,8,512]{2,1,0:T(8,128)}, u32[]{:S(2)}) copy-start(f32[8,8,512]{2,1,0:T(8,128)} %param.7) | copy-start | bytes 393220
  14.1 7.1 %copy-start.6 = (f32[8,8,512]{2,1,0:T(8,128)S(1)}, f32[8,8,512]{2,1,0:T(8,128)}, u32[]{:S(2)}) copy-start(f32[8,8,512]{2,1,0:T(8,128)} %param.8) | copy-start | bytes 393220
  14.1 7.0 %copy-start.68 = (f32[8,8,512]{2,1,0:T(8,128)S(1)}, f32[8,8,512]{2,1,0:T(8,128)}, u32[]{:S(2)}) copy-start(f32[8,8,512]{2,1,0:T(8,128)} %param.9) | copy-start | bytes 393220
  14.1 7.0 %collective-permute-start.3 = (f32[10,1,512]{2,1,0:T(1,128)S(1)}, f32[10,1,512]{2,1,0:T(1,128)S(1)}, u32[]{:S(2)}, u32[]{:S(2)}) collective-permute-start(f32[10,1,512]{2,1,0:T(1,128)S(1)} %get-tuple-element.768), channel_id=1, source_target_pairs={{0,1},{1,2},{2,3},{3,4},{4,5},{5,6},{6,7},{7,8},{8,9},{9,10},{10,1... | collective-permute-start | bytes 61448 | tf_op jit(solution)/shard_map/ppermute | solution.py:22
  17.5 172.9 %copy-start.61 = (f32[512]{0:T(512)}, f32[512]{0:T(512)S(1)}, u32[]{:S(2)}) copy-start(f32[512]{0:T(512)S(1)} %reduce_sum.99) | copy-start | bytes 6148
  23.1 6.2 %collective-permute-start.4 = (f32[1,8,512]{2,1,0:T(8,128)S(1)}, f32[1,8,512]{2,1,0:T(8,128)S(1)}, u32[]{:S(2)}, u32[]{:S(2)}) collective-permute-start(f32[1,8,512]{2,1,0:T(8,128)S(1)} %get-tuple-element.776), channel_id=1, source_target_pairs={{16,0},{32,16},{48,32},{64,48},{80,64},{96,80},{112,96},{128,112},... | collective-permute-start | bytes 49160 | tf_op jit(solution)/shard_map/ppermute | solution.py:24
  27.4 7.2 %collective-permute-start.5 = (f32[1,8,512]{2,1,0:T(8,128)S(1)}, f32[1,8,512]{2,1,0:T(8,128)S(1)}, u32[]{:S(2)}, u32[]{:S(2)}) collective-permute-start(f32[1,8,512]{2,1,0:T(8,128)S(1)} %get-tuple-element.775), channel_id=1, source_target_pairs={{0,16},{16,32},{32,48},{48,64},{64,80},{80,96},{96,112},{112,128},... | collective-permute-start | bytes 49160 | tf_op jit(solution)/shard_map/ppermute | solution.py:22
  34.6 5.9 %collective-permute-start.6 = (f32[10,1,512]{2,1,0:T(1,128)S(1)}, f32[10,1,512]{2,1,0:T(1,128)S(1)}, u32[]{:S(2)}, u32[]{:S(2)}) collective-permute-start(f32[10,1,512]{2,1,0:T(1,128)S(1)} %get-tuple-element.765), channel_id=1, source_target_pairs={{1,0},{2,1},{3,2},{4,3},{5,4},{6,5},{7,6},{8,7},{9,8},{10,9},{11,1... | collective-permute-start | bytes 61448 | tf_op jit(solution)/shard_map/ppermute | solution.py:24
  37.0 6.9 %collective-permute-start.7 = (f32[10,1,512]{2,1,0:T(1,128)S(1)}, f32[10,1,512]{2,1,0:T(1,128)S(1)}, u32[]{:S(2)}, u32[]{:S(2)}) collective-permute-start(f32[10,1,512]{2,1,0:T(1,128)S(1)} %get-tuple-element.766), channel_id=1, source_target_pairs={{0,1},{1,2},{2,3},{3,4},{4,5},{5,6},{6,7},{7,8},{8,9},{9,10},{10,1... | collective-permute-start | bytes 61448 | tf_op jit(solution)/shard_map/ppermute | solution.py:22
  44.7 4.4 %collective-permute-start.8 = (f32[1,8,512]{2,1,0:T(8,128)S(1)}, f32[1,8,512]{2,1,0:T(8,128)S(1)}, u32[]{:S(2)}, u32[]{:S(2)}) collective-permute-start(f32[1,8,512]{2,1,0:T(8,128)S(1)} %get-tuple-element.774), channel_id=1, source_target_pairs={{16,0},{32,16},{48,32},{64,48},{80,64},{96,80},{112,96},{128,112},... | collective-permute-start | bytes 49160 | tf_op jit(solution)/shard_map/ppermute | solution.py:24
  46.7 7.2 %collective-permute-start.9 = (f32[1,8,512]{2,1,0:T(8,128)S(1)}, f32[1,8,512]{2,1,0:T(8,128)S(1)}, u32[]{:S(2)}, u32[]{:S(2)}) collective-permute-start(f32[1,8,512]{2,1,0:T(8,128)S(1)} %get-tuple-element.773), channel_id=1, source_target_pairs={{0,16},{16,32},{32,48},{48,64},{64,80},{80,96},{96,112},{112,128},... | collective-permute-start | bytes 49160 | tf_op jit(solution)/shard_map/ppermute | solution.py:22
  53.8 7.1 %collective-permute-start.10 = (f32[10,1,512]{2,1,0:T(1,128)S(1)}, f32[10,1,512]{2,1,0:T(1,128)S(1)}, u32[]{:S(2)}, u32[]{:S(2)}) collective-permute-start(f32[10,1,512]{2,1,0:T(1,128)S(1)} %get-tuple-element.763), channel_id=1, source_target_pairs={{1,0},{2,1},{3,2},{4,3},{5,4},{6,5},{7,6},{8,7},{9,8},{10,9},{11,1... | collective-permute-start | bytes 61448 | tf_op jit(solution)/shard_map/ppermute | solution.py:24
  55.8 6.9 %collective-permute-start.11 = (f32[10,1,512]{2,1,0:T(1,128)S(1)}, f32[10,1,512]{2,1,0:T(1,128)S(1)}, u32[]{:S(2)}, u32[]{:S(2)}) collective-permute-start(f32[10,1,512]{2,1,0:T(1,128)S(1)} %get-tuple-element.764), channel_id=1, source_target_pairs={{0,1},{1,2},{2,3},{3,4},{4,5},{5,6},{6,7},{7,8},{8,9},{9,10},{10,1... | collective-permute-start | bytes 61448 | tf_op jit(solution)/shard_map/ppermute | solution.py:22
  63.6 108.1 %copy-start.3 = (f32[4,4,512]{2,1,0:T(4,128)}, f32[4,4,512]{2,1,0:T(4,128)S(1)}, u32[]{:S(2)}) copy-start(f32[4,4,512]{2,1,0:T(4,128)S(1)} %reduce_sum.100) | copy-start | bytes 98308
  64.3 98.6 %collective-permute-start.12 = (f32[1,4,512]{2,1,0:T(4,128)}, f32[1,4,512]{2,1,0:T(4,128)S(1)}, u32[]{:S(2)}, u32[]{:S(2)}) collective-permute-start(f32[1,4,512]{2,1,0:T(4,128)} %get-tuple-element.799), channel_id=1, source_target_pairs={{16,0},{32,16},{48,32},{64,48},{80,64},{96,80},{112,96},{128,112},... | collective-permute-start | bytes 24584 | tf_op jit(solution)/shard_map/ppermute | solution.py:24
  66.2 96.7 %collective-permute-start.13 = (f32[1,4,512]{2,1,0:T(4,128)S(1)}, f32[1,4,512]{2,1,0:T(4,128)S(1)}, u32[]{:S(2)}, u32[]{:S(2)}) collective-permute-start(f32[1,4,512]{2,1,0:T(4,128)S(1)} %get-tuple-element.798), channel_id=1, source_target_pairs={{0,16},{16,32},{32,48},{48,64},{64,80},{80,96},{96,112},{112,128},... | collective-permute-start | bytes 24584 | tf_op jit(solution)/shard_map/ppermute | solution.py:22
  138.7 23.7 %copy-start.188 = (pred[64]{0:T(512)(128)(4,1)S(1)}, pred[64]{0:T(512)(128)(4,1)}, u32[]{:S(2)}) copy-start(pred[64]{0:T(512)(128)(4,1)} %iota_compare_fusion.1) | copy-start | bytes 196
  162.9 24.7 %copy-start.2 = (f32[2,512,64]{1,0,2:T(2,128)}, f32[2,512,64]{1,0,2:T(2,128)S(1)}, u32[]{:S(2)}) copy-start(f32[2,512,64]{1,0,2:T(2,128)S(1)} %get-tuple-element.756) | copy-start | bytes 786436
  163.0 6.1 %collective-permute-start.14 = (f32[6,1,512]{2,1,0:T(1,128)S(1)}, f32[6,1,512]{2,1,0:T(1,128)S(1)}, u32[]{:S(2)}, u32[]{:S(2)}) collective-permute-start(f32[6,1,512]{2,1,0:T(1,128)S(1)} %get-tuple-element.785), channel_id=1, source_target_pairs={{1,0},{2,1},{3,2},{4,3},{5,4},{6,5},{7,6},{8,7},{9,8},{10,9},{11,1... | collective-permute-start | bytes 36872 | tf_op jit(solution)/shard_map/ppermute | solution.py:24
  164.9 6.8 %collective-permute-start.15 = (f32[6,1,512]{2,1,0:T(1,128)S(1)}, f32[6,1,512]{2,1,0:T(1,128)S(1)}, u32[]{:S(2)}, u32[]{:S(2)}) collective-permute-start(f32[6,1,512]{2,1,0:T(1,128)S(1)} %get-tuple-element.786), channel_id=1, source_target_pairs={{0,1},{1,2},{2,3},{3,4},{4,5},{5,6},{6,7},{7,8},{8,9},{9,10},{10,1... | collective-permute-start | bytes 36872 | tf_op jit(solution)/shard_map/ppermute | solution.py:22
  172.3 18.1 %copy-start.7 = (f32[4,4,512]{2,1,0:T(4,128)}, f32[4,4,512]{2,1,0:T(4,128)S(1)}, u32[]{:S(2)}) copy-start(f32[4,4,512]{2,1,0:T(4,128)S(1)} %fusion.146) | copy-start | bytes 98308
  172.4 4.4 %collective-permute-start.16 = (f32[1,4,512]{2,1,0:T(4,128)S(1)}, f32[1,4,512]{2,1,0:T(4,128)S(1)}, u32[]{:S(2)}, u32[]{:S(2)}) collective-permute-start(f32[1,4,512]{2,1,0:T(4,128)S(1)} %get-tuple-element.792), channel_id=1, source_target_pairs={{16,0},{32,16},{48,32},{64,48},{80,64},{96,80},{112,96},{128,112},... | collective-permute-start | bytes 24584 | tf_op jit(solution)/shard_map/ppermute | solution.py:24
  174.6 7.1 %collective-permute-start.17 = (f32[1,4,512]{2,1,0:T(4,128)S(1)}, f32[1,4,512]{2,1,0:T(4,128)S(1)}, u32[]{:S(2)}, u32[]{:S(2)}) collective-permute-start(f32[1,4,512]{2,1,0:T(4,128)S(1)} %get-tuple-element.791), channel_id=1, source_target_pairs={{0,16},{16,32},{32,48},{48,64},{64,80},{80,96},{96,112},{112,128},... | collective-permute-start | bytes 24584 | tf_op jit(solution)/shard_map/ppermute | solution.py:22
  181.7 6.6 %collective-permute-start.18 = (f32[6,1,512]{2,1,0:T(1,128)S(1)}, f32[6,1,512]{2,1,0:T(1,128)S(1)}, u32[]{:S(2)}, u32[]{:S(2)}) collective-permute-start(f32[6,1,512]{2,1,0:T(1,128)S(1)} %get-tuple-element.783), channel_id=1, source_target_pairs={{1,0},{2,1},{3,2},{4,3},{5,4},{6,5},{7,6},{8,7},{9,8},{10,9},{11,1... | collective-permute-start | bytes 36872 | tf_op jit(solution)/shard_map/ppermute | solution.py:24
  183.6 6.8 %collective-permute-start.19 = (f32[6,1,512]{2,1,0:T(1,128)S(1)}, f32[6,1,512]{2,1,0:T(1,128)S(1)}, u32[]{:S(2)}, u32[]{:S(2)}) collective-permute-start(f32[6,1,512]{2,1,0:T(1,128)S(1)} %get-tuple-element.784), channel_id=1, source_target_pairs={{0,1},{1,2},{2,3},{3,4},{4,5},{5,6},{6,7},{7,8},{8,9},{9,10},{10,1... | collective-permute-start | bytes 36872 | tf_op jit(solution)/shard_map/ppermute | solution.py:22
  188.3 26.5 %copy-start.79 = (f32[2,512,1]{1,0,2:T(2,128)}, f32[2,512,1]{1,0,2:T(2,128)S(1)}, u32[]{:S(2)}) copy-start(f32[2,512,1]{1,0,2:T(2,128)S(1)} %get-tuple-element.641) | copy-start | bytes 12292
  188.3 28.0 %copy-start.63 = (f32[2,512,1]{1,0,2:T(2,128)}, f32[2,512,1]{1,0,2:T(2,128)S(1)}, u32[]{:S(2)}) copy-start(f32[2,512,1]{1,0,2:T(2,128)S(1)} %get-tuple-element.640) | copy-start | bytes 12292
  217.5 4.4 %copy-start.45 = (f32[2,512,1]{1,0,2:T(2,128)}, f32[2,512,1]{1,0,2:T(2,128)S(1)}, u32[]{:S(2)}) copy-start(f32[2,512,1]{1,0,2:T(2,128)S(1)} %get-tuple-element.601) | copy-start | bytes 12292
  217.5 4.4 %copy-start.43 = (f32[2,512,1]{1,0,2:T(2,128)}, f32[2,512,1]{1,0,2:T(2,128)S(1)}, u32[]{:S(2)}) copy-start(f32[2,512,1]{1,0,2:T(2,128)S(1)} %get-tuple-element.595) | copy-start | bytes 12292
  217.5 4.5 %copy-start.39 = (f32[2,512,1]{1,0,2:T(2,128)}, f32[2,512,1]{1,0,2:T(2,128)S(1)}, u32[]{:S(2)}) copy-start(f32[2,512,1]{1,0,2:T(2,128)S(1)} %get-tuple-element.589) | copy-start | bytes 12292
  217.6 4.5 %copy-start.35 = (f32[2,512,1]{1,0,2:T(2,128)}, f32[2,512,1]{1,0,2:T(2,128)S(1)}, u32[]{:S(2)}) copy-start(f32[2,512,1]{1,0,2:T(2,128)S(1)} %get-tuple-element.583) | copy-start | bytes 12292
  217.6 4.5 %copy-start.31 = (f32[2,512,1]{1,0,2:T(2,128)}, f32[2,512,1]{1,0,2:T(2,128)S(1)}, u32[]{:S(2)}) copy-start(f32[2,512,1]{1,0,2:T(2,128)S(1)} %get-tuple-element.577) | copy-start | bytes 12292
  217.6 4.5 %copy-start.27 = (f32[2,512,1]{1,0,2:T(2,128)}, f32[2,512,1]{1,0,2:T(2,128)S(1)}, u32[]{:S(2)}) copy-start(f32[2,512,1]{1,0,2:T(2,128)S(1)} %get-tuple-element.571) | copy-start | bytes 12292
  217.6 4.6 %copy-start.23 = (f32[2,512,1]{1,0,2:T(2,128)}, f32[2,512,1]{1,0,2:T(2,128)S(1)}, u32[]{:S(2)}) copy-start(f32[2,512,1]{1,0,2:T(2,128)S(1)} %get-tuple-element.565) | copy-start | bytes 12292
  217.6 4.6 %copy-start.17 = (f32[2,512,1]{1,0,2:T(2,128)}, f32[2,512,1]{1,0,2:T(2,128)S(1)}, u32[]{:S(2)}) copy-start(f32[2,512,1]{1,0,2:T(2,128)S(1)} %get-tuple-element.559) | copy-start | bytes 12292
  217.6 4.6 %copy-start.11 = (f32[2,512,1]{1,0,2:T(2,128)}, f32[2,512,1]{1,0,2:T(2,128)S(1)}, u32[]{:S(2)}) copy-start(f32[2,512,1]{1,0,2:T(2,128)S(1)} %get-tuple-element.553) | copy-start | bytes 12292
  223.5 7.9 %collective-permute-start.20 = (f32[64,1,512]{2,0,1:T(8,128)}, f32[64,1,512]{2,0,1:T(8,128)}, u32[]{:S(2)}, u32[]{:S(2)}) collective-permute-start(f32[64,1,512]{2,0,1:T(8,128)} %get-tuple-element.754), channel_id=1, source_target_pairs={{1,0},{2,1},{3,2},{4,3},{5,4},{6,5},{7,6},{8,7},{9,8},{10,9},{11,1... | collective-permute-start | bytes 393224 | tf_op jit(solution)/shard_map/ppermute | solution.py:24
  225.4 9.2 %collective-permute-start.21 = (f32[64,1,512]{2,0,1:T(8,128)}, f32[64,1,512]{2,0,1:T(8,128)}, u32[]{:S(2)}, u32[]{:S(2)}) collective-permute-start(f32[64,1,512]{2,0,1:T(8,128)} %get-tuple-element.755), channel_id=1, source_target_pairs={{0,1},{1,2},{2,3},{3,4},{4,5},{5,6},{6,7},{7,8},{8,9},{9,10},{10,1... | collective-permute-start | bytes 393224 | tf_op jit(solution)/shard_map/ppermute | solution.py:22
  244.4 6.9 %collective-permute-start.22 = (f32[64,1,512]{2,1,0:T(1,128)S(1)}, f32[64,1,512]{2,1,0:T(1,128)S(1)}, u32[]{:S(2)}, u32[]{:S(2)}) collective-permute-start(f32[64,1,512]{2,1,0:T(1,128)S(1)} %get-tuple-element.690), channel_id=1, source_target_pairs={{1,0},{2,1},{3,2},{4,3},{5,4},{6,5},{7,6},{8,7},{9,8},{10,9},{11,1... | collective-permute-start | bytes 393224 | tf_op jit(solution)/shard_map/ppermute | solution.py:24
  246.3 8.1 %collective-permute-start.23 = (f32[64,1,512]{2,1,0:T(1,128)S(1)}, f32[64,1,512]{2,1,0:T(1,128)S(1)}, u32[]{:S(2)}, u32[]{:S(2)}) collective-permute-start(f32[64,1,512]{2,1,0:T(1,128)S(1)} %get-tuple-element.691), channel_id=1, source_target_pairs={{0,1},{1,2},{2,3},{3,4},{4,5},{5,6},{6,7},{7,8},{8,9},{9,10},{10,1... | collective-permute-start | bytes 393224 | tf_op jit(solution)/shard_map/ppermute | solution.py:22
  260.3 6.9 %collective-permute-start.24 = (f32[64,1,512]{2,1,0:T(1,128)S(1)}, f32[64,1,512]{2,1,0:T(1,128)S(1)}, u32[]{:S(2)}, u32[]{:S(2)}) collective-permute-start(f32[64,1,512]{2,1,0:T(1,128)S(1)} %get-tuple-element.686), channel_id=1, source_target_pairs={{1,0},{2,1},{3,2},{4,3},{5,4},{6,5},{7,6},{8,7},{9,8},{10,9},{11,1... | collective-permute-start | bytes 393224 | tf_op jit(solution)/shard_map/ppermute | solution.py:24
  262.2 8.1 %collective-permute-start.25 = (f32[64,1,512]{2,1,0:T(1,128)S(1)}, f32[64,1,512]{2,1,0:T(1,128)S(1)}, u32[]{:S(2)}, u32[]{:S(2)}) collective-permute-start(f32[64,1,512]{2,1,0:T(1,128)S(1)} %get-tuple-element.687), channel_id=1, source_target_pairs={{0,1},{1,2},{2,3},{3,4},{4,5},{5,6},{6,7},{7,8},{8,9},{9,10},{10,1... | collective-permute-start | bytes 393224 | tf_op jit(solution)/shard_map/ppermute | solution.py:22
  275.8 4.4 %collective-permute-start.26 = (f32[1,4,512]{2,1,0:T(4,128)S(1)}, f32[1,4,512]{2,1,0:T(4,128)S(1)}, u32[]{:S(2)}, u32[]{:S(2)}) collective-permute-start(f32[1,4,512]{2,1,0:T(4,128)S(1)} %get-tuple-element.790), channel_id=1, source_target_pairs={{16,0},{32,16},{48,32},{64,48},{80,64},{96,80},{112,96},{128,112},... | collective-permute-start | bytes 24584 | tf_op jit(solution)/shard_map/ppermute | solution.py:24
  277.7 15.9 %copy-start.5 = (f32[4,4,512]{2,1,0:T(4,128)S(1)}, f32[4,4,512]{2,1,0:T(4,128)}, u32[]{:S(2)}) copy-start(f32[4,4,512]{2,1,0:T(4,128)} %copy-done.3) | copy-start | bytes 98308
  277.8 7.1 %collective-permute-start.27 = (f32[1,4,512]{2,1,0:T(4,128)S(1)}, f32[1,4,512]{2,1,0:T(4,128)S(1)}, u32[]{:S(2)}, u32[]{:S(2)}) collective-permute-start(f32[1,4,512]{2,1,0:T(4,128)S(1)} %get-tuple-element.789), channel_id=1, source_target_pairs={{0,16},{16,32},{32,48},{48,64},{64,80},{80,96},{96,112},{112,128},... | collective-permute-start | bytes 24584 | tf_op jit(solution)/shard_map/ppermute | solution.py:22
  284.9 8.7 %copy-start.62 = (f32[512]{0:T(512)S(1)}, f32[512]{0:T(512)}, u32[]{:S(2)}) copy-start(f32[512]{0:T(512)} %copy-done.61) | copy-start | bytes 6148
  284.9 5.9 %collective-permute-start.28 = (f32[6,1,512]{2,1,0:T(1,128)S(1)}, f32[6,1,512]{2,1,0:T(1,128)S(1)}, u32[]{:S(2)}, u32[]{:S(2)}) collective-permute-start(f32[6,1,512]{2,1,0:T(1,128)S(1)} %get-tuple-element.781), channel_id=1, source_target_pairs={{1,0},{2,1},{3,2},{4,3},{5,4},{6,5},{7,6},{8,7},{9,8},{10,9},{11,1... | collective-permute-start | bytes 36872 | tf_op jit(solution)/shard_map/ppermute | solution.py:24
  286.8 6.8 %collective-permute-start.29 = (f32[6,1,512]{2,1,0:T(1,128)S(1)}, f32[6,1,512]{2,1,0:T(1,128)S(1)}, u32[]{:S(2)}, u32[]{:S(2)}) collective-permute-start(f32[6,1,512]{2,1,0:T(1,128)S(1)} %get-tuple-element.782), channel_id=1, source_target_pairs={{0,1},{1,2},{2,3},{3,4},{4,5},{5,6},{6,7},{7,8},{8,9},{9,10},{10,1... | collective-permute-start | bytes 36872 | tf_op jit(solution)/shard_map/ppermute | solution.py:22
  294.3 4.3 %collective-permute-start.30 = (f32[1,4,512]{2,1,0:T(4,128)S(1)}, f32[1,4,512]{2,1,0:T(4,128)S(1)}, u32[]{:S(2)}, u32[]{:S(2)}) collective-permute-start(f32[1,4,512]{2,1,0:T(4,128)S(1)} %get-tuple-element.788), channel_id=1, source_target_pairs={{16,0},{32,16},{48,32},{64,48},{80,64},{96,80},{112,96},{128,112},... | collective-permute-start | bytes 24584 | tf_op jit(solution)/shard_map/ppermute | solution.py:24
  296.2 7.1 %collective-permute-start.31 = (f32[1,4,512]{2,1,0:T(4,128)S(1)}, f32[1,4,512]{2,1,0:T(4,128)S(1)}, u32[]{:S(2)}, u32[]{:S(2)}) collective-permute-start(f32[1,4,512]{2,1,0:T(4,128)S(1)} %get-tuple-element.787), channel_id=1, source_target_pairs={{0,16},{16,32},{32,48},{48,64},{64,80},{80,96},{96,112},{112,128},... | collective-permute-start | bytes 24584 | tf_op jit(solution)/shard_map/ppermute | solution.py:22
  303.3 5.9 %collective-permute-start.32 = (f32[6,1,512]{2,1,0:T(1,128)S(1)}, f32[6,1,512]{2,1,0:T(1,128)S(1)}, u32[]{:S(2)}, u32[]{:S(2)}) collective-permute-start(f32[6,1,512]{2,1,0:T(1,128)S(1)} %get-tuple-element.779), channel_id=1, source_target_pairs={{1,0},{2,1},{3,2},{4,3},{5,4},{6,5},{7,6},{8,7},{9,8},{10,9},{11,1... | collective-permute-start | bytes 36872 | tf_op jit(solution)/shard_map/ppermute | solution.py:24
  305.2 6.8 %collective-permute-start.33 = (f32[6,1,512]{2,1,0:T(1,128)S(1)}, f32[6,1,512]{2,1,0:T(1,128)S(1)}, u32[]{:S(2)}, u32[]{:S(2)}) collective-permute-start(f32[6,1,512]{2,1,0:T(1,128)S(1)} %get-tuple-element.780), channel_id=1, source_target_pairs={{0,1},{1,2},{2,3},{3,4},{4,5},{5,6},{6,7},{7,8},{8,9},{9,10},{10,1... | collective-permute-start | bytes 36872 | tf_op jit(solution)/shard_map/ppermute | solution.py:22
  313.0 4.3 %collective-permute-start.34 = (f32[1,8,512]{2,1,0:T(8,128)S(1)}, f32[1,8,512]{2,1,0:T(8,128)S(1)}, u32[]{:S(2)}, u32[]{:S(2)}) collective-permute-start(f32[1,8,512]{2,1,0:T(8,128)S(1)} %get-tuple-element.772), channel_id=1, source_target_pairs={{16,0},{32,16},{48,32},{64,48},{80,64},{96,80},{112,96},{128,112},... | collective-permute-start | bytes 49160 | tf_op jit(solution)/shard_map/ppermute | solution.py:24
  314.9 7.2 %collective-permute-start.35 = (f32[1,8,512]{2,1,0:T(8,128)S(1)}, f32[1,8,512]{2,1,0:T(8,128)S(1)}, u32[]{:S(2)}, u32[]{:S(2)}) collective-permute-start(f32[1,8,512]{2,1,0:T(8,128)S(1)} %get-tuple-element.771), channel_id=1, source_target_pairs={{0,16},{16,32},{32,48},{48,64},{64,80},{80,96},{96,112},{112,128},... | collective-permute-start | bytes 49160 | tf_op jit(solution)/shard_map/ppermute | solution.py:22
  322.1 5.9 %collective-permute-start.36 = (f32[10,1,512]{2,1,0:T(1,128)S(1)}, f32[10,1,512]{2,1,0:T(1,128)S(1)}, u32[]{:S(2)}, u32[]{:S(2)}) collective-permute-start(f32[10,1,512]{2,1,0:T(1,128)S(1)} %get-tuple-element.761), channel_id=1, source_target_pairs={{1,0},{2,1},{3,2},{4,3},{5,4},{6,5},{7,6},{8,7},{9,8},{10,9},{11,1... | collective-permute-start | bytes 61448 | tf_op jit(solution)/shard_map/ppermute | solution.py:24
  324.0 6.9 %collective-permute-start.37 = (f32[10,1,512]{2,1,0:T(1,128)S(1)}, f32[10,1,512]{2,1,0:T(1,128)S(1)}, u32[]{:S(2)}, u32[]{:S(2)}) collective-permute-start(f32[10,1,512]{2,1,0:T(1,128)S(1)} %get-tuple-element.762), channel_id=1, source_target_pairs={{0,1},{1,2},{2,3},{3,4},{4,5},{5,6},{6,7},{7,8},{8,9},{9,10},{10,1... | collective-permute-start | bytes 61448 | tf_op jit(solution)/shard_map/ppermute | solution.py:22
  331.7 4.3 %collective-permute-start.38 = (f32[1,8,512]{2,1,0:T(8,128)S(1)}, f32[1,8,512]{2,1,0:T(8,128)S(1)}, u32[]{:S(2)}, u32[]{:S(2)}) collective-permute-start(f32[1,8,512]{2,1,0:T(8,128)S(1)} %get-tuple-element.770), channel_id=1, source_target_pairs={{16,0},{32,16},{48,32},{64,48},{80,64},{96,80},{112,96},{128,112},... | collective-permute-start | bytes 49160 | tf_op jit(solution)/shard_map/ppermute | solution.py:24
  333.7 7.2 %collective-permute-start.39 = (f32[1,8,512]{2,1,0:T(8,128)S(1)}, f32[1,8,512]{2,1,0:T(8,128)S(1)}, u32[]{:S(2)}, u32[]{:S(2)}) collective-permute-start(f32[1,8,512]{2,1,0:T(8,128)S(1)} %get-tuple-element.769), channel_id=1, source_target_pairs={{0,16},{16,32},{32,48},{48,64},{64,80},{80,96},{96,112},{112,128},... | collective-permute-start | bytes 49160 | tf_op jit(solution)/shard_map/ppermute | solution.py:22
  340.9 5.9 %collective-permute-start.40 = (f32[10,1,512]{2,1,0:T(1,128)S(1)}, f32[10,1,512]{2,1,0:T(1,128)S(1)}, u32[]{:S(2)}, u32[]{:S(2)}) collective-permute-start(f32[10,1,512]{2,1,0:T(1,128)S(1)} %get-tuple-element.759), channel_id=1, source_target_pairs={{1,0},{2,1},{3,2},{4,3},{5,4},{6,5},{7,6},{8,7},{9,8},{10,9},{11,1... | collective-permute-start | bytes 61448 | tf_op jit(solution)/shard_map/ppermute | solution.py:24
  342.8 6.9 %collective-permute-start.41 = (f32[10,1,512]{2,1,0:T(1,128)S(1)}, f32[10,1,512]{2,1,0:T(1,128)S(1)}, u32[]{:S(2)}, u32[]{:S(2)}) collective-permute-start(f32[10,1,512]{2,1,0:T(1,128)S(1)} %get-tuple-element.760), channel_id=1, source_target_pairs={{0,1},{1,2},{2,3},{3,4},{4,5},{5,6},{6,7},{7,8},{8,9},{9,10},{10,1... | collective-permute-start | bytes 61448 | tf_op jit(solution)/shard_map/ppermute | solution.py:22
  (167 other events, 196.3 us)
where the time goes:
time: 353 us; the launch traced here: 351 us
  blocking collectives  117 us (33%)
  starting transfers between devices  115 us (33%)
  waiting for transfers between devices  71.1 us (20%)
  other arithmetic  20.4 us (6%)
  local copies, waits for them, and re-layouts  12.1 us (3%)
  matrix products  11.6 us (3%)
  between operations  4 us (1%)
    ppermute x21, waiting for transfers between devices, extended(): lax.ppermute(tail, axis, [(i, (i + 1) % count) for i in range(ends)])  68.2 us
    ppermute x21, starting transfers between devices, extended(): lax.ppermute(tail, axis, [(i, (i + 1) % count) for i in range(ends)])  65.5 us
    ppermute x21, starting transfers between devices, extended(): lax.ppermute(head, axis, [((i + 1) % count, i) for i in range(ends)])  49.5 us
    all_gather x1, blocking collectives, body(): lax.all_gather(low4[0], 'liq', axis=0, tiled=True)  23.9 us
    all_gather x1, blocking collectives, body(): lax.all_gather(low4[3], 'liq', axis=0, tiled=True)  23.7 us
    all_gather x1, blocking collectives, body(): lax.all_gather(rhs_low, 'liq', axis=0, tiled=True)  23.5 us
    all_gather x1, blocking collectives, body(): lax.all_gather(low4[2], 'liq', axis=0, tiled=True)  23 us
    all_gather x1, blocking collectives, body(): lax.all_gather(low4[1], 'liq', axis=0, tiled=True)  22.8 us
  transfers between devices with their start and end apart: 42, of which 23 were waited for; matrix products, arithmetic and copies ran while one was open for 2% of the time, Pallas kernels for 0%

commit v1 on v0

v1 whole, which is shorter than its diff:
```python
import functools

import jax
import jax.numpy as jnp
from jax import lax
from jax.experimental import pallas as pl
from jax.experimental.pallas import tpu as pltpu
from jax.sharding import PartitionSpec as P

SWEEPS = 4
OMEGA = 0.8
DISCOUNT = 0.05
LANES = 128
F32 = jnp.float32
BF16 = jnp.bfloat16

Z = 4
TILE = 8


def first_half(shape):
    return lax.broadcasted_iota(jnp.int32, shape, len(shape) - 2) % TILE < Z


def swapped(x):
    return pltpu.roll(x.reshape(-1, TILE, LANES), Z, 1).reshape(x.shape)


def later(x):
    return pltpu.roll(x, x.shape[0] - Z, 0)


def earlier(x):
    return pltpu.roll(x, Z, 0)


def pair_sums(x):
    total = x + swapped(x)
    total = total.reshape(-1, 2, TILE, LANES)
    first, second = total[:, 0], total[:, 1]
    return jnp.where(first_half(first.shape), first, second).reshape(-1, LANES)


def doubled(x):
    other = swapped(x).reshape(-1, 1, TILE, LANES)
    x = x.reshape(-1, 1, TILE, LANES)
    mask = first_half(x.shape)
    pair = jnp.concatenate([jnp.where(mask, x, other), jnp.where(mask, other, x)], axis=1)
    return pair.reshape(-1, LANES)


def spread(outflow, rows):
    return jnp.concatenate([outflow] * (rows // TILE), axis=0)


def row(ref, a, width):
    return ref[pl.ds(a * width, width), :]


def product(wide, jhi_ref, jlo_ref):
    high = wide.astype(BF16)
    rest = (wide - high.astype(F32)).astype(BF16)
    dot = functools.partial(jnp.dot, preferred_element_type=F32)
    return dot(high, jhi_ref[...]) + (dot(high, jlo_ref[...]) + dot(rest, jhi_ref[...]))


def income(src, dst, pieces, jhi_ref, jlo_ref):
    wide = jnp.concatenate(
        [
            jnp.concatenate([src[pl.ds(s + c, n, stride=Z), :] for s, _, n in pieces], axis=0)
            for c in range(Z)
        ],
        axis=1,
    )
    result = product(wide, jhi_ref, jlo_ref)
    at = 0
    for _, d, n in pieces:
        for c in range(Z):
            dst[pl.ds(d + c, n, stride=Z), :] = result[at : at + n, c * LANES : (c + 1) * LANES]
        at += n


def rates_kernel(j_ref, jhi_ref, jlo_ref, out_ref):
    rates = j_ref[...]
    high = rates.astype(BF16)
    jhi_ref[...] = high
    jlo_ref[...] = (rates - high.astype(F32)).astype(BF16)
    total = jnp.sum(rates, axis=0, keepdims=True)
    for c in range(Z):
        piece = total[:, c * LANES : (c + 1) * LANES]
        out_ref[c : c + 1, :] = piece
        out_ref[c + Z : c + Z + 1, :] = piece


def pack_kernel(rhs, value, speed_a, speed_b, flag_a, flag_b, lo_ref, hi_ref):
    half = lo_ref.shape[2] // Z
    for a in range(rhs.shape[0]):
        up_a = flag_a[a].astype(F32)
        up_b = flag_b[a].astype(F32)
        fields = (
            value[a],
            rhs[a],
            speed_a[a] * up_a,
            speed_a[a] * (1.0 - up_a),
            speed_b[a] * up_b,
            speed_b[a] * (1.0 - up_b),
        )
        for k, x in enumerate(fields):
            for c in range(Z):
                piece = x[:, c * LANES : (c + 1) * LANES]
                lo_ref[k, a, pl.ds(c, half, stride=Z), :] = piece[:half]
                hi_ref[k, a, pl.ds(c, half, stride=Z), :] = piece[half:]


def widen_kernel(lo, hi, below, above, first_ref, second_ref):
    width = lo.shape[2]
    for out, start in ((first_ref, 0), (second_ref, 4)):
        for i, src in enumerate((below, lo, hi, above)):
            out[:, :, i * width : (i + 1) * width, :] = src[:, start : start + 4]


def fine_kernel(
    below, first, second, above, jhi, jlo, out,
    fine_ref, val_ref, rlo_ref, rhi_ref, mid_ref, low_ref, v0, v1, inc, res,
):
    outflow = spread(out[...], 64)
    for a in range(16):
        src = (below, first, second, above)[a // 4]
        here = pl.ds(64 * a, 64)
        v0[here, :] = src[0, a % 4]
        total = DISCOUNT + outflow
        for k in range(1, 6):
            x = src[k, a % 4]
            fine_ref[k - 1, here, :] = x
            if k > 1:
                total = total + x
        fine_ref[5, here, :] = OMEGA / total

    def applied(src, a):
        here = pl.ds(64 * a, 64)
        center = src[here, :]
        total = fine_ref[0, here, :] + inc[here, :]
        total = total + fine_ref[1, here, :] * row(src, a + 1, 64)
        total = total + fine_ref[2, here, :] * row(src, a - 1, 64)
        total = total + fine_ref[3, here, :] * later(center)
        total = total + fine_ref[4, here, :] * earlier(center)
        return center, total

    def sweep(src, dst, begin, end):
        income(src, inc, [(64 * begin, 64 * begin, 16 * (end - begin))], jhi, jlo)
        for a in range(begin, end):
            center, total = applied(src, a)
            here = pl.ds(64 * a, 64)
            dst[here, :] = (1.0 - OMEGA) * center + fine_ref[5, here, :] * total

    sweep(v0, v1, 1, 15)
    sweep(v1, val_ref, 2, 14)
    income(val_ref, inc, [(64 * 4, 64 * 4, 16 * 8)], jhi, jlo)

    def residual(a):
        center, total = applied(val_ref, a)
        here = pl.ds(64 * a, 64)
        diag = DISCOUNT + outflow
        for k in range(1, 5):
            diag = diag + fine_ref[k, here, :]
        return (total - diag * center)[16:48]

    for m in range(4):
        coarse = 0.25 * pair_sums(residual(4 + 2 * m) + residual(5 + 2 * m))
        rlo_ref[pl.ds(8 * m, 8), :] = coarse[:8]
        rhi_ref[pl.ds(8 * m, 8), :] = coarse[8:]

    outflow = spread(out[...], 32)
    for m in range(8):
        here = pl.ds(32 * m, 32)
        total = DISCOUNT + outflow
        for k in range(4):
            both = fine_ref[k + 1, pl.ds(128 * m, 64), :] + fine_ref[k + 1, pl.ds(128 * m + 64, 64), :]
            x = 0.125 * pair_sums(both)
            mid_ref[k, here, :] = x
            total = total + x
        mid_ref[4, here, :] = OMEGA / total
    for k in range(4):
        for m in range(2):
            at = 32 * (2 + 2 * m) + 8
            both = mid_ref[k, pl.ds(at, 16), :] + mid_ref[k, pl.ds(at + 32, 16), :]
            low_ref[k, pl.ds(8 * m, 8), :] = 0.125 * pair_sums(both)


def widen_mid_kernel(lo, hi, below, above, first_ref, second_ref):
    for m in range(4):
        out = (first_ref, second_ref)[m // 2]
        for i, src in enumerate((below, lo, hi, above)):
            out[pl.ds(32 * (m % 2) + 8 * i, 8), :] = src[pl.ds(8 * m, 8), :]


def mid_kernel(
    below, first, second, above, mid, low, jhi, jlo, out, pay_ref, err_ref, rhs_ref, e0, e1, inc
):
    for i, src in enumerate((below, first, second, above)):
        rhs_ref[pl.ds(64 * i, 64), :] = src[...]
    e0[...] = mid[4] * rhs_ref[...]

    def applied(src, a):
        here = pl.ds(32 * a, 32)
        center = src[here, :]
        total = rhs_ref[here, :] + inc[here, :]
        total = total + mid[0, here, :] * row(src, a + 1, 32)
        total = total + mid[1, here, :] * row(src, a - 1, 32)
        total = total + mid[2, here, :] * later(center)
        total = total + mid[3, here, :] * earlier(center)
        return center, total

    income(e0, inc, [(32, 32, 8 * 6)], jhi, jlo)
    for a in range(1, 7):
        center, total = applied(e0, a)
        here = pl.ds(32 * a, 32)
        e1[here, :] = (1.0 - OMEGA) * center + mid[4, here, :] * total
    income(e1, inc, [(64, 64, 8 * 4)], jhi, jlo)
    outflow = spread(out[...], 32)

    def residual(a):
        center, total = applied(e1, a)
        here = pl.ds(32 * a, 32)
        diag = DISCOUNT + outflow
        for k in range(4):
            diag = diag + mid[k, here, :]
        return (total - diag * center)[8:24]

    for m in range(2):
        pay_ref[pl.ds(8 * m, 8), :] = 0.25 * pair_sums(residual(2 + 2 * m) + residual(3 + 2 * m))
    for k in range(4):
        pay_ref[pl.ds(16 * (k + 1), 16), :] = low[k]
    for a in range(4):
        err_ref[pl.ds(16 * a, 16), :] = e1[pl.ds(32 * (a + 2) + 8, 16), :]


def solve_lines(target, weight, carry, link, middle, y, x_ref, offset):
    count = y.shape[0] // TILE
    half = count // 2
    top = bottom = None
    for i in range(half):
        j = count - 1 - i
        t = weight(i) * target(i)
        u = weight(j) * target(j)
        top = t if i == 0 else t + carry(i) * top
        bottom = u if i == 0 else u + carry(j) * bottom
        if i < half - 1:
            y[pl.ds(TILE * i, TILE), :] = top
            y[pl.ds(TILE * j, TILE), :] = bottom
    head = (top + link(half - 1) * bottom) * middle
    tail = bottom + link(half) * head
    for i in range(half - 1, -1, -1):
        j = count - 1 - i
        if i < half - 1:
            head = row(y, i, TILE) + link(i) * head
            tail = row(y, j, TILE) + link(j) * tail
        x_ref[pl.ds(offset + TILE * i, TILE), :] = head
        x_ref[pl.ds(offset + TILE * j, TILE), :] = tail


def send_lines(e, lo_ref, hi_ref):
    pairs = e[...].reshape(-1, 2, TILE, LANES)
    first, second = pairs[:, 0], pairs[:, 1]
    mask = first_half(first.shape)
    lo_ref[...] = jnp.where(mask, first, pltpu.roll(second, Z, 1)).reshape(-1, LANES)
    hi_ref[...] = jnp.where(mask, pltpu.roll(first, Z, 1), second).reshape(-1, LANES)


def first_solve_kernel(gathered, out, fac_ref, middle_ref, e_ref, lo_ref, hi_ref, y):
    count = e_ref.shape[0] // TILE
    half = count // 2

    def part(k, a):
        return gathered[pl.ds(80 * (a // 2) + 16 * k + 8 * (a % 2), TILE), :]

    outflow = DISCOUNT + out[...]
    gaps = [None, None]
    links = [None, None]
    for i in range(half):
        for side, a in ((0, i), (1, count - 1 - i)):
            here = pl.ds(TILE * a, TILE)
            inner, outer = (part(1, a), part(2, a)) if side == 0 else (part(2, a), part(1, a))
            fb, bb = part(3, a), part(4, a)
            slack = outflow + fb + bb
            slack = slack + (outer if i == 0 else outer * gaps[side])
            weight = 1.0 / (slack + inner)
            links[side] = inner * weight
            gaps[side] = slack * weight
            fac_ref[0, here, :] = part(0, a)
            fac_ref[1, here, :] = fb
            fac_ref[2, here, :] = bb
            fac_ref[3, here, :] = weight
            fac_ref[4, here, :] = outer * weight
            fac_ref[5, here, :] = links[side]
    middle_ref[...] = 1.0 / (gaps[0] + links[0] * gaps[1])
    solve_lines(
        lambda a: row(fac_ref.at[0], a, TILE),
        lambda a: row(fac_ref.at[3], a, TILE),
        lambda a: row(fac_ref.at[4], a, TILE),
        lambda a: row(fac_ref.at[5], a, TILE),
        middle_ref[...], y, e_ref, 0,
    )
    send_lines(e_ref, lo_ref, hi_ref)


def local_target_kernel(e, fac, jhi, jlo, t_ref):
    income(e, t_ref, [(0, 0, e.shape[0] // Z)], jhi, jlo)
    other = swapped(e[...])
    mask = first_half(other.shape)
    t_ref[...] = t_ref[...] + fac[0] + jnp.where(mask, fac[1], fac[2]) * other


def swept(t, fac, middle, below, above, y, x_ref, offset):
    mask = first_half((TILE, LANES))

    def target(a):
        low_side, high_side = row(below, a // 2, TILE), row(above, a // 2, TILE)
        if a % 2:
            low_side = pltpu.roll(low_side, Z, 0)
        else:
            high_side = pltpu.roll(high_side, Z, 0)
        near = jnp.where(mask, low_side, high_side)
        coupling = jnp.where(mask, row(fac.at[2], a, TILE), row(fac.at[1], a, TILE))
        return row(t, a, TILE) + coupling * near

    solve_lines(
        target,
        lambda a: row(fac.at[3], a, TILE),
        lambda a: row(fac.at[4], a, TILE),
        lambda a: row(fac.at[5], a, TILE),
        middle[...], y, x_ref, offset,
    )


def sweep_kernel(t, fac, middle, below, above, e_ref, lo_ref, hi_ref, y):
    swept(t, fac, middle, below, above, y, e_ref, 0)
    send_lines(e_ref, lo_ref, hi_ref)


def last_sweep_kernel(place, t, fac, middle, below, above, err, err_lo, err_hi, sum_ref, y, x):
    edge = 2 * TILE
    x[0:edge, :] = jnp.zeros((edge, LANES), F32)
    x[pl.ds(x.shape[0] - edge, edge), :] = jnp.zeros((edge, LANES), F32)
    swept(t, fac, middle, below, above, y, x, edge)
    start = place[0] * 2 * TILE
    for i in range(6):
        low = x[pl.ds(pl.multiple_of(start + i * TILE, TILE), TILE), :]
        fill = doubled(low)
        for m in (2 * i, 2 * i + 1):
            src = (err_lo, err, err_hi)[m // 4]
            sum_ref[pl.ds(16 * m, 16), :] = src[pl.ds(16 * (m % 4), 16), :] + fill


def last_kernel(
    own, below, above, mid, rhs_mid, fine, val, jhi, jlo, out_ref, ev, e1, e2, v0, v1, v2, inc
):
    for a in range(12):
        for i, src in enumerate((below, own, above)):
            ev[pl.ds(48 * a + 16 * i, 16), :] = src[pl.ds(16 * a, 16), :]

    income(ev, inc, [(48 * (a + 2) + 8, 32 * a, 8) for a in range(8)], jhi, jlo)
    for a in range(8):
        here = pl.ds(32 * a, 32)
        center = row(ev, a + 2, 48)
        total = rhs_mid[here, :] + inc[here, :]
        total = total + mid[0, here, :] * ev[pl.ds(48 * (a + 3) + 8, 32), :]
        total = total + mid[1, here, :] * ev[pl.ds(48 * (a + 1) + 8, 32), :]
        total = total + mid[2, here, :] * later(center)[8:40]
        total = total + mid[3, here, :] * earlier(center)[8:40]
        e1[here, :] = (1.0 - OMEGA) * center[8:40] + mid[4, here, :] * total

    income(e1, inc, [(32, 32, 8 * 6)], jhi, jlo)
    for a in range(1, 7):
        here = pl.ds(32 * a, 32)
        center = e1[here, :]
        total = rhs_mid[here, :] + inc[here, :]
        total = total + mid[0, here, :] * row(e1, a + 1, 32)
        total = total + mid[1, here, :] * row(e1, a - 1, 32)
        total = total + mid[2, here, :] * later(center)
        total = total + mid[3, here, :] * earlier(center)
        error = (1.0 - OMEGA) * center + mid[4, here, :] * total
        fill = doubled(error)
        for f in (2 * a, 2 * a + 1):
            v0[pl.ds(64 * f, 64), :] = val[pl.ds(64 * f, 64), :] + fill

    def sweep(src, dst, begin, end):
        income(src, inc, [(64 * begin, 64 * begin, 16 * (end - begin))], jhi, jlo)
        for a in range(begin, end):
            here = pl.ds(64 * a, 64)
            center = src[here, :]
            total = fine[0, here, :] + inc[here, :]
            total = total + fine[1, here, :] * row(src, a + 1, 64)
            total = total + fine[2, here, :] * row(src, a - 1, 64)
            total = total + fine[3, here, :] * later(center)
            total = total + fine[4, here, :] * earlier(center)
            dst[here, :] = (1.0 - OMEGA) * center + fine[5, here, :] * total

    sweep(v0, v1, 3, 13)
    sweep(v1, v2, 4, 12)
    for a in range(8):
        for c in range(Z):
            piece = v2[pl.ds(64 * (a + 4) + 16 + c, 8, stride=Z), :]
            out_ref[a, :, c * LANES : (c + 1) * LANES] = piece


def call(kernel, args, outs, scratch=(), flops=0, smem=0, limit=32):
    outs = [jax.ShapeDtypeStruct(*o) if isinstance(o, tuple) and isinstance(o[0], tuple) else jax.ShapeDtypeStruct(o, F32) for o in outs]
    spec = pl.BlockSpec(memory_space=pltpu.VMEM)
    moved = sum(x.size * x.dtype.itemsize for x in (*args, *outs))
    return pl.pallas_call(
        kernel,
        out_shape=outs,
        in_specs=[pl.BlockSpec(memory_space=pltpu.SMEM)] * smem + [spec] * (len(args) - smem),
        out_specs=[spec] * len(outs),
        scratch_shapes=[pltpu.VMEM(s, F32) for s in scratch],
        compiler_params=pltpu.CompilerParams(vmem_limit_bytes=limit * 2**20),
        cost_estimate=pl.CostEstimate(flops=flops, bytes_accessed=moved, transcendentals=0),
    )(*args)


def neighbours(lo, hi, axis):
    count = lax.axis_size(axis)
    below = lax.ppermute(hi, axis, [(i, i + 1) for i in range(count - 1)])
    above = lax.ppermute(lo, axis, [(i + 1, i) for i in range(count - 1)])
    return below, above


def body(right_side, value_guess, speed_liq, speed_ill, flag_liq, flag_ill, jump_rates):
    nz = jump_rates.shape[0]
    dot_flops = 2 * 3 * nz * nz
    half = (6, 8, 16, LANES)
    lo, hi = call(
        pack_kernel,
        (right_side, value_guess, speed_liq, speed_ill, flag_liq, flag_ill),
        [half, half],
    )
    jhi, jlo, out = call(
        rates_kernel, (jump_rates,), [((nz, nz), BF16), ((nz, nz), BF16), (TILE, LANES)]
    )
    below, above = neighbours(lo, hi, "ill")
    wide = (6, 4, 64, LANES)
    first, second = call(widen_kernel, (lo, hi, below, above), [wide, wide])
    below, above = neighbours(first, second, "liq")
    whole = (1024, LANES)
    fine, value, rlo, rhi, mid, low = call(
        fine_kernel,
        (below, first, second, above, jhi, jlo, out),
        [(6, 1024, LANES), whole, (32, LANES), (32, LANES), (5, 256, LANES), (4, 16, LANES)],
        [whole] * 4,
        flops=dot_flops * 550,
    )
    below, above = neighbours(rlo, rhi, "ill")
    first, second = call(widen_mid_kernel, (rlo, rhi, below, above), [(64, LANES)] * 2)
    below, above = neighbours(first, second, "liq")
    payload, error_mid, rhs_mid = call(
        mid_kernel,
        (below, first, second, above, mid, low, jhi, jlo, out),
        [(80, LANES), (64, LANES), (256, LANES)],
        [(256, LANES)] * 3,
        flops=dot_flops * 80,
    )
    err_lo, err_hi = neighbours(error_mid, error_mid, "liq")
    gathered = lax.all_gather(payload, "liq", axis=0, tiled=True)
    lines = gathered.shape[0] // 80 * 2 * TILE
    line, message = (lines, LANES), (lines // 2, LANES)
    fac, middle, e, lo, hi = call(
        first_solve_kernel, (gathered, out), [(6, *line), (TILE, LANES), line, message, message], [line]
    )
    for step in range(SWEEPS - 1):
        below, above = neighbours(lo, hi, "ill")
        (target,) = call(
            local_target_kernel, (e, fac, jhi, jlo), [line], flops=dot_flops * lines // Z
        )
        if step < SWEEPS - 2:
            e, lo, hi = call(
                sweep_kernel, (target, fac, middle, below, above), [line, message, message], [line]
            )
    place = lax.axis_index("liq").astype(jnp.int32).reshape(1)
    (total,) = call(
        last_sweep_kernel,
        (place, target, fac, middle, below, above, error_mid, err_lo, err_hi),
        [(192, LANES)],
        [line, (lines + 4 * TILE, LANES)],
        smem=1,
    )
    below, above = neighbours(total, total, "ill")
    (result,) = call(
        last_kernel,
        (total, below, above, mid, rhs_mid, fine, value, jhi, jlo),
        [right_side.shape],
        [(576, LANES), (256, LANES), (256, LANES), whole, whole, whole, whole],
        flops=dot_flops * 400,
    )
    return result


def solution(mesh):
    block = P("liq", "ill", None)
    return jax.shard_map(
        body, mesh=mesh, in_specs=(block,) * 6 + (P(),), out_specs=block, check_vma=False
    )
```

time: 353 us -> 197 us (0.56)
  the two profiles are of different devices: /device:TPU:400 before, /device:TPU:103 now
where the time goes in v1:
time: 197 us
  waiting for transfers between devices  108 us (55%)
  starting transfers between devices  54.6 us (28%)
  between operations  13.7 us (7%)
  Pallas kernels  10.3 us (5%)
  local copies, waits for them, and re-layouts  9.93 us (5%)
    all_gather x1, waiting for transfers between devices, body(): gathered = lax.all_gather(payload, 'liq', axis=0, tiled=True)  57.4 us
    ppermute x9, waiting for transfers between devices, neighbours(): above = lax.ppermute(lo, axis, [(i + 1, i) for i in range(count - 1)])  37.9 us
    ppermute x9, starting transfers between devices, neighbours(): below = lax.ppermute(hi, axis, [(i, i + 1) for i in range(count - 1)])  34.9 us
    ppermute x9, starting transfers between devices, neighbours(): above = lax.ppermute(lo, axis, [(i + 1, i) for i in range(count - 1)])  19.7 us
    ppermute x9, waiting for transfers between devices, neighbours(): below = lax.ppermute(hi, axis, [(i, i + 1) for i in range(count - 1)])  12.9 us
    pallas_call x14, Pallas kernels, call(): pl.pallas_call(kernel, out_shape=outs, in_specs=[pl.BlockSpec(memory_spac...  10.3 us
    unnamed x28, local copies, waits for them, and re-layouts  9.93 us
  transfers between devices with their start and end apart: 19, of which 12 were waited for; matrix products, arithmetic and copies ran while one was open for 0% of the time, Pallas kernels for 1%

profile of v1, /device:TPU:103, one launch (start us, length us, event | category | flops | bytes accessed | tf_op | source)
XLA Modules:
  0.0 196.7 jit_solution(7852218473168114817)
XLA Ops:
  6.5 0.0 all-gather.2.cloned.1.call-start
  6.5 1.0 copy-done.8
  7.5 0.9 copy-done.9
  8.4 0.9 copy-done.10
  9.3 0.9 copy-done.11
  10.2 0.9 copy-done.12
  11.2 0.9 copy-done.13
  12.1 0.1 shard_map.73
  12.2 4.8 %collective-permute-start = (f32[6,8,16,128]{3,2,1,0:T(8,128)S(1)}, f32[6,8,16,128]{3,2,1,0:T(8,128)S(1)}, u32[]{:S(2)}, u32[]{:S(2)}) collective-permute-start(f32[6,8,16,128]{3,2,1,0:T(8,128)S(1)} %get-tuple-element.35.hi), channel_id=1, source_target_pairs={{0,1},{1,2},{2,3},{3,4},{4,5},{5,6},{6,7},{7,8},{8,9},{9,10},{10,1... | collective-permute-start | bytes 1179656 | tf_op jit(solution)/shard_map/ppermute | solution.py:424
  17.0 1.9 collective-permute-start.1
  18.9 5.8 %collective-permute-done.below = f32[6,8,16,128]{3,2,1,0:T(8,128)S(1)} collective-permute-done((f32[6,8,16,128]{3,2,1,0:T(8,128)S(1)}, f32[6,8,16,128]{3,2,1,0:T(8,128)S(1)}, u32[]{:S(2)}, u32[]{:S(2)}) %collective-permute-start) | collective-permute-done | bytes 393248 | tf_op jit(solution)/shard_map/ppermute | solution.py:424
  24.7 5.0 %collective-permute-done.1.above = f32[6,8,16,128]{3,2,1,0:T(8,128)S(1)} collective-permute-done((f32[6,8,16,128]{3,2,1,0:T(8,128)S(1)}, f32[6,8,16,128]{3,2,1,0:T(8,128)S(1)}, u32[]{:S(2)}, u32[]{:S(2)}) %collective-permute-start.1) | collective-permute-done | bytes 393248 | tf_op jit(solution)/shard_map/ppermute | solution.py:425
  29.7 0.1 shard_map.74
  29.8 4.9 %collective-permute-start.2 = (f32[6,4,64,128]{3,2,1,0:T(8,128)S(1)}, f32[6,4,64,128]{3,2,1,0:T(8,128)S(1)}, u32[]{:S(2)}, u32[]{:S(2)}) collective-permute-start(f32[6,4,64,128]{3,2,1,0:T(8,128)S(1)} %get-tuple-element.36.second), channel_id=1, source_target_pairs={{0,16},{16,32},{32,48},{48,64},{64,80},{80,96},{96,112},{112,128},... | collective-permute-start | bytes 2359304 | tf_op jit(solution)/shard_map/ppermute | solution.py:424
  34.7 1.9 collective-permute-start.3
  36.6 0.0 copy-done.3
  36.7 0.2 shard_map.75
  36.8 6.8 %collective-permute-done.2.below = f32[6,4,64,128]{3,2,1,0:T(8,128)S(1)} collective-permute-done((f32[6,4,64,128]{3,2,1,0:T(8,128)S(1)}, f32[6,4,64,128]{3,2,1,0:T(8,128)S(1)}, u32[]{:S(2)}, u32[]{:S(2)}) %collective-permute-start.2) | collective-permute-done | bytes 786464 | tf_op jit(solution)/shard_map/ppermute | solution.py:424
  43.6 6.5 %collective-permute-done.3.above = f32[6,4,64,128]{3,2,1,0:T(8,128)S(1)} collective-permute-done((f32[6,4,64,128]{3,2,1,0:T(8,128)S(1)}, f32[6,4,64,128]{3,2,1,0:T(8,128)S(1)}, u32[]{:S(2)}, u32[]{:S(2)}) %collective-permute-start.3) | collective-permute-done | bytes 786464 | tf_op jit(solution)/shard_map/ppermute | solution.py:425
  50.1 2.2 %shard_map.76 = (f32[6,1024,128]{2,1,0:T(8,128)S(1)}, f32[1024,128]{1,0:T(8,128)S(1)}, f32[32,128]{1,0:T(8,128)S(1)}, f32[32,128]{1,0:T(8,128)S(1)}, f32[5,256,1...) custom-call(f32[6,4,64,128]{3,2,1,0:T(8,128)S(1)} %collective-permute-done.2.below, ...), custom_call_target="tpu_custom_call" | custom-call | flops 865075200 | bytes 8589312 | tf_op jit(solution)/shard_map/pallas_call | solution.py:411
  52.3 1.6 copy-done
  54.0 0.8 copy-done.4
  54.8 2.5 %collective-permute-start.4 = (f32[32,128]{1,0:T(8,128)S(1)}, f32[32,128]{1,0:T(8,128)S(1)}, u32[]{:S(2)}, u32[]{:S(2)}) collective-permute-start(f32[32,128]{1,0:T(8,128)S(1)} %get-tuple-element.42.hi), channel_id=1, source_target_pairs={{0,1},{1,2},{2,3},{3,4},{4,5},{5,6},{6,7},{7,8},{8,9},{9,10},{10,1... | collective-permute-start | bytes 49160 | tf_op jit(solution)/shard_map/ppermute | solution.py:424
  57.3 2.8 %collective-permute-start.5 = (f32[32,128]{1,0:T(8,128)S(1)}, f32[32,128]{1,0:T(8,128)S(1)}, u32[]{:S(2)}, u32[]{:S(2)}) collective-permute-start(f32[32,128]{1,0:T(8,128)S(1)} %get-tuple-element.41.lo), channel_id=1, source_target_pairs={{1,0},{2,1},{3,2},{4,3},{5,4},{6,5},{7,6},{8,7},{9,8},{10,9},{11,1... | collective-permute-start | bytes 49160 | tf_op jit(solution)/shard_map/ppermute | solution.py:425
  60.0 0.0 collective-permute-done.4.below
  60.1 2.9 %collective-permute-done.5.above = f32[32,128]{1,0:T(8,128)S(1)} collective-permute-done((f32[32,128]{1,0:T(8,128)S(1)}, f32[32,128]{1,0:T(8,128)S(1)}, u32[]{:S(2)}, u32[]{:S(2)}) %collective-permute-start.5) | collective-permute-done | bytes 16416 | tf_op jit(solution)/shard_map/ppermute | solution.py:425
  63.0 3.2 %collective-permute-start.6 = (f32[64,128]{1,0:T(8,128)S(1)}, f32[64,128]{1,0:T(8,128)S(1)}, u32[]{:S(2)}, u32[]{:S(2)}) collective-permute-start(f32[64,128]{1,0:T(8,128)S(1)} %get-tuple-element.43.second), channel_id=1, source_target_pairs={{0,16},{16,32},{32,48},{48,64},{64,80},{80,96},{96,112},{112,128},... | collective-permute-start | bytes 98312 | tf_op jit(solution)/shard_map/ppermute | solution.py:424
  66.1 1.9 collective-permute-start.7
  68.1 0.0 collective-permute-done.6.below
  68.1 5.4 %collective-permute-done.7.above = f32[64,128]{1,0:T(8,128)S(1)} collective-permute-done((f32[64,128]{1,0:T(8,128)S(1)}, f32[64,128]{1,0:T(8,128)S(1)}, u32[]{:S(2)}, u32[]{:S(2)}) %collective-permute-start.7) | collective-permute-done | bytes 32800 | tf_op jit(solution)/shard_map/ppermute | solution.py:425
  73.5 1.4 shard_map.78
  74.9 0.6 copy-done.6
  75.5 0.0 all-gather.2.cloned.1.call-update
  75.5 57.4 %all-gather.2.cloned.1.call-done.gathered = f32[2560,128]{1,0:T(8,128)} async-done(((f32[80,128]{1,0:T(8,128)}), f32[2560,128]{1,0:T(8,128)}) %all-gather.2.cloned.1.call-update) | async-done | bytes 1310736 | tf_op jit(solution)/shard_map/all_gather | solution.py:464
  132.9 1.3 copy-done.2
  134.2 0.4 shard_map.79
  134.7 4.4 %collective-permute-start.8 = (f32[256,128]{1,0:T(8,128)S(1)}, f32[256,128]{1,0:T(8,128)S(1)}, u32[]{:S(2)}, u32[]{:S(2)}) collective-permute-start(f32[256,128]{1,0:T(8,128)S(1)} %get-tuple-element.51), channel_id=1, source_target_pairs={{0,1},{1,2},{2,3},{3,4},{4,5},{5,6},{6,7},{7,8},{8,9},{9,10},{10,1... | collective-permute-start | bytes 393224 | tf_op jit(solution)/shard_map/ppermute | solution.py:424
  139.1 1.9 collective-permute-start.9
  141.0 0.4 shard_map.80.t
  141.4 0.3 collective-permute-done.8.below
  141.7 5.0 %collective-permute-done.9.above = f32[256,128]{1,0:T(8,128)S(1)} collective-permute-done((f32[256,128]{1,0:T(8,128)S(1)}, f32[256,128]{1,0:T(8,128)S(1)}, u32[]{:S(2)}, u32[]{:S(2)}) %collective-permute-start.9) | collective-permute-done | bytes 131104 | tf_op jit(solution)/shard_map/ppermute | solution.py:425
  146.7 0.2 shard_map.81
  146.9 2.0 %collective-permute-start.10 = (f32[256,128]{1,0:T(8,128)S(1)}, f32[256,128]{1,0:T(8,128)S(1)}, u32[]{:S(2)}, u32[]{:S(2)}) collective-permute-start(f32[256,128]{1,0:T(8,128)S(1)} %get-tuple-element.54), channel_id=1, source_target_pairs={{0,1},{1,2},{2,3},{3,4},{4,5},{5,6},{6,7},{7,8},{8,9},{9,10},{10,1... | collective-permute-start | bytes 393224 | tf_op jit(solution)/shard_map/ppermute | solution.py:424
  148.9 3.3 %collective-permute-start.11 = (f32[256,128]{1,0:T(8,128)S(1)}, f32[256,128]{1,0:T(8,128)S(1)}, u32[]{:S(2)}, u32[]{:S(2)}) collective-permute-start(f32[256,128]{1,0:T(8,128)S(1)} %get-tuple-element.55), channel_id=1, source_target_pairs={{1,0},{2,1},{3,2},{4,3},{5,4},{6,5},{7,6},{8,7},{9,8},{10,9},{11,1... | collective-permute-start | bytes 393224 | tf_op jit(solution)/shard_map/ppermute | solution.py:425
  152.2 0.4 shard_map.82.t
  152.6 0.0 collective-permute-done.10.below
  152.6 3.2 %collective-permute-done.11.above = f32[256,128]{1,0:T(8,128)S(1)} collective-permute-done((f32[256,128]{1,0:T(8,128)S(1)}, f32[256,128]{1,0:T(8,128)S(1)}, u32[]{:S(2)}, u32[]{:S(2)}) %collective-permute-start.11) | collective-permute-done | bytes 131104 | tf_op jit(solution)/shard_map/ppermute | solution.py:425
  155.8 0.9 shard_map.83
  156.7 3.1 %collective-permute-start.12 = (f32[256,128]{1,0:T(8,128)}, f32[256,128]{1,0:T(8,128)}, u32[]{:S(2)}, u32[]{:S(2)}) collective-permute-start(f32[256,128]{1,0:T(8,128)} %get-tuple-element.57), channel_id=1, source_target_pairs={{0,1},{1,2},{2,3},{3,4},{4,5},{5,6},{6,7},{7,8},{8,9},{9,10},{10,1... | collective-permute-start | bytes 393224 | tf_op jit(solution)/shard_map/ppermute | solution.py:424
  159.8 2.1 %collective-permute-start.13 = (f32[256,128]{1,0:T(8,128)}, f32[256,128]{1,0:T(8,128)}, u32[]{:S(2)}, u32[]{:S(2)}) collective-permute-start(f32[256,128]{1,0:T(8,128)} %get-tuple-element.58), channel_id=1, source_target_pairs={{1,0},{2,1},{3,2},{4,3},{5,4},{6,5},{7,6},{8,7},{9,8},{10,9},{11,1... | collective-permute-start | bytes 393224 | tf_op jit(solution)/shard_map/ppermute | solution.py:425
  161.9 6.3 %collective-permute-start.14 = (f32[64,128]{1,0:T(8,128)}, f32[64,128]{1,0:T(8,128)}, u32[]{:S(2)}, u32[]{:S(2)}) collective-permute-start(f32[64,128]{1,0:T(8,128)} %get-tuple-element.59.err), channel_id=1, source_target_pairs={{0,16},{16,32},{32,48},{48,64},{64,80},{80,96},{96,112},{112,128},... | collective-permute-start | bytes 98312 | tf_op jit(solution)/shard_map/ppermute | solution.py:424
  168.3 1.9 collective-permute-start.15
  170.2 0.4 shard_map.84.t
  170.7 0.0 collective-permute-done.14.err_lo
  170.7 5.3 %collective-permute-done.15.err_hi = f32[64,128]{1,0:T(8,128)} collective-permute-done((f32[64,128]{1,0:T(8,128)}, f32[64,128]{1,0:T(8,128)}, u32[]{:S(2)}, u32[]{:S(2)}) %collective-permute-start.15) | collective-permute-done | bytes 32800 | tf_op jit(solution)/shard_map/ppermute | solution.py:425
  175.9 0.0 collective-permute-done.12.below
  176.0 0.0 collective-permute-done.13.above
  176.0 1.2 shard_map.85.own
  177.1 3.8 %collective-permute-start.16 = (f32[192,128]{1,0:T(8,128)S(1)}, f32[192,128]{1,0:T(8,128)S(1)}, u32[]{:S(2)}, u32[]{:S(2)}) collective-permute-start(f32[192,128]{1,0:T(8,128)S(1)} %shard_map.85.own), channel_id=1, source_target_pairs={{0,1},{1,2},{2,3},{3,4},{4,5},{5,6},{6,7},{7,8},{8,9},{9,10},{10,1... | collective-permute-start | bytes 294920 | tf_op jit(solution)/shard_map/ppermute | solution.py:424
  180.9 1.9 collective-permute-start.17
  182.8 0.0 collective-permute-done.16.below
  182.8 4.6 %collective-permute-done.17.above = f32[192,128]{1,0:T(8,128)S(1)} collective-permute-done((f32[192,128]{1,0:T(8,128)S(1)}, f32[192,128]{1,0:T(8,128)S(1)}, u32[]{:S(2)}, u32[]{:S(2)}) %collective-permute-start.17) | collective-permute-done | bytes 98336 | tf_op jit(solution)/shard_map/ppermute | solution.py:425
  187.5 0.0 copy-done.7
  187.5 2.4 %shard_map.86 = f32[8,8,512]{2,1,0:T(8,128)} custom-call(f32[192,128]{1,0:T(8,128)S(1)} %shard_map.85.own, f32[192,128]{1,0:T(8,128)S(1)} %collective-permute-done.16.below, f32[192,128]{1,0:T(8,128)S(1)} %collective-permute-done.17.above, f32[5,256,128]{2,1,0:T(8,128)S(1)} %get-tuple-element.45.mid, f32[256,128]{1,0:T(8,128)S(1)} %copy-done.7, ...), custom_call_target="tpu_custom_call" | custom-call | flops 629145600 | bytes 5931008 | tf_op jit(solution)/shard_map/pallas_call | solution.py:411
  (17 shorter events, 0.0 us)
Async XLA Ops:
  6.5 30.1 %copy-start.3 = (f32[512,512]{1,0:T(8,128)S(1)}, f32[512,512]{1,0:T(8,128)}, u32[]{:S(2)}) copy-start(f32[512,512]{1,0:T(8,128)} %j_ref.1) | copy-start | bytes 3145732
  6.5 126.4 %all-gather.2.cloned.1.call-start = ((), (), s32[]{:S(2)}) async-start(), calls=%async_computation | async-start | bytes 1351680 | tf_op jit(solution)/shard_map/all_gather | solution.py:464
  6.5 1.0 copy-start.8
  7.5 0.9 copy-start.9
  8.4 0.9 copy-start.10
  9.3 0.9 copy-start.11
  10.2 0.9 copy-start.12
  11.2 0.9 copy-start.13
  12.2 12.5 %collective-permute-start = (f32[6,8,16,128]{3,2,1,0:T(8,128)S(1)}, f32[6,8,16,128]{3,2,1,0:T(8,128)S(1)}, u32[]{:S(2)}, u32[]{:S(2)}) collective-permute-start(f32[6,8,16,128]{3,2,1,0:T(8,128)S(1)} %get-tuple-element.35.hi), channel_id=1, source_target_pairs={{0,1},{1,2},{2,3},{3,4},{4,5},{5,6},{6,7},{7,8},{8,9},{9,10},{10,1... | collective-permute-start | bytes 1179656 | tf_op jit(solution)/shard_map/ppermute | solution.py:424
  17.0 12.8 %collective-permute-start.1 = (f32[6,8,16,128]{3,2,1,0:T(8,128)S(1)}, f32[6,8,16,128]{3,2,1,0:T(8,128)S(1)}, u32[]{:S(2)}, u32[]{:S(2)}) collective-permute-start(f32[6,8,16,128]{3,2,1,0:T(8,128)S(1)} %get-tuple-element.34.lo), channel_id=1, source_target_pairs={{1,0},{2,1},{3,2},{4,3},{5,4},{6,5},{7,6},{8,7},{9,8},{10,9},{11,1... | collective-permute-start | bytes 1179656 | tf_op jit(solution)/shard_map/ppermute | solution.py:425
  29.8 13.8 %collective-permute-start.2 = (f32[6,4,64,128]{3,2,1,0:T(8,128)S(1)}, f32[6,4,64,128]{3,2,1,0:T(8,128)S(1)}, u32[]{:S(2)}, u32[]{:S(2)}) collective-permute-start(f32[6,4,64,128]{3,2,1,0:T(8,128)S(1)} %get-tuple-element.36.second), channel_id=1, source_target_pairs={{0,16},{16,32},{32,48},{48,64},{64,80},{80,96},{96,112},{112,128},... | collective-permute-start | bytes 2359304 | tf_op jit(solution)/shard_map/ppermute | solution.py:424
  34.7 15.4 %collective-permute-start.3 = (f32[6,4,64,128]{3,2,1,0:T(8,128)S(1)}, f32[6,4,64,128]{3,2,1,0:T(8,128)S(1)}, u32[]{:S(2)}, u32[]{:S(2)}) collective-permute-start(f32[6,4,64,128]{3,2,1,0:T(8,128)S(1)} %get-tuple-element.37.first), channel_id=1, source_target_pairs={{16,0},{32,16},{48,32},{64,48},{80,64},{96,80},{112,96},{128,112},... | collective-permute-start | bytes 2359304 | tf_op jit(solution)/shard_map/ppermute | solution.py:425
  52.3 1.6 copy-start
  54.0 0.8 copy-start.4
  54.8 5.3 %collective-permute-start.4 = (f32[32,128]{1,0:T(8,128)S(1)}, f32[32,128]{1,0:T(8,128)S(1)}, u32[]{:S(2)}, u32[]{:S(2)}) collective-permute-start(f32[32,128]{1,0:T(8,128)S(1)} %get-tuple-element.42.hi), channel_id=1, source_target_pairs={{0,1},{1,2},{2,3},{3,4},{4,5},{5,6},{6,7},{7,8},{8,9},{9,10},{10,1... | collective-permute-start | bytes 49160 | tf_op jit(solution)/shard_map/ppermute | solution.py:424
  57.3 5.7 %collective-permute-start.5 = (f32[32,128]{1,0:T(8,128)S(1)}, f32[32,128]{1,0:T(8,128)S(1)}, u32[]{:S(2)}, u32[]{:S(2)}) collective-permute-start(f32[32,128]{1,0:T(8,128)S(1)} %get-tuple-element.41.lo), channel_id=1, source_target_pairs={{1,0},{2,1},{3,2},{4,3},{5,4},{6,5},{7,6},{8,7},{9,8},{10,9},{11,1... | collective-permute-start | bytes 49160 | tf_op jit(solution)/shard_map/ppermute | solution.py:425
  63.0 5.1 %collective-permute-start.6 = (f32[64,128]{1,0:T(8,128)S(1)}, f32[64,128]{1,0:T(8,128)S(1)}, u32[]{:S(2)}, u32[]{:S(2)}) collective-permute-start(f32[64,128]{1,0:T(8,128)S(1)} %get-tuple-element.43.second), channel_id=1, source_target_pairs={{0,16},{16,32},{32,48},{48,64},{64,80},{80,96},{96,112},{112,128},... | collective-permute-start | bytes 98312 | tf_op jit(solution)/shard_map/ppermute | solution.py:424
  66.1 7.3 %collective-permute-start.7 = (f32[64,128]{1,0:T(8,128)S(1)}, f32[64,128]{1,0:T(8,128)S(1)}, u32[]{:S(2)}, u32[]{:S(2)}) collective-permute-start(f32[64,128]{1,0:T(8,128)S(1)} %get-tuple-element.44.first), channel_id=1, source_target_pairs={{16,0},{32,16},{48,32},{64,48},{80,64},{96,80},{112,96},{128,112},... | collective-permute-start | bytes 98312 | tf_op jit(solution)/shard_map/ppermute | solution.py:425
  74.9 0.6 copy-start.6
  132.9 1.3 copy-start.2
  134.7 7.0 %collective-permute-start.8 = (f32[256,128]{1,0:T(8,128)S(1)}, f32[256,128]{1,0:T(8,128)S(1)}, u32[]{:S(2)}, u32[]{:S(2)}) collective-permute-start(f32[256,128]{1,0:T(8,128)S(1)} %get-tuple-element.51), channel_id=1, source_target_pairs={{0,1},{1,2},{2,3},{3,4},{4,5},{5,6},{6,7},{7,8},{8,9},{9,10},{10,1... | collective-permute-start | bytes 393224 | tf_op jit(solution)/shard_map/ppermute | solution.py:424
  139.1 7.6 %collective-permute-start.9 = (f32[256,128]{1,0:T(8,128)S(1)}, f32[256,128]{1,0:T(8,128)S(1)}, u32[]{:S(2)}, u32[]{:S(2)}) collective-permute-start(f32[256,128]{1,0:T(8,128)S(1)} %get-tuple-element.52), channel_id=1, source_target_pairs={{1,0},{2,1},{3,2},{4,3},{5,4},{6,5},{7,6},{8,7},{9,8},{10,9},{11,1... | collective-permute-start | bytes 393224 | tf_op jit(solution)/shard_map/ppermute | solution.py:425
  146.9 5.7 %collective-permute-start.10 = (f32[256,128]{1,0:T(8,128)S(1)}, f32[256,128]{1,0:T(8,128)S(1)}, u32[]{:S(2)}, u32[]{:S(2)}) collective-permute-start(f32[256,128]{1,0:T(8,128)S(1)} %get-tuple-element.54), channel_id=1, source_target_pairs={{0,1},{1,2},{2,3},{3,4},{4,5},{5,6},{6,7},{7,8},{8,9},{9,10},{10,1... | collective-permute-start | bytes 393224 | tf_op jit(solution)/shard_map/ppermute | solution.py:424
  148.9 6.9 %collective-permute-start.11 = (f32[256,128]{1,0:T(8,128)S(1)}, f32[256,128]{1,0:T(8,128)S(1)}, u32[]{:S(2)}, u32[]{:S(2)}) collective-permute-start(f32[256,128]{1,0:T(8,128)S(1)} %get-tuple-element.55), channel_id=1, source_target_pairs={{1,0},{2,1},{3,2},{4,3},{5,4},{6,5},{7,6},{8,7},{9,8},{10,9},{11,1... | collective-permute-start | bytes 393224 | tf_op jit(solution)/shard_map/ppermute | solution.py:425
  156.7 19.3 %collective-permute-start.12 = (f32[256,128]{1,0:T(8,128)}, f32[256,128]{1,0:T(8,128)}, u32[]{:S(2)}, u32[]{:S(2)}) collective-permute-start(f32[256,128]{1,0:T(8,128)} %get-tuple-element.57), channel_id=1, source_target_pairs={{0,1},{1,2},{2,3},{3,4},{4,5},{5,6},{6,7},{7,8},{8,9},{9,10},{10,1... | collective-permute-start | bytes 393224 | tf_op jit(solution)/shard_map/ppermute | solution.py:424
  159.8 16.2 %collective-permute-start.13 = (f32[256,128]{1,0:T(8,128)}, f32[256,128]{1,0:T(8,128)}, u32[]{:S(2)}, u32[]{:S(2)}) collective-permute-start(f32[256,128]{1,0:T(8,128)} %get-tuple-element.58), channel_id=1, source_target_pairs={{1,0},{2,1},{3,2},{4,3},{5,4},{6,5},{7,6},{8,7},{9,8},{10,9},{11,1... | collective-permute-start | bytes 393224 | tf_op jit(solution)/shard_map/ppermute | solution.py:425
  161.9 8.7 %collective-permute-start.14 = (f32[64,128]{1,0:T(8,128)}, f32[64,128]{1,0:T(8,128)}, u32[]{:S(2)}, u32[]{:S(2)}) collective-permute-start(f32[64,128]{1,0:T(8,128)} %get-tuple-element.59.err), channel_id=1, source_target_pairs={{0,16},{16,32},{32,48},{48,64},{64,80},{80,96},{96,112},{112,128},... | collective-permute-start | bytes 98312 | tf_op jit(solution)/shard_map/ppermute | solution.py:424
  168.3 7.7 %collective-permute-start.15 = (f32[64,128]{1,0:T(8,128)}, f32[64,128]{1,0:T(8,128)}, u32[]{:S(2)}, u32[]{:S(2)}) collective-permute-start(f32[64,128]{1,0:T(8,128)} %get-tuple-element.59.err), channel_id=1, source_target_pairs={{16,0},{32,16},{48,32},{64,48},{80,64},{96,80},{112,96},{128,112},... | collective-permute-start | bytes 98312 | tf_op jit(solution)/shard_map/ppermute | solution.py:425
  170.2 17.2 %copy-start.1 = (f32[6,1024,128]{2,1,0:T(8,128)S(1)}, f32[6,1024,128]{2,1,0:T(8,128)}, u32[]{:S(2)}) copy-start(f32[6,1024,128]{2,1,0:T(8,128)} %copy-done) | copy-start | bytes 9437188
  170.7 16.8 %copy-start.5 = (f32[1024,128]{1,0:T(8,128)S(1)}, f32[1024,128]{1,0:T(8,128)}, u32[]{:S(2)}) copy-start(f32[1024,128]{1,0:T(8,128)} %copy-done.4) | copy-start | bytes 1572868
  170.7 16.8 %copy-start.7 = (f32[256,128]{1,0:T(8,128)S(1)}, f32[256,128]{1,0:T(8,128)}, u32[]{:S(2)}) copy-start(f32[256,128]{1,0:T(8,128)} %copy-done.6) | copy-start | bytes 393220
  177.1 5.7 %collective-permute-start.16 = (f32[192,128]{1,0:T(8,128)S(1)}, f32[192,128]{1,0:T(8,128)S(1)}, u32[]{:S(2)}, u32[]{:S(2)}) collective-permute-start(f32[192,128]{1,0:T(8,128)S(1)} %shard_map.85.own), channel_id=1, source_target_pairs={{0,1},{1,2},{2,3},{3,4},{4,5},{5,6},{6,7},{7,8},{8,9},{9,10},{10,1... | collective-permute-start | bytes 294920 | tf_op jit(solution)/shard_map/ppermute | solution.py:424
  180.9 6.6 %collective-permute-start.17 = (f32[192,128]{1,0:T(8,128)S(1)}, f32[192,128]{1,0:T(8,128)S(1)}, u32[]{:S(2)}, u32[]{:S(2)}) collective-permute-start(f32[192,128]{1,0:T(8,128)S(1)} %shard_map.85.own), channel_id=1, source_target_pairs={{1,0},{2,1},{3,2},{4,3},{5,4},{6,5},{7,6},{8,7},{9,8},{10,9},{11,1... | collective-permute-start | bytes 294920 | tf_op jit(solution)/shard_map/ppermute | solution.py:425
Sparse Core Ops, SparseCore 0:
  75.7 57.2 all-gather.1

commit v2 on v1

--- a/solution.py
+++ b/solution.py
@@ -92,24 +92,45 @@
         out_ref[c + Z : c + Z + 1, :] = piece
 
 
-def pack_kernel(rhs, value, speed_a, speed_b, flag_a, flag_b, lo_ref, hi_ref):
+def pack_kernel(*refs):
+    sources, (lo_ref, hi_ref, low_ref), buffers = refs[:6], refs[6:9], refs[9:15]
+    mid, sems = refs[15:]
+    copies = [
+        pltpu.make_async_copy(src, dst, sems.at[i])
+        for i, (src, dst) in enumerate(zip(sources, buffers))
+    ]
+    for copy in copies:
+        copy.start()
+    rhs, value, speed_a, speed_b, flag_a, flag_b = buffers
     half = lo_ref.shape[2] // Z
-    for a in range(rhs.shape[0]):
-        up_a = flag_a[a].astype(F32)
-        up_b = flag_b[a].astype(F32)
-        fields = (
-            value[a],
-            rhs[a],
-            speed_a[a] * up_a,
-            speed_a[a] * (1.0 - up_a),
-            speed_b[a] * up_b,
-            speed_b[a] * (1.0 - up_b),
-        )
-        for k, x in enumerate(fields):
-            for c in range(Z):
-                piece = x[:, c * LANES : (c + 1) * LANES]
-                lo_ref[k, a, pl.ds(c, half, stride=Z), :] = piece[:half]
-                hi_ref[k, a, pl.ds(c, half, stride=Z), :] = piece[half:]
+
+    def put(k, a, x):
+        for c in range(Z):
+            piece = x[:, c * LANES : (c + 1) * LANES]
+            lo_ref[k, a, pl.ds(c, half, stride=Z), :] = piece[:half]
+            hi_ref[k, a, pl.ds(c, half, stride=Z), :] = piece[half:]
+
+    for copy in copies[2:]:
+        copy.wait()
+    points = rhs.shape[0]
+    for a in range(points):
+        for k, speed, flag in ((2, speed_a, flag_a), (4, speed_b, flag_b)):
+            up = flag[a].astype(F32)
+            put(k, a, speed[a] * up)
+            put(k + 1, a, speed[a] * (1.0 - up))
+    for k in range(2, 6):
+        for m in range(points // 2):
+            for i, src in enumerate((lo_ref, hi_ref)):
+                both = src[k, 2 * m] + src[k, 2 * m + 1]
+                mid[pl.ds(16 * m + 8 * i, 8), :] = 0.125 * pair_sums(both)
+        for m in range(points // 4):
+            both = mid[pl.ds(32 * m, 16), :] + mid[pl.ds(32 * m + 16, 16), :]
+            low_ref[pl.ds(16 * (k - 2) + 8 * m, 8), :] = 0.125 * pair_sums(both)
+    for copy in copies[:2]:
+        copy.wait()
+    for a in range(points):
+        put(0, a, value[a])
+        put(1, a, rhs[a])
 
 
 def widen_kernel(lo, hi, below, above, first_ref, second_ref):
@@ -121,7 +142,7 @@
 
 def fine_kernel(
     below, first, second, above, jhi, jlo, out,
-    fine_ref, val_ref, rlo_ref, rhi_ref, mid_ref, low_ref, v0, v1, inc, res,
+    fine_out, val_out, rlo_ref, rhi_ref, mid_ref, fine_ref, val_ref, v0, v1, inc, sems,
 ):
     outflow = spread(out[...], 64)
     for a in range(16):
@@ -135,6 +156,8 @@
             if k > 1:
                 total = total + x
         fine_ref[5, here, :] = OMEGA / total
+    keep_fine = pltpu.make_async_copy(fine_ref, fine_out, sems.at[0])
+    keep_fine.start()
 
     def applied(src, a):
         here = pl.ds(64 * a, 64)
@@ -155,6 +178,11 @@
 
     sweep(v0, v1, 1, 15)
     sweep(v1, val_ref, 2, 14)
+    edge = jnp.zeros((128, LANES), F32)
+    val_ref[0:128, :] = edge
+    val_ref[896:1024, :] = edge
+    keep_val = pltpu.make_async_copy(val_ref, val_out, sems.at[1])
+    keep_val.start()
     income(val_ref, inc, [(64 * 4, 64 * 4, 16 * 8)], jhi, jlo)
 
     def residual(a):
@@ -180,11 +208,8 @@
             mid_ref[k, here, :] = x
             total = total + x
         mid_ref[4, here, :] = OMEGA / total
-    for k in range(4):
-        for m in range(2):
-            at = 32 * (2 + 2 * m) + 8
-            both = mid_ref[k, pl.ds(at, 16), :] + mid_ref[k, pl.ds(at + 32, 16), :]
-            low_ref[k, pl.ds(8 * m, 8), :] = 0.125 * pair_sums(both)
+    keep_fine.wait()
+    keep_val.wait()
 
 
 def widen_mid_kernel(lo, hi, below, above, first_ref, second_ref):
@@ -195,7 +220,7 @@
 
 
 def mid_kernel(
-    below, first, second, above, mid, low, jhi, jlo, out, pay_ref, err_ref, rhs_ref, e0, e1, inc
+    below, first, second, above, mid, jhi, jlo, out, pay_ref, err_ref, rhs_ref, e0, e1, inc
 ):
     for i, src in enumerate((below, first, second, above)):
         rhs_ref[pl.ds(64 * i, 64), :] = src[...]
@@ -229,8 +254,6 @@
 
     for m in range(2):
         pay_ref[pl.ds(8 * m, 8), :] = 0.25 * pair_sums(residual(2 + 2 * m) + residual(3 + 2 * m))
-    for k in range(4):
-        pay_ref[pl.ds(16 * (k + 1), 16), :] = low[k]
     for a in range(4):
         err_ref[pl.ds(16 * a, 16), :] = e1[pl.ds(32 * (a + 2) + 8, 16), :]
 
@@ -267,48 +290,53 @@
     hi_ref[...] = jnp.where(mask, pltpu.roll(first, Z, 1), second).reshape(-1, LANES)
 
 
-def first_solve_kernel(gathered, out, fac_ref, middle_ref, e_ref, lo_ref, hi_ref, y):
-    count = e_ref.shape[0] // TILE
-    half = count // 2
+def factor_kernel(gathered, out, fac_ref, middle_ref):
+    count = fac_ref.shape[1] // TILE
 
     def part(k, a):
-        return gathered[pl.ds(80 * (a // 2) + 16 * k + 8 * (a % 2), TILE), :]
+        return gathered[pl.ds(64 * (a // 2) + 16 * k + 8 * (a % 2), TILE), :]
 
     outflow = DISCOUNT + out[...]
     gaps = [None, None]
     links = [None, None]
-    for i in range(half):
+    for i in range(count // 2):
         for side, a in ((0, i), (1, count - 1 - i)):
             here = pl.ds(TILE * a, TILE)
-            inner, outer = (part(1, a), part(2, a)) if side == 0 else (part(2, a), part(1, a))
-            fb, bb = part(3, a), part(4, a)
+            inner, outer = (part(0, a), part(1, a)) if side == 0 else (part(1, a), part(0, a))
+            fb, bb = part(2, a), part(3, a)
             slack = outflow + fb + bb
             slack = slack + (outer if i == 0 else outer * gaps[side])
             weight = 1.0 / (slack + inner)
             links[side] = inner * weight
             gaps[side] = slack * weight
-            fac_ref[0, here, :] = part(0, a)
-            fac_ref[1, here, :] = fb
-            fac_ref[2, here, :] = bb
-            fac_ref[3, here, :] = weight
-            fac_ref[4, here, :] = outer * weight
-            fac_ref[5, here, :] = links[side]
+            fac_ref[0, here, :] = fb
+            fac_ref[1, here, :] = bb
+            fac_ref[2, here, :] = weight
+            fac_ref[3, here, :] = outer * weight
+            fac_ref[4, here, :] = links[side]
     middle_ref[...] = 1.0 / (gaps[0] + links[0] * gaps[1])
+
+
+def first_solve_kernel(
+    rhs, fac, middle, err, err_lo, err_hi, e_ref, lo_ref, hi_ref, wide_ref, y
+):
+    for i, src in enumerate((err_lo, err, err_hi)):
+        wide_ref[pl.ds(64 * i, 64), :] = src[...]
     solve_lines(
-        lambda a: row(fac_ref.at[0], a, TILE),
-        lambda a: row(fac_ref.at[3], a, TILE),
-        lambda a: row(fac_ref.at[4], a, TILE),
-        lambda a: row(fac_ref.at[5], a, TILE),
-        middle_ref[...], y, e_ref, 0,
+        lambda a: row(rhs, a, TILE),
+        lambda a: row(fac.at[2], a, TILE),
+        lambda a: row(fac.at[3], a, TILE),
+        lambda a: row(fac.at[4], a, TILE),
+        middle[...], y, e_ref, 0,
     )
     send_lines(e_ref, lo_ref, hi_ref)
 
 
-def local_target_kernel(e, fac, jhi, jlo, t_ref):
+def local_target_kernel(e, rhs, fac, jhi, jlo, t_ref):
     income(e, t_ref, [(0, 0, e.shape[0] // Z)], jhi, jlo)
     other = swapped(e[...])
     mask = first_half(other.shape)
-    t_ref[...] = t_ref[...] + fac[0] + jnp.where(mask, fac[1], fac[2]) * other
+    t_ref[...] = t_ref[...] + rhs[...] + jnp.where(mask, fac[0], fac[1]) * other
 
 
 def swept(t, fac, middle, below, above, y, x_ref, offset):
@@ -321,14 +349,14 @@
         else:
             high_side = pltpu.roll(high_side, Z, 0)
         near = jnp.where(mask, low_side, high_side)
-        coupling = jnp.where(mask, row(fac.at[2], a, TILE), row(fac.at[1], a, TILE))
+        coupling = jnp.where(mask, row(fac.at[1], a, TILE), row(fac.at[0], a, TILE))
         return row(t, a, TILE) + coupling * near
 
     solve_lines(
         target,
+        lambda a: row(fac.at[2], a, TILE),
         lambda a: row(fac.at[3], a, TILE),
         lambda a: row(fac.at[4], a, TILE),
-        lambda a: row(fac.at[5], a, TILE),
         middle[...], y, x_ref, offset,
     )
 
@@ -338,7 +366,7 @@
     send_lines(e_ref, lo_ref, hi_ref)
 
 
-def last_sweep_kernel(place, t, fac, middle, below, above, err, err_lo, err_hi, sum_ref, y, x):
+def last_sweep_kernel(place, t, fac, middle, below, above, err, sum_ref, y, x):
     edge = 2 * TILE
     x[0:edge, :] = jnp.zeros((edge, LANES), F32)
     x[pl.ds(x.shape[0] - edge, edge), :] = jnp.zeros((edge, LANES), F32)
@@ -348,8 +376,7 @@
         low = x[pl.ds(pl.multiple_of(start + i * TILE, TILE), TILE), :]
         fill = doubled(low)
         for m in (2 * i, 2 * i + 1):
-            src = (err_lo, err, err_hi)[m // 4]
-            sum_ref[pl.ds(16 * m, 16), :] = src[pl.ds(16 * (m % 4), 16), :] + fill
+            sum_ref[pl.ds(16 * m, 16), :] = err[pl.ds(16 * m, 16), :] + fill
 
 
 def last_kernel(
@@ -404,16 +431,20 @@
             out_ref[a, :, c * LANES : (c + 1) * LANES] = piece
 
 
-def call(kernel, args, outs, scratch=(), flops=0, smem=0, limit=32):
-    outs = [jax.ShapeDtypeStruct(*o) if isinstance(o, tuple) and isinstance(o[0], tuple) else jax.ShapeDtypeStruct(o, F32) for o in outs]
-    spec = pl.BlockSpec(memory_space=pltpu.VMEM)
+def call(kernel, args, outs, scratch=(), flops=0, places=(), out_places=(), limit=24):
+    outs = [x if isinstance(x, jax.ShapeDtypeStruct) else jax.ShapeDtypeStruct(x, F32) for x in outs]
     moved = sum(x.size * x.dtype.itemsize for x in (*args, *outs))
+
+    def specs(kinds, count):
+        kinds = list(kinds) + [pltpu.VMEM] * (count - len(kinds))
+        return [pl.BlockSpec(memory_space=kind) for kind in kinds]
+
     return pl.pallas_call(
         kernel,
         out_shape=outs,
-        in_specs=[pl.BlockSpec(memory_space=pltpu.SMEM)] * smem + [spec] * (len(args) - smem),
-        out_specs=[spec] * len(outs),
-        scratch_shapes=[pltpu.VMEM(s, F32) for s in scratch],
+        in_specs=specs(places, len(args)),
+        out_specs=specs(out_places, len(outs)),
+        scratch_shapes=[pltpu.VMEM(s, F32) if isinstance(s, tuple) else s for s in scratch],
         compiler_params=pltpu.CompilerParams(vmem_limit_bytes=limit * 2**20),
         cost_estimate=pl.CostEstimate(flops=flops, bytes_accessed=moved, transcendentals=0),
     )(*args)
@@ -429,48 +460,57 @@
 def body(right_side, value_guess, speed_liq, speed_ill, flag_liq, flag_ill, jump_rates):
     nz = jump_rates.shape[0]
     dot_flops = 2 * 3 * nz * nz
+    inputs = (right_side, value_guess, speed_liq, speed_ill, flag_liq, flag_ill)
     half = (6, 8, 16, LANES)
-    lo, hi = call(
+    lo, hi, low = call(
         pack_kernel,
-        (right_side, value_guess, speed_liq, speed_ill, flag_liq, flag_ill),
-        [half, half],
-    )
-    jhi, jlo, out = call(
-        rates_kernel, (jump_rates,), [((nz, nz), BF16), ((nz, nz), BF16), (TILE, LANES)]
-    )
+        inputs,
+        [half, half, (64, LANES)],
+        [pltpu.VMEM(x.shape, x.dtype) for x in inputs]
+        + [(64, LANES), pltpu.SemaphoreType.DMA((6,))],
+        places=[pltpu.HBM] * 6,
+    )
+    coefs = lax.all_gather(low, "liq", axis=0, tiled=True)
+    rates = jax.ShapeDtypeStruct((nz, nz), BF16)
+    jhi, jlo, out = call(rates_kernel, (jump_rates,), [rates, rates, (TILE, LANES)])
     below, above = neighbours(lo, hi, "ill")
     wide = (6, 4, 64, LANES)
     first, second = call(widen_kernel, (lo, hi, below, above), [wide, wide])
     below, above = neighbours(first, second, "liq")
-    whole = (1024, LANES)
-    fine, value, rlo, rhi, mid, low = call(
+    whole, six = (1024, LANES), (6, 1024, LANES)
+    fine, value, rlo, rhi, mid = call(
         fine_kernel,
         (below, first, second, above, jhi, jlo, out),
-        [(6, 1024, LANES), whole, (32, LANES), (32, LANES), (5, 256, LANES), (4, 16, LANES)],
-        [whole] * 4,
+        [six, whole, (32, LANES), (32, LANES), (5, 256, LANES)],
+        [six, whole, whole, whole, whole, pltpu.SemaphoreType.DMA((2,))],
         flops=dot_flops * 550,
+        out_places=[pltpu.HBM] * 2,
     )
     below, above = neighbours(rlo, rhi, "ill")
     first, second = call(widen_mid_kernel, (rlo, rhi, below, above), [(64, LANES)] * 2)
     below, above = neighbours(first, second, "liq")
-    payload, error_mid, rhs_mid = call(
+    rhs_low, error_mid, rhs_mid = call(
         mid_kernel,
-        (below, first, second, above, mid, low, jhi, jlo, out),
-        [(80, LANES), (64, LANES), (256, LANES)],
+        (below, first, second, above, mid, jhi, jlo, out),
+        [(16, LANES), (64, LANES), (256, LANES)],
         [(256, LANES)] * 3,
         flops=dot_flops * 80,
     )
     err_lo, err_hi = neighbours(error_mid, error_mid, "liq")
-    gathered = lax.all_gather(payload, "liq", axis=0, tiled=True)
-    lines = gathered.shape[0] // 80 * 2 * TILE
+    rhs = lax.all_gather(rhs_low, "liq", axis=0, tiled=True)
+    lines = rhs.shape[0]
     line, message = (lines, LANES), (lines // 2, LANES)
-    fac, middle, e, lo, hi = call(
-        first_solve_kernel, (gathered, out), [(6, *line), (TILE, LANES), line, message, message], [line]
+    fac, middle = call(factor_kernel, (coefs, out), [(5, *line), (TILE, LANES)])
+    e, lo, hi, err = call(
+        first_solve_kernel,
+        (rhs, fac, middle, error_mid, err_lo, err_hi),
+        [line, message, message, (192, LANES)],
+        [line],
     )
     for step in range(SWEEPS - 1):
         below, above = neighbours(lo, hi, "ill")
         (target,) = call(
-            local_target_kernel, (e, fac, jhi, jlo), [line], flops=dot_flops * lines // Z
+            local_target_kernel, (e, rhs, fac, jhi, jlo), [line], flops=dot_flops * lines // Z
         )
         if step < SWEEPS - 2:
             e, lo, hi = call(
@@ -479,10 +519,10 @@
     place = lax.axis_index("liq").astype(jnp.int32).reshape(1)
     (total,) = call(
         last_sweep_kernel,
-        (place, target, fac, middle, below, above, error_mid, err_lo, err_hi),
+        (place, target, fac, middle, below, above, err),
         [(192, LANES)],
         [line, (lines + 4 * TILE, LANES)],
-        smem=1,
+        places=[pltpu.SMEM],
     )
     below, above = neighbours(total, total, "ill")
     (result,) = call(

time: 197 us -> 168 us (0.85)
  the two profiles are of different devices: /device:TPU:103 before, /device:TPU:64 now
where the time goes in v2:
time: 168 us; the launch traced here: 167 us
  starting transfers between devices  58.9 us (35%)
  waiting for transfers between devices  39.9 us (24%)
  blocking collectives  31.1 us (19%)
  between operations  13.7 us (8%)
  local copies, waits for them, and re-layouts  11.7 us (7%)
  Pallas kernels  11.5 us (7%)
    ppermute x9, starting transfers between devices, neighbours(): below = lax.ppermute(hi, axis, [(i, i + 1) for i in range(count - 1)])  43.1 us
    all_gather x1, blocking collectives, body(): rhs = lax.all_gather(rhs_low, 'liq', axis=0, tiled=True)  31.1 us
    ppermute x9, waiting for transfers between devices, neighbours(): above = lax.ppermute(lo, axis, [(i + 1, i) for i in range(count - 1)])  30.6 us
    ppermute x9, starting transfers between devices, neighbours(): above = lax.ppermute(lo, axis, [(i + 1, i) for i in range(count - 1)])  15.8 us
    unnamed x32, local copies, waits for them, and re-layouts  11.7 us
    pallas_call x15, Pallas kernels, call(): pl.pallas_call(kernel, out_shape=outs, in_specs=specs(places, len(args)),...  11.5 us
    ppermute x9, waiting for transfers between devices, neighbours(): below = lax.ppermute(hi, axis, [(i, i + 1) for i in range(count - 1)])  9.29 us
  transfers between devices with their start and end apart: 19, of which 13 were waited for; matrix products, arithmetic and copies ran while one was open for 0% of the time, Pallas kernels for 3%

profile of v2, /device:TPU:64, one launch (start us, length us, event | category | flops | bytes accessed | tf_op | source)
XLA Modules:
  0.0 166.9 jit_solution(7285082282350313432)
XLA Ops:
  6.5 0.9 copy-done.8
  7.4 0.9 copy-done.9
  8.3 0.9 copy-done.10
  9.3 0.9 copy-done.11
  10.2 0.9 copy-done.12
  11.1 0.9 copy-done.13
  12.0 1.8 %shard_map.73 = (f32[6,8,16,128]{3,2,1,0:T(8,128)S(1)}, f32[6,8,16,128]{3,2,1,0:T(8,128)S(1)}, f32[64,128]{1,0:T(8,128)}) custom-call(f32[8,8,512]{2,1,0:T(8,128)S(1)} %copy-done.8, f32[8,8,512]{2,1,0:T(8,128)S(1)} %copy-done.9, f32[8,8,512]{2,1,0:T(8,128)S(1)} %copy-done.10, f32[8,8,512]{2,1,0:T(8,128)S(1)} %copy-done.11, s32[8,8,512]{2,1,0:T(8,128)S(1)} %copy-done.12, ...), custom_call_target="tpu_custom_call" | custom-call | bytes 1605632 | tf_op jit(solution)/shard_map/pallas_call | solution.py:442
  13.8 0.0 all-gather.2.cloned.1.call-update
  13.8 3.8 %collective-permute-start = (f32[6,8,16,128]{3,2,1,0:T(8,128)S(1)}, f32[6,8,16,128]{3,2,1,0:T(8,128)S(1)}, u32[]{:S(2)}, u32[]{:S(2)}) collective-permute-start(f32[6,8,16,128]{3,2,1,0:T(8,128)S(1)} %get-tuple-element.36.hi), channel_id=1, source_target_pairs={{0,1},{1,2},{2,3},{3,4},{4,5},{5,6},{6,7},{7,8},{8,9},{9,10},{10,1... | collective-permute-start | bytes 1179656 | tf_op jit(solution)/shard_map/ppermute | solution.py:455
  17.6 2.0 %collective-permute-start.1 = (f32[6,8,16,128]{3,2,1,0:T(8,128)S(1)}, f32[6,8,16,128]{3,2,1,0:T(8,128)S(1)}, u32[]{:S(2)}, u32[]{:S(2)}) collective-permute-start(f32[6,8,16,128]{3,2,1,0:T(8,128)S(1)} %get-tuple-element.35.lo), channel_id=1, source_target_pairs={{1,0},{2,1},{3,2},{4,3},{5,4},{6,5},{7,6},{8,7},{9,8},{10,9},{11,1... | collective-permute-start | bytes 1179656 | tf_op jit(solution)/shard_map/ppermute | solution.py:456
  19.7 6.9 %collective-permute-done.below = f32[6,8,16,128]{3,2,1,0:T(8,128)S(1)} collective-permute-done((f32[6,8,16,128]{3,2,1,0:T(8,128)S(1)}, f32[6,8,16,128]{3,2,1,0:T(8,128)S(1)}, u32[]{:S(2)}, u32[]{:S(2)}) %collective-permute-start) | collective-permute-done | bytes 393248 | tf_op jit(solution)/shard_map/ppermute | solution.py:455
  26.5 4.9 %collective-permute-done.1.above = f32[6,8,16,128]{3,2,1,0:T(8,128)S(1)} collective-permute-done((f32[6,8,16,128]{3,2,1,0:T(8,128)S(1)}, f32[6,8,16,128]{3,2,1,0:T(8,128)S(1)}, u32[]{:S(2)}, u32[]{:S(2)}) %collective-permute-start.1) | collective-permute-done | bytes 393248 | tf_op jit(solution)/shard_map/ppermute | solution.py:456
  31.5 0.1 shard_map.74
  31.6 1.3 collective-permute-start.2
  32.9 1.3 collective-permute-start.3
  34.2 0.0 copy-start.2
  34.3 1.2 copy-done.2
  35.5 0.2 shard_map.75
  35.7 0.0 collective-permute-done.2.below
  35.7 3.1 %collective-permute-done.3.above = f32[6,4,64,128]{3,2,1,0:T(8,128)S(1)} collective-permute-done((f32[6,4,64,128]{3,2,1,0:T(8,128)S(1)}, f32[6,4,64,128]{3,2,1,0:T(8,128)S(1)}, u32[]{:S(2)}, u32[]{:S(2)}) %collective-permute-start.3) | collective-permute-done | bytes 786464 | tf_op jit(solution)/shard_map/ppermute | solution.py:456
  38.8 2.4 %shard_map.76 = (f32[6,1024,128]{2,1,0:T(8,128)S(1)}, f32[1024,128]{1,0:T(8,128)S(1)}, f32[32,128]{1,0:T(8,128)S(1)}, f32[32,128]{1,0:T(8,128)S(1)}, f32[5,256,128]{2,1,0:T(8,128)S(1)}) custom-call(f32[6,4,64,128]{3,2,1,0:T(8,128)S(1)} %collective-permute-done.2.below, f32[6,4,64,128]{3,2,1,0:T(8,128)S(1)} %get-tuple-element.38.first, ...), custom_call_target="tpu_custom_call" | custom-call | flops 865075200 | bytes 8556544 | tf_op jit(solution)/shard_map/pallas_call | solution.py:442
  41.2 1.6 copy-done
  42.9 4.8 %collective-permute-start.4 = (f32[32,128]{1,0:T(8,128)S(1)}, f32[32,128]{1,0:T(8,128)S(1)}, u32[]{:S(2)}, u32[]{:S(2)}) collective-permute-start(f32[32,128]{1,0:T(8,128)S(1)} %get-tuple-element.43.hi), channel_id=1, source_target_pairs={{0,1},{1,2},{2,3},{3,4},{4,5},{5,6},{6,7},{7,8},{8,9},{9,10},{10,1... | collective-permute-start | bytes 49160 | tf_op jit(solution)/shard_map/ppermute | solution.py:455
  47.7 1.9 %collective-permute-start.5 = (f32[32,128]{1,0:T(8,128)S(1)}, f32[32,128]{1,0:T(8,128)S(1)}, u32[]{:S(2)}, u32[]{:S(2)}) collective-permute-start(f32[32,128]{1,0:T(8,128)S(1)} %get-tuple-element.42.lo), channel_id=1, source_target_pairs={{1,0},{2,1},{3,2},{4,3},{5,4},{6,5},{7,6},{8,7},{9,8},{10,9},{11,1... | collective-permute-start | bytes 49160 | tf_op jit(solution)/shard_map/ppermute | solution.py:456
  49.6 0.0 collective-permute-done.4.below
  49.6 3.7 %collective-permute-done.5.above = f32[32,128]{1,0:T(8,128)S(1)} collective-permute-done((f32[32,128]{1,0:T(8,128)S(1)}, f32[32,128]{1,0:T(8,128)S(1)}, u32[]{:S(2)}, u32[]{:S(2)}) %collective-permute-start.5) | collective-permute-done | bytes 16416 | tf_op jit(solution)/shard_map/ppermute | solution.py:456
  53.3 10.4 %collective-permute-start.6 = (f32[64,128]{1,0:T(8,128)S(1)}, f32[64,128]{1,0:T(8,128)S(1)}, u32[]{:S(2)}, u32[]{:S(2)}) collective-permute-start(f32[64,128]{1,0:T(8,128)S(1)} %get-tuple-element.44.second), channel_id=1, source_target_pairs={{0,16},{16,32},{32,48},{48,64},{64,80},{80,96},{96,112},{112,128},... | collective-permute-start | bytes 98312 | tf_op jit(solution)/shard_map/ppermute | solution.py:455
  63.8 1.3 collective-permute-start.7
  65.1 0.0 collective-permute-done.6.below
  65.1 2.6 %collective-permute-done.7.above = f32[64,128]{1,0:T(8,128)S(1)} collective-permute-done((f32[64,128]{1,0:T(8,128)S(1)}, f32[64,128]{1,0:T(8,128)S(1)}, u32[]{:S(2)}, u32[]{:S(2)}) %collective-permute-start.7) | collective-permute-done | bytes 32800 | tf_op jit(solution)/shard_map/ppermute | solution.py:456
  67.6 0.8 shard_map.78
  68.4 0.7 copy-done.6
  69.1 5.1 %collective-permute-start.8 = (f32[64,128]{1,0:T(8,128)S(1)}, f32[64,128]{1,0:T(8,128)S(1)}, u32[]{:S(2)}, u32[]{:S(2)}) collective-permute-start(f32[64,128]{1,0:T(8,128)S(1)} %get-tuple-element.51.err), channel_id=1, source_target_pairs={{0,16},{16,32},{32,48},{48,64},{64,80},{80,96},{96,112},{112,128},... | collective-permute-start | bytes 98312 | tf_op jit(solution)/shard_map/ppermute | solution.py:455
  74.2 1.3 collective-permute-start.9
  75.5 31.1 %all_gather.6.rhs = f32[512,128]{1,0:T(8,128)S(1)} all-gather(f32[16,128]{1,0:T(8,128)S(1)} %get-tuple-element.47), channel_id=1, replica_groups=mesh['liq'=32,'ill'=16] {'liq'}, dimensions={0}, use_global_device_ids=true | all-gather | bytes 270336 | tf_op jit(solution)/shard_map/all_gather | solution.py:500
  106.6 1.2 copy-done.3
  107.8 0.3 shard_map.79
  108.1 0.0 collective-permute-done.9.err_hi
  108.2 0.1 shard_map.80
  108.3 0.6 copy-done.14
  108.9 4.1 %collective-permute-start.10 = (f32[256,128]{1,0:T(8,128)S(1)}, f32[256,128]{1,0:T(8,128)S(1)}, u32[]{:S(2)}, u32[]{:S(2)}) collective-permute-start(f32[256,128]{1,0:T(8,128)S(1)} %get-tuple-element.53), channel_id=1, source_target_pairs={{0,1},{1,2},{2,3},{3,4},{4,5},{5,6},{6,7},{7,8},{8,9},{9,10},{10,1... | collective-permute-start | bytes 393224 | tf_op jit(solution)/shard_map/ppermute | solution.py:455
  113.1 1.9 %collective-permute-start.11 = (f32[256,128]{1,0:T(8,128)S(1)}, f32[256,128]{1,0:T(8,128)S(1)}, u32[]{:S(2)}, u32[]{:S(2)}) collective-permute-start(f32[256,128]{1,0:T(8,128)S(1)} %get-tuple-element.54), channel_id=1, source_target_pairs={{1,0},{2,1},{3,2},{4,3},{5,4},{6,5},{7,6},{8,7},{9,8},{10,9},{11,1... | collective-permute-start | bytes 393224 | tf_op jit(solution)/shard_map/ppermute | solution.py:456
  115.0 0.4 shard_map.81.t
  115.4 1.1 collective-permute-done.10.below
  116.6 3.9 %collective-permute-done.11.above = f32[256,128]{1,0:T(8,128)S(1)} collective-permute-done((f32[256,128]{1,0:T(8,128)S(1)}, f32[256,128]{1,0:T(8,128)S(1)}, u32[]{:S(2)}, u32[]{:S(2)}) %collective-permute-start.11) | collective-permute-done | bytes 131104 | tf_op jit(solution)/shard_map/ppermute | solution.py:456
  120.4 0.2 shard_map.82
  120.6 4.8 %collective-permute-start.12 = (f32[256,128]{1,0:T(8,128)S(1)}, f32[256,128]{1,0:T(8,128)S(1)}, u32[]{:S(2)}, u32[]{:S(2)}) collective-permute-start(f32[256,128]{1,0:T(8,128)S(1)} %get-tuple-element.56), channel_id=1, source_target_pairs={{0,1},{1,2},{2,3},{3,4},{4,5},{5,6},{6,7},{7,8},{8,9},{9,10},{10,1... | collective-permute-start | bytes 393224 | tf_op jit(solution)/shard_map/ppermute | solution.py:455
  125.4 1.9 %collective-permute-start.13 = (f32[256,128]{1,0:T(8,128)S(1)}, f32[256,128]{1,0:T(8,128)S(1)}, u32[]{:S(2)}, u32[]{:S(2)}) collective-permute-start(f32[256,128]{1,0:T(8,128)S(1)} %get-tuple-element.57), channel_id=1, source_target_pairs={{1,0},{2,1},{3,2},{4,3},{5,4},{6,5},{7,6},{8,7},{9,8},{10,9},{11,1... | collective-permute-start | bytes 393224 | tf_op jit(solution)/shard_map/ppermute | solution.py:456
  127.3 0.4 shard_map.83.t
  127.8 0.2 collective-permute-done.12.below
  127.9 4.4 %collective-permute-done.13.above = f32[256,128]{1,0:T(8,128)S(1)} collective-permute-done((f32[256,128]{1,0:T(8,128)S(1)}, f32[256,128]{1,0:T(8,128)S(1)}, u32[]{:S(2)}, u32[]{:S(2)}) %collective-permute-start.13) | collective-permute-done | bytes 131104 | tf_op jit(solution)/shard_map/ppermute | solution.py:456
  132.3 0.9 shard_map.84
  133.1 5.1 %collective-permute-start.14 = (f32[256,128]{1,0:T(8,128)}, f32[256,128]{1,0:T(8,128)}, u32[]{:S(2)}, u32[]{:S(2)}) collective-permute-start(f32[256,128]{1,0:T(8,128)} %get-tuple-element.59), channel_id=1, source_target_pairs={{0,1},{1,2},{2,3},{3,4},{4,5},{5,6},{6,7},{7,8},{8,9},{9,10},{10,1... | collective-permute-start | bytes 393224 | tf_op jit(solution)/shard_map/ppermute | solution.py:455
  138.2 1.9 %collective-permute-start.15 = (f32[256,128]{1,0:T(8,128)}, f32[256,128]{1,0:T(8,128)}, u32[]{:S(2)}, u32[]{:S(2)}) collective-permute-start(f32[256,128]{1,0:T(8,128)} %get-tuple-element.60), channel_id=1, source_target_pairs={{1,0},{2,1},{3,2},{4,3},{5,4},{6,5},{7,6},{8,7},{9,8},{10,9},{11,1... | collective-permute-start | bytes 393224 | tf_op jit(solution)/shard_map/ppermute | solution.py:456
  140.2 0.4 shard_map.85.t
  140.6 0.4 collective-permute-done.14.below
  141.0 4.4 %collective-permute-done.15.above = f32[256,128]{1,0:T(8,128)} collective-permute-done((f32[256,128]{1,0:T(8,128)}, f32[256,128]{1,0:T(8,128)}, u32[]{:S(2)}, u32[]{:S(2)}) %collective-permute-start.15) | collective-permute-done | bytes 131104 | tf_op jit(solution)/shard_map/ppermute | solution.py:456
  145.4 0.9 copy-done.15
  146.3 1.1 shard_map.86.own
  147.4 3.6 %collective-permute-start.16 = (f32[192,128]{1,0:T(8,128)S(1)}, f32[192,128]{1,0:T(8,128)S(1)}, u32[]{:S(2)}, u32[]{:S(2)}) collective-permute-start(f32[192,128]{1,0:T(8,128)S(1)} %shard_map.86.own), channel_id=1, source_target_pairs={{0,1},{1,2},{2,3},{3,4},{4,5},{5,6},{6,7},{7,8},{8,9},{9,10},{10,1... | collective-permute-start | bytes 294920 | tf_op jit(solution)/shard_map/ppermute | solution.py:455
  151.1 2.2 %collective-permute-start.17 = (f32[192,128]{1,0:T(8,128)S(1)}, f32[192,128]{1,0:T(8,128)S(1)}, u32[]{:S(2)}, u32[]{:S(2)}) collective-permute-start(f32[192,128]{1,0:T(8,128)S(1)} %shard_map.86.own), channel_id=1, source_target_pairs={{1,0},{2,1},{3,2},{4,3},{5,4},{6,5},{7,6},{8,7},{9,8},{10,9},{11,1... | collective-permute-start | bytes 294920 | tf_op jit(solution)/shard_map/ppermute | solution.py:456
  153.3 0.7 collective-permute-done.16.below
  153.9 3.6 %collective-permute-done.17.above = f32[192,128]{1,0:T(8,128)S(1)} collective-permute-done((f32[192,128]{1,0:T(8,128)S(1)}, f32[192,128]{1,0:T(8,128)S(1)}, u32[]{:S(2)}, u32[]{:S(2)}) %collective-permute-start.17) | collective-permute-done | bytes 98336 | tf_op jit(solution)/shard_map/ppermute | solution.py:456
  157.6 2.4 %shard_map.87 = f32[8,8,512]{2,1,0:T(8,128)} custom-call(f32[192,128]{1,0:T(8,128)S(1)} %shard_map.86.own, f32[192,128]{1,0:T(8,128)S(1)} %collective-permute-done.16.below, f32[192,128]{1,0:T(8,128)S(1)} %collective-permute-done.17.above, f32[5,256,128]{2,1,0:T(8,128)S(1)} %get-tuple-element.46.mid, f32[256,128]{1,0:T(8,128)S(1)} %copy-done.7, ...), custom_call_target="tpu_custom_call" | custom-call | flops 629145600 | bytes 5931008 | tf_op jit(solution)/shard_map/pallas_call | solution.py:442
  (23 shorter events, 0.0 us)
Async XLA Ops:
  6.5 100.0 %all-gather.2.cloned.1.call-start = ((), (), s32[]{:S(2)}) async-start(), calls=%async_computation | async-start | bytes 1081344 | tf_op jit(solution)/shard_map/all_gather | solution.py:473
  6.5 0.9 copy-start.8
  7.4 0.9 copy-start.9
  8.3 0.9 copy-start.10
  9.3 0.9 copy-start.11
  10.2 0.9 copy-start.12
  11.1 0.9 copy-start.13
  13.8 12.7 %collective-permute-start = (f32[6,8,16,128]{3,2,1,0:T(8,128)S(1)}, f32[6,8,16,128]{3,2,1,0:T(8,128)S(1)}, u32[]{:S(2)}, u32[]{:S(2)}) collective-permute-start(f32[6,8,16,128]{3,2,1,0:T(8,128)S(1)} %get-tuple-element.36.hi), channel_id=1, source_target_pairs={{0,1},{1,2},{2,3},{3,4},{4,5},{5,6},{6,7},{7,8},{8,9},{9,10},{10,1... | collective-permute-start | bytes 1179656 | tf_op jit(solution)/shard_map/ppermute | solution.py:455
  17.6 13.9 %collective-permute-start.1 = (f32[6,8,16,128]{3,2,1,0:T(8,128)S(1)}, f32[6,8,16,128]{3,2,1,0:T(8,128)S(1)}, u32[]{:S(2)}, u32[]{:S(2)}) collective-permute-start(f32[6,8,16,128]{3,2,1,0:T(8,128)S(1)} %get-tuple-element.35.lo), channel_id=1, source_target_pairs={{1,0},{2,1},{3,2},{4,3},{5,4},{6,5},{7,6},{8,7},{9,8},{10,9},{11,1... | collective-permute-start | bytes 1179656 | tf_op jit(solution)/shard_map/ppermute | solution.py:456
  31.6 4.1 %collective-permute-start.2 = (f32[6,4,64,128]{3,2,1,0:T(8,128)S(1)}, f32[6,4,64,128]{3,2,1,0:T(8,128)S(1)}, u32[]{:S(2)}, u32[]{:S(2)}) collective-permute-start(f32[6,4,64,128]{3,2,1,0:T(8,128)S(1)} %get-tuple-element.37.second), channel_id=1, source_target_pairs={{0,16},{16,32},{32,48},{48,64},{64,80},{80,96},{96,112},{112,128},... | collective-permute-start | bytes 2359304 | tf_op jit(solution)/shard_map/ppermute | solution.py:455
  32.9 5.9 %collective-permute-start.3 = (f32[6,4,64,128]{3,2,1,0:T(8,128)S(1)}, f32[6,4,64,128]{3,2,1,0:T(8,128)S(1)}, u32[]{:S(2)}, u32[]{:S(2)}) collective-permute-start(f32[6,4,64,128]{3,2,1,0:T(8,128)S(1)} %get-tuple-element.38.first), channel_id=1, source_target_pairs={{16,0},{32,16},{48,32},{64,48},{80,64},{96,80},{112,96},{128,112},... | collective-permute-start | bytes 2359304 | tf_op jit(solution)/shard_map/ppermute | solution.py:456
  34.2 1.2 copy-start.2
  41.2 1.6 copy-start
  42.9 32.6 %copy-start.4 = (f32[1024,128]{1,0:T(8,128)}, f32[1024,128]{1,0:T(8,128)S(1)}, u32[]{:S(2)}) copy-start(f32[1024,128]{1,0:T(8,128)S(1)} %get-tuple-element.64.val) | copy-start | bytes 1572868
  42.9 6.8 %collective-permute-start.4 = (f32[32,128]{1,0:T(8,128)S(1)}, f32[32,128]{1,0:T(8,128)S(1)}, u32[]{:S(2)}, u32[]{:S(2)}) collective-permute-start(f32[32,128]{1,0:T(8,128)S(1)} %get-tuple-element.43.hi), channel_id=1, source_target_pairs={{0,1},{1,2},{2,3},{3,4},{4,5},{5,6},{6,7},{7,8},{8,9},{9,10},{10,1... | collective-permute-start | bytes 49160 | tf_op jit(solution)/shard_map/ppermute | solution.py:455
  47.7 5.6 %collective-permute-start.5 = (f32[32,128]{1,0:T(8,128)S(1)}, f32[32,128]{1,0:T(8,128)S(1)}, u32[]{:S(2)}, u32[]{:S(2)}) collective-permute-start(f32[32,128]{1,0:T(8,128)S(1)} %get-tuple-element.42.lo), channel_id=1, source_target_pairs={{1,0},{2,1},{3,2},{4,3},{5,4},{6,5},{7,6},{8,7},{9,8},{10,9},{11,1... | collective-permute-start | bytes 49160 | tf_op jit(solution)/shard_map/ppermute | solution.py:456
  53.3 11.7 %collective-permute-start.6 = (f32[64,128]{1,0:T(8,128)S(1)}, f32[64,128]{1,0:T(8,128)S(1)}, u32[]{:S(2)}, u32[]{:S(2)}) collective-permute-start(f32[64,128]{1,0:T(8,128)S(1)} %get-tuple-element.44.second), channel_id=1, source_target_pairs={{0,16},{16,32},{32,48},{48,64},{64,80},{80,96},{96,112},{112,128},... | collective-permute-start | bytes 98312 | tf_op jit(solution)/shard_map/ppermute | solution.py:455
  63.8 3.9 %collective-permute-start.7 = (f32[64,128]{1,0:T(8,128)S(1)}, f32[64,128]{1,0:T(8,128)S(1)}, u32[]{:S(2)}, u32[]{:S(2)}) collective-permute-start(f32[64,128]{1,0:T(8,128)S(1)} %get-tuple-element.45.first), channel_id=1, source_target_pairs={{16,0},{32,16},{48,32},{64,48},{80,64},{96,80},{112,96},{128,112},... | collective-permute-start | bytes 98312 | tf_op jit(solution)/shard_map/ppermute | solution.py:456
  68.4 0.7 copy-start.6
  69.1 39.1 %collective-permute-start.8 = (f32[64,128]{1,0:T(8,128)S(1)}, f32[64,128]{1,0:T(8,128)S(1)}, u32[]{:S(2)}, u32[]{:S(2)}) collective-permute-start(f32[64,128]{1,0:T(8,128)S(1)} %get-tuple-element.51.err), channel_id=1, source_target_pairs={{0,16},{16,32},{32,48},{48,64},{64,80},{80,96},{96,112},{112,128},... | collective-permute-start | bytes 98312 | tf_op jit(solution)/shard_map/ppermute | solution.py:455
  74.2 34.0 %collective-permute-start.9 = (f32[64,128]{1,0:T(8,128)S(1)}, f32[64,128]{1,0:T(8,128)S(1)}, u32[]{:S(2)}, u32[]{:S(2)}) collective-permute-start(f32[64,128]{1,0:T(8,128)S(1)} %get-tuple-element.51.err), channel_id=1, source_target_pairs={{16,0},{32,16},{48,32},{64,48},{80,64},{96,80},{112,96},{128,112},... | collective-permute-start | bytes 98312 | tf_op jit(solution)/shard_map/ppermute | solution.py:456
  106.6 1.2 copy-start.3
  108.3 0.6 copy-start.14
  108.9 7.6 %collective-permute-start.10 = (f32[256,128]{1,0:T(8,128)S(1)}, f32[256,128]{1,0:T(8,128)S(1)}, u32[]{:S(2)}, u32[]{:S(2)}) collective-permute-start(f32[256,128]{1,0:T(8,128)S(1)} %get-tuple-element.53), channel_id=1, source_target_pairs={{0,1},{1,2},{2,3},{3,4},{4,5},{5,6},{6,7},{7,8},{8,9},{9,10},{10,1... | collective-permute-start | bytes 393224 | tf_op jit(solution)/shard_map/ppermute | solution.py:455
  113.1 7.4 %collective-permute-start.11 = (f32[256,128]{1,0:T(8,128)S(1)}, f32[256,128]{1,0:T(8,128)S(1)}, u32[]{:S(2)}, u32[]{:S(2)}) collective-permute-start(f32[256,128]{1,0:T(8,128)S(1)} %get-tuple-element.54), channel_id=1, source_target_pairs={{1,0},{2,1},{3,2},{4,3},{5,4},{6,5},{7,6},{8,7},{9,8},{10,9},{11,1... | collective-permute-start | bytes 393224 | tf_op jit(solution)/shard_map/ppermute | solution.py:456
  120.6 7.3 %collective-permute-start.12 = (f32[256,128]{1,0:T(8,128)S(1)}, f32[256,128]{1,0:T(8,128)S(1)}, u32[]{:S(2)}, u32[]{:S(2)}) collective-permute-start(f32[256,128]{1,0:T(8,128)S(1)} %get-tuple-element.56), channel_id=1, source_target_pairs={{0,1},{1,2},{2,3},{3,4},{4,5},{5,6},{6,7},{7,8},{8,9},{9,10},{10,1... | collective-permute-start | bytes 393224 | tf_op jit(solution)/shard_map/ppermute | solution.py:455
  125.4 6.9 %collective-permute-start.13 = (f32[256,128]{1,0:T(8,128)S(1)}, f32[256,128]{1,0:T(8,128)S(1)}, u32[]{:S(2)}, u32[]{:S(2)}) collective-permute-start(f32[256,128]{1,0:T(8,128)S(1)} %get-tuple-element.57), channel_id=1, source_target_pairs={{1,0},{2,1},{3,2},{4,3},{5,4},{6,5},{7,6},{8,7},{9,8},{10,9},{11,1... | collective-permute-start | bytes 393224 | tf_op jit(solution)/shard_map/ppermute | solution.py:456
  133.1 7.9 %collective-permute-start.14 = (f32[256,128]{1,0:T(8,128)}, f32[256,128]{1,0:T(8,128)}, u32[]{:S(2)}, u32[]{:S(2)}) collective-permute-start(f32[256,128]{1,0:T(8,128)} %get-tuple-element.59), channel_id=1, source_target_pairs={{0,1},{1,2},{2,3},{3,4},{4,5},{5,6},{6,7},{7,8},{8,9},{9,10},{10,1... | collective-permute-start | bytes 393224 | tf_op jit(solution)/shard_map/ppermute | solution.py:455
  138.2 7.2 %collective-permute-start.15 = (f32[256,128]{1,0:T(8,128)}, f32[256,128]{1,0:T(8,128)}, u32[]{:S(2)}, u32[]{:S(2)}) collective-permute-start(f32[256,128]{1,0:T(8,128)} %get-tuple-element.60), channel_id=1, source_target_pairs={{1,0},{2,1},{3,2},{4,3},{5,4},{6,5},{7,6},{8,7},{9,8},{10,9},{11,1... | collective-permute-start | bytes 393224 | tf_op jit(solution)/shard_map/ppermute | solution.py:456
  140.1 17.5 %copy-start.1 = (f32[6,1024,128]{2,1,0:T(8,128)S(1)}, f32[6,1024,128]{2,1,0:T(8,128)}, u32[]{:S(2)}) copy-start(f32[6,1024,128]{2,1,0:T(8,128)} %copy-done) | copy-start | bytes 9437188
  140.2 17.4 %copy-start.5 = (f32[1024,128]{1,0:T(8,128)S(1)}, f32[1024,128]{1,0:T(8,128)}, u32[]{:S(2)}) copy-start(f32[1024,128]{1,0:T(8,128)} %copy-done.4) | copy-start | bytes 1572868
  140.2 17.4 %copy-start.7 = (f32[256,128]{1,0:T(8,128)S(1)}, f32[256,128]{1,0:T(8,128)}, u32[]{:S(2)}) copy-start(f32[256,128]{1,0:T(8,128)} %copy-done.6) | copy-start | bytes 393220
  145.4 0.9 copy-start.15
  147.4 6.5 %collective-permute-start.16 = (f32[192,128]{1,0:T(8,128)S(1)}, f32[192,128]{1,0:T(8,128)S(1)}, u32[]{:S(2)}, u32[]{:S(2)}) collective-permute-start(f32[192,128]{1,0:T(8,128)S(1)} %shard_map.86.own), channel_id=1, source_target_pairs={{0,1},{1,2},{2,3},{3,4},{4,5},{5,6},{6,7},{7,8},{8,9},{9,10},{10,1... | collective-permute-start | bytes 294920 | tf_op jit(solution)/shard_map/ppermute | solution.py:455
  151.1 6.5 %collective-permute-start.17 = (f32[192,128]{1,0:T(8,128)S(1)}, f32[192,128]{1,0:T(8,128)S(1)}, u32[]{:S(2)}, u32[]{:S(2)}) collective-permute-start(f32[192,128]{1,0:T(8,128)S(1)} %shard_map.86.own), channel_id=1, source_target_pairs={{1,0},{2,1},{3,2},{4,3},{5,4},{6,5},{7,6},{8,7},{9,8},{10,9},{11,1... | collective-permute-start | bytes 294920 | tf_op jit(solution)/shard_map/ppermute | solution.py:456
Sparse Core Ops, SparseCore 0:
  13.9 61.9 all-gather.1

commit v3 on v2

--- a/solution.py
+++ b/solution.py
@@ -80,7 +80,8 @@
         at += n
 
 
-def rates_kernel(j_ref, jhi_ref, jlo_ref, out_ref):
+def rates_kernel(j_ref, own, jhi_ref, jlo_ref, out_ref, own_ref):
+    own_ref[...] = own[...]
     rates = j_ref[...]
     high = rates.astype(BF16)
     jhi_ref[...] = high
@@ -93,8 +94,8 @@
 
 
 def pack_kernel(*refs):
-    sources, (lo_ref, hi_ref, low_ref), buffers = refs[:6], refs[6:9], refs[9:15]
-    mid, sems = refs[15:]
+    sources, (own_ref, lo_ref, hi_ref, low_ref), buffers = refs[:6], refs[6:10], refs[10:16]
+    sems = refs[16]
     copies = [
         pltpu.make_async_copy(src, dst, sems.at[i])
         for i, (src, dst) in enumerate(zip(sources, buffers))
@@ -102,128 +103,167 @@
     for copy in copies:
         copy.start()
     rhs, value, speed_a, speed_b, flag_a, flag_b = buffers
-    half = lo_ref.shape[2] // Z
-
-    def put(k, a, x):
+
+    def put(start, x):
         for c in range(Z):
-            piece = x[:, c * LANES : (c + 1) * LANES]
-            lo_ref[k, a, pl.ds(c, half, stride=Z), :] = piece[:half]
-            hi_ref[k, a, pl.ds(c, half, stride=Z), :] = piece[half:]
-
-    for copy in copies[2:]:
+            own_ref[pl.ds(start + c, 8, stride=Z), :] = x[:, c * LANES : (c + 1) * LANES]
+
+    for copy in copies:
         copy.wait()
-    points = rhs.shape[0]
-    for a in range(points):
+    for a in range(8):
+        put(32 * a, value[a])
+        put(256 + 32 * a, rhs[a])
         for k, speed, flag in ((2, speed_a, flag_a), (4, speed_b, flag_b)):
             up = flag[a].astype(F32)
-            put(k, a, speed[a] * up)
-            put(k + 1, a, speed[a] * (1.0 - up))
-    for k in range(2, 6):
-        for m in range(points // 2):
-            for i, src in enumerate((lo_ref, hi_ref)):
-                both = src[k, 2 * m] + src[k, 2 * m + 1]
-                mid[pl.ds(16 * m + 8 * i, 8), :] = 0.125 * pair_sums(both)
-        for m in range(points // 4):
-            both = mid[pl.ds(32 * m, 16), :] + mid[pl.ds(32 * m + 16, 16), :]
-            low_ref[pl.ds(16 * (k - 2) + 8 * m, 8), :] = 0.125 * pair_sums(both)
-    for copy in copies[:2]:
-        copy.wait()
-    for a in range(points):
-        put(0, a, value[a])
-        put(1, a, rhs[a])
-
-
-def widen_kernel(lo, hi, below, above, first_ref, second_ref):
-    width = lo.shape[2]
-    for out, start in ((first_ref, 0), (second_ref, 4)):
-        for i, src in enumerate((below, lo, hi, above)):
-            out[:, :, i * width : (i + 1) * width, :] = src[:, start : start + 4]
+            put(256 * k + 32 * a, speed[a] * up)
+            put(256 * (k + 1) + 32 * a, speed[a] * (1.0 - up))
+    for k in range(4):
+        for m in range(4):
+            at = 256 * (k + 2) + 64 * m
+            mid = 0.125 * pair_sums(own_ref[pl.ds(at, 32), :] + own_ref[pl.ds(at + 32, 32), :])
+            own_ref[pl.ds(1536 + 64 * k + 16 * m, 16), :] = mid
+            lo_ref[pl.ds(448 + 32 * k + 8 * m, 8), :] = mid[:8]
+            hi_ref[pl.ds(448 + 32 * k + 8 * m, 8), :] = mid[8:]
+    for a in range(8):
+        lo_ref[pl.ds(16 * a, 16), :] = own_ref[pl.ds(32 * a, 16), :]
+        hi_ref[pl.ds(16 * a, 16), :] = own_ref[pl.ds(32 * a + 16, 16), :]
+        for k in range(5):
+            at = 256 * (k + 1) + 32 * a
+            lo_ref[pl.ds(128 + 64 * k + 8 * a, 8), :] = own_ref[pl.ds(at, 8), :]
+            hi_ref[pl.ds(128 + 64 * k + 8 * a, 8), :] = own_ref[pl.ds(at + 24, 8), :]
+    for k in range(4):
+        for m in range(2):
+            at = 1536 + 64 * k + 32 * m
+            both = own_ref[pl.ds(at, 16), :] + own_ref[pl.ds(at + 16, 16), :]
+            low_ref[pl.ds(16 * k + 8 * m, 8), :] = 0.125 * pair_sums(both)
+
+
+def widen_kernel(own, below, above, wide_ref, up_ref, down_ref):
+    def put(begin, piece, up, down):
+        wide_ref[pl.ds(begin, piece.shape[0]), :] = piece
+        if up is not None:
+            up_ref[pl.ds(up, piece.shape[0]), :] = piece
+        if down is not None:
+            down_ref[pl.ds(down, piece.shape[0]), :] = piece
+
+    def joined(at, width, other, part):
+        ends = [src[pl.ds(other, part), :] for src in (below, above)]
+        return jnp.concatenate([ends[0], own[pl.ds(at, width), :], ends[1]], axis=0)
+
+    for a in range(8):
+        piece = joined(32 * a, 32, 16 * a, 16)
+        put(64 * a, piece, 64 * (a - 1) if a > 0 else None, 64 * a if a < 7 else None)
+        for k in range(5):
+            piece = joined(256 * (k + 1) + 32 * a, 32, 128 + 64 * k + 8 * a, 8)
+            at = 448 + 288 * k
+            up = at + 48 * (a - 2) if a > 1 else None
+            put(512 + 384 * k + 48 * a, piece, up, at + 48 * a if a < 6 else None)
+    for m in range(4):
+        for k in range(4):
+            piece = joined(1536 + 64 * k + 16 * m, 16, 448 + 32 * k + 8 * m, 8)
+            at = 1888 + 64 * k
+            up = at + 32 * (m - 2) if m > 1 else None
+            put(2432 + 128 * k + 32 * m, piece, up, at + 32 * m if m < 2 else None)
 
 
 def fine_kernel(
-    below, first, second, above, jhi, jlo, out,
-    fine_out, val_out, rlo_ref, rhi_ref, mid_ref, fine_ref, val_ref, v0, v1, inc, sems,
+    below, own, above, jhi, jlo, out,
+    keep_ref, val_ref, rhs_ref, lo_ref, hi_ref, mid_ref, v0, v1, v2, inc, f,
 ):
-    outflow = spread(out[...], 64)
-    for a in range(16):
-        src = (below, first, second, above)[a // 4]
-        here = pl.ds(64 * a, 64)
-        v0[here, :] = src[0, a % 4]
+    v0[0:448, :] = below[0:448, :]
+    v0[448:960, :] = own[0:512, :]
+    v0[960:1408, :] = above[0:448, :]
+    outflow = spread(out[...], 48)
+    for a in range(20):
+        here = pl.ds(48 * a, 48)
         total = DISCOUNT + outflow
-        for k in range(1, 6):
-            x = src[k, a % 4]
-            fine_ref[k - 1, here, :] = x
-            if k > 1:
+        for k in range(5):
+            if a < 6:
+                x = below[pl.ds(448 + 288 * k + 48 * a, 48), :]
+            elif a < 14:
+                x = own[pl.ds(512 + 384 * k + 48 * (a - 6), 48), :]
+            else:
+                x = above[pl.ds(448 + 288 * k + 48 * (a - 14), 48), :]
+            f[k, here, :] = x
+            if k:
                 total = total + x
-        fine_ref[5, here, :] = OMEGA / total
-    keep_fine = pltpu.make_async_copy(fine_ref, fine_out, sems.at[0])
-    keep_fine.start()
+        f[5, here, :] = OMEGA / total
+
+    def rest(a):
+        here = pl.ds(48 * a, 48)
+        return f[0, here, :], f[1, here, :], f[2, here, :], f[3, here, :], f[4, here, :]
+
+    income(v0, inc, [(64, 64, 16 * 20)], jhi, jlo)
+    for a in range(20):
+        rhs, fa, ba, fb, bb = rest(a)
+        center = row(v0, a + 1, 64)
+        total = rhs + inc[pl.ds(64 * (a + 1) + 8, 48), :]
+        total = total + fa * v0[pl.ds(64 * (a + 2) + 8, 48), :]
+        total = total + ba * v0[pl.ds(64 * a + 8, 48), :]
+        total = total + fb * later(center)[8:56] + bb * earlier(center)[8:56]
+        here = pl.ds(48 * a, 48)
+        v1[here, :] = (1.0 - OMEGA) * center[8:56] + f[5, here, :] * total
 
     def applied(src, a):
-        here = pl.ds(64 * a, 64)
-        center = src[here, :]
-        total = fine_ref[0, here, :] + inc[here, :]
-        total = total + fine_ref[1, here, :] * row(src, a + 1, 64)
-        total = total + fine_ref[2, here, :] * row(src, a - 1, 64)
-        total = total + fine_ref[3, here, :] * later(center)
-        total = total + fine_ref[4, here, :] * earlier(center)
-        return center, total
-
-    def sweep(src, dst, begin, end):
-        income(src, inc, [(64 * begin, 64 * begin, 16 * (end - begin))], jhi, jlo)
-        for a in range(begin, end):
-            center, total = applied(src, a)
-            here = pl.ds(64 * a, 64)
-            dst[here, :] = (1.0 - OMEGA) * center + fine_ref[5, here, :] * total
-
-    sweep(v0, v1, 1, 15)
-    sweep(v1, val_ref, 2, 14)
-    edge = jnp.zeros((128, LANES), F32)
-    val_ref[0:128, :] = edge
-    val_ref[896:1024, :] = edge
-    keep_val = pltpu.make_async_copy(val_ref, val_out, sems.at[1])
-    keep_val.start()
-    income(val_ref, inc, [(64 * 4, 64 * 4, 16 * 8)], jhi, jlo)
+        rhs, fa, ba, fb, bb = rest(a)
+        center = row(src, a, 48)
+        total = rhs + row(inc, a, 48) + fa * row(src, a + 1, 48) + ba * row(src, a - 1, 48)
+        return center, total + fb * later(center) + bb * earlier(center)
+
+    income(v1, inc, [(48, 48, 12 * 18)], jhi, jlo)
+    for a in range(1, 19):
+        center, total = applied(v1, a)
+        here = pl.ds(48 * a, 48)
+        v2[here, :] = (1.0 - OMEGA) * center + f[5, here, :] * total
+    income(v2, inc, [(96, 96, 12 * 16)], jhi, jlo)
 
     def residual(a):
-        center, total = applied(val_ref, a)
-        here = pl.ds(64 * a, 64)
+        center, total = applied(v2, a)
         diag = DISCOUNT + outflow
-        for k in range(1, 5):
-            diag = diag + fine_ref[k, here, :]
-        return (total - diag * center)[16:48]
-
-    for m in range(4):
-        coarse = 0.25 * pair_sums(residual(4 + 2 * m) + residual(5 + 2 * m))
-        rlo_ref[pl.ds(8 * m, 8), :] = coarse[:8]
-        rhi_ref[pl.ds(8 * m, 8), :] = coarse[8:]
+        for x in rest(a)[1:]:
+            diag = diag + x
+        return (total - diag * center)[8:40]
+
+    for m in range(8):
+        coarse = 0.25 * pair_sums(residual(2 + 2 * m) + residual(3 + 2 * m))
+        rhs_ref[pl.ds(16 * m, 16), :] = coarse
+        lo_ref[pl.ds(8 * m, 8), :] = coarse[:8]
+        hi_ref[pl.ds(8 * m, 8), :] = coarse[8:]
+    for a in range(12):
+        value = row(v2, a + 4, 48)[8:40]
+        val_ref[pl.ds(32 * a, 32), :] = value
+        lo_ref[pl.ds(64 + 8 * a, 8), :] = value[:8]
+        hi_ref[pl.ds(64 + 8 * a, 8), :] = value[24:]
+    for k in range(6):
+        keep_ref[k] = f[k, pl.ds(48 * 4, 48 * 12), :]
 
     outflow = spread(out[...], 32)
     for m in range(8):
         here = pl.ds(32 * m, 32)
         total = DISCOUNT + outflow
         for k in range(4):
-            both = fine_ref[k + 1, pl.ds(128 * m, 64), :] + fine_ref[k + 1, pl.ds(128 * m + 64, 64), :]
-            x = 0.125 * pair_sums(both)
+            if m < 2:
+                x = below[pl.ds(1888 + 64 * k + 32 * m, 32), :]
+            elif m < 6:
+                x = own[pl.ds(2432 + 128 * k + 32 * (m - 2), 32), :]
+            else:
+                x = above[pl.ds(1888 + 64 * k + 32 * (m - 6), 32), :]
             mid_ref[k, here, :] = x
             total = total + x
         mid_ref[4, here, :] = OMEGA / total
-    keep_fine.wait()
-    keep_val.wait()
-
-
-def widen_mid_kernel(lo, hi, below, above, first_ref, second_ref):
-    for m in range(4):
-        out = (first_ref, second_ref)[m // 2]
-        for i, src in enumerate((below, lo, hi, above)):
-            out[pl.ds(32 * (m % 2) + 8 * i, 8), :] = src[pl.ds(8 * m, 8), :]
 
 
 def mid_kernel(
-    below, first, second, above, mid, jhi, jlo, out, pay_ref, err_ref, rhs_ref, e0, e1, inc
+    own, val, below, above, mid, jhi, jlo, out, pay_ref, err_ref, rhs_ref, wide_ref, e0, e1, inc
 ):
-    for i, src in enumerate((below, first, second, above)):
-        rhs_ref[pl.ds(64 * i, 64), :] = src[...]
+    for a in range(8):
+        for i, piece in enumerate((below[pl.ds(8 * a, 8), :], row(own, a, 16), above[pl.ds(8 * a, 8), :])):
+            rhs_ref[pl.ds(32 * a + (0, 8, 24)[i], piece.shape[0]), :] = piece
+    for a in range(12):
+        ends = [src[pl.ds(64 + 8 * a, 8), :] for src in (below, above)]
+        wide_ref[pl.ds(48 * a, 8), :] = ends[0]
+        wide_ref[pl.ds(48 * a + 8, 32), :] = row(val, a, 32)
+        wide_ref[pl.ds(48 * a + 40, 8), :] = ends[1]
     e0[...] = mid[4] * rhs_ref[...]
 
     def applied(src, a):
@@ -407,43 +447,39 @@
         total = total + mid[2, here, :] * later(center)
         total = total + mid[3, here, :] * earlier(center)
         error = (1.0 - OMEGA) * center + mid[4, here, :] * total
-        fill = doubled(error)
-        for f in (2 * a, 2 * a + 1):
-            v0[pl.ds(64 * f, 64), :] = val[pl.ds(64 * f, 64), :] + fill
+        fill = doubled(error)[8:56]
+        for f in (2 * a - 2, 2 * a - 1):
+            v0[pl.ds(48 * f, 48), :] = row(val, f, 48) + fill
 
     def sweep(src, dst, begin, end):
-        income(src, inc, [(64 * begin, 64 * begin, 16 * (end - begin))], jhi, jlo)
+        income(src, inc, [(48 * begin, 48 * begin, 12 * (end - begin))], jhi, jlo)
         for a in range(begin, end):
-            here = pl.ds(64 * a, 64)
+            here = pl.ds(48 * a, 48)
             center = src[here, :]
             total = fine[0, here, :] + inc[here, :]
-            total = total + fine[1, here, :] * row(src, a + 1, 64)
-            total = total + fine[2, here, :] * row(src, a - 1, 64)
+            total = total + fine[1, here, :] * row(src, a + 1, 48)
+            total = total + fine[2, here, :] * row(src, a - 1, 48)
             total = total + fine[3, here, :] * later(center)
             total = total + fine[4, here, :] * earlier(center)
             dst[here, :] = (1.0 - OMEGA) * center + fine[5, here, :] * total
 
-    sweep(v0, v1, 3, 13)
-    sweep(v1, v2, 4, 12)
+    sweep(v0, v1, 1, 11)
+    sweep(v1, v2, 2, 10)
     for a in range(8):
         for c in range(Z):
-            piece = v2[pl.ds(64 * (a + 4) + 16 + c, 8, stride=Z), :]
+            piece = v2[pl.ds(48 * (a + 2) + 8 + c, 8, stride=Z), :]
             out_ref[a, :, c * LANES : (c + 1) * LANES] = piece
 
 
-def call(kernel, args, outs, scratch=(), flops=0, places=(), out_places=(), limit=24):
+def call(kernel, args, outs, scratch=(), flops=0, places=(), limit=24):
     outs = [x if isinstance(x, jax.ShapeDtypeStruct) else jax.ShapeDtypeStruct(x, F32) for x in outs]
     moved = sum(x.size * x.dtype.itemsize for x in (*args, *outs))
-
-    def specs(kinds, count):
-        kinds = list(kinds) + [pltpu.VMEM] * (count - len(kinds))
-        return [pl.BlockSpec(memory_space=kind) for kind in kinds]
-
+    kinds = list(places) + [pltpu.VMEM] * (len(args) - len(places))
     return pl.pallas_call(
         kernel,
         out_shape=outs,
-        in_specs=specs(places, len(args)),
-        out_specs=specs(out_places, len(outs)),
+        in_specs=[pl.BlockSpec(memory_space=kind) for kind in kinds],
+        out_specs=[pl.BlockSpec(memory_space=pltpu.VMEM)] * len(outs),
         scratch_shapes=[pltpu.VMEM(s, F32) if isinstance(s, tuple) else s for s in scratch],
         compiler_params=pltpu.CompilerParams(vmem_limit_bytes=limit * 2**20),
         cost_estimate=pl.CostEstimate(flops=flops, bytes_accessed=moved, transcendentals=0),
@@ -461,38 +497,36 @@
     nz = jump_rates.shape[0]
     dot_flops = 2 * 3 * nz * nz
     inputs = (right_side, value_guess, speed_liq, speed_ill, flag_liq, flag_ill)
-    half = (6, 8, 16, LANES)
-    lo, hi, low = call(
+    own, lo, hi, low = call(
         pack_kernel,
         inputs,
-        [half, half, (64, LANES)],
-        [pltpu.VMEM(x.shape, x.dtype) for x in inputs]
-        + [(64, LANES), pltpu.SemaphoreType.DMA((6,))],
+        [(1792, LANES), (576, LANES), (576, LANES), (64, LANES)],
+        [pltpu.VMEM(x.shape, x.dtype) for x in inputs] + [pltpu.SemaphoreType.DMA((6,))],
         places=[pltpu.HBM] * 6,
-    )
+        limit=57,
+    )
+    below, above = neighbours(lo, hi, "ill")
     coefs = lax.all_gather(low, "liq", axis=0, tiled=True)
     rates = jax.ShapeDtypeStruct((nz, nz), BF16)
-    jhi, jlo, out = call(rates_kernel, (jump_rates,), [rates, rates, (TILE, LANES)])
+    jhi, jlo, out, own = call(
+        rates_kernel, (jump_rates, own), [rates, rates, (TILE, LANES), own.shape]
+    )
+    wide, up, down = call(
+        widen_kernel, (own, below, above), [(2944, LANES), (2144, LANES), (2144, LANES)]
+    )
+    below, above = neighbours(down, up, "liq")
+    fine, value, rhs_mid, lo, hi, mid = call(
+        fine_kernel,
+        (below, wide, above, jhi, jlo, out),
+        [(6, 576, LANES), (384, LANES), (128, LANES), (160, LANES), (160, LANES), (5, 256, LANES)],
+        [(1408, LANES), (960, LANES), (960, LANES), (1408, LANES), (6, 960, LANES)],
+        flops=dot_flops * 730,
+    )
     below, above = neighbours(lo, hi, "ill")
-    wide = (6, 4, 64, LANES)
-    first, second = call(widen_kernel, (lo, hi, below, above), [wide, wide])
-    below, above = neighbours(first, second, "liq")
-    whole, six = (1024, LANES), (6, 1024, LANES)
-    fine, value, rlo, rhi, mid = call(
-        fine_kernel,
-        (below, first, second, above, jhi, jlo, out),
-        [six, whole, (32, LANES), (32, LANES), (5, 256, LANES)],
-        [six, whole, whole, whole, whole, pltpu.SemaphoreType.DMA((2,))],
-        flops=dot_flops * 550,
-        out_places=[pltpu.HBM] * 2,
-    )
-    below, above = neighbours(rlo, rhi, "ill")
-    first, second = call(widen_mid_kernel, (rlo, rhi, below, above), [(64, LANES)] * 2)
-    below, above = neighbours(first, second, "liq")
-    rhs_low, error_mid, rhs_mid = call(
+    rhs_low, error_mid, rhs_mid, value = call(
         mid_kernel,
-        (below, first, second, above, mid, jhi, jlo, out),
-        [(16, LANES), (64, LANES), (256, LANES)],
+        (rhs_mid, value, below, above, mid, jhi, jlo, out),
+        [(16, LANES), (64, LANES), (256, LANES), (576, LANES)],
         [(256, LANES)] * 3,
         flops=dot_flops * 80,
     )
@@ -510,7 +544,10 @@
     for step in range(SWEEPS - 1):
         below, above = neighbours(lo, hi, "ill")
         (target,) = call(
-            local_target_kernel, (e, rhs, fac, jhi, jlo), [line], flops=dot_flops * lines // Z
+            local_target_kernel,
+            (e, rhs, fac, jhi, jlo),
+            [line],
+            flops=dot_flops * lines // Z,
         )
         if step < SWEEPS - 2:
             e, lo, hi = call(
@@ -529,8 +566,8 @@
         last_kernel,
         (total, below, above, mid, rhs_mid, fine, value, jhi, jlo),
         [right_side.shape],
-        [(576, LANES), (256, LANES), (256, LANES), whole, whole, whole, whole],
-        flops=dot_flops * 400,
+        [(576, LANES), (256, LANES), (256, LANES)] + [(576, LANES)] * 4,
+        flops=dot_flops * 330,
     )
     return result
 

time: 168 us -> 154 us (0.917)
  the two profiles are of different devices: /device:TPU:64 before, /device:TPU:32 now
where the time goes in v3:
time: 154 us
  starting transfers between devices  57.3 us (37%)
  waiting for transfers between devices  34.1 us (22%)
  blocking collectives  30.6 us (20%)
  between operations  13.7 us (9%)
  Pallas kernels  12.4 us (8%)
  local copies, waits for them, and re-layouts  5.64 us (4%)
    ppermute x8, starting transfers between devices, neighbours(): below = lax.ppermute(hi, axis, [(i, i + 1) for i in range(count - 1)])  39.4 us
    all_gather x1, blocking collectives, body(): rhs = lax.all_gather(rhs_low, 'liq', axis=0, tiled=True)  30.6 us
    ppermute x8, waiting for transfers between devices, neighbours(): above = lax.ppermute(lo, axis, [(i + 1, i) for i in range(count - 1)])  29.8 us
    ppermute x8, starting transfers between devices, neighbours(): above = lax.ppermute(lo, axis, [(i + 1, i) for i in range(count - 1)])  17.9 us
    pallas_call x14, Pallas kernels, call(): pl.pallas_call(kernel, out_shape=outs, in_specs=[pl.BlockSpec(memory_spac...  12.4 us
    unnamed x22, local copies, waits for them, and re-layouts  5.64 us
    ppermute x8, waiting for transfers between devices, neighbours(): below = lax.ppermute(hi, axis, [(i, i + 1) for i in range(count - 1)])  4.21 us
  transfers between devices with their start and end apart: 17, of which 14 were waited for; matrix products, arithmetic and copies ran while one was open for 0% of the time, Pallas kernels for 3%

profile of v3, /device:TPU:32, one launch (start us, length us, event | category | flops | bytes accessed | tf_op | source)
XLA Modules:
  0.0 153.7 jit_solution(16878174300163357653)
XLA Ops:
  6.5 0.0 all-gather.2.cloned.1.call-start
  6.5 2.5 %shard_map.73 = (f32[1792,128]{1,0:T(8,128)}, f32[576,128]{1,0:T(8,128)}, f32[576,128]{1,0:T(8,128)}, f32[64,128]{1,0:T(8,128)}) custom-call(f32[8,8,512]{2,1,0:T(8,128)} %refs_0_.1, f32[8,8,512]{2,1,0:T(8,128)} %refs_1_.1, f32[8,8,512]{2,1,0:T(8,128)} %refs_2_.1, f32[8,8,512]{2,1,0:T(8,128)} %refs_3_.1, s32[8,8,512]{2,1,0:T(8,128)} %refs_4_.1, ...), custom_call_target="tpu_custom_call" | custom-call | bytes 2326528 | tf_op jit(solution)/shard_map/pallas_call | solution.py:478
  9.0 0.0 all-gather.2.cloned.1.call-update
  9.0 3.8 %collective-permute-start = (f32[576,128]{1,0:T(8,128)}, f32[576,128]{1,0:T(8,128)S(1)}, u32[]{:S(2)}, u32[]{:S(2)}) collective-permute-start(f32[576,128]{1,0:T(8,128)} %get-tuple-element.40), channel_id=1, source_target_pairs={{0,1},{1,2},{2,3},{3,4},{4,5},{5,6},{6,7},{7,8},{8,9},{9,10},{10,1... | collective-permute-start | bytes 884744 | tf_op jit(solution)/shard_map/ppermute | solution.py:491
  12.9 4.9 %collective-permute-start.1 = (f32[576,128]{1,0:T(8,128)}, f32[576,128]{1,0:T(8,128)S(1)}, u32[]{:S(2)}, u32[]{:S(2)}) collective-permute-start(f32[576,128]{1,0:T(8,128)} %get-tuple-element.41), channel_id=1, source_target_pairs={{1,0},{2,1},{3,2},{4,3},{5,4},{6,5},{7,6},{8,7},{9,8},{10,9},{11,1... | collective-permute-start | bytes 884744 | tf_op jit(solution)/shard_map/ppermute | solution.py:492
  17.8 0.0 copy-start.3
  17.8 1.2 copy-done.3
  19.0 1.2 copy-done.4
  20.2 0.2 shard_map.74
  20.4 0.3 collective-permute-done.below
  20.7 2.9 %collective-permute-done.1.above = f32[576,128]{1,0:T(8,128)S(1)} collective-permute-done((f32[576,128]{1,0:T(8,128)}, f32[576,128]{1,0:T(8,128)S(1)}, u32[]{:S(2)}, u32[]{:S(2)}) %collective-permute-start.1) | collective-permute-done | bytes 294944 | tf_op jit(solution)/shard_map/ppermute | solution.py:492
  23.6 0.2 shard_map.75
  23.9 1.4 collective-permute-start.2
  25.2 1.3 collective-permute-start.3
  26.5 1.0 collective-permute-done.2.below
  27.5 4.0 %collective-permute-done.3.above = f32[2144,128]{1,0:T(8,128)S(1)} collective-permute-done((f32[2144,128]{1,0:T(8,128)S(1)}, f32[2144,128]{1,0:T(8,128)S(1)}, u32[]{:S(2)}, u32[]{:S(2)}) %collective-permute-start.3) | collective-permute-done | bytes 1097760 | tf_op jit(solution)/shard_map/ppermute | solution.py:492
  31.5 2.5 %shard_map.76 = (f32[6,576,128]{2,1,0:T(8,128)S(1)}, f32[384,128]{1,0:T(8,128)S(1)}, f32[128,128]{1,0:T(8,128)S(1)}, f32[160,128]{1,0:T(8,128)S(1)}, f32[160,128]{1,0:T(8,128)S(1)}, /*index=5*/f32[5,256,128]{2,1,0:T(8,128)S(1)}) custom-call(f32[2144,128]{1,0:T(8,128)S(1)} %collective-permute-done.2.below, f32[2944,128]{1,0:T(8,128)S(1)} %get-tuple-element.43.own, ...), custom_call_target="tpu_custom_call" | custom-call | flops 1148190720 | bytes 7606272 | tf_op jit(solution)/shard_map/pallas_call | solution.py:478
  34.0 0.0 copy-start
  34.0 5.0 %collective-permute-start.4 = (f32[160,128]{1,0:T(8,128)S(1)}, f32[160,128]{1,0:T(8,128)S(1)}, u32[]{:S(2)}, u32[]{:S(2)}) collective-permute-start(f32[160,128]{1,0:T(8,128)S(1)} %get-tuple-element.50), channel_id=1, source_target_pairs={{0,1},{1,2},{2,3},{3,4},{4,5},{5,6},{6,7},{7,8},{8,9},{9,10},{10,1... | collective-permute-start | bytes 245768 | tf_op jit(solution)/shard_map/ppermute | solution.py:491
  39.0 1.9 %collective-permute-start.5 = (f32[160,128]{1,0:T(8,128)S(1)}, f32[160,128]{1,0:T(8,128)S(1)}, u32[]{:S(2)}, u32[]{:S(2)}) collective-permute-start(f32[160,128]{1,0:T(8,128)S(1)} %get-tuple-element.51), channel_id=1, source_target_pairs={{1,0},{2,1},{3,2},{4,3},{5,4},{6,5},{7,6},{8,7},{9,8},{10,9},{11,1... | collective-permute-start | bytes 245768 | tf_op jit(solution)/shard_map/ppermute | solution.py:492
  41.0 0.1 collective-permute-done.4.below
  41.1 5.2 %collective-permute-done.5.above = f32[160,128]{1,0:T(8,128)S(1)} collective-permute-done((f32[160,128]{1,0:T(8,128)S(1)}, f32[160,128]{1,0:T(8,128)S(1)}, u32[]{:S(2)}, u32[]{:S(2)}) %collective-permute-start.5) | collective-permute-done | bytes 81952 | tf_op jit(solution)/shard_map/ppermute | solution.py:492
  46.3 0.8 shard_map.77
  47.1 0.0 copy-start.5
  47.1 0.7 copy-done.5
  47.8 0.7 copy-done.7
  48.5 13.7 %collective-permute-start.6 = (f32[64,128]{1,0:T(8,128)S(1)}, f32[64,128]{1,0:T(8,128)S(1)}, u32[]{:S(2)}, u32[]{:S(2)}) collective-permute-start(f32[64,128]{1,0:T(8,128)S(1)} %get-tuple-element.57.err), channel_id=1, source_target_pairs={{0,16},{16,32},{32,48},{48,64},{64,80},{80,96},{96,112},{112,128},... | collective-permute-start | bytes 98312 | tf_op jit(solution)/shard_map/ppermute | solution.py:491
  62.2 1.3 collective-permute-start.7
  63.5 0.0 copy-done
  63.5 30.6 %all_gather.6.rhs = f32[512,128]{1,0:T(8,128)S(1)} all-gather(f32[16,128]{1,0:T(8,128)S(1)} %get-tuple-element.53), channel_id=1, replica_groups=mesh['liq'=32,'ill'=16] {'liq'}, dimensions={0}, use_global_device_ids=true | all-gather | bytes 270336 | tf_op jit(solution)/shard_map/all_gather | solution.py:534
  94.1 1.2 copy-done.2
  95.4 0.3 shard_map.78
  95.7 0.0 collective-permute-done.6.err_lo
  95.7 0.0 collective-permute-done.7.err_hi
  95.7 0.1 shard_map.79
  95.9 0.0 copy-start.9
  95.9 0.6 copy-done.9
  96.5 3.9 %collective-permute-start.8 = (f32[256,128]{1,0:T(8,128)S(1)}, f32[256,128]{1,0:T(8,128)S(1)}, u32[]{:S(2)}, u32[]{:S(2)}) collective-permute-start(f32[256,128]{1,0:T(8,128)S(1)} %get-tuple-element.59), channel_id=1, source_target_pairs={{0,1},{1,2},{2,3},{3,4},{4,5},{5,6},{6,7},{7,8},{8,9},{9,10},{10,1... | collective-permute-start | bytes 393224 | tf_op jit(solution)/shard_map/ppermute | solution.py:491
  100.4 1.9 %collective-permute-start.9 = (f32[256,128]{1,0:T(8,128)S(1)}, f32[256,128]{1,0:T(8,128)S(1)}, u32[]{:S(2)}, u32[]{:S(2)}) collective-permute-start(f32[256,128]{1,0:T(8,128)S(1)} %get-tuple-element.60), channel_id=1, source_target_pairs={{1,0},{2,1},{3,2},{4,3},{5,4},{6,5},{7,6},{8,7},{9,8},{10,9},{11,1... | collective-permute-start | bytes 393224 | tf_op jit(solution)/shard_map/ppermute | solution.py:492
  102.3 0.4 shard_map.80.t
  102.8 1.4 collective-permute-done.8.below
  104.1 4.0 %collective-permute-done.9.above = f32[256,128]{1,0:T(8,128)S(1)} collective-permute-done((f32[256,128]{1,0:T(8,128)S(1)}, f32[256,128]{1,0:T(8,128)S(1)}, u32[]{:S(2)}, u32[]{:S(2)}) %collective-permute-start.9) | collective-permute-done | bytes 131104 | tf_op jit(solution)/shard_map/ppermute | solution.py:492
  108.1 0.2 shard_map.81
  108.3 3.7 %collective-permute-start.10 = (f32[256,128]{1,0:T(8,128)S(1)}, f32[256,128]{1,0:T(8,128)S(1)}, u32[]{:S(2)}, u32[]{:S(2)}) collective-permute-start(f32[256,128]{1,0:T(8,128)S(1)} %get-tuple-element.62), channel_id=1, source_target_pairs={{0,1},{1,2},{2,3},{3,4},{4,5},{5,6},{6,7},{7,8},{8,9},{9,10},{10,1... | collective-permute-start | bytes 393224 | tf_op jit(solution)/shard_map/ppermute | solution.py:491
  112.0 2.1 %collective-permute-start.11 = (f32[256,128]{1,0:T(8,128)S(1)}, f32[256,128]{1,0:T(8,128)S(1)}, u32[]{:S(2)}, u32[]{:S(2)}) collective-permute-start(f32[256,128]{1,0:T(8,128)S(1)} %get-tuple-element.63), channel_id=1, source_target_pairs={{1,0},{2,1},{3,2},{4,3},{5,4},{6,5},{7,6},{8,7},{9,8},{10,9},{11,1... | collective-permute-start | bytes 393224 | tf_op jit(solution)/shard_map/ppermute | solution.py:492
  114.2 0.4 shard_map.82.t
  114.6 0.6 collective-permute-done.10.below
  115.2 4.7 %collective-permute-done.11.above = f32[256,128]{1,0:T(8,128)S(1)} collective-permute-done((f32[256,128]{1,0:T(8,128)S(1)}, f32[256,128]{1,0:T(8,128)S(1)}, u32[]{:S(2)}, u32[]{:S(2)}) %collective-permute-start.11) | collective-permute-done | bytes 131104 | tf_op jit(solution)/shard_map/ppermute | solution.py:492
  119.8 0.9 shard_map.83
  120.7 3.9 %collective-permute-start.12 = (f32[256,128]{1,0:T(8,128)}, f32[256,128]{1,0:T(8,128)}, u32[]{:S(2)}, u32[]{:S(2)}) collective-permute-start(f32[256,128]{1,0:T(8,128)} %get-tuple-element.65), channel_id=1, source_target_pairs={{0,1},{1,2},{2,3},{3,4},{4,5},{5,6},{6,7},{7,8},{8,9},{9,10},{10,1... | collective-permute-start | bytes 393224 | tf_op jit(solution)/shard_map/ppermute | solution.py:491
  124.6 2.6 %collective-permute-start.13 = (f32[256,128]{1,0:T(8,128)}, f32[256,128]{1,0:T(8,128)}, u32[]{:S(2)}, u32[]{:S(2)}) collective-permute-start(f32[256,128]{1,0:T(8,128)} %get-tuple-element.66), channel_id=1, source_target_pairs={{1,0},{2,1},{3,2},{4,3},{5,4},{6,5},{7,6},{8,7},{9,8},{10,9},{11,1... | collective-permute-start | bytes 393224 | tf_op jit(solution)/shard_map/ppermute | solution.py:492
  127.2 0.0 copy-start.10
  127.2 0.0 copy-start.6
  127.2 0.4 shard_map.84.t
  127.6 0.2 collective-permute-done.12.below
  127.9 5.1 %collective-permute-done.13.above = f32[256,128]{1,0:T(8,128)} collective-permute-done((f32[256,128]{1,0:T(8,128)}, f32[256,128]{1,0:T(8,128)}, u32[]{:S(2)}, u32[]{:S(2)}) %collective-permute-start.13) | collective-permute-done | bytes 131104 | tf_op jit(solution)/shard_map/ppermute | solution.py:492
  132.9 1.1 shard_map.85.own
  134.1 3.9 %collective-permute-start.14 = (f32[192,128]{1,0:T(8,128)S(1)}, f32[192,128]{1,0:T(8,128)S(1)}, u32[]{:S(2)}, u32[]{:S(2)}) collective-permute-start(f32[192,128]{1,0:T(8,128)S(1)} %shard_map.85.own), channel_id=1, source_target_pairs={{0,1},{1,2},{2,3},{3,4},{4,5},{5,6},{6,7},{7,8},{8,9},{9,10},{10,1... | collective-permute-start | bytes 294920 | tf_op jit(solution)/shard_map/ppermute | solution.py:491
  138.0 1.9 %collective-permute-start.15 = (f32[192,128]{1,0:T(8,128)S(1)}, f32[192,128]{1,0:T(8,128)S(1)}, u32[]{:S(2)}, u32[]{:S(2)}) collective-permute-start(f32[192,128]{1,0:T(8,128)S(1)} %shard_map.85.own), channel_id=1, source_target_pairs={{1,0},{2,1},{3,2},{4,3},{5,4},{6,5},{7,6},{8,7},{9,8},{10,9},{11,1... | collective-permute-start | bytes 294920 | tf_op jit(solution)/shard_map/ppermute | solution.py:492
  139.9 0.7 collective-permute-done.14.below
  140.6 3.9 %collective-permute-done.15.above = f32[192,128]{1,0:T(8,128)S(1)} collective-permute-done((f32[192,128]{1,0:T(8,128)S(1)}, f32[192,128]{1,0:T(8,128)S(1)}, u32[]{:S(2)}, u32[]{:S(2)}) %collective-permute-start.15) | collective-permute-done | bytes 98336 | tf_op jit(solution)/shard_map/ppermute | solution.py:492
  144.5 0.0 copy-done.6
  144.5 0.0 copy-done.8
  144.5 2.3 %shard_map.86 = f32[8,8,512]{2,1,0:T(8,128)} custom-call(f32[192,128]{1,0:T(8,128)S(1)} %shard_map.85.own, f32[192,128]{1,0:T(8,128)S(1)} %collective-permute-done.14.below, f32[192,128]{1,0:T(8,128)S(1)} %collective-permute-done.15.above, f32[5,256,128]{2,1,0:T(8,128)S(1)} %get-tuple-element.52.mid, f32[256,128]{1,0:T(8,128)S(1)} %copy-done.8, ...), custom_call_target="tpu_custom_call" | custom-call | flops 519045120 | bytes 4325376 | tf_op jit(solution)/shard_map/pallas_call | solution.py:478
  (8 shorter events, 0.0 us)
Async XLA Ops:
  6.5 87.6 %all-gather.2.cloned.1.call-start = ((), (), s32[]{:S(2)}) async-start(), calls=%async_computation | async-start | bytes 1081344 | tf_op jit(solution)/shard_map/all_gather | solution.py:509
  9.0 11.7 %collective-permute-start = (f32[576,128]{1,0:T(8,128)}, f32[576,128]{1,0:T(8,128)S(1)}, u32[]{:S(2)}, u32[]{:S(2)}) collective-permute-start(f32[576,128]{1,0:T(8,128)} %get-tuple-element.40), channel_id=1, source_target_pairs={{0,1},{1,2},{2,3},{3,4},{4,5},{5,6},{6,7},{7,8},{8,9},{9,10},{10,1... | collective-permute-start | bytes 884744 | tf_op jit(solution)/shard_map/ppermute | solution.py:491
  12.9 10.8 %collective-permute-start.1 = (f32[576,128]{1,0:T(8,128)}, f32[576,128]{1,0:T(8,128)S(1)}, u32[]{:S(2)}, u32[]{:S(2)}) collective-permute-start(f32[576,128]{1,0:T(8,128)} %get-tuple-element.41), channel_id=1, source_target_pairs={{1,0},{2,1},{3,2},{4,3},{5,4},{6,5},{7,6},{8,7},{9,8},{10,9},{11,1... | collective-permute-start | bytes 884744 | tf_op jit(solution)/shard_map/ppermute | solution.py:492
  17.8 1.2 copy-start.3
  19.0 1.2 copy-start.4
  23.9 3.6 %collective-permute-start.2 = (f32[2144,128]{1,0:T(8,128)S(1)}, f32[2144,128]{1,0:T(8,128)S(1)}, u32[]{:S(2)}, u32[]{:S(2)}) collective-permute-start(f32[2144,128]{1,0:T(8,128)S(1)} %get-tuple-element.42), channel_id=1, source_target_pairs={{0,16},{16,32},{32,48},{48,64},{64,80},{80,96},{96,112},{112,128},... | collective-permute-start | bytes 3293192 | tf_op jit(solution)/shard_map/ppermute | solution.py:491
  25.2 6.3 %collective-permute-start.3 = (f32[2144,128]{1,0:T(8,128)S(1)}, f32[2144,128]{1,0:T(8,128)S(1)}, u32[]{:S(2)}, u32[]{:S(2)}) collective-permute-start(f32[2144,128]{1,0:T(8,128)S(1)} %get-tuple-element.44), channel_id=1, source_target_pairs={{16,0},{32,16},{48,32},{64,48},{80,64},{96,80},{112,96},{128,112},... | collective-permute-start | bytes 3293192 | tf_op jit(solution)/shard_map/ppermute | solution.py:492
  34.0 29.5 %copy-start = (f32[6,576,128]{2,1,0:T(8,128)}, f32[6,576,128]{2,1,0:T(8,128)S(1)}, u32[]{:S(2)}) copy-start(f32[6,576,128]{2,1,0:T(8,128)S(1)} %get-tuple-element.69.fine) | copy-start | bytes 5308420
  34.0 7.1 %collective-permute-start.4 = (f32[160,128]{1,0:T(8,128)S(1)}, f32[160,128]{1,0:T(8,128)S(1)}, u32[]{:S(2)}, u32[]{:S(2)}) collective-permute-start(f32[160,128]{1,0:T(8,128)S(1)} %get-tuple-element.50), channel_id=1, source_target_pairs={{0,1},{1,2},{2,3},{3,4},{4,5},{5,6},{6,7},{7,8},{8,9},{9,10},{10,1... | collective-permute-start | bytes 245768 | tf_op jit(solution)/shard_map/ppermute | solution.py:491
  39.0 7.3 %collective-permute-start.5 = (f32[160,128]{1,0:T(8,128)S(1)}, f32[160,128]{1,0:T(8,128)S(1)}, u32[]{:S(2)}, u32[]{:S(2)}) collective-permute-start(f32[160,128]{1,0:T(8,128)S(1)} %get-tuple-element.51), channel_id=1, source_target_pairs={{1,0},{2,1},{3,2},{4,3},{5,4},{6,5},{7,6},{8,7},{9,8},{10,9},{11,1... | collective-permute-start | bytes 245768 | tf_op jit(solution)/shard_map/ppermute | solution.py:492
  47.1 0.7 copy-start.5
  47.8 0.7 copy-start.7
  48.5 47.2 %collective-permute-start.6 = (f32[64,128]{1,0:T(8,128)S(1)}, f32[64,128]{1,0:T(8,128)S(1)}, u32[]{:S(2)}, u32[]{:S(2)}) collective-permute-start(f32[64,128]{1,0:T(8,128)S(1)} %get-tuple-element.57.err), channel_id=1, source_target_pairs={{0,16},{16,32},{32,48},{48,64},{64,80},{80,96},{96,112},{112,128},... | collective-permute-start | bytes 98312 | tf_op jit(solution)/shard_map/ppermute | solution.py:491
  62.2 33.5 %collective-permute-start.7 = (f32[64,128]{1,0:T(8,128)S(1)}, f32[64,128]{1,0:T(8,128)S(1)}, u32[]{:S(2)}, u32[]{:S(2)}) collective-permute-start(f32[64,128]{1,0:T(8,128)S(1)} %get-tuple-element.57.err), channel_id=1, source_target_pairs={{16,0},{32,16},{48,32},{64,48},{80,64},{96,80},{112,96},{128,112},... | collective-permute-start | bytes 98312 | tf_op jit(solution)/shard_map/ppermute | solution.py:492
  94.1 1.2 copy-start.2
  95.9 0.6 copy-start.9
  96.5 7.6 %collective-permute-start.8 = (f32[256,128]{1,0:T(8,128)S(1)}, f32[256,128]{1,0:T(8,128)S(1)}, u32[]{:S(2)}, u32[]{:S(2)}) collective-permute-start(f32[256,128]{1,0:T(8,128)S(1)} %get-tuple-element.59), channel_id=1, source_target_pairs={{0,1},{1,2},{2,3},{3,4},{4,5},{5,6},{6,7},{7,8},{8,9},{9,10},{10,1... | collective-permute-start | bytes 393224 | tf_op jit(solution)/shard_map/ppermute | solution.py:491
  100.4 7.7 %collective-permute-start.9 = (f32[256,128]{1,0:T(8,128)S(1)}, f32[256,128]{1,0:T(8,128)S(1)}, u32[]{:S(2)}, u32[]{:S(2)}) collective-permute-start(f32[256,128]{1,0:T(8,128)S(1)} %get-tuple-element.60), channel_id=1, source_target_pairs={{1,0},{2,1},{3,2},{4,3},{5,4},{6,5},{7,6},{8,7},{9,8},{10,9},{11,1... | collective-permute-start | bytes 393224 | tf_op jit(solution)/shard_map/ppermute | solution.py:492
  108.3 6.9 %collective-permute-start.10 = (f32[256,128]{1,0:T(8,128)S(1)}, f32[256,128]{1,0:T(8,128)S(1)}, u32[]{:S(2)}, u32[]{:S(2)}) collective-permute-start(f32[256,128]{1,0:T(8,128)S(1)} %get-tuple-element.62), channel_id=1, source_target_pairs={{0,1},{1,2},{2,3},{3,4},{4,5},{5,6},{6,7},{7,8},{8,9},{9,10},{10,1... | collective-permute-start | bytes 393224 | tf_op jit(solution)/shard_map/ppermute | solution.py:491
  112.0 7.8 %collective-permute-start.11 = (f32[256,128]{1,0:T(8,128)S(1)}, f32[256,128]{1,0:T(8,128)S(1)}, u32[]{:S(2)}, u32[]{:S(2)}) collective-permute-start(f32[256,128]{1,0:T(8,128)S(1)} %get-tuple-element.63), channel_id=1, source_target_pairs={{1,0},{2,1},{3,2},{4,3},{5,4},{6,5},{7,6},{8,7},{9,8},{10,9},{11,1... | collective-permute-start | bytes 393224 | tf_op jit(solution)/shard_map/ppermute | solution.py:492
  120.7 7.2 %collective-permute-start.12 = (f32[256,128]{1,0:T(8,128)}, f32[256,128]{1,0:T(8,128)}, u32[]{:S(2)}, u32[]{:S(2)}) collective-permute-start(f32[256,128]{1,0:T(8,128)} %get-tuple-element.65), channel_id=1, source_target_pairs={{0,1},{1,2},{2,3},{3,4},{4,5},{5,6},{6,7},{7,8},{8,9},{9,10},{10,1... | collective-permute-start | bytes 393224 | tf_op jit(solution)/shard_map/ppermute | solution.py:491
  124.6 8.3 %collective-permute-start.13 = (f32[256,128]{1,0:T(8,128)}, f32[256,128]{1,0:T(8,128)}, u32[]{:S(2)}, u32[]{:S(2)}) collective-permute-start(f32[256,128]{1,0:T(8,128)} %get-tuple-element.66), channel_id=1, source_target_pairs={{1,0},{2,1},{3,2},{4,3},{5,4},{6,5},{7,6},{8,7},{9,8},{10,9},{11,1... | collective-permute-start | bytes 393224 | tf_op jit(solution)/shard_map/ppermute | solution.py:492
  127.2 5.8 %copy-start.10 = (f32[192,128]{1,0:T(8,128)S(1)}, f32[192,128]{1,0:T(8,128)}, u32[]{:S(2)}) copy-start(f32[192,128]{1,0:T(8,128)} %copy-done.9) | copy-start | bytes 294916
  127.2 17.3 %copy-start.6 = (f32[576,128]{1,0:T(8,128)S(1)}, f32[576,128]{1,0:T(8,128)}, u32[]{:S(2)}) copy-start(f32[576,128]{1,0:T(8,128)} %copy-done.5) | copy-start | bytes 884740
  127.6 16.9 %copy-start.1 = (f32[6,576,128]{2,1,0:T(8,128)S(1)}, f32[6,576,128]{2,1,0:T(8,128)}, u32[]{:S(2)}) copy-start(f32[6,576,128]{2,1,0:T(8,128)} %copy-done) | copy-start | bytes 5308420
  127.6 16.9 %copy-start.8 = (f32[256,128]{1,0:T(8,128)S(1)}, f32[256,128]{1,0:T(8,128)}, u32[]{:S(2)}) copy-start(f32[256,128]{1,0:T(8,128)} %copy-done.7) | copy-start | bytes 393220
  134.1 6.5 %collective-permute-start.14 = (f32[192,128]{1,0:T(8,128)S(1)}, f32[192,128]{1,0:T(8,128)S(1)}, u32[]{:S(2)}, u32[]{:S(2)}) collective-permute-start(f32[192,128]{1,0:T(8,128)S(1)} %shard_map.85.own), channel_id=1, source_target_pairs={{0,1},{1,2},{2,3},{3,4},{4,5},{5,6},{6,7},{7,8},{8,9},{9,10},{10,1... | collective-permute-start | bytes 294920 | tf_op jit(solution)/shard_map/ppermute | solution.py:491
  138.0 6.5 %collective-permute-start.15 = (f32[192,128]{1,0:T(8,128)S(1)}, f32[192,128]{1,0:T(8,128)S(1)}, u32[]{:S(2)}, u32[]{:S(2)}) collective-permute-start(f32[192,128]{1,0:T(8,128)S(1)} %shard_map.85.own), channel_id=1, source_target_pairs={{1,0},{2,1},{3,2},{4,3},{5,4},{6,5},{7,6},{8,7},{9,8},{10,9},{11,1... | collective-permute-start | bytes 294920 | tf_op jit(solution)/shard_map/ppermute | solution.py:492
Sparse Core Ops, SparseCore 0:
  10.5 62.7 all-gather.1

commit v4 on v3

--- a/solution.py
+++ b/solution.py
@@ -94,8 +94,8 @@
 
 
 def pack_kernel(*refs):
-    sources, (own_ref, lo_ref, hi_ref, low_ref), buffers = refs[:6], refs[6:10], refs[10:16]
-    sems = refs[16]
+    sources, outs, buffers, sems = refs[:6], refs[6:12], refs[12:18], refs[18]
+    own_ref, lo_ref, hi_ref, up_ref, down_ref, low_ref = outs
     copies = [
         pltpu.make_async_copy(src, dst, sems.at[i])
         for i, (src, dst) in enumerate(zip(sources, buffers))
@@ -131,6 +131,12 @@
             at = 256 * (k + 1) + 32 * a
             lo_ref[pl.ds(128 + 64 * k + 8 * a, 8), :] = own_ref[pl.ds(at, 8), :]
             hi_ref[pl.ds(128 + 64 * k + 8 * a, 8), :] = own_ref[pl.ds(at + 24, 8), :]
+    up_ref[0:224, :] = own_ref[32:256, :]
+    down_ref[0:224, :] = own_ref[0:224, :]
+    for k in range(5):
+        here = pl.ds(224 + 192 * k, 192)
+        up_ref[here, :] = own_ref[pl.ds(256 * (k + 1) + 64, 192), :]
+        down_ref[here, :] = own_ref[pl.ds(256 * (k + 1), 192), :]
     for k in range(4):
         for m in range(2):
             at = 1536 + 64 * k + 32 * m
@@ -138,52 +144,68 @@
             low_ref[pl.ds(16 * k + 8 * m, 8), :] = 0.125 * pair_sums(both)
 
 
-def widen_kernel(own, below, above, wide_ref, up_ref, down_ref):
-    def put(begin, piece, up, down):
-        wide_ref[pl.ds(begin, piece.shape[0]), :] = piece
-        if up is not None:
-            up_ref[pl.ds(up, piece.shape[0]), :] = piece
-        if down is not None:
-            down_ref[pl.ds(down, piece.shape[0]), :] = piece
-
-    def joined(at, width, other, part):
-        ends = [src[pl.ds(other, part), :] for src in (below, above)]
-        return jnp.concatenate([ends[0], own[pl.ds(at, width), :], ends[1]], axis=0)
-
-    for a in range(8):
-        piece = joined(32 * a, 32, 16 * a, 16)
-        put(64 * a, piece, 64 * (a - 1) if a > 0 else None, 64 * a if a < 7 else None)
+def corner_kernel(below, above, up_ref, down_ref):
+    def put(out, at, src, width):
+        out[pl.ds(at, width), :] = below[pl.ds(src, width), :]
+        out[pl.ds(at + width, width), :] = above[pl.ds(src, width), :]
+
+    for out, shift in ((up_ref, 1), (down_ref, 0)):
+        for i in range(6):
+            put(out, 32 * i, 16 * (i + 2 * shift), 16)
         for k in range(5):
-            piece = joined(256 * (k + 1) + 32 * a, 32, 128 + 64 * k + 8 * a, 8)
-            at = 448 + 288 * k
-            up = at + 48 * (a - 2) if a > 1 else None
-            put(512 + 384 * k + 48 * a, piece, up, at + 48 * a if a < 6 else None)
-    for m in range(4):
+            for i in range(5):
+                put(out, 192 + 80 * k + 16 * i, 128 + 64 * k + 8 * (i + 3 * shift), 8)
         for k in range(4):
-            piece = joined(1536 + 64 * k + 16 * m, 16, 448 + 32 * k + 8 * m, 8)
-            at = 1888 + 64 * k
-            up = at + 32 * (m - 2) if m > 1 else None
-            put(2432 + 128 * k + 32 * m, piece, up, at + 32 * m if m < 2 else None)
+            for i in range(2):
+                put(out, 592 + 32 * k + 16 * i, 448 + 32 * k + 8 * (i + 2 * shift), 8)
 
 
 def fine_kernel(
-    below, own, above, jhi, jlo, out,
+    own, ill_below, ill_above, below, above, far_below, far_above, jhi, jlo, out,
     keep_ref, val_ref, rhs_ref, lo_ref, hi_ref, mid_ref, v0, v1, v2, inc, f,
 ):
-    v0[0:448, :] = below[0:448, :]
-    v0[448:960, :] = own[0:512, :]
-    v0[960:1408, :] = above[0:448, :]
+    def joined(first, middle, last):
+        parts = [ref[pl.ds(at, width), :] for ref, at, width in (first, middle, last)]
+        return jnp.concatenate(parts, axis=0)
+
+    def padded(middle, width):
+        edge = jnp.zeros((width, LANES), F32)
+        ref, at, count = middle
+        return jnp.concatenate([edge, ref[pl.ds(at, count), :], edge], axis=0)
+
+    for a in range(22):
+        if a < 7:
+            i, far, middle = a - 1, far_below, (below, 32 * a, 32)
+        elif a < 15:
+            i, far, middle = a - 7, None, (own, 32 * (a - 7), 32)
+        else:
+            i, far, middle = a - 15, far_above, (above, 32 * (a - 15), 32)
+        if far is None:
+            x = joined((ill_below, 16 * i, 16), middle, (ill_above, 16 * i, 16))
+        elif 0 <= i < 6:
+            x = joined((far, 32 * i, 16), middle, (far, 32 * i + 16, 16))
+        else:
+            x = padded(middle, 16)
+        v0[pl.ds(64 * a, 64), :] = x
     outflow = spread(out[...], 48)
     for a in range(20):
         here = pl.ds(48 * a, 48)
         total = DISCOUNT + outflow
         for k in range(5):
             if a < 6:
-                x = below[pl.ds(448 + 288 * k + 48 * a, 48), :]
+                i, far, middle = a - 1, far_below, (below, 224 + 192 * k + 32 * a, 32)
             elif a < 14:
-                x = own[pl.ds(512 + 384 * k + 48 * (a - 6), 48), :]
+                i, far, middle = a - 6, None, (own, 256 * (k + 1) + 32 * (a - 6), 32)
             else:
-                x = above[pl.ds(448 + 288 * k + 48 * (a - 14), 48), :]
+                i, far, middle = a - 14, far_above, (above, 224 + 192 * k + 32 * (a - 14), 32)
+            if far is None:
+                at = 128 + 64 * k + 8 * i
+                x = joined((ill_below, at, 8), middle, (ill_above, at, 8))
+            elif 0 <= i < 5:
+                at = 192 + 80 * k + 16 * i
+                x = joined((far, at, 8), middle, (far, at + 8, 8))
+            else:
+                x = padded(middle, 8)
             f[k, here, :] = x
             if k:
                 total = total + x
@@ -242,12 +264,14 @@
         here = pl.ds(32 * m, 32)
         total = DISCOUNT + outflow
         for k in range(4):
-            if m < 2:
-                x = below[pl.ds(1888 + 64 * k + 32 * m, 32), :]
-            elif m < 6:
-                x = own[pl.ds(2432 + 128 * k + 32 * (m - 2), 32), :]
+            if m < 2 or m > 5:
+                far, at = (far_below, 592 + 32 * k + 16 * m) if m < 2 else (far_above, 592 + 32 * k + 16 * (m - 6))
+                both = f[k + 1, pl.ds(48 * (2 + 2 * m) + 8, 32), :] + f[k + 1, pl.ds(48 * (3 + 2 * m) + 8, 32), :]
+                middle = 0.125 * pair_sums(both)
+                x = jnp.concatenate([far[pl.ds(at, 8), :], middle, far[pl.ds(at + 8, 8), :]], axis=0)
             else:
-                x = above[pl.ds(1888 + 64 * k + 32 * (m - 6), 32), :]
+                at = 448 + 32 * k + 8 * (m - 2)
+                x = joined((ill_below, at, 8), (own, 1536 + 64 * k + 16 * (m - 2), 16), (ill_above, at, 8))
             mid_ref[k, here, :] = x
             total = total + x
         mid_ref[4, here, :] = OMEGA / total
@@ -294,8 +318,9 @@
 
     for m in range(2):
         pay_ref[pl.ds(8 * m, 8), :] = 0.25 * pair_sums(residual(2 + 2 * m) + residual(3 + 2 * m))
-    for a in range(4):
-        err_ref[pl.ds(16 * a, 16), :] = e1[pl.ds(32 * (a + 2) + 8, 16), :]
+    for a in range(6):
+        err_ref[pl.ds(16 * a, 16), :] = e1[pl.ds(32 * (a + 1) + 8, 16), :]
+    pay_ref[16:48, :] = err_ref[32:64, :]
 
 
 def solve_lines(target, weight, carry, link, middle, y, x_ref, offset):
@@ -357,13 +382,9 @@
     middle_ref[...] = 1.0 / (gaps[0] + links[0] * gaps[1])
 
 
-def first_solve_kernel(
-    rhs, fac, middle, err, err_lo, err_hi, e_ref, lo_ref, hi_ref, wide_ref, y
-):
-    for i, src in enumerate((err_lo, err, err_hi)):
-        wide_ref[pl.ds(64 * i, 64), :] = src[...]
+def first_solve_kernel(gathered, fac, middle, e_ref, lo_ref, hi_ref, y):
     solve_lines(
-        lambda a: row(rhs, a, TILE),
+        lambda a: gathered[pl.ds(48 * (a // 2) + 8 * (a % 2), TILE), :],
         lambda a: row(fac.at[2], a, TILE),
         lambda a: row(fac.at[3], a, TILE),
         lambda a: row(fac.at[4], a, TILE),
@@ -372,11 +393,25 @@
     send_lines(e_ref, lo_ref, hi_ref)
 
 
-def local_target_kernel(e, rhs, fac, jhi, jlo, t_ref):
+def local_target(e, rhs, fac, jhi, jlo, t_ref):
     income(e, t_ref, [(0, 0, e.shape[0] // Z)], jhi, jlo)
     other = swapped(e[...])
     mask = first_half(other.shape)
     t_ref[...] = t_ref[...] + rhs[...] + jnp.where(mask, fac[0], fac[1]) * other
+
+
+def first_target_kernel(place, gathered, err, e, fac, jhi, jlo, t_ref, rhs_ref, wide_ref):
+    blocks = e.shape[0] // (2 * TILE)
+    for i in range(blocks):
+        rhs_ref[pl.ds(16 * i, 16), :] = gathered[pl.ds(48 * i, 16), :]
+    local_target(e, rhs_ref, fac, jhi, jlo, t_ref)
+    here = place[0]
+    wide_ref[32:128, :] = err[...]
+    for at, block, inside in ((0, here - 1, here > 0), (128, here + 1, here < blocks - 1)):
+        block = jnp.minimum(jnp.maximum(block, 0), blocks - 1)
+        start = pl.multiple_of(block * 48 + 16, 16)
+        piece = gathered[pl.ds(start, 32), :]
+        wide_ref[pl.ds(at, 32), :] = jnp.where(inside, piece, jnp.zeros_like(piece))
 
 
 def swept(t, fac, middle, below, above, y, x_ref, offset):
@@ -415,24 +450,25 @@
     for i in range(6):
         low = x[pl.ds(pl.multiple_of(start + i * TILE, TILE), TILE), :]
         fill = doubled(low)
-        for m in (2 * i, 2 * i + 1):
-            sum_ref[pl.ds(16 * m, 16), :] = err[pl.ds(16 * m, 16), :] + fill
+        for m in (2 * i - 1, 2 * i):
+            if 0 <= m < 10:
+                sum_ref[pl.ds(16 * m, 16), :] = err[pl.ds(16 * m, 16), :] + fill
 
 
 def last_kernel(
     own, below, above, mid, rhs_mid, fine, val, jhi, jlo, out_ref, ev, e1, e2, v0, v1, v2, inc
 ):
-    for a in range(12):
+    for a in range(10):
         for i, src in enumerate((below, own, above)):
             ev[pl.ds(48 * a + 16 * i, 16), :] = src[pl.ds(16 * a, 16), :]
 
-    income(ev, inc, [(48 * (a + 2) + 8, 32 * a, 8) for a in range(8)], jhi, jlo)
+    income(ev, inc, [(48 * (a + 1) + 8, 32 * a, 8) for a in range(8)], jhi, jlo)
     for a in range(8):
         here = pl.ds(32 * a, 32)
-        center = row(ev, a + 2, 48)
+        center = row(ev, a + 1, 48)
         total = rhs_mid[here, :] + inc[here, :]
-        total = total + mid[0, here, :] * ev[pl.ds(48 * (a + 3) + 8, 32), :]
-        total = total + mid[1, here, :] * ev[pl.ds(48 * (a + 1) + 8, 32), :]
+        total = total + mid[0, here, :] * ev[pl.ds(48 * (a + 2) + 8, 32), :]
+        total = total + mid[1, here, :] * ev[pl.ds(48 * a + 8, 32), :]
         total = total + mid[2, here, :] * later(center)[8:40]
         total = total + mid[3, here, :] * earlier(center)[8:40]
         e1[here, :] = (1.0 - OMEGA) * center[8:40] + mid[4, here, :] * total
@@ -497,67 +533,67 @@
     nz = jump_rates.shape[0]
     dot_flops = 2 * 3 * nz * nz
     inputs = (right_side, value_guess, speed_liq, speed_ill, flag_liq, flag_ill)
-    own, lo, hi, low = call(
+    own, lo, hi, up, down, low = call(
         pack_kernel,
         inputs,
-        [(1792, LANES), (576, LANES), (576, LANES), (64, LANES)],
+        [(1792, LANES)] + [(576, LANES)] * 2 + [(1184, LANES)] * 2 + [(64, LANES)],
         [pltpu.VMEM(x.shape, x.dtype) for x in inputs] + [pltpu.SemaphoreType.DMA((6,))],
         places=[pltpu.HBM] * 6,
         limit=57,
     )
-    below, above = neighbours(lo, hi, "ill")
+    ill_below, ill_above = neighbours(lo, hi, "ill")
+    below, above = neighbours(down, up, "liq")
     coefs = lax.all_gather(low, "liq", axis=0, tiled=True)
     rates = jax.ShapeDtypeStruct((nz, nz), BF16)
     jhi, jlo, out, own = call(
         rates_kernel, (jump_rates, own), [rates, rates, (TILE, LANES), own.shape]
     )
-    wide, up, down = call(
-        widen_kernel, (own, below, above), [(2944, LANES), (2144, LANES), (2144, LANES)]
-    )
-    below, above = neighbours(down, up, "liq")
+    up, down = call(corner_kernel, (ill_below, ill_above), [(720, LANES)] * 2)
+    far_below, far_above = neighbours(down, up, "liq")
     fine, value, rhs_mid, lo, hi, mid = call(
         fine_kernel,
-        (below, wide, above, jhi, jlo, out),
+        (own, ill_below, ill_above, below, above, far_below, far_above, jhi, jlo, out),
         [(6, 576, LANES), (384, LANES), (128, LANES), (160, LANES), (160, LANES), (5, 256, LANES)],
         [(1408, LANES), (960, LANES), (960, LANES), (1408, LANES), (6, 960, LANES)],
         flops=dot_flops * 730,
     )
     below, above = neighbours(lo, hi, "ill")
-    rhs_low, error_mid, rhs_mid, value = call(
+    payload, err, rhs_mid, value = call(
         mid_kernel,
         (rhs_mid, value, below, above, mid, jhi, jlo, out),
-        [(16, LANES), (64, LANES), (256, LANES), (576, LANES)],
+        [(48, LANES), (96, LANES), (256, LANES), (576, LANES)],
         [(256, LANES)] * 3,
         flops=dot_flops * 80,
     )
-    err_lo, err_hi = neighbours(error_mid, error_mid, "liq")
-    rhs = lax.all_gather(rhs_low, "liq", axis=0, tiled=True)
-    lines = rhs.shape[0]
+    gathered = lax.all_gather(payload, "liq", axis=0, tiled=True)
+    lines = gathered.shape[0] // 48 * 2 * TILE
     line, message = (lines, LANES), (lines // 2, LANES)
     fac, middle = call(factor_kernel, (coefs, out), [(5, *line), (TILE, LANES)])
-    e, lo, hi, err = call(
-        first_solve_kernel,
-        (rhs, fac, middle, error_mid, err_lo, err_hi),
-        [line, message, message, (192, LANES)],
-        [line],
-    )
+    e, lo, hi = call(
+        first_solve_kernel, (gathered, fac, middle), [line, message, message], [line]
+    )
+    place = lax.axis_index("liq").astype(jnp.int32).reshape(1)
     for step in range(SWEEPS - 1):
         below, above = neighbours(lo, hi, "ill")
-        (target,) = call(
-            local_target_kernel,
-            (e, rhs, fac, jhi, jlo),
-            [line],
-            flops=dot_flops * lines // Z,
-        )
+        flops = dot_flops * lines // Z
+        if step == 0:
+            target, rhs, err = call(
+                first_target_kernel,
+                (place, gathered, err, e, fac, jhi, jlo),
+                [line, line, (160, LANES)],
+                flops=flops,
+                places=[pltpu.SMEM],
+            )
+        else:
+            (target,) = call(local_target, (e, rhs, fac, jhi, jlo), [line], flops=flops)
         if step < SWEEPS - 2:
             e, lo, hi = call(
                 sweep_kernel, (target, fac, middle, below, above), [line, message, message], [line]
             )
-    place = lax.axis_index("liq").astype(jnp.int32).reshape(1)
     (total,) = call(
         last_sweep_kernel,
         (place, target, fac, middle, below, above, err),
-        [(192, LANES)],
+        [(160, LANES)],
         [line, (lines + 4 * TILE, LANES)],
         places=[pltpu.SMEM],
     )
@@ -566,7 +602,7 @@
         last_kernel,
         (total, below, above, mid, rhs_mid, fine, value, jhi, jlo),
         [right_side.shape],
-        [(576, LANES), (256, LANES), (256, LANES)] + [(576, LANES)] * 4,
+        [(480, LANES), (256, LANES), (256, LANES)] + [(576, LANES)] * 4,
         flops=dot_flops * 330,
     )
     return result

time: 154 us -> 140 us (0.909)
  the two profiles are of different devices: /device:TPU:32 before, /device:TPU:64 now
where the time goes in v4:
time: 140 us; the launch traced here: 139 us
  starting transfers between devices  43.9 us (31%)
  waiting for transfers between devices  32 us (23%)
  blocking collectives  31.1 us (22%)
  between operations  13.7 us (10%)
  Pallas kernels  12.7 us (9%)
  local copies, waits for them, and re-layouts  5.94 us (4%)
    all_gather x1, blocking collectives, body(): gathered = lax.all_gather(payload, 'liq', axis=0, tiled=True)  31.1 us
    ppermute x8, starting transfers between devices, neighbours(): below = lax.ppermute(hi, axis, [(i, i + 1) for i in range(count - 1)])  29.7 us
    ppermute x8, waiting for transfers between devices, neighbours(): above = lax.ppermute(lo, axis, [(i + 1, i) for i in range(count - 1)])  28.6 us
    ppermute x8, starting transfers between devices, neighbours(): above = lax.ppermute(lo, axis, [(i + 1, i) for i in range(count - 1)])  14.2 us
    pallas_call x14, Pallas kernels, call(): pl.pallas_call(kernel, out_shape=outs, in_specs=[pl.BlockSpec(memory_spac...  12.7 us
    unnamed x22, local copies, waits for them, and re-layouts  5.94 us
    ppermute x8, waiting for transfers between devices, neighbours(): below = lax.ppermute(hi, axis, [(i, i + 1) for i in range(count - 1)])  3.36 us
  transfers between devices with their start and end apart: 17, of which 13 were waited for; matrix products, arithmetic and copies ran while one was open for 0% of the time, Pallas kernels for 3%

profile of v4, /device:TPU:64, one launch (start us, length us, event | category | flops | bytes accessed | tf_op | source)
XLA Modules:
  0.0 139.4 jit_solution(5588752359327309033)
XLA Ops:
  6.5 0.0 all-gather.2.cloned.1.call-start
  6.5 3.0 %shard_map.73 = (f32[1792,128]{1,0:T(8,128)}, f32[576,128]{1,0:T(8,128)}, f32[576,128]{1,0:T(8,128)}, f32[1184,128]{1,0:T(8,128)}, f32[1184,128]{1,0:T(8,128)}, /*index=5*/f32[64,128]{1,0:T(8,128)}) custom-call(f32[8,8,512]{2,1,0:T(8,128)} %refs_0_.1, f32[8,8,512]{2,1,0:T(8,128)} %refs_1_.1, f32[8,8,512]{2,1,0:T(8,128)} %refs_2_.1, f32[8,8,512]{2,1,0:T(8,128)} %refs_3_.1, ...), custom_call_target="tpu_custom_call" | custom-call | bytes 3538944 | tf_op jit(solution)/shard_map/pallas_call | solution.py:514
  9.5 0.0 all-gather.2.cloned.1.call-update
  9.6 3.8 %collective-permute-start = (f32[576,128]{1,0:T(8,128)}, f32[576,128]{1,0:T(8,128)S(1)}, u32[]{:S(2)}, u32[]{:S(2)}) collective-permute-start(f32[576,128]{1,0:T(8,128)} %get-tuple-element.43), channel_id=1, source_target_pairs={{0,1},{1,2},{2,3},{3,4},{4,5},{5,6},{6,7},{7,8},{8,9},{9,10},{10,1... | collective-permute-start | bytes 884744 | tf_op jit(solution)/shard_map/ppermute | solution.py:527
  13.4 2.0 %collective-permute-start.1 = (f32[576,128]{1,0:T(8,128)}, f32[576,128]{1,0:T(8,128)S(1)}, u32[]{:S(2)}, u32[]{:S(2)}) collective-permute-start(f32[576,128]{1,0:T(8,128)} %get-tuple-element.44), channel_id=1, source_target_pairs={{1,0},{2,1},{3,2},{4,3},{5,4},{6,5},{7,6},{8,7},{9,8},{10,9},{11,1... | collective-permute-start | bytes 884744 | tf_op jit(solution)/shard_map/ppermute | solution.py:528
  15.4 1.4 %collective-permute-start.2 = (f32[1184,128]{1,0:T(8,128)}, f32[1184,128]{1,0:T(8,128)S(1)}, u32[]{:S(2)}, u32[]{:S(2)}) collective-permute-start(f32[1184,128]{1,0:T(8,128)} %get-tuple-element.45), channel_id=1, source_target_pairs={{0,16},{16,32},{32,48},{48,64},{64,80},{80,96},{96,112},{112,128},... | collective-permute-start | bytes 1818632 | tf_op jit(solution)/shard_map/ppermute | solution.py:527
  16.8 1.3 collective-permute-start.3
  18.1 2.3 %collective-permute-done.below.ill_below = f32[576,128]{1,0:T(8,128)S(1)} collective-permute-done((f32[576,128]{1,0:T(8,128)}, f32[576,128]{1,0:T(8,128)S(1)}, u32[]{:S(2)}, u32[]{:S(2)}) %collective-permute-start) | collective-permute-done | bytes 294944 | tf_op jit(solution)/shard_map/ppermute | solution.py:527
  20.4 4.9 %collective-permute-done.1.above.ill_above = f32[576,128]{1,0:T(8,128)S(1)} collective-permute-done((f32[576,128]{1,0:T(8,128)}, f32[576,128]{1,0:T(8,128)S(1)}, u32[]{:S(2)}, u32[]{:S(2)}) %collective-permute-start.1) | collective-permute-done | bytes 294944 | tf_op jit(solution)/shard_map/ppermute | solution.py:528
  25.4 1.3 collective-permute-start.4
  26.7 1.3 collective-permute-start.5
  28.0 0.0 copy-done.5
  28.0 0.0 copy-start.6
  28.1 1.2 copy-done.6
  29.2 0.2 shard_map.74
  29.5 0.0 collective-permute-done.2.below
  29.5 0.0 collective-permute-done.3.above
  29.5 0.0 collective-permute-done.4.far_below
  29.5 2.5 %collective-permute-done.5.far_above = f32[720,128]{1,0:T(8,128)S(1)} collective-permute-done((f32[720,128]{1,0:T(8,128)S(1)}, f32[720,128]{1,0:T(8,128)S(1)}, u32[]{:S(2)}, u32[]{:S(2)}) %collective-permute-start.5) | collective-permute-done | bytes 368672 | tf_op jit(solution)/shard_map/ppermute | solution.py:528
  32.0 2.5 %shard_map.76 = (f32[6,576,128]{2,1,0:T(8,128)S(1)}, f32[384,128]{1,0:T(8,128)S(1)}, f32[128,128]{1,0:T(8,128)S(1)}, f32[160,128]{1,0:T(8,128)S(1)}, f32[160,128]{1,0:T(8,128)S(1)}, /*index=5*/f32[5,256,128]{2,1,0:T(8,128)S(1)}) custom-call(f32[1792,128]{1,0:T(8,128)S(1)} %get-tuple-element.42.own, f32[576,128]{1,0:T(8,128)S(1)} %collective-permute-done.below.ill_below, ...), custom_call_target="tpu_custom_call" | custom-call | flops 1148190720 | bytes 7360512 | tf_op jit(solution)/shard_map/pallas_call | solution.py:514
  34.5 0.0 copy-start.2
  34.5 1.2 copy-done.2
  35.8 4.9 %collective-permute-start.6 = (f32[160,128]{1,0:T(8,128)S(1)}, f32[160,128]{1,0:T(8,128)S(1)}, u32[]{:S(2)}, u32[]{:S(2)}) collective-permute-start(f32[160,128]{1,0:T(8,128)S(1)} %get-tuple-element.54), channel_id=1, source_target_pairs={{0,1},{1,2},{2,3},{3,4},{4,5},{5,6},{6,7},{7,8},{8,9},{9,10},{10,1... | collective-permute-start | bytes 245768 | tf_op jit(solution)/shard_map/ppermute | solution.py:527
  40.6 1.9 %collective-permute-start.7 = (f32[160,128]{1,0:T(8,128)S(1)}, f32[160,128]{1,0:T(8,128)S(1)}, u32[]{:S(2)}, u32[]{:S(2)}) collective-permute-start(f32[160,128]{1,0:T(8,128)S(1)} %get-tuple-element.55), channel_id=1, source_target_pairs={{1,0},{2,1},{3,2},{4,3},{5,4},{6,5},{7,6},{8,7},{9,8},{10,9},{11,1... | collective-permute-start | bytes 245768 | tf_op jit(solution)/shard_map/ppermute | solution.py:528
  42.6 0.1 collective-permute-done.6.below
  42.7 4.3 %collective-permute-done.7.above = f32[160,128]{1,0:T(8,128)S(1)} collective-permute-done((f32[160,128]{1,0:T(8,128)S(1)}, f32[160,128]{1,0:T(8,128)S(1)}, u32[]{:S(2)}, u32[]{:S(2)}) %collective-permute-start.7) | collective-permute-done | bytes 81952 | tf_op jit(solution)/shard_map/ppermute | solution.py:528
  47.0 0.8 shard_map.77
  47.8 0.0 copy-done
  47.8 0.0 copy-start.9
  47.8 0.6 copy-done.9
  48.4 31.1 %all_gather.6.gathered = f32[1536,128]{1,0:T(8,128)S(1)} all-gather(f32[48,128]{1,0:T(8,128)S(1)} %get-tuple-element.57), channel_id=1, replica_groups=mesh['liq'=32,'ill'=16] {'liq'}, dimensions={0}, use_global_device_ids=true | all-gather | bytes 811008 | tf_op jit(solution)/shard_map/all_gather | solution.py:568
  79.5 1.2 copy-done.4
  80.8 0.3 shard_map.78
  81.1 0.8 shard_map.79
  81.9 0.7 copy-done.7
  82.6 4.1 %collective-permute-start.8 = (f32[256,128]{1,0:T(8,128)}, f32[256,128]{1,0:T(8,128)}, u32[]{:S(2)}, u32[]{:S(2)}) collective-permute-start(f32[256,128]{1,0:T(8,128)} %get-tuple-element.64), channel_id=1, source_target_pairs={{0,1},{1,2},{2,3},{3,4},{4,5},{5,6},{6,7},{7,8},{8,9},{9,10},{10,1... | collective-permute-start | bytes 393224 | tf_op jit(solution)/shard_map/ppermute | solution.py:527
  86.8 1.9 %collective-permute-start.9 = (f32[256,128]{1,0:T(8,128)}, f32[256,128]{1,0:T(8,128)}, u32[]{:S(2)}, u32[]{:S(2)}) collective-permute-start(f32[256,128]{1,0:T(8,128)} %get-tuple-element.65), channel_id=1, source_target_pairs={{1,0},{2,1},{3,2},{4,3},{5,4},{6,5},{7,6},{8,7},{9,8},{10,9},{11,1... | collective-permute-start | bytes 393224 | tf_op jit(solution)/shard_map/ppermute | solution.py:528
  88.7 0.0 copy-start.8
  88.7 0.9 copy-done.8
  89.7 0.4 shard_map.80
  90.1 0.5 collective-permute-done.8.below
  90.6 3.9 %collective-permute-done.9.above = f32[256,128]{1,0:T(8,128)} collective-permute-done((f32[256,128]{1,0:T(8,128)}, f32[256,128]{1,0:T(8,128)}, u32[]{:S(2)}, u32[]{:S(2)}) %collective-permute-start.9) | collective-permute-done | bytes 131104 | tf_op jit(solution)/shard_map/ppermute | solution.py:528
  94.5 1.1 shard_map.81
  95.6 4.8 %collective-permute-start.10 = (f32[256,128]{1,0:T(8,128)S(1)}, f32[256,128]{1,0:T(8,128)S(1)}, u32[]{:S(2)}, u32[]{:S(2)}) collective-permute-start(f32[256,128]{1,0:T(8,128)S(1)} %get-tuple-element.68), channel_id=1, source_target_pairs={{0,1},{1,2},{2,3},{3,4},{4,5},{5,6},{6,7},{7,8},{8,9},{9,10},{10,1... | collective-permute-start | bytes 393224 | tf_op jit(solution)/shard_map/ppermute | solution.py:527
  100.5 1.9 %collective-permute-start.11 = (f32[256,128]{1,0:T(8,128)S(1)}, f32[256,128]{1,0:T(8,128)S(1)}, u32[]{:S(2)}, u32[]{:S(2)}) collective-permute-start(f32[256,128]{1,0:T(8,128)S(1)} %get-tuple-element.69), channel_id=1, source_target_pairs={{1,0},{2,1},{3,2},{4,3},{5,4},{6,5},{7,6},{8,7},{9,8},{10,9},{11,1... | collective-permute-start | bytes 393224 | tf_op jit(solution)/shard_map/ppermute | solution.py:528
  102.4 0.4 shard_map.82.t
  102.8 0.2 collective-permute-done.10.below
  103.0 4.4 %collective-permute-done.11.above = f32[256,128]{1,0:T(8,128)S(1)} collective-permute-done((f32[256,128]{1,0:T(8,128)S(1)}, f32[256,128]{1,0:T(8,128)S(1)}, u32[]{:S(2)}, u32[]{:S(2)}) %collective-permute-start.11) | collective-permute-done | bytes 131104 | tf_op jit(solution)/shard_map/ppermute | solution.py:528
  107.3 0.2 shard_map.83
  107.5 5.1 %collective-permute-start.12 = (f32[256,128]{1,0:T(8,128)S(1)}, f32[256,128]{1,0:T(8,128)S(1)}, u32[]{:S(2)}, u32[]{:S(2)}) collective-permute-start(f32[256,128]{1,0:T(8,128)S(1)} %get-tuple-element.71), channel_id=1, source_target_pairs={{0,1},{1,2},{2,3},{3,4},{4,5},{5,6},{6,7},{7,8},{8,9},{9,10},{10,1... | collective-permute-start | bytes 393224 | tf_op jit(solution)/shard_map/ppermute | solution.py:527
  112.6 1.9 %collective-permute-start.13 = (f32[256,128]{1,0:T(8,128)S(1)}, f32[256,128]{1,0:T(8,128)S(1)}, u32[]{:S(2)}, u32[]{:S(2)}) collective-permute-start(f32[256,128]{1,0:T(8,128)S(1)} %get-tuple-element.72), channel_id=1, source_target_pairs={{1,0},{2,1},{3,2},{4,3},{5,4},{6,5},{7,6},{8,7},{9,8},{10,9},{11,1... | collective-permute-start | bytes 393224 | tf_op jit(solution)/shard_map/ppermute | solution.py:528
  114.5 0.0 copy-start.3
  114.5 0.4 shard_map.84.t
  115.0 0.0 copy-start.1
  115.0 0.0 copy-start.10
  115.0 0.1 collective-permute-done.12.below
  115.1 4.4 %collective-permute-done.13.above = f32[256,128]{1,0:T(8,128)S(1)} collective-permute-done((f32[256,128]{1,0:T(8,128)S(1)}, f32[256,128]{1,0:T(8,128)S(1)}, u32[]{:S(2)}, u32[]{:S(2)}) %collective-permute-start.13) | collective-permute-done | bytes 131104 | tf_op jit(solution)/shard_map/ppermute | solution.py:528
  119.5 0.2 shard_map.85.own
  119.7 4.2 %collective-permute-start.14 = (f32[160,128]{1,0:T(8,128)S(1)}, f32[160,128]{1,0:T(8,128)S(1)}, u32[]{:S(2)}, u32[]{:S(2)}) collective-permute-start(f32[160,128]{1,0:T(8,128)S(1)} %shard_map.85.own), channel_id=1, source_target_pairs={{0,1},{1,2},{2,3},{3,4},{4,5},{5,6},{6,7},{7,8},{8,9},{9,10},{10,1... | collective-permute-start | bytes 245768 | tf_op jit(solution)/shard_map/ppermute | solution.py:527
  123.9 1.9 %collective-permute-start.15 = (f32[160,128]{1,0:T(8,128)S(1)}, f32[160,128]{1,0:T(8,128)S(1)}, u32[]{:S(2)}, u32[]{:S(2)}) collective-permute-start(f32[160,128]{1,0:T(8,128)S(1)} %shard_map.85.own), channel_id=1, source_target_pairs={{1,0},{2,1},{3,2},{4,3},{5,4},{6,5},{7,6},{8,7},{9,8},{10,9},{11,1... | collective-permute-start | bytes 245768 | tf_op jit(solution)/shard_map/ppermute | solution.py:528
  125.8 0.2 collective-permute-done.14.below
  126.0 4.2 %collective-permute-done.15.above = f32[160,128]{1,0:T(8,128)S(1)} collective-permute-done((f32[160,128]{1,0:T(8,128)S(1)}, f32[160,128]{1,0:T(8,128)S(1)}, u32[]{:S(2)}, u32[]{:S(2)}) %collective-permute-start.15) | collective-permute-done | bytes 81952 | tf_op jit(solution)/shard_map/ppermute | solution.py:528
  130.2 0.0 copy-done.1
  130.3 2.3 %shard_map.86 = f32[8,8,512]{2,1,0:T(8,128)} custom-call(f32[160,128]{1,0:T(8,128)S(1)} %shard_map.85.own, f32[160,128]{1,0:T(8,128)S(1)} %collective-permute-done.14.below, f32[160,128]{1,0:T(8,128)S(1)} %collective-permute-done.15.above, f32[5,256,128]{2,1,0:T(8,128)S(1)} %copy-done.1, f32[256,128]{1,0:T(8,128)S(1)} %copy-done.10, ...), custom_call_target="tpu_custom_call" | custom-call | flops 519045120 | bytes 4276224 | tf_op jit(solution)/shard_map/pallas_call | solution.py:514
  (8 shorter events, 0.1 us)
Async XLA Ops:
  6.5 21.5 %copy-start.5 = (f32[512,512]{1,0:T(8,128)S(1)}, f32[512,512]{1,0:T(8,128)}, u32[]{:S(2)}) copy-start(f32[512,512]{1,0:T(8,128)} %j_ref.1) | copy-start | bytes 3145732
  6.5 73.0 %all-gather.2.cloned.1.call-start = ((), (), s32[]{:S(2)}) async-start(), calls=%async_computation | async-start | bytes 1081344 | tf_op jit(solution)/shard_map/all_gather | solution.py:546
  9.6 10.9 %collective-permute-start = (f32[576,128]{1,0:T(8,128)}, f32[576,128]{1,0:T(8,128)S(1)}, u32[]{:S(2)}, u32[]{:S(2)}) collective-permute-start(f32[576,128]{1,0:T(8,128)} %get-tuple-element.43), channel_id=1, source_target_pairs={{0,1},{1,2},{2,3},{3,4},{4,5},{5,6},{6,7},{7,8},{8,9},{9,10},{10,1... | collective-permute-start | bytes 884744 | tf_op jit(solution)/shard_map/ppermute | solution.py:527
  13.4 12.0 %collective-permute-start.1 = (f32[576,128]{1,0:T(8,128)}, f32[576,128]{1,0:T(8,128)S(1)}, u32[]{:S(2)}, u32[]{:S(2)}) collective-permute-start(f32[576,128]{1,0:T(8,128)} %get-tuple-element.44), channel_id=1, source_target_pairs={{1,0},{2,1},{3,2},{4,3},{5,4},{6,5},{7,6},{8,7},{9,8},{10,9},{11,1... | collective-permute-start | bytes 884744 | tf_op jit(solution)/shard_map/ppermute | solution.py:528
  15.4 14.0 %collective-permute-start.2 = (f32[1184,128]{1,0:T(8,128)}, f32[1184,128]{1,0:T(8,128)S(1)}, u32[]{:S(2)}, u32[]{:S(2)}) collective-permute-start(f32[1184,128]{1,0:T(8,128)} %get-tuple-element.45), channel_id=1, source_target_pairs={{0,16},{16,32},{32,48},{48,64},{64,80},{80,96},{96,112},{112,128},... | collective-permute-start | bytes 1818632 | tf_op jit(solution)/shard_map/ppermute | solution.py:527
  16.8 12.6 %collective-permute-start.3 = (f32[1184,128]{1,0:T(8,128)}, f32[1184,128]{1,0:T(8,128)S(1)}, u32[]{:S(2)}, u32[]{:S(2)}) collective-permute-start(f32[1184,128]{1,0:T(8,128)} %get-tuple-element.46), channel_id=1, source_target_pairs={{16,0},{32,16},{48,32},{64,48},{80,64},{96,80},{112,96},{128,112},... | collective-permute-start | bytes 1818632 | tf_op jit(solution)/shard_map/ppermute | solution.py:528
  25.4 4.1 %collective-permute-start.4 = (f32[720,128]{1,0:T(8,128)S(1)}, f32[720,128]{1,0:T(8,128)S(1)}, u32[]{:S(2)}, u32[]{:S(2)}) collective-permute-start(f32[720,128]{1,0:T(8,128)S(1)} %get-tuple-element.47), channel_id=1, source_target_pairs={{0,16},{16,32},{32,48},{48,64},{64,80},{80,96},{96,112},{112,128},... | collective-permute-start | bytes 1105928 | tf_op jit(solution)/shard_map/ppermute | solution.py:527
  26.7 5.3 %collective-permute-start.5 = (f32[720,128]{1,0:T(8,128)S(1)}, f32[720,128]{1,0:T(8,128)S(1)}, u32[]{:S(2)}, u32[]{:S(2)}) collective-permute-start(f32[720,128]{1,0:T(8,128)S(1)} %get-tuple-element.48), channel_id=1, source_target_pairs={{16,0},{32,16},{48,32},{64,48},{80,64},{96,80},{112,96},{128,112},... | collective-permute-start | bytes 1105928 | tf_op jit(solution)/shard_map/ppermute | solution.py:528
  28.0 1.2 copy-start.6
  34.5 1.2 copy-start.2
  35.8 12.0 %copy-start = (f32[5,256,128]{2,1,0:T(8,128)}, f32[5,256,128]{2,1,0:T(8,128)S(1)}, u32[]{:S(2)}) copy-start(f32[5,256,128]{2,1,0:T(8,128)S(1)} %get-tuple-element.56.mid) | copy-start | bytes 1966084
  35.8 6.9 %collective-permute-start.6 = (f32[160,128]{1,0:T(8,128)S(1)}, f32[160,128]{1,0:T(8,128)S(1)}, u32[]{:S(2)}, u32[]{:S(2)}) collective-permute-start(f32[160,128]{1,0:T(8,128)S(1)} %get-tuple-element.54), channel_id=1, source_target_pairs={{0,1},{1,2},{2,3},{3,4},{4,5},{5,6},{6,7},{7,8},{8,9},{9,10},{10,1... | collective-permute-start | bytes 245768 | tf_op jit(solution)/shard_map/ppermute | solution.py:527
  40.6 6.3 %collective-permute-start.7 = (f32[160,128]{1,0:T(8,128)S(1)}, f32[160,128]{1,0:T(8,128)S(1)}, u32[]{:S(2)}, u32[]{:S(2)}) collective-permute-start(f32[160,128]{1,0:T(8,128)S(1)} %get-tuple-element.55), channel_id=1, source_target_pairs={{1,0},{2,1},{3,2},{4,3},{5,4},{6,5},{7,6},{8,7},{9,8},{10,9},{11,1... | collective-permute-start | bytes 245768 | tf_op jit(solution)/shard_map/ppermute | solution.py:528
  47.8 0.7 copy-start.9
  79.5 1.2 copy-start.4
  81.9 0.7 copy-start.7
  82.6 8.0 %collective-permute-start.8 = (f32[256,128]{1,0:T(8,128)}, f32[256,128]{1,0:T(8,128)}, u32[]{:S(2)}, u32[]{:S(2)}) collective-permute-start(f32[256,128]{1,0:T(8,128)} %get-tuple-element.64), channel_id=1, source_target_pairs={{0,1},{1,2},{2,3},{3,4},{4,5},{5,6},{6,7},{7,8},{8,9},{9,10},{10,1... | collective-permute-start | bytes 393224 | tf_op jit(solution)/shard_map/ppermute | solution.py:527
  86.8 7.7 %collective-permute-start.9 = (f32[256,128]{1,0:T(8,128)}, f32[256,128]{1,0:T(8,128)}, u32[]{:S(2)}, u32[]{:S(2)}) collective-permute-start(f32[256,128]{1,0:T(8,128)} %get-tuple-element.65), channel_id=1, source_target_pairs={{1,0},{2,1},{3,2},{4,3},{5,4},{6,5},{7,6},{8,7},{9,8},{10,9},{11,1... | collective-permute-start | bytes 393224 | tf_op jit(solution)/shard_map/ppermute | solution.py:528
  88.7 1.0 copy-start.8
  95.6 7.3 %collective-permute-start.10 = (f32[256,128]{1,0:T(8,128)S(1)}, f32[256,128]{1,0:T(8,128)S(1)}, u32[]{:S(2)}, u32[]{:S(2)}) collective-permute-start(f32[256,128]{1,0:T(8,128)S(1)} %get-tuple-element.68), channel_id=1, source_target_pairs={{0,1},{1,2},{2,3},{3,4},{4,5},{5,6},{6,7},{7,8},{8,9},{9,10},{10,1... | collective-permute-start | bytes 393224 | tf_op jit(solution)/shard_map/ppermute | solution.py:527
  100.5 6.9 %collective-permute-start.11 = (f32[256,128]{1,0:T(8,128)S(1)}, f32[256,128]{1,0:T(8,128)S(1)}, u32[]{:S(2)}, u32[]{:S(2)}) collective-permute-start(f32[256,128]{1,0:T(8,128)S(1)} %get-tuple-element.69), channel_id=1, source_target_pairs={{1,0},{2,1},{3,2},{4,3},{5,4},{6,5},{7,6},{8,7},{9,8},{10,9},{11,1... | collective-permute-start | bytes 393224 | tf_op jit(solution)/shard_map/ppermute | solution.py:528
  107.5 7.6 %collective-permute-start.12 = (f32[256,128]{1,0:T(8,128)S(1)}, f32[256,128]{1,0:T(8,128)S(1)}, u32[]{:S(2)}, u32[]{:S(2)}) collective-permute-start(f32[256,128]{1,0:T(8,128)S(1)} %get-tuple-element.71), channel_id=1, source_target_pairs={{0,1},{1,2},{2,3},{3,4},{4,5},{5,6},{6,7},{7,8},{8,9},{9,10},{10,1... | collective-permute-start | bytes 393224 | tf_op jit(solution)/shard_map/ppermute | solution.py:527
  112.6 6.9 %collective-permute-start.13 = (f32[256,128]{1,0:T(8,128)S(1)}, f32[256,128]{1,0:T(8,128)S(1)}, u32[]{:S(2)}, u32[]{:S(2)}) collective-permute-start(f32[256,128]{1,0:T(8,128)S(1)} %get-tuple-element.72), channel_id=1, source_target_pairs={{1,0},{2,1},{3,2},{4,3},{5,4},{6,5},{7,6},{8,7},{9,8},{10,9},{11,1... | collective-permute-start | bytes 393224 | tf_op jit(solution)/shard_map/ppermute | solution.py:528
  114.5 15.7 %copy-start.3 = (f32[6,576,128]{2,1,0:T(8,128)S(1)}, f32[6,576,128]{2,1,0:T(8,128)}, u32[]{:S(2)}) copy-start(f32[6,576,128]{2,1,0:T(8,128)} %copy-done.2) | copy-start | bytes 5308420
  115.0 15.3 %copy-start.1 = (f32[5,256,128]{2,1,0:T(8,128)S(1)}, f32[5,256,128]{2,1,0:T(8,128)}, u32[]{:S(2)}) copy-start(f32[5,256,128]{2,1,0:T(8,128)} %copy-done) | copy-start | bytes 1966084
  115.0 15.3 %copy-start.10 = (f32[256,128]{1,0:T(8,128)S(1)}, f32[256,128]{1,0:T(8,128)}, u32[]{:S(2)}) copy-start(f32[256,128]{1,0:T(8,128)} %copy-done.9) | copy-start | bytes 393220
  119.7 6.3 %collective-permute-start.14 = (f32[160,128]{1,0:T(8,128)S(1)}, f32[160,128]{1,0:T(8,128)S(1)}, u32[]{:S(2)}, u32[]{:S(2)}) collective-permute-start(f32[160,128]{1,0:T(8,128)S(1)} %shard_map.85.own), channel_id=1, source_target_pairs={{0,1},{1,2},{2,3},{3,4},{4,5},{5,6},{6,7},{7,8},{8,9},{9,10},{10,1... | collective-permute-start | bytes 245768 | tf_op jit(solution)/shard_map/ppermute | solution.py:527
  123.9 6.3 %collective-permute-start.15 = (f32[160,128]{1,0:T(8,128)S(1)}, f32[160,128]{1,0:T(8,128)S(1)}, u32[]{:S(2)}, u32[]{:S(2)}) collective-permute-start(f32[160,128]{1,0:T(8,128)S(1)} %shard_map.85.own), channel_id=1, source_target_pairs={{1,0},{2,1},{3,2},{4,3},{5,4},{6,5},{7,6},{8,7},{9,8},{10,9},{11,1... | collective-permute-start | bytes 245768 | tf_op jit(solution)/shard_map/ppermute | solution.py:528
Sparse Core Ops, SparseCore 0:
  10.5 61.9 all-gather.1

commit v5 on v4

--- a/solution.py
+++ b/solution.py
@@ -61,7 +61,9 @@
     high = wide.astype(BF16)
     rest = (wide - high.astype(F32)).astype(BF16)
     dot = functools.partial(jnp.dot, preferred_element_type=F32)
-    return dot(high, jhi_ref[...]) + (dot(high, jlo_ref[...]) + dot(rest, jhi_ref[...]))
+    count = wide.shape[0]
+    both = dot(jnp.concatenate([high, rest], axis=0), jhi_ref[...])
+    return both[:count] + (both[count:] + dot(high, jlo_ref[...]))
 
 
 def income(src, dst, pieces, jhi_ref, jlo_ref):
@@ -93,9 +95,7 @@
         out_ref[c + Z : c + Z + 1, :] = piece
 
 
-def pack_kernel(*refs):
-    sources, outs, buffers, sems = refs[:6], refs[6:12], refs[12:18], refs[18]
-    own_ref, lo_ref, hi_ref, up_ref, down_ref, low_ref = outs
+def unpack(sources, buffers, own_ref, sems):
     copies = [
         pltpu.make_async_copy(src, dst, sems.at[i])
         for i, (src, dst) in enumerate(zip(sources, buffers))
@@ -122,6 +122,16 @@
             at = 256 * (k + 2) + 64 * m
             mid = 0.125 * pair_sums(own_ref[pl.ds(at, 32), :] + own_ref[pl.ds(at + 32, 32), :])
             own_ref[pl.ds(1536 + 64 * k + 16 * m, 16), :] = mid
+
+
+def pack_kernel(*refs):
+    sources, outs, buffers = refs[:6], refs[6:11], refs[11:17]
+    lo_ref, hi_ref, up_ref, down_ref, low_ref = outs
+    own_ref, sems = refs[17:]
+    unpack(sources, buffers, own_ref, sems)
+    for k in range(4):
+        for m in range(4):
+            mid = own_ref[pl.ds(1536 + 64 * k + 16 * m, 16), :]
             lo_ref[pl.ds(448 + 32 * k + 8 * m, 8), :] = mid[:8]
             hi_ref[pl.ds(448 + 32 * k + 8 * m, 8), :] = mid[8:]
     for a in range(8):
@@ -144,6 +154,10 @@
             low_ref[pl.ds(16 * k + 8 * m, 8), :] = 0.125 * pair_sums(both)
 
 
+def own_kernel(*refs):
+    unpack(refs[:6], refs[7:13], refs[6], refs[13])
+
+
 def corner_kernel(below, above, up_ref, down_ref):
     def put(out, at, src, width):
         out[pl.ds(at, width), :] = below[pl.ds(src, width), :]
@@ -160,10 +174,7 @@
                 put(out, 592 + 32 * k + 16 * i, 448 + 32 * k + 8 * (i + 2 * shift), 8)
 
 
-def fine_kernel(
-    own, ill_below, ill_above, below, above, far_below, far_above, jhi, jlo, out,
-    keep_ref, val_ref, rhs_ref, lo_ref, hi_ref, mid_ref, v0, v1, v2, inc, f,
-):
+def assemblers(own, ill_below, ill_above, below, above, far_below, far_above):
     def joined(first, middle, last):
         parts = [ref[pl.ds(at, width), :] for ref, at, width in (first, middle, last)]
         return jnp.concatenate(parts, axis=0)
@@ -173,7 +184,7 @@
         ref, at, count = middle
         return jnp.concatenate([edge, ref[pl.ds(at, count), :], edge], axis=0)
 
-    for a in range(22):
+    def value(a):
         if a < 7:
             i, far, middle = a - 1, far_below, (below, 32 * a, 32)
         elif a < 15:
@@ -181,31 +192,77 @@
         else:
             i, far, middle = a - 15, far_above, (above, 32 * (a - 15), 32)
         if far is None:
-            x = joined((ill_below, 16 * i, 16), middle, (ill_above, 16 * i, 16))
-        elif 0 <= i < 6:
-            x = joined((far, 32 * i, 16), middle, (far, 32 * i + 16, 16))
+            return joined((ill_below, 16 * i, 16), middle, (ill_above, 16 * i, 16))
+        if 0 <= i < 6:
+            return joined((far, 32 * i, 16), middle, (far, 32 * i + 16, 16))
+        return padded(middle, 16)
+
+    def field(k, a):
+        if a < 6:
+            i, far, middle = a - 1, far_below, (below, 224 + 192 * k + 32 * a, 32)
+        elif a < 14:
+            i, far, middle = a - 6, None, (own, 256 * (k + 1) + 32 * (a - 6), 32)
         else:
-            x = padded(middle, 16)
-        v0[pl.ds(64 * a, 64), :] = x
+            i, far, middle = a - 14, far_above, (above, 224 + 192 * k + 32 * (a - 14), 32)
+        if far is None:
+            at = 128 + 64 * k + 8 * i
+            return joined((ill_below, at, 8), middle, (ill_above, at, 8))
+        if 0 <= i < 5:
+            at = 192 + 80 * k + 16 * i
+            return joined((far, at, 8), middle, (far, at + 8, 8))
+        return padded(middle, 8)
+
+    def mid(k, m):
+        if 1 < m < 6:
+            at = 448 + 32 * k + 8 * (m - 2)
+            middle = (own, 1536 + 64 * k + 16 * (m - 2), 16)
+            return joined((ill_below, at, 8), middle, (ill_above, at, 8))
+        near, i = (below, 2 * m + 2) if m < 2 else (above, 2 * m - 12)
+        at = 224 + 192 * (k + 1) + 32 * i
+        far, corner = (far_below, 16 * m) if m < 2 else (far_above, 16 * (m - 6))
+        corner += 592 + 32 * k
+        middle = 0.125 * pair_sums(near[pl.ds(at, 32), :] + near[pl.ds(at + 32, 32), :])
+        return jnp.concatenate([far[pl.ds(corner, 8), :], middle, far[pl.ds(corner + 8, 8), :]], axis=0)
+
+    return value, field, mid
+
+
+def keep_kernel(own, ill_below, ill_above, below, above, far_below, far_above, out, keep_ref, mid_ref):
+    _, field, mid = assemblers(own, ill_below, ill_above, below, above, far_below, far_above)
+    outflow = spread(out[...], 48)
+    for a in range(12):
+        here = pl.ds(48 * a, 48)
+        total = DISCOUNT + outflow
+        for k in range(5):
+            x = field(k, a + 4)
+            keep_ref[k, here, :] = x
+            if k:
+                total = total + x
+        keep_ref[5, here, :] = OMEGA / total
+    outflow = spread(out[...], 32)
+    for m in range(8):
+        here = pl.ds(32 * m, 32)
+        total = DISCOUNT + outflow
+        for k in range(4):
+            x = mid(k, m)
+            mid_ref[k, here, :] = x
+            total = total + x
+        mid_ref[4, here, :] = OMEGA / total
+
+
+def fine_kernel(
+    own, ill_below, ill_above, below, above, far_below, far_above, jhi, jlo, out,
+    val_ref, rhs_ref, lo_ref, hi_ref, v0, v1, v2, inc, f,
+):
+    value, field, _ = assemblers(own, ill_below, ill_above, below, above, far_below, far_above)
+    for a in range(22):
+        v0[pl.ds(64 * a, 64), :] = value(a)
     outflow = spread(out[...], 48)
     for a in range(20):
         here = pl.ds(48 * a, 48)
         total = DISCOUNT + outflow
         for k in range(5):
-            if a < 6:
-                i, far, middle = a - 1, far_below, (below, 224 + 192 * k + 32 * a, 32)
-            elif a < 14:
-                i, far, middle = a - 6, None, (own, 256 * (k + 1) + 32 * (a - 6), 32)
-            else:
-                i, far, middle = a - 14, far_above, (above, 224 + 192 * k + 32 * (a - 14), 32)
-            if far is None:
-                at = 128 + 64 * k + 8 * i
-                x = joined((ill_below, at, 8), middle, (ill_above, at, 8))
-            elif 0 <= i < 5:
-                at = 192 + 80 * k + 16 * i
-                x = joined((far, at, 8), middle, (far, at + 8, 8))
-            else:
-                x = padded(middle, 8)
+            x = field(k, a)
             f[k, here, :] = x
             if k:
                 total = total + x
@@ -256,38 +313,24 @@
         val_ref[pl.ds(32 * a, 32), :] = value
         lo_ref[pl.ds(64 + 8 * a, 8), :] = value[:8]
         hi_ref[pl.ds(64 + 8 * a, 8), :] = value[24:]
-    for k in range(6):
-        keep_ref[k] = f[k, pl.ds(48 * 4, 48 * 12), :]
-
-    outflow = spread(out[...], 32)
-    for m in range(8):
-        here = pl.ds(32 * m, 32)
-        total = DISCOUNT + outflow
-        for k in range(4):
-            if m < 2 or m > 5:
-                far, at = (far_below, 592 + 32 * k + 16 * m) if m < 2 else (far_above, 592 + 32 * k + 16 * (m - 6))
-                both = f[k + 1, pl.ds(48 * (2 + 2 * m) + 8, 32), :] + f[k + 1, pl.ds(48 * (3 + 2 * m) + 8, 32), :]
-                middle = 0.125 * pair_sums(both)
-                x = jnp.concatenate([far[pl.ds(at, 8), :], middle, far[pl.ds(at + 8, 8), :]], axis=0)
-            else:
-                at = 448 + 32 * k + 8 * (m - 2)
-                x = joined((ill_below, at, 8), (own, 1536 + 64 * k + 16 * (m - 2), 16), (ill_above, at, 8))
-            mid_ref[k, here, :] = x
-            total = total + x
-        mid_ref[4, here, :] = OMEGA / total
-
-
-def mid_kernel(
-    own, val, below, above, mid, jhi, jlo, out, pay_ref, err_ref, rhs_ref, wide_ref, e0, e1, inc
-):
+
+
+def widen_rhs(own, below, above, rhs_ref):
     for a in range(8):
         for i, piece in enumerate((below[pl.ds(8 * a, 8), :], row(own, a, 16), above[pl.ds(8 * a, 8), :])):
             rhs_ref[pl.ds(32 * a + (0, 8, 24)[i], piece.shape[0]), :] = piece
+
+
+def widen_value(val, below, above, wide_ref):
     for a in range(12):
         ends = [src[pl.ds(64 + 8 * a, 8), :] for src in (below, above)]
         wide_ref[pl.ds(48 * a, 8), :] = ends[0]
         wide_ref[pl.ds(48 * a + 8, 32), :] = row(val, a, 32)
         wide_ref[pl.ds(48 * a + 40, 8), :] = ends[1]
+
+
+def mid_kernel(own, below, above, mid, jhi, jlo, out, pay_ref, err_ref, rhs_ref, e0, e1, inc):
+    widen_rhs(own, below, above, rhs_ref)
     e0[...] = mid[4] * rhs_ref[...]
 
     def applied(src, a):
@@ -400,12 +443,17 @@
     t_ref[...] = t_ref[...] + rhs[...] + jnp.where(mask, fac[0], fac[1]) * other
 
 
-def first_target_kernel(place, gathered, err, e, fac, jhi, jlo, t_ref, rhs_ref, wide_ref):
+def first_target_kernel(
+    gathered, err, e, fac, jhi, jlo, rhs_mid, val, below, above,
+    t_ref, rhs_ref, wide_ref, rhs_wide_ref, val_wide_ref,
+):
     blocks = e.shape[0] // (2 * TILE)
     for i in range(blocks):
         rhs_ref[pl.ds(16 * i, 16), :] = gathered[pl.ds(48 * i, 16), :]
     local_target(e, rhs_ref, fac, jhi, jlo, t_ref)
-    here = place[0]
+    widen_rhs(rhs_mid, below, above, rhs_wide_ref)
+    widen_value(val, below, above, val_wide_ref)
+    here = lax.axis_index("liq")
     wide_ref[32:128, :] = err[...]
     for at, block, inside in ((0, here - 1, here > 0), (128, here + 1, here < blocks - 1)):
         block = jnp.minimum(jnp.maximum(block, 0), blocks - 1)
@@ -441,12 +489,12 @@
     send_lines(e_ref, lo_ref, hi_ref)
 
 
-def last_sweep_kernel(place, t, fac, middle, below, above, err, sum_ref, y, x):
+def last_sweep_kernel(t, fac, middle, below, above, err, sum_ref, y, x):
     edge = 2 * TILE
     x[0:edge, :] = jnp.zeros((edge, LANES), F32)
     x[pl.ds(x.shape[0] - edge, edge), :] = jnp.zeros((edge, LANES), F32)
     swept(t, fac, middle, below, above, y, x, edge)
-    start = place[0] * 2 * TILE
+    start = lax.axis_index("liq") * 2 * TILE
     for i in range(6):
         low = x[pl.ds(pl.multiple_of(start + i * TILE, TILE), TILE), :]
         fill = doubled(low)
@@ -533,11 +581,13 @@
     nz = jump_rates.shape[0]
     dot_flops = 2 * 3 * nz * nz
     inputs = (right_side, value_guess, speed_liq, speed_ill, flag_liq, flag_ill)
-    own, lo, hi, up, down, low = call(
+    buffers = [pltpu.VMEM(x.shape, x.dtype) for x in inputs]
+    sems = pltpu.SemaphoreType.DMA((6,))
+    lo, hi, up, down, low = call(
         pack_kernel,
         inputs,
-        [(1792, LANES)] + [(576, LANES)] * 2 + [(1184, LANES)] * 2 + [(64, LANES)],
-        [pltpu.VMEM(x.shape, x.dtype) for x in inputs] + [pltpu.SemaphoreType.DMA((6,))],
+        [(576, LANES)] * 2 + [(1184, LANES)] * 2 + [(64, LANES)],
+        buffers + [(1792, LANES), sems],
         places=[pltpu.HBM] * 6,
         limit=57,
     )
@@ -545,24 +595,29 @@
     below, above = neighbours(down, up, "liq")
     coefs = lax.all_gather(low, "liq", axis=0, tiled=True)
     rates = jax.ShapeDtypeStruct((nz, nz), BF16)
+    (own,) = call(
+        own_kernel, inputs, [(1792, LANES)], buffers + [sems], places=[pltpu.HBM] * 6, limit=57
+    )
     jhi, jlo, out, own = call(
         rates_kernel, (jump_rates, own), [rates, rates, (TILE, LANES), own.shape]
     )
     up, down = call(corner_kernel, (ill_below, ill_above), [(720, LANES)] * 2)
     far_below, far_above = neighbours(down, up, "liq")
-    fine, value, rhs_mid, lo, hi, mid = call(
+    pieces = (own, ill_below, ill_above, below, above, far_below, far_above)
+    value, rhs_mid, lo, hi = call(
         fine_kernel,
-        (own, ill_below, ill_above, below, above, far_below, far_above, jhi, jlo, out),
-        [(6, 576, LANES), (384, LANES), (128, LANES), (160, LANES), (160, LANES), (5, 256, LANES)],
+        (*pieces, jhi, jlo, out),
+        [(384, LANES), (128, LANES), (160, LANES), (160, LANES)],
         [(1408, LANES), (960, LANES), (960, LANES), (1408, LANES), (6, 960, LANES)],
         flops=dot_flops * 730,
     )
-    below, above = neighbours(lo, hi, "ill")
-    payload, err, rhs_mid, value = call(
+    mid_below, mid_above = neighbours(lo, hi, "ill")
+    fine, mid = call(keep_kernel, (*pieces, out), [(6, 576, LANES), (5, 256, LANES)])
+    payload, err = call(
         mid_kernel,
-        (rhs_mid, value, below, above, mid, jhi, jlo, out),
-        [(48, LANES), (96, LANES), (256, LANES), (576, LANES)],
-        [(256, LANES)] * 3,
+        (rhs_mid, mid_below, mid_above, mid, jhi, jlo, out),
+        [(48, LANES), (96, LANES)],
+        [(256, LANES)] * 4,
         flops=dot_flops * 80,
     )
     gathered = lax.all_gather(payload, "liq", axis=0, tiled=True)
@@ -572,17 +627,15 @@
     e, lo, hi = call(
         first_solve_kernel, (gathered, fac, middle), [line, message, message], [line]
     )
-    place = lax.axis_index("liq").astype(jnp.int32).reshape(1)
     for step in range(SWEEPS - 1):
         below, above = neighbours(lo, hi, "ill")
         flops = dot_flops * lines // Z
         if step == 0:
-            target, rhs, err = call(
+            target, rhs, err, rhs_mid, value = call(
                 first_target_kernel,
-                (place, gathered, err, e, fac, jhi, jlo),
-                [line, line, (160, LANES)],
+                (gathered, err, e, fac, jhi, jlo, rhs_mid, value, mid_below, mid_above),
+                [line, line, (160, LANES), (256, LANES), (576, LANES)],
                 flops=flops,
-                places=[pltpu.SMEM],
             )
         else:
             (target,) = call(local_target, (e, rhs, fac, jhi, jlo), [line], flops=flops)
@@ -592,10 +645,9 @@
             )
     (total,) = call(
         last_sweep_kernel,
-        (place, target, fac, middle, below, above, err),
+        (target, fac, middle, below, above, err),
         [(160, LANES)],
         [line, (lines + 4 * TILE, LANES)],
-        places=[pltpu.SMEM],
     )
     below, above = neighbours(total, total, "ill")
     (result,) = call(

time: 140 us -> 135 us (0.964)
  local copies, waits for them, and re-layouts: 5.94 us -> 2.41 us
  waiting for transfers between devices: 32 us -> 30.2 us
    unnamed x22 -> x10, local copies, waits for them, and re-layouts: 5.94 us -> 2.41 us
    ppermute x8, waiting for transfers between devices: 28.6 us -> 26.1 us  [neighbours(): above = lax.ppermute(lo, axis, [(i + 1, i) for i in range(count - 1)])]
    pallas_call x14 -> x16, Pallas kernels: 12.7 us -> 12.6 us  [call(): pl.pallas_call(kernel, out_shape=outs, in_specs=[pl.BlockSpec(memory_spac...]
  transfers between devices with their start and end apart: 17 -> 17, of which waited for: 13 -> 12; matrix products, arithmetic and copies ran while one was open for 0% -> 0% of each run, Pallas kernels for 3% -> 5%
where the time goes in v5:
time: 135 us; the launch traced here: 134 us
  starting transfers between devices  43.8 us (32%)
  blocking collectives  31.2 us (23%)
  waiting for transfers between devices  30.2 us (22%)
  between operations  13.7 us (10%)
  Pallas kernels  12.6 us (9%)
  local copies, waits for them, and re-layouts  2.41 us (2%)
    all_gather x1, blocking collectives, body(): gathered = lax.all_gather(payload, 'liq', axis=0, tiled=True)  31.2 us
    ppermute x8, starting transfers between devices, neighbours(): below = lax.ppermute(hi, axis, [(i, i + 1) for i in range(count - 1)])  29.5 us
    ppermute x8, waiting for transfers between devices, neighbours(): above = lax.ppermute(lo, axis, [(i + 1, i) for i in range(count - 1)])  26.1 us
    ppermute x8, starting transfers between devices, neighbours(): above = lax.ppermute(lo, axis, [(i + 1, i) for i in range(count - 1)])  14.2 us
    pallas_call x16, Pallas kernels, call(): pl.pallas_call(kernel, out_shape=outs, in_specs=[pl.BlockSpec(memory_spac...  12.6 us
    ppermute x8, waiting for transfers between devices, neighbours(): below = lax.ppermute(hi, axis, [(i, i + 1) for i in range(count - 1)])  4.1 us
  transfers between devices with their start and end apart: 17, of which 12 were waited for; matrix products, arithmetic and copies ran while one was open for 0% of the time, Pallas kernels for 5%

profile of v5, /device:TPU:64, one launch (start us, length us, event | category | flops | bytes accessed | tf_op | source)
XLA Modules:
  0.0 133.9 jit_solution(2583557058414314640)
XLA Ops:
  6.5 0.0 copy-start.4
  6.5 0.0 all-gather.2.cloned.1.call-start
  6.5 2.7 %shard_map.75 = (f32[576,128]{1,0:T(8,128)}, f32[576,128]{1,0:T(8,128)}, f32[1184,128]{1,0:T(8,128)}, f32[1184,128]{1,0:T(8,128)}, f32[64,128]{1,0:T(8,128)}) custom-call(f32[8,8,512]{2,1,0:T(8,128)} %refs_0_.3, f32[8,8,512]{2,1,0:T(8,128)} %refs_1_.3, f32[8,8,512]{2,1,0:T(8,128)} %refs_2_.3, f32[8,8,512]{2,1,0:T(8,128)} %refs_3_.3, s32[8,8,512]{2,1,0:T(8,128)} %refs_4_.3, ...), custom_call_target="tpu_custom_call" | custom-call | bytes 2621440 | tf_op jit(solution)/shard_map/pallas_call | solution.py:562
  9.3 0.0 all-gather.2.cloned.1.call-update
  9.3 3.8 %collective-permute-start = (f32[576,128]{1,0:T(8,128)}, f32[576,128]{1,0:T(8,128)S(1)}, u32[]{:S(2)}, u32[]{:S(2)}) collective-permute-start(f32[576,128]{1,0:T(8,128)} %get-tuple-element.41), channel_id=1, source_target_pairs={{0,1},{1,2},{2,3},{3,4},{4,5},{5,6},{6,7},{7,8},{8,9},{9,10},{10,1... | collective-permute-start | bytes 884744 | tf_op jit(solution)/shard_map/ppermute | solution.py:575
  13.1 2.0 %collective-permute-start.1 = (f32[576,128]{1,0:T(8,128)}, f32[576,128]{1,0:T(8,128)S(1)}, u32[]{:S(2)}, u32[]{:S(2)}) collective-permute-start(f32[576,128]{1,0:T(8,128)} %get-tuple-element.42), channel_id=1, source_target_pairs={{1,0},{2,1},{3,2},{4,3},{5,4},{6,5},{7,6},{8,7},{9,8},{10,9},{11,1... | collective-permute-start | bytes 884744 | tf_op jit(solution)/shard_map/ppermute | solution.py:576
  15.1 1.4 %collective-permute-start.2 = (f32[1184,128]{1,0:T(8,128)}, f32[1184,128]{1,0:T(8,128)S(1)}, u32[]{:S(2)}, u32[]{:S(2)}) collective-permute-start(f32[1184,128]{1,0:T(8,128)} %get-tuple-element.43), channel_id=1, source_target_pairs={{0,16},{16,32},{32,48},{48,64},{64,80},{80,96},{96,112},{112,128},... | collective-permute-start | bytes 1818632 | tf_op jit(solution)/shard_map/ppermute | solution.py:575
  16.5 1.3 collective-permute-start.3
  17.8 2.3 %collective-permute-done.below.ill_below = f32[576,128]{1,0:T(8,128)S(1)} collective-permute-done((f32[576,128]{1,0:T(8,128)}, f32[576,128]{1,0:T(8,128)S(1)}, u32[]{:S(2)}, u32[]{:S(2)}) %collective-permute-start) | collective-permute-done | bytes 294944 | tf_op jit(solution)/shard_map/ppermute | solution.py:575
  20.1 4.9 %collective-permute-done.1.above.ill_above = f32[576,128]{1,0:T(8,128)S(1)} collective-permute-done((f32[576,128]{1,0:T(8,128)}, f32[576,128]{1,0:T(8,128)S(1)}, u32[]{:S(2)}, u32[]{:S(2)}) %collective-permute-start.1) | collective-permute-done | bytes 294944 | tf_op jit(solution)/shard_map/ppermute | solution.py:576
  25.1 1.3 collective-permute-start.4
  26.5 1.3 collective-permute-start.5
  27.8 2.3 %shard_map.73.own = f32[1792,128]{1,0:T(8,128)} custom-call(f32[8,8,512]{2,1,0:T(8,128)} %refs_0_.3, f32[8,8,512]{2,1,0:T(8,128)} %refs_1_.3, f32[8,8,512]{2,1,0:T(8,128)} %refs_2_.3, f32[8,8,512]{2,1,0:T(8,128)} %refs_3_.3, s32[8,8,512]{2,1,0:T(8,128)} %refs_4_.3, s32[8,8,512]{2,1,0:T(8,128)} %refs_5_.3), custom_call_target="tpu_custom_call" | custom-call | bytes 1703936 | tf_op jit(solution)/shard_map/pallas_call | solution.py:562
  30.0 0.0 copy-done.4
  30.0 0.0 copy-start
  30.1 1.2 copy-done
  31.2 0.2 shard_map.74
  31.5 0.0 collective-permute-done.2.below
  31.5 0.0 collective-permute-done.3.above
  31.5 0.0 collective-permute-done.4.far_below
  31.5 0.2 collective-permute-done.5.far_above
  31.7 2.2 %shard_map.77 = (f32[384,128]{1,0:T(8,128)S(1)}, f32[128,128]{1,0:T(8,128)S(1)}, f32[160,128]{1,0:T(8,128)S(1)}, f32[160,128]{1,0:T(8,128)S(1)}) custom-call(f32[1792,128]{1,0:T(8,128)S(1)} %get-tuple-element.40.own, f32[576,128]{1,0:T(8,128)S(1)} %collective-permute-done.below.ill_below, f32[576,128]{1,0:T(8,128)S(1)} %collective-permute-done.1.above.ill_above, ...), custom_call_target="tpu_custom_call" | custom-call | flops 1148190720 | bytes 4935680 | tf_op jit(solution)/shard_map/pallas_call | solution.py:562
  34.0 4.8 %collective-permute-start.6 = (f32[160,128]{1,0:T(8,128)S(1)}, f32[160,128]{1,0:T(8,128)S(1)}, u32[]{:S(2)}, u32[]{:S(2)}) collective-permute-start(f32[160,128]{1,0:T(8,128)S(1)} %get-tuple-element.51), channel_id=1, source_target_pairs={{0,1},{1,2},{2,3},{3,4},{4,5},{5,6},{6,7},{7,8},{8,9},{9,10},{10,1... | collective-permute-start | bytes 245768 | tf_op jit(solution)/shard_map/ppermute | solution.py:575
  38.8 1.9 %collective-permute-start.7 = (f32[160,128]{1,0:T(8,128)S(1)}, f32[160,128]{1,0:T(8,128)S(1)}, u32[]{:S(2)}, u32[]{:S(2)}) collective-permute-start(f32[160,128]{1,0:T(8,128)S(1)} %get-tuple-element.52), channel_id=1, source_target_pairs={{1,0},{2,1},{3,2},{4,3},{5,4},{6,5},{7,6},{8,7},{9,8},{10,9},{11,1... | collective-permute-start | bytes 245768 | tf_op jit(solution)/shard_map/ppermute | solution.py:576
  40.8 0.2 shard_map.78
  41.0 0.0 copy-start.1
  41.0 0.0 collective-permute-done.6.below
  41.0 4.2 %collective-permute-done.7.above = f32[160,128]{1,0:T(8,128)S(1)} collective-permute-done((f32[160,128]{1,0:T(8,128)S(1)}, f32[160,128]{1,0:T(8,128)S(1)}, u32[]{:S(2)}, u32[]{:S(2)}) %collective-permute-start.7) | collective-permute-done | bytes 81952 | tf_op jit(solution)/shard_map/ppermute | solution.py:576
  45.2 0.6 shard_map.79
  45.8 0.0 copy-done.1
  45.8 31.2 %all_gather.6.gathered = f32[1536,128]{1,0:T(8,128)S(1)} all-gather(f32[48,128]{1,0:T(8,128)S(1)} %get-tuple-element.54), channel_id=1, replica_groups=mesh['liq'=32,'ill'=16] {'liq'}, dimensions={0}, use_global_device_ids=true | all-gather | bytes 811008 | tf_op jit(solution)/shard_map/all_gather | solution.py:623
  77.0 0.0 all-gather.2.cloned.1.call-done.gathered
  77.0 0.0 copy-start.3
  77.0 1.2 copy-done.3
  78.2 0.3 shard_map.80
  78.5 0.1 shard_map.81
  78.7 4.1 %collective-permute-start.8 = (f32[256,128]{1,0:T(8,128)S(1)}, f32[256,128]{1,0:T(8,128)S(1)}, u32[]{:S(2)}, u32[]{:S(2)}) collective-permute-start(f32[256,128]{1,0:T(8,128)S(1)} %get-tuple-element.62), channel_id=1, source_target_pairs={{0,1},{1,2},{2,3},{3,4},{4,5},{5,6},{6,7},{7,8},{8,9},{9,10},{10,1... | collective-permute-start | bytes 393224 | tf_op jit(solution)/shard_map/ppermute | solution.py:575
  82.8 1.9 %collective-permute-start.9 = (f32[256,128]{1,0:T(8,128)S(1)}, f32[256,128]{1,0:T(8,128)S(1)}, u32[]{:S(2)}, u32[]{:S(2)}) collective-permute-start(f32[256,128]{1,0:T(8,128)S(1)} %get-tuple-element.63), channel_id=1, source_target_pairs={{1,0},{2,1},{3,2},{4,3},{5,4},{6,5},{7,6},{8,7},{9,8},{10,9},{11,1... | collective-permute-start | bytes 393224 | tf_op jit(solution)/shard_map/ppermute | solution.py:576
  84.7 0.4 shard_map.82
  85.1 1.2 collective-permute-done.8.below
  86.3 3.9 %collective-permute-done.9.above = f32[256,128]{1,0:T(8,128)S(1)} collective-permute-done((f32[256,128]{1,0:T(8,128)S(1)}, f32[256,128]{1,0:T(8,128)S(1)}, u32[]{:S(2)}, u32[]{:S(2)}) %collective-permute-start.9) | collective-permute-done | bytes 131104 | tf_op jit(solution)/shard_map/ppermute | solution.py:576
  90.2 0.2 shard_map.83
  90.4 4.9 %collective-permute-start.10 = (f32[256,128]{1,0:T(8,128)S(1)}, f32[256,128]{1,0:T(8,128)S(1)}, u32[]{:S(2)}, u32[]{:S(2)}) collective-permute-start(f32[256,128]{1,0:T(8,128)S(1)} %get-tuple-element.66), channel_id=1, source_target_pairs={{0,1},{1,2},{2,3},{3,4},{4,5},{5,6},{6,7},{7,8},{8,9},{9,10},{10,1... | collective-permute-start | bytes 393224 | tf_op jit(solution)/shard_map/ppermute | solution.py:575
  95.3 1.9 %collective-permute-start.11 = (f32[256,128]{1,0:T(8,128)S(1)}, f32[256,128]{1,0:T(8,128)S(1)}, u32[]{:S(2)}, u32[]{:S(2)}) collective-permute-start(f32[256,128]{1,0:T(8,128)S(1)} %get-tuple-element.67), channel_id=1, source_target_pairs={{1,0},{2,1},{3,2},{4,3},{5,4},{6,5},{7,6},{8,7},{9,8},{10,9},{11,1... | collective-permute-start | bytes 393224 | tf_op jit(solution)/shard_map/ppermute | solution.py:576
  97.3 0.4 shard_map.84.t
  97.7 0.2 collective-permute-done.10.below
  97.8 4.4 %collective-permute-done.11.above = f32[256,128]{1,0:T(8,128)S(1)} collective-permute-done((f32[256,128]{1,0:T(8,128)S(1)}, f32[256,128]{1,0:T(8,128)S(1)}, u32[]{:S(2)}, u32[]{:S(2)}) %collective-permute-start.11) | collective-permute-done | bytes 131104 | tf_op jit(solution)/shard_map/ppermute | solution.py:576
  102.2 0.2 shard_map.85
  102.4 5.0 %collective-permute-start.12 = (f32[256,128]{1,0:T(8,128)S(1)}, f32[256,128]{1,0:T(8,128)S(1)}, u32[]{:S(2)}, u32[]{:S(2)}) collective-permute-start(f32[256,128]{1,0:T(8,128)S(1)} %get-tuple-element.69), channel_id=1, source_target_pairs={{0,1},{1,2},{2,3},{3,4},{4,5},{5,6},{6,7},{7,8},{8,9},{9,10},{10,1... | collective-permute-start | bytes 393224 | tf_op jit(solution)/shard_map/ppermute | solution.py:575
  107.4 1.9 %collective-permute-start.13 = (f32[256,128]{1,0:T(8,128)S(1)}, f32[256,128]{1,0:T(8,128)S(1)}, u32[]{:S(2)}, u32[]{:S(2)}) collective-permute-start(f32[256,128]{1,0:T(8,128)S(1)} %get-tuple-element.70), channel_id=1, source_target_pairs={{1,0},{2,1},{3,2},{4,3},{5,4},{6,5},{7,6},{8,7},{9,8},{10,9},{11,1... | collective-permute-start | bytes 393224 | tf_op jit(solution)/shard_map/ppermute | solution.py:576
  109.3 0.4 shard_map.86.t
  109.7 0.0 copy-start.2
  109.7 0.2 collective-permute-done.12.below
  109.9 4.4 %collective-permute-done.13.above = f32[256,128]{1,0:T(8,128)S(1)} collective-permute-done((f32[256,128]{1,0:T(8,128)S(1)}, f32[256,128]{1,0:T(8,128)S(1)}, u32[]{:S(2)}, u32[]{:S(2)}) %collective-permute-start.13) | collective-permute-done | bytes 131104 | tf_op jit(solution)/shard_map/ppermute | solution.py:576
  114.3 0.2 shard_map.87.own
  114.4 4.1 %collective-permute-start.14 = (f32[160,128]{1,0:T(8,128)S(1)}, f32[160,128]{1,0:T(8,128)S(1)}, u32[]{:S(2)}, u32[]{:S(2)}) collective-permute-start(f32[160,128]{1,0:T(8,128)S(1)} %shard_map.87.own), channel_id=1, source_target_pairs={{0,1},{1,2},{2,3},{3,4},{4,5},{5,6},{6,7},{7,8},{8,9},{9,10},{10,1... | collective-permute-start | bytes 245768 | tf_op jit(solution)/shard_map/ppermute | solution.py:575
  118.6 1.9 %collective-permute-start.15 = (f32[160,128]{1,0:T(8,128)S(1)}, f32[160,128]{1,0:T(8,128)S(1)}, u32[]{:S(2)}, u32[]{:S(2)}) collective-permute-start(f32[160,128]{1,0:T(8,128)S(1)} %shard_map.87.own), channel_id=1, source_target_pairs={{1,0},{2,1},{3,2},{4,3},{5,4},{6,5},{7,6},{8,7},{9,8},{10,9},{11,1... | collective-permute-start | bytes 245768 | tf_op jit(solution)/shard_map/ppermute | solution.py:576
  120.5 0.3 collective-permute-done.14.below
  120.8 4.1 %collective-permute-done.15.above = f32[160,128]{1,0:T(8,128)S(1)} collective-permute-done((f32[160,128]{1,0:T(8,128)S(1)}, f32[160,128]{1,0:T(8,128)S(1)}, u32[]{:S(2)}, u32[]{:S(2)}) %collective-permute-start.15) | collective-permute-done | bytes 81952 | tf_op jit(solution)/shard_map/ppermute | solution.py:576
  124.9 0.0 copy-done.2
  124.9 2.1 %shard_map.88 = f32[8,8,512]{2,1,0:T(8,128)} custom-call(f32[160,128]{1,0:T(8,128)S(1)} %shard_map.87.own, f32[160,128]{1,0:T(8,128)S(1)} %collective-permute-done.14.below, f32[160,128]{1,0:T(8,128)S(1)} %collective-permute-done.15.above, f32[5,256,128]{2,1,0:T(8,128)S(1)} %get-tuple-element.53.mid, f32[256,128]{1,0:T(8,128)S(1)} %get-tuple-element.72.rhs_mid, ...), custom_call_target="tpu_custom_call" | custom-call | flops 519045120 | bytes 4276224 | tf_op jit(solution)/shard_map/pallas_call | solution.py:562
  (1 shorter events, 0.0 us)
Async XLA Ops:
  6.5 23.5 %copy-start.4 = (f32[512,512]{1,0:T(8,128)S(1)}, f32[512,512]{1,0:T(8,128)}, u32[]{:S(2)}) copy-start(f32[512,512]{1,0:T(8,128)} %j_ref.1) | copy-start | bytes 3145732
  6.5 70.5 %all-gather.2.cloned.1.call-start = ((), (), s32[]{:S(2)}) async-start(), calls=%async_computation | async-start | bytes 1081344 | tf_op jit(solution)/shard_map/all_gather | solution.py:596
  9.3 10.9 %collective-permute-start = (f32[576,128]{1,0:T(8,128)}, f32[576,128]{1,0:T(8,128)S(1)}, u32[]{:S(2)}, u32[]{:S(2)}) collective-permute-start(f32[576,128]{1,0:T(8,128)} %get-tuple-element.41), channel_id=1, source_target_pairs={{0,1},{1,2},{2,3},{3,4},{4,5},{5,6},{6,7},{7,8},{8,9},{9,10},{10,1... | collective-permute-start | bytes 884744 | tf_op jit(solution)/shard_map/ppermute | solution.py:575
  13.1 12.0 %collective-permute-start.1 = (f32[576,128]{1,0:T(8,128)}, f32[576,128]{1,0:T(8,128)S(1)}, u32[]{:S(2)}, u32[]{:S(2)}) collective-permute-start(f32[576,128]{1,0:T(8,128)} %get-tuple-element.42), channel_id=1, source_target_pairs={{1,0},{2,1},{3,2},{4,3},{5,4},{6,5},{7,6},{8,7},{9,8},{10,9},{11,1... | collective-permute-start | bytes 884744 | tf_op jit(solution)/shard_map/ppermute | solution.py:576
  15.1 16.3 %collective-permute-start.2 = (f32[1184,128]{1,0:T(8,128)}, f32[1184,128]{1,0:T(8,128)S(1)}, u32[]{:S(2)}, u32[]{:S(2)}) collective-permute-start(f32[1184,128]{1,0:T(8,128)} %get-tuple-element.43), channel_id=1, source_target_pairs={{0,16},{16,32},{32,48},{48,64},{64,80},{80,96},{96,112},{112,128},... | collective-permute-start | bytes 1818632 | tf_op jit(solution)/shard_map/ppermute | solution.py:575
  16.5 14.9 %collective-permute-start.3 = (f32[1184,128]{1,0:T(8,128)}, f32[1184,128]{1,0:T(8,128)S(1)}, u32[]{:S(2)}, u32[]{:S(2)}) collective-permute-start(f32[1184,128]{1,0:T(8,128)} %get-tuple-element.44), channel_id=1, source_target_pairs={{16,0},{32,16},{48,32},{64,48},{80,64},{96,80},{112,96},{128,112},... | collective-permute-start | bytes 1818632 | tf_op jit(solution)/shard_map/ppermute | solution.py:576
  25.1 6.4 %collective-permute-start.4 = (f32[720,128]{1,0:T(8,128)S(1)}, f32[720,128]{1,0:T(8,128)S(1)}, u32[]{:S(2)}, u32[]{:S(2)}) collective-permute-start(f32[720,128]{1,0:T(8,128)S(1)} %get-tuple-element.45), channel_id=1, source_target_pairs={{0,16},{16,32},{32,48},{48,64},{64,80},{80,96},{96,112},{112,128},... | collective-permute-start | bytes 1105928 | tf_op jit(solution)/shard_map/ppermute | solution.py:575
  26.5 5.3 %collective-permute-start.5 = (f32[720,128]{1,0:T(8,128)S(1)}, f32[720,128]{1,0:T(8,128)S(1)}, u32[]{:S(2)}, u32[]{:S(2)}) collective-permute-start(f32[720,128]{1,0:T(8,128)S(1)} %get-tuple-element.46), channel_id=1, source_target_pairs={{16,0},{32,16},{48,32},{64,48},{80,64},{96,80},{112,96},{128,112},... | collective-permute-start | bytes 1105928 | tf_op jit(solution)/shard_map/ppermute | solution.py:576
  30.0 1.2 copy-start
  34.0 7.0 %collective-permute-start.6 = (f32[160,128]{1,0:T(8,128)S(1)}, f32[160,128]{1,0:T(8,128)S(1)}, u32[]{:S(2)}, u32[]{:S(2)}) collective-permute-start(f32[160,128]{1,0:T(8,128)S(1)} %get-tuple-element.51), channel_id=1, source_target_pairs={{0,1},{1,2},{2,3},{3,4},{4,5},{5,6},{6,7},{7,8},{8,9},{9,10},{10,1... | collective-permute-start | bytes 245768 | tf_op jit(solution)/shard_map/ppermute | solution.py:575
  38.8 6.3 %collective-permute-start.7 = (f32[160,128]{1,0:T(8,128)S(1)}, f32[160,128]{1,0:T(8,128)S(1)}, u32[]{:S(2)}, u32[]{:S(2)}) collective-permute-start(f32[160,128]{1,0:T(8,128)S(1)} %get-tuple-element.52), channel_id=1, source_target_pairs={{1,0},{2,1},{3,2},{4,3},{5,4},{6,5},{7,6},{8,7},{9,8},{10,9},{11,1... | collective-permute-start | bytes 245768 | tf_op jit(solution)/shard_map/ppermute | solution.py:576
  41.0 4.8 %copy-start.1 = (f32[6,576,128]{2,1,0:T(8,128)}, f32[6,576,128]{2,1,0:T(8,128)S(1)}, u32[]{:S(2)}) copy-start(f32[6,576,128]{2,1,0:T(8,128)S(1)} %get-tuple-element.73.fine) | copy-start | bytes 5308420
  77.0 1.2 copy-start.3
  78.7 7.6 %collective-permute-start.8 = (f32[256,128]{1,0:T(8,128)S(1)}, f32[256,128]{1,0:T(8,128)S(1)}, u32[]{:S(2)}, u32[]{:S(2)}) collective-permute-start(f32[256,128]{1,0:T(8,128)S(1)} %get-tuple-element.62), channel_id=1, source_target_pairs={{0,1},{1,2},{2,3},{3,4},{4,5},{5,6},{6,7},{7,8},{8,9},{9,10},{10,1... | collective-permute-start | bytes 393224 | tf_op jit(solution)/shard_map/ppermute | solution.py:575
  82.8 7.4 %collective-permute-start.9 = (f32[256,128]{1,0:T(8,128)S(1)}, f32[256,128]{1,0:T(8,128)S(1)}, u32[]{:S(2)}, u32[]{:S(2)}) collective-permute-start(f32[256,128]{1,0:T(8,128)S(1)} %get-tuple-element.63), channel_id=1, source_target_pairs={{1,0},{2,1},{3,2},{4,3},{5,4},{6,5},{7,6},{8,7},{9,8},{10,9},{11,1... | collective-permute-start | bytes 393224 | tf_op jit(solution)/shard_map/ppermute | solution.py:576
  90.4 7.4 %collective-permute-start.10 = (f32[256,128]{1,0:T(8,128)S(1)}, f32[256,128]{1,0:T(8,128)S(1)}, u32[]{:S(2)}, u32[]{:S(2)}) collective-permute-start(f32[256,128]{1,0:T(8,128)S(1)} %get-tuple-element.66), channel_id=1, source_target_pairs={{0,1},{1,2},{2,3},{3,4},{4,5},{5,6},{6,7},{7,8},{8,9},{9,10},{10,1... | collective-permute-start | bytes 393224 | tf_op jit(solution)/shard_map/ppermute | solution.py:575
  95.3 6.9 %collective-permute-start.11 = (f32[256,128]{1,0:T(8,128)S(1)}, f32[256,128]{1,0:T(8,128)S(1)}, u32[]{:S(2)}, u32[]{:S(2)}) collective-permute-start(f32[256,128]{1,0:T(8,128)S(1)} %get-tuple-element.67), channel_id=1, source_target_pairs={{1,0},{2,1},{3,2},{4,3},{5,4},{6,5},{7,6},{8,7},{9,8},{10,9},{11,1... | collective-permute-start | bytes 393224 | tf_op jit(solution)/shard_map/ppermute | solution.py:576
  102.4 7.5 %collective-permute-start.12 = (f32[256,128]{1,0:T(8,128)S(1)}, f32[256,128]{1,0:T(8,128)S(1)}, u32[]{:S(2)}, u32[]{:S(2)}) collective-permute-start(f32[256,128]{1,0:T(8,128)S(1)} %get-tuple-element.69), channel_id=1, source_target_pairs={{0,1},{1,2},{2,3},{3,4},{4,5},{5,6},{6,7},{7,8},{8,9},{9,10},{10,1... | collective-permute-start | bytes 393224 | tf_op jit(solution)/shard_map/ppermute | solution.py:575
  107.4 6.9 %collective-permute-start.13 = (f32[256,128]{1,0:T(8,128)S(1)}, f32[256,128]{1,0:T(8,128)S(1)}, u32[]{:S(2)}, u32[]{:S(2)}) collective-permute-start(f32[256,128]{1,0:T(8,128)S(1)} %get-tuple-element.70), channel_id=1, source_target_pairs={{1,0},{2,1},{3,2},{4,3},{5,4},{6,5},{7,6},{8,7},{9,8},{10,9},{11,1... | collective-permute-start | bytes 393224 | tf_op jit(solution)/shard_map/ppermute | solution.py:576
  109.7 15.2 %copy-start.2 = (f32[6,576,128]{2,1,0:T(8,128)S(1)}, f32[6,576,128]{2,1,0:T(8,128)}, u32[]{:S(2)}) copy-start(f32[6,576,128]{2,1,0:T(8,128)} %copy-done.1) | copy-start | bytes 5308420
  114.4 6.3 %collective-permute-start.14 = (f32[160,128]{1,0:T(8,128)S(1)}, f32[160,128]{1,0:T(8,128)S(1)}, u32[]{:S(2)}, u32[]{:S(2)}) collective-permute-start(f32[160,128]{1,0:T(8,128)S(1)} %shard_map.87.own), channel_id=1, source_target_pairs={{0,1},{1,2},{2,3},{3,4},{4,5},{5,6},{6,7},{7,8},{8,9},{9,10},{10,1... | collective-permute-start | bytes 245768 | tf_op jit(solution)/shard_map/ppermute | solution.py:575
  118.6 6.3 %collective-permute-start.15 = (f32[160,128]{1,0:T(8,128)S(1)}, f32[160,128]{1,0:T(8,128)S(1)}, u32[]{:S(2)}, u32[]{:S(2)}) collective-permute-start(f32[160,128]{1,0:T(8,128)S(1)} %shard_map.87.own), channel_id=1, source_target_pairs={{1,0},{2,1},{3,2},{4,3},{5,4},{6,5},{7,6},{8,7},{9,8},{10,9},{11,1... | collective-permute-start | bytes 245768 | tf_op jit(solution)/shard_map/ppermute | solution.py:576
Sparse Core Ops, SparseCore 0:
  10.5 61.9 all-gather.1

commit v6 on v5

--- a/solution.py
+++ b/solution.py
@@ -126,7 +126,7 @@
 
 def pack_kernel(*refs):
     sources, outs, buffers = refs[:6], refs[6:11], refs[11:17]
-    lo_ref, hi_ref, up_ref, down_ref, low_ref = outs
+    lo_ref, hi_ref, up_ref, down_ref, copies_ref = outs
     own_ref, sems = refs[17:]
     unpack(sources, buffers, own_ref, sems)
     for k in range(4):
@@ -151,7 +151,9 @@
         for m in range(2):
             at = 1536 + 64 * k + 32 * m
             both = own_ref[pl.ds(at, 16), :] + own_ref[pl.ds(at + 16, 16), :]
-            low_ref[pl.ds(16 * k + 8 * m, 8), :] = 0.125 * pair_sums(both)
+            low = 0.125 * pair_sums(both)
+            for i in range(copies_ref.shape[0] // 64):
+                copies_ref[pl.ds(64 * i + 16 * k + 8 * m, 8), :] = low
 
 
 def own_kernel(*refs):
@@ -329,7 +331,7 @@
         wide_ref[pl.ds(48 * a + 40, 8), :] = ends[1]
 
 
-def mid_kernel(own, below, above, mid, jhi, jlo, out, pay_ref, err_ref, rhs_ref, e0, e1, inc):
+def mid_kernel(own, below, above, mid, jhi, jlo, out, _, pay_ref, err_ref, rhs_ref, e0, e1, inc):
     widen_rhs(own, below, above, rhs_ref)
     e0[...] = mid[4] * rhs_ref[...]
 
@@ -583,17 +585,17 @@
     inputs = (right_side, value_guess, speed_liq, speed_ill, flag_liq, flag_ill)
     buffers = [pltpu.VMEM(x.shape, x.dtype) for x in inputs]
     sems = pltpu.SemaphoreType.DMA((6,))
-    lo, hi, up, down, low = call(
+    lo, hi, up, down, copies = call(
         pack_kernel,
         inputs,
-        [(576, LANES)] * 2 + [(1184, LANES)] * 2 + [(64, LANES)],
+        [(576, LANES)] * 2 + [(1184, LANES)] * 2 + [(64 * lax.axis_size("liq"), LANES)],
         buffers + [(1792, LANES), sems],
         places=[pltpu.HBM] * 6,
         limit=57,
     )
     ill_below, ill_above = neighbours(lo, hi, "ill")
     below, above = neighbours(down, up, "liq")
-    coefs = lax.all_gather(low, "liq", axis=0, tiled=True)
+    coefs = lax.all_to_all(copies, "liq", 0, 0, tiled=True)
     rates = jax.ShapeDtypeStruct((nz, nz), BF16)
     (own,) = call(
         own_kernel, inputs, [(1792, LANES)], buffers + [sems], places=[pltpu.HBM] * 6, limit=57
@@ -613,17 +615,17 @@
     )
     mid_below, mid_above = neighbours(lo, hi, "ill")
     fine, mid = call(keep_kernel, (*pieces, out), [(6, 576, LANES), (5, 256, LANES)])
+    lines = coefs.shape[0] // 4
+    line, message = (lines, LANES), (lines // 2, LANES)
+    fac, middle = call(factor_kernel, (coefs, out), [(5, *line), (TILE, LANES)])
     payload, err = call(
         mid_kernel,
-        (rhs_mid, mid_below, mid_above, mid, jhi, jlo, out),
+        (rhs_mid, mid_below, mid_above, mid, jhi, jlo, out, middle),
         [(48, LANES), (96, LANES)],
         [(256, LANES)] * 4,
         flops=dot_flops * 80,
     )
     gathered = lax.all_gather(payload, "liq", axis=0, tiled=True)
-    lines = gathered.shape[0] // 48 * 2 * TILE
-    line, message = (lines, LANES), (lines // 2, LANES)
-    fac, middle = call(factor_kernel, (coefs, out), [(5, *line), (TILE, LANES)])
     e, lo, hi = call(
         first_solve_kernel, (gathered, fac, middle), [line, message, message], [line]
     )

time: 135 us -> 130 us (0.963)
  between operations: 13.7 us -> 0.36 us
  starting transfers between devices: 43.8 us -> 51.9 us
  waiting for transfers between devices: 30.2 us -> 27.2 us
  Pallas kernels: 12.6 us -> 15.3 us
    all_to_all x0 -> x1, starting transfers between devices: none -> 7.47 us  [body(): coefs = lax.all_to_all(copies, 'liq', 0, 0, tiled=True)]
    pallas_call x16, Pallas kernels: 12.6 us -> 15.3 us  [call(): pl.pallas_call(kernel, out_shape=outs, in_specs=[pl.BlockSpec(memory_spac...]
    ppermute x8, waiting for transfers between devices: 26.1 us -> 24.3 us  [neighbours(): above = lax.ppermute(lo, axis, [(i + 1, i) for i in range(count - 1)])]
    unnamed x10 -> x20, local copies, waits for them, and re-layouts: 2.41 us -> 3.73 us
  transfers between devices with their start and end apart: 17 -> 17, of which waited for: 12 -> 12; matrix products, arithmetic and copies ran while one was open for 0% -> 0% of each run, Pallas kernels for 5% -> 6%
where the time goes in v6:
time: 130 us; the launch traced here: 129 us
  starting transfers between devices  51.9 us (40%)
  blocking collectives  30.8 us (24%)
  waiting for transfers between devices  27.2 us (21%)
  Pallas kernels  15.3 us (12%)
  local copies, waits for them, and re-layouts  3.73 us (3%)
    all_gather x1, blocking collectives, body(): gathered = lax.all_gather(payload, 'liq', axis=0, tiled=True)  30.8 us
    ppermute x8, starting transfers between devices, neighbours(): below = lax.ppermute(hi, axis, [(i, i + 1) for i in range(count - 1)])  30.2 us
    ppermute x8, waiting for transfers between devices, neighbours(): above = lax.ppermute(lo, axis, [(i + 1, i) for i in range(count - 1)])  24.3 us
    pallas_call x16, Pallas kernels, call(): pl.pallas_call(kernel, out_shape=outs, in_specs=[pl.BlockSpec(memory_spac...  15.3 us
    ppermute x8, starting transfers between devices, neighbours(): above = lax.ppermute(lo, axis, [(i + 1, i) for i in range(count - 1)])  14.2 us
    all_to_all x1, starting transfers between devices, body(): coefs = lax.all_to_all(copies, 'liq', 0, 0, tiled=True)  7.47 us
    unnamed x20, local copies, waits for them, and re-layouts  3.73 us
    ppermute x8, waiting for transfers between devices, neighbours(): below = lax.ppermute(hi, axis, [(i, i + 1) for i in range(count - 1)])  2.9 us
  transfers between devices with their start and end apart: 17, of which 12 were waited for; matrix products, arithmetic and copies ran while one was open for 0% of the time, Pallas kernels for 6%

profile of v6, /device:TPU:64, one launch (start us, length us, event | category | flops | bytes accessed | tf_op | source)
XLA Modules:
  0.0 129.2 jit_solution(16336943393080568286)
XLA Ops:
  0.0 2.9 %shard_map.75 = (f32[576,128]{1,0:T(8,128)}, f32[576,128]{1,0:T(8,128)}, f32[1184,128]{1,0:T(8,128)}, f32[1184,128]{1,0:T(8,128)}, f32[2048,128]{1,0:T(8,128)}) custom-call(f32[8,8,512]{2,1,0:T(8,128)} %refs_0_.3, f32[8,8,512]{2,1,0:T(8,128)} %refs_1_.3, f32[8,8,512]{2,1,0:T(8,128)} %refs_2_.3, f32[8,8,512]{2,1,0:T(8,128)} %refs_3_.3, s32[8,8,512]{2,1,0:T(8,128)} %refs_4_.3, ...), custom_call_target="tpu_custom_call" | custom-call | bytes 3637248 | tf_op jit(solution)/shard_map/pallas_call | solution.py:564
  2.9 0.0 copy-start.9
  2.9 0.0 copy-start.8
  2.9 7.5 %all-to-all-start = ((f32[32,64,128]{2,1,0:T(8,128)}), f32[32,64,128]{2,1,0:T(8,128)S(1)}, u32[]{:S(2)}, u32[]{:S(2)}) async-start(f32[32,64,128]{2,1,0:T(8,128)} %bitcast.3), calls=%async_computation | async-start | bytes 2097152 | tf_op jit(solution)/shard_map/all_to_all | solution.py:598
  10.4 0.0 copy-start.3
  10.4 0.0 copy-done.9
  10.4 4.0 %collective-permute-start = (f32[576,128]{1,0:T(8,128)S(1)}, f32[576,128]{1,0:T(8,128)S(1)}, u32[]{:S(2)}, u32[]{:S(2)}) collective-permute-start(f32[576,128]{1,0:T(8,128)S(1)} %copy-done.9), channel_id=1, source_target_pairs={{0,1},{1,2},{2,3},{3,4},{4,5},{5,6},{6,7},{7,8},{8,9},{9,10},{10,1... | collective-permute-start | bytes 884744 | tf_op jit(solution)/shard_map/ppermute | solution.py:577
  14.4 0.0 copy-done.8
  14.4 2.0 %collective-permute-start.1 = (f32[576,128]{1,0:T(8,128)S(1)}, f32[576,128]{1,0:T(8,128)S(1)}, u32[]{:S(2)}, u32[]{:S(2)}) collective-permute-start(f32[576,128]{1,0:T(8,128)S(1)} %copy-done.8), channel_id=1, source_target_pairs={{1,0},{2,1},{3,2},{4,3},{5,4},{6,5},{7,6},{8,7},{9,8},{10,9},{11,1... | collective-permute-start | bytes 884744 | tf_op jit(solution)/shard_map/ppermute | solution.py:578
  16.4 1.8 %collective-permute-start.2 = (f32[1184,128]{1,0:T(8,128)}, f32[1184,128]{1,0:T(8,128)S(1)}, u32[]{:S(2)}, u32[]{:S(2)}) collective-permute-start(f32[1184,128]{1,0:T(8,128)} %get-tuple-element.43), channel_id=1, source_target_pairs={{0,16},{16,32},{32,48},{48,64},{64,80},{80,96},{96,112},{112,128},... | collective-permute-start | bytes 1818632 | tf_op jit(solution)/shard_map/ppermute | solution.py:577
  18.3 1.3 collective-permute-start.3
  19.6 2.1 %collective-permute-done.below.ill_below = f32[576,128]{1,0:T(8,128)S(1)} collective-permute-done((f32[576,128]{1,0:T(8,128)S(1)}, f32[576,128]{1,0:T(8,128)S(1)}, u32[]{:S(2)}, u32[]{:S(2)}) %collective-permute-start) | collective-permute-done | bytes 294944 | tf_op jit(solution)/shard_map/ppermute | solution.py:577
  21.6 5.0 %collective-permute-done.1.above.ill_above = f32[576,128]{1,0:T(8,128)S(1)} collective-permute-done((f32[576,128]{1,0:T(8,128)S(1)}, f32[576,128]{1,0:T(8,128)S(1)}, u32[]{:S(2)}, u32[]{:S(2)}) %collective-permute-start.1) | collective-permute-done | bytes 294944 | tf_op jit(solution)/shard_map/ppermute | solution.py:578
  26.7 1.4 %collective-permute-start.4 = (f32[720,128]{1,0:T(8,128)S(1)}, f32[720,128]{1,0:T(8,128)S(1)}, u32[]{:S(2)}, u32[]{:S(2)}) collective-permute-start(f32[720,128]{1,0:T(8,128)S(1)} %get-tuple-element.45), channel_id=1, source_target_pairs={{0,16},{16,32},{32,48},{48,64},{64,80},{80,96},{96,112},{112,128},... | collective-permute-start | bytes 1105928 | tf_op jit(solution)/shard_map/ppermute | solution.py:577
  28.1 1.3 collective-permute-start.5
  29.4 2.3 %shard_map.73.own = f32[1792,128]{1,0:T(8,128)} custom-call(f32[8,8,512]{2,1,0:T(8,128)} %refs_0_.3, f32[8,8,512]{2,1,0:T(8,128)} %refs_1_.3, f32[8,8,512]{2,1,0:T(8,128)} %refs_2_.3, f32[8,8,512]{2,1,0:T(8,128)} %refs_3_.3, s32[8,8,512]{2,1,0:T(8,128)} %refs_4_.3, s32[8,8,512]{2,1,0:T(8,128)} %refs_5_.3), custom_call_target="tpu_custom_call" | custom-call | bytes 1703936 | tf_op jit(solution)/shard_map/pallas_call | solution.py:564
  31.6 0.0 copy-done.3
  31.7 0.0 copy-start
  31.7 1.2 copy-done
  32.8 0.2 shard_map.74
  33.1 0.0 copy-start.6
  33.1 0.0 collective-permute-done.2.below
  33.1 0.0 collective-permute-done.3.above
  33.1 0.0 collective-permute-done.4.far_below
  33.1 0.3 collective-permute-done.5.far_above
  33.4 2.8 %shard_map.77 = (f32[384,128]{1,0:T(8,128)S(1)}, f32[128,128]{1,0:T(8,128)S(1)}, f32[160,128]{1,0:T(8,128)}, f32[160,128]{1,0:T(8,128)}) custom-call(f32[1792,128]{1,0:T(8,128)S(1)} %get-tuple-element.40.own, f32[576,128]{1,0:T(8,128)S(1)} %collective-permute-done.below.ill_below, f32[576,128]{1,0:T(8,128)S(1)} %collective-permute-done.1.above.ill_above, ...), custom_call_target="tpu_custom_call" | custom-call | flops 1148190720 | bytes 4935680 | tf_op jit(solution)/shard_map/pallas_call | solution.py:564
  36.2 0.7 copy-done.4
  36.9 4.8 %collective-permute-start.6 = (f32[160,128]{1,0:T(8,128)}, f32[160,128]{1,0:T(8,128)}, u32[]{:S(2)}, u32[]{:S(2)}) collective-permute-start(f32[160,128]{1,0:T(8,128)} %get-tuple-element.51), channel_id=1, source_target_pairs={{0,1},{1,2},{2,3},{3,4},{4,5},{5,6},{6,7},{7,8},{8,9},{9,10},{10,1... | collective-permute-start | bytes 245768 | tf_op jit(solution)/shard_map/ppermute | solution.py:577
  41.8 1.9 %collective-permute-start.7 = (f32[160,128]{1,0:T(8,128)}, f32[160,128]{1,0:T(8,128)}, u32[]{:S(2)}, u32[]{:S(2)}) collective-permute-start(f32[160,128]{1,0:T(8,128)} %get-tuple-element.52), channel_id=1, source_target_pairs={{1,0},{2,1},{3,2},{4,3},{5,4},{6,5},{7,6},{8,7},{9,8},{10,9},{11,1... | collective-permute-start | bytes 245768 | tf_op jit(solution)/shard_map/ppermute | solution.py:578
  43.7 0.2 shard_map.78
  43.9 1.2 copy-done.1
  45.1 0.0 all-to-all-done
  45.1 0.7 copy-done.7
  45.8 0.3 shard_map.79
  46.1 0.0 collective-permute-done.6.below
  46.1 2.3 %collective-permute-done.7.above = f32[160,128]{1,0:T(8,128)} collective-permute-done((f32[160,128]{1,0:T(8,128)}, f32[160,128]{1,0:T(8,128)}, u32[]{:S(2)}, u32[]{:S(2)}) %collective-permute-start.7) | collective-permute-done | bytes 81952 | tf_op jit(solution)/shard_map/ppermute | solution.py:578
  48.4 1.5 %shard_map.80 = (f32[48,128]{1,0:T(8,128)S(1)}, f32[96,128]{1,0:T(8,128)S(1)}) custom-call(f32[128,128]{1,0:T(8,128)S(1)} %get-tuple-element.50.own.rhs_mid, f32[160,128]{1,0:T(8,128)} %collective-permute-done.6.below, f32[160,128]{1,0:T(8,128)} %collective-permute-done.7.above, f32[5,256,128]{2,1,0:T(8,128)S(1)} %get-tuple-element.53.mid, ...), custom_call_target="tpu_custom_call" | custom-call | flops 125829120 | bytes 2015232 | tf_op jit(solution)/shard_map/pallas_call | solution.py:564
  49.9 30.8 %all_gather.3.gathered = f32[1536,128]{1,0:T(8,128)S(1)} all-gather(f32[48,128]{1,0:T(8,128)S(1)} %get-tuple-element.56), channel_id=1, replica_groups=mesh['liq'=32,'ill'=16] {'liq'}, dimensions={0}, use_global_device_ids=true | all-gather | bytes 811008 | tf_op jit(solution)/shard_map/all_gather | solution.py:628
  80.7 0.1 shard_map.81
  80.9 4.1 %collective-permute-start.8 = (f32[256,128]{1,0:T(8,128)S(1)}, f32[256,128]{1,0:T(8,128)S(1)}, u32[]{:S(2)}, u32[]{:S(2)}) collective-permute-start(f32[256,128]{1,0:T(8,128)S(1)} %get-tuple-element.62), channel_id=1, source_target_pairs={{0,1},{1,2},{2,3},{3,4},{4,5},{5,6},{6,7},{7,8},{8,9},{9,10},{10,1... | collective-permute-start | bytes 393224 | tf_op jit(solution)/shard_map/ppermute | solution.py:577
  85.0 1.9 %collective-permute-start.9 = (f32[256,128]{1,0:T(8,128)S(1)}, f32[256,128]{1,0:T(8,128)S(1)}, u32[]{:S(2)}, u32[]{:S(2)}) collective-permute-start(f32[256,128]{1,0:T(8,128)S(1)} %get-tuple-element.63), channel_id=1, source_target_pairs={{1,0},{2,1},{3,2},{4,3},{5,4},{6,5},{7,6},{8,7},{9,8},{10,9},{11,1... | collective-permute-start | bytes 393224 | tf_op jit(solution)/shard_map/ppermute | solution.py:578
  86.9 1.4 %shard_map.82 = (f32[512,128]{1,0:T(8,128)S(1)}, f32[512,128]{1,0:T(8,128)S(1)}, f32[160,128]{1,0:T(8,128)S(1)}, f32[256,128]{1,0:T(8,128)S(1)}, f32[576,128]{1,0:T(8,128)S(1)}) custom-call(f32[1536,128]{1,0:T(8,128)S(1)} %all_gather.3.gathered, f32[96,128]{1,0:T(8,128)S(1)} %get-tuple-element.57.err, f32[512,128]{1,0:T(8,128)S(1)} %get-tuple-element.59.e, ...), custom_call_target="tpu_custom_call" | custom-call | flops 201326592 | bytes 4915200 | tf_op jit(solution)/shard_map/pallas_call | solution.py:564
  88.3 0.2 collective-permute-done.8.below
  88.5 3.8 %collective-permute-done.9.above = f32[256,128]{1,0:T(8,128)S(1)} collective-permute-done((f32[256,128]{1,0:T(8,128)S(1)}, f32[256,128]{1,0:T(8,128)S(1)}, u32[]{:S(2)}, u32[]{:S(2)}) %collective-permute-start.9) | collective-permute-done | bytes 131104 | tf_op jit(solution)/shard_map/ppermute | solution.py:578
  92.4 0.2 shard_map.83
  92.5 4.8 %collective-permute-start.10 = (f32[256,128]{1,0:T(8,128)S(1)}, f32[256,128]{1,0:T(8,128)S(1)}, u32[]{:S(2)}, u32[]{:S(2)}) collective-permute-start(f32[256,128]{1,0:T(8,128)S(1)} %get-tuple-element.66), channel_id=1, source_target_pairs={{0,1},{1,2},{2,3},{3,4},{4,5},{5,6},{6,7},{7,8},{8,9},{9,10},{10,1... | collective-permute-start | bytes 393224 | tf_op jit(solution)/shard_map/ppermute | solution.py:577
  97.4 1.9 %collective-permute-start.11 = (f32[256,128]{1,0:T(8,128)S(1)}, f32[256,128]{1,0:T(8,128)S(1)}, u32[]{:S(2)}, u32[]{:S(2)}) collective-permute-start(f32[256,128]{1,0:T(8,128)S(1)} %get-tuple-element.67), channel_id=1, source_target_pairs={{1,0},{2,1},{3,2},{4,3},{5,4},{6,5},{7,6},{8,7},{9,8},{10,9},{11,1... | collective-permute-start | bytes 393224 | tf_op jit(solution)/shard_map/ppermute | solution.py:578
  99.3 0.4 shard_map.84.t
  99.7 0.2 collective-permute-done.10.below
  99.9 4.4 %collective-permute-done.11.above = f32[256,128]{1,0:T(8,128)S(1)} collective-permute-done((f32[256,128]{1,0:T(8,128)S(1)}, f32[256,128]{1,0:T(8,128)S(1)}, u32[]{:S(2)}, u32[]{:S(2)}) %collective-permute-start.11) | collective-permute-done | bytes 131104 | tf_op jit(solution)/shard_map/ppermute | solution.py:578
  104.2 0.2 shard_map.85
  104.4 5.1 %collective-permute-start.12 = (f32[256,128]{1,0:T(8,128)S(1)}, f32[256,128]{1,0:T(8,128)S(1)}, u32[]{:S(2)}, u32[]{:S(2)}) collective-permute-start(f32[256,128]{1,0:T(8,128)S(1)} %get-tuple-element.69), channel_id=1, source_target_pairs={{0,1},{1,2},{2,3},{3,4},{4,5},{5,6},{6,7},{7,8},{8,9},{9,10},{10,1... | collective-permute-start | bytes 393224 | tf_op jit(solution)/shard_map/ppermute | solution.py:577
  109.6 1.9 %collective-permute-start.13 = (f32[256,128]{1,0:T(8,128)S(1)}, f32[256,128]{1,0:T(8,128)S(1)}, u32[]{:S(2)}, u32[]{:S(2)}) collective-permute-start(f32[256,128]{1,0:T(8,128)S(1)} %get-tuple-element.70), channel_id=1, source_target_pairs={{1,0},{2,1},{3,2},{4,3},{5,4},{6,5},{7,6},{8,7},{9,8},{10,9},{11,1... | collective-permute-start | bytes 393224 | tf_op jit(solution)/shard_map/ppermute | solution.py:578
  111.5 0.4 shard_map.86.t
  111.9 0.0 copy-start.2
  111.9 0.2 collective-permute-done.12.below
  112.1 4.4 %collective-permute-done.13.above = f32[256,128]{1,0:T(8,128)S(1)} collective-permute-done((f32[256,128]{1,0:T(8,128)S(1)}, f32[256,128]{1,0:T(8,128)S(1)}, u32[]{:S(2)}, u32[]{:S(2)}) %collective-permute-start.13) | collective-permute-done | bytes 131104 | tf_op jit(solution)/shard_map/ppermute | solution.py:578
  116.4 0.2 shard_map.87.own
  116.6 4.1 %collective-permute-start.14 = (f32[160,128]{1,0:T(8,128)S(1)}, f32[160,128]{1,0:T(8,128)S(1)}, u32[]{:S(2)}, u32[]{:S(2)}) collective-permute-start(f32[160,128]{1,0:T(8,128)S(1)} %shard_map.87.own), channel_id=1, source_target_pairs={{0,1},{1,2},{2,3},{3,4},{4,5},{5,6},{6,7},{7,8},{8,9},{9,10},{10,1... | collective-permute-start | bytes 245768 | tf_op jit(solution)/shard_map/ppermute | solution.py:577
  120.7 1.9 %collective-permute-start.15 = (f32[160,128]{1,0:T(8,128)S(1)}, f32[160,128]{1,0:T(8,128)S(1)}, u32[]{:S(2)}, u32[]{:S(2)}) collective-permute-start(f32[160,128]{1,0:T(8,128)S(1)} %shard_map.87.own), channel_id=1, source_target_pairs={{1,0},{2,1},{3,2},{4,3},{5,4},{6,5},{7,6},{8,7},{9,8},{10,9},{11,1... | collective-permute-start | bytes 245768 | tf_op jit(solution)/shard_map/ppermute | solution.py:578
  122.6 0.3 collective-permute-done.14.below
  122.9 4.1 %collective-permute-done.15.above = f32[160,128]{1,0:T(8,128)S(1)} collective-permute-done((f32[160,128]{1,0:T(8,128)S(1)}, f32[160,128]{1,0:T(8,128)S(1)}, u32[]{:S(2)}, u32[]{:S(2)}) %collective-permute-start.15) | collective-permute-done | bytes 81952 | tf_op jit(solution)/shard_map/ppermute | solution.py:578
  127.0 0.0 copy-done.2
  127.1 2.2 %shard_map.88 = f32[8,8,512]{2,1,0:T(8,128)} custom-call(f32[160,128]{1,0:T(8,128)S(1)} %shard_map.87.own, f32[160,128]{1,0:T(8,128)S(1)} %collective-permute-done.14.below, f32[160,128]{1,0:T(8,128)S(1)} %collective-permute-done.15.above, f32[5,256,128]{2,1,0:T(8,128)S(1)} %get-tuple-element.53.mid, f32[256,128]{1,0:T(8,128)S(1)} %get-tuple-element.72.rhs_mid, ...), custom_call_target="tpu_custom_call" | custom-call | flops 519045120 | bytes 4276224 | tf_op jit(solution)/shard_map/pallas_call | solution.py:564
  (7 shorter events, 0.1 us)
Async XLA Ops:
  2.9 7.5 %copy-start.9 = (f32[576,128]{1,0:T(8,128)S(1)}, f32[576,128]{1,0:T(8,128)}, u32[]{:S(2)}) copy-start(f32[576,128]{1,0:T(8,128)} %get-tuple-element.41) | copy-start | bytes 884740
  2.9 11.5 %copy-start.8 = (f32[576,128]{1,0:T(8,128)S(1)}, f32[576,128]{1,0:T(8,128)}, u32[]{:S(2)}) copy-start(f32[576,128]{1,0:T(8,128)} %get-tuple-element.42) | copy-start | bytes 884740
  2.9 42.1 %all-to-all-start = ((f32[32,64,128]{2,1,0:T(8,128)}), f32[32,64,128]{2,1,0:T(8,128)S(1)}, u32[]{:S(2)}, u32[]{:S(2)}) async-start(f32[32,64,128]{2,1,0:T(8,128)} %bitcast.3), calls=%async_computation | async-start | bytes 2097152 | tf_op jit(solution)/shard_map/all_to_all | solution.py:598
  10.4 21.2 %copy-start.3 = (f32[512,512]{1,0:T(8,128)S(1)}, f32[512,512]{1,0:T(8,128)}, u32[]{:S(2)}) copy-start(f32[512,512]{1,0:T(8,128)} %j_ref.1) | copy-start | bytes 3145732
  10.4 11.2 %collective-permute-start = (f32[576,128]{1,0:T(8,128)S(1)}, f32[576,128]{1,0:T(8,128)S(1)}, u32[]{:S(2)}, u32[]{:S(2)}) collective-permute-start(f32[576,128]{1,0:T(8,128)S(1)} %copy-done.9), channel_id=1, source_target_pairs={{0,1},{1,2},{2,3},{3,4},{4,5},{5,6},{6,7},{7,8},{8,9},{9,10},{10,1... | collective-permute-start | bytes 884744 | tf_op jit(solution)/shard_map/ppermute | solution.py:577
  14.4 12.2 %collective-permute-start.1 = (f32[576,128]{1,0:T(8,128)S(1)}, f32[576,128]{1,0:T(8,128)S(1)}, u32[]{:S(2)}, u32[]{:S(2)}) collective-permute-start(f32[576,128]{1,0:T(8,128)S(1)} %copy-done.8), channel_id=1, source_target_pairs={{1,0},{2,1},{3,2},{4,3},{5,4},{6,5},{7,6},{8,7},{9,8},{10,9},{11,1... | collective-permute-start | bytes 884744 | tf_op jit(solution)/shard_map/ppermute | solution.py:578
  16.4 16.7 %collective-permute-start.2 = (f32[1184,128]{1,0:T(8,128)}, f32[1184,128]{1,0:T(8,128)S(1)}, u32[]{:S(2)}, u32[]{:S(2)}) collective-permute-start(f32[1184,128]{1,0:T(8,128)} %get-tuple-element.43), channel_id=1, source_target_pairs={{0,16},{16,32},{32,48},{48,64},{64,80},{80,96},{96,112},{112,128},... | collective-permute-start | bytes 1818632 | tf_op jit(solution)/shard_map/ppermute | solution.py:577
  18.3 14.8 %collective-permute-start.3 = (f32[1184,128]{1,0:T(8,128)}, f32[1184,128]{1,0:T(8,128)S(1)}, u32[]{:S(2)}, u32[]{:S(2)}) collective-permute-start(f32[1184,128]{1,0:T(8,128)} %get-tuple-element.44), channel_id=1, source_target_pairs={{16,0},{32,16},{48,32},{64,48},{80,64},{96,80},{112,96},{128,112},... | collective-permute-start | bytes 1818632 | tf_op jit(solution)/shard_map/ppermute | solution.py:578
  26.7 6.5 %collective-permute-start.4 = (f32[720,128]{1,0:T(8,128)S(1)}, f32[720,128]{1,0:T(8,128)S(1)}, u32[]{:S(2)}, u32[]{:S(2)}) collective-permute-start(f32[720,128]{1,0:T(8,128)S(1)} %get-tuple-element.45), channel_id=1, source_target_pairs={{0,16},{16,32},{32,48},{48,64},{64,80},{80,96},{96,112},{112,128},... | collective-permute-start | bytes 1105928 | tf_op jit(solution)/shard_map/ppermute | solution.py:577
  28.1 5.4 %collective-permute-start.5 = (f32[720,128]{1,0:T(8,128)S(1)}, f32[720,128]{1,0:T(8,128)S(1)}, u32[]{:S(2)}, u32[]{:S(2)}) collective-permute-start(f32[720,128]{1,0:T(8,128)S(1)} %get-tuple-element.46), channel_id=1, source_target_pairs={{16,0},{32,16},{48,32},{64,48},{80,64},{96,80},{112,96},{128,112},... | collective-permute-start | bytes 1105928 | tf_op jit(solution)/shard_map/ppermute | solution.py:578
  31.7 1.2 copy-start
  33.1 10.6 %copy-start.6 = (f32[8,128]{1,0:T(8,128)}, f32[8,128]{1,0:T(8,128)S(1)}, u32[]{:S(2)}) copy-start(f32[8,128]{1,0:T(8,128)S(1)} %get-tuple-element.49.out) | copy-start | bytes 12292
  36.2 0.7 copy-start.4
  36.9 9.2 %collective-permute-start.6 = (f32[160,128]{1,0:T(8,128)}, f32[160,128]{1,0:T(8,128)}, u32[]{:S(2)}, u32[]{:S(2)}) collective-permute-start(f32[160,128]{1,0:T(8,128)} %get-tuple-element.51), channel_id=1, source_target_pairs={{0,1},{1,2},{2,3},{3,4},{4,5},{5,6},{6,7},{7,8},{8,9},{9,10},{10,1... | collective-permute-start | bytes 245768 | tf_op jit(solution)/shard_map/ppermute | solution.py:577
  41.8 6.7 %collective-permute-start.7 = (f32[160,128]{1,0:T(8,128)}, f32[160,128]{1,0:T(8,128)}, u32[]{:S(2)}, u32[]{:S(2)}) collective-permute-start(f32[160,128]{1,0:T(8,128)} %get-tuple-element.52), channel_id=1, source_target_pairs={{1,0},{2,1},{3,2},{4,3},{5,4},{6,5},{7,6},{8,7},{9,8},{10,9},{11,1... | collective-permute-start | bytes 245768 | tf_op jit(solution)/shard_map/ppermute | solution.py:578
  43.9 1.2 copy-start.1
  45.1 0.7 copy-start.7
  49.9 37.0 %copy-start.5 = (f32[384,128]{1,0:T(8,128)S(1)}, f32[384,128]{1,0:T(8,128)}, u32[]{:S(2)}) copy-start(f32[384,128]{1,0:T(8,128)} %copy-done.4) | copy-start | bytes 589828
  80.9 7.6 %collective-permute-start.8 = (f32[256,128]{1,0:T(8,128)S(1)}, f32[256,128]{1,0:T(8,128)S(1)}, u32[]{:S(2)}, u32[]{:S(2)}) collective-permute-start(f32[256,128]{1,0:T(8,128)S(1)} %get-tuple-element.62), channel_id=1, source_target_pairs={{0,1},{1,2},{2,3},{3,4},{4,5},{5,6},{6,7},{7,8},{8,9},{9,10},{10,1... | collective-permute-start | bytes 393224 | tf_op jit(solution)/shard_map/ppermute | solution.py:577
  85.0 7.4 %collective-permute-start.9 = (f32[256,128]{1,0:T(8,128)S(1)}, f32[256,128]{1,0:T(8,128)S(1)}, u32[]{:S(2)}, u32[]{:S(2)}) collective-permute-start(f32[256,128]{1,0:T(8,128)S(1)} %get-tuple-element.63), channel_id=1, source_target_pairs={{1,0},{2,1},{3,2},{4,3},{5,4},{6,5},{7,6},{8,7},{9,8},{10,9},{11,1... | collective-permute-start | bytes 393224 | tf_op jit(solution)/shard_map/ppermute | solution.py:578
  92.5 7.3 %collective-permute-start.10 = (f32[256,128]{1,0:T(8,128)S(1)}, f32[256,128]{1,0:T(8,128)S(1)}, u32[]{:S(2)}, u32[]{:S(2)}) collective-permute-start(f32[256,128]{1,0:T(8,128)S(1)} %get-tuple-element.66), channel_id=1, source_target_pairs={{0,1},{1,2},{2,3},{3,4},{4,5},{5,6},{6,7},{7,8},{8,9},{9,10},{10,1... | collective-permute-start | bytes 393224 | tf_op jit(solution)/shard_map/ppermute | solution.py:577
  97.4 6.9 %collective-permute-start.11 = (f32[256,128]{1,0:T(8,128)S(1)}, f32[256,128]{1,0:T(8,128)S(1)}, u32[]{:S(2)}, u32[]{:S(2)}) collective-permute-start(f32[256,128]{1,0:T(8,128)S(1)} %get-tuple-element.67), channel_id=1, source_target_pairs={{1,0},{2,1},{3,2},{4,3},{5,4},{6,5},{7,6},{8,7},{9,8},{10,9},{11,1... | collective-permute-start | bytes 393224 | tf_op jit(solution)/shard_map/ppermute | solution.py:578
  104.4 7.6 %collective-permute-start.12 = (f32[256,128]{1,0:T(8,128)S(1)}, f32[256,128]{1,0:T(8,128)S(1)}, u32[]{:S(2)}, u32[]{:S(2)}) collective-permute-start(f32[256,128]{1,0:T(8,128)S(1)} %get-tuple-element.69), channel_id=1, source_target_pairs={{0,1},{1,2},{2,3},{3,4},{4,5},{5,6},{6,7},{7,8},{8,9},{9,10},{10,1... | collective-permute-start | bytes 393224 | tf_op jit(solution)/shard_map/ppermute | solution.py:577
  109.6 6.9 %collective-permute-start.13 = (f32[256,128]{1,0:T(8,128)S(1)}, f32[256,128]{1,0:T(8,128)S(1)}, u32[]{:S(2)}, u32[]{:S(2)}) collective-permute-start(f32[256,128]{1,0:T(8,128)S(1)} %get-tuple-element.70), channel_id=1, source_target_pairs={{1,0},{2,1},{3,2},{4,3},{5,4},{6,5},{7,6},{8,7},{9,8},{10,9},{11,1... | collective-permute-start | bytes 393224 | tf_op jit(solution)/shard_map/ppermute | solution.py:578
  111.9 15.2 %copy-start.2 = (f32[6,576,128]{2,1,0:T(8,128)S(1)}, f32[6,576,128]{2,1,0:T(8,128)}, u32[]{:S(2)}) copy-start(f32[6,576,128]{2,1,0:T(8,128)} %copy-done.1) | copy-start | bytes 5308420
  116.6 6.3 %collective-permute-start.14 = (f32[160,128]{1,0:T(8,128)S(1)}, f32[160,128]{1,0:T(8,128)S(1)}, u32[]{:S(2)}, u32[]{:S(2)}) collective-permute-start(f32[160,128]{1,0:T(8,128)S(1)} %shard_map.87.own), channel_id=1, source_target_pairs={{0,1},{1,2},{2,3},{3,4},{4,5},{5,6},{6,7},{7,8},{8,9},{9,10},{10,1... | collective-permute-start | bytes 245768 | tf_op jit(solution)/shard_map/ppermute | solution.py:577
  120.7 6.3 %collective-permute-start.15 = (f32[160,128]{1,0:T(8,128)S(1)}, f32[160,128]{1,0:T(8,128)S(1)}, u32[]{:S(2)}, u32[]{:S(2)}) collective-permute-start(f32[160,128]{1,0:T(8,128)S(1)} %shard_map.87.own), channel_id=1, source_target_pairs={{1,0},{2,1},{3,2},{4,3},{5,4},{6,5},{7,6},{8,7},{9,8},{10,9},{11,1... | collective-permute-start | bytes 245768 | tf_op jit(solution)/shard_map/ppermute | solution.py:578

commit v7 on v6

--- a/solution.py
+++ b/solution.py
@@ -126,7 +126,7 @@
 
 def pack_kernel(*refs):
     sources, outs, buffers = refs[:6], refs[6:11], refs[11:17]
-    lo_ref, hi_ref, up_ref, down_ref, copies_ref = outs
+    lo_ref, hi_ref, up_ref, down_ref, low_ref = outs
     own_ref, sems = refs[17:]
     unpack(sources, buffers, own_ref, sems)
     for k in range(4):
@@ -151,9 +151,13 @@
         for m in range(2):
             at = 1536 + 64 * k + 32 * m
             both = own_ref[pl.ds(at, 16), :] + own_ref[pl.ds(at + 16, 16), :]
-            low = 0.125 * pair_sums(both)
-            for i in range(copies_ref.shape[0] // 64):
-                copies_ref[pl.ds(64 * i + 16 * k + 8 * m, 8), :] = low
+            low_ref[pl.ds(16 * k + 8 * m, 8), :] = 0.125 * pair_sums(both)
+
+
+def copies_kernel(low, _, all_ref):
+    piece = low[...]
+    for i in range(all_ref.shape[0] // 64):
+        all_ref[pl.ds(64 * i, 64), :] = piece
 
 
 def own_kernel(*refs):
@@ -361,11 +365,12 @@
             diag = diag + mid[k, here, :]
         return (total - diag * center)[8:24]
 
-    for m in range(2):
-        pay_ref[pl.ds(8 * m, 8), :] = 0.25 * pair_sums(residual(2 + 2 * m) + residual(3 + 2 * m))
+    low = [0.25 * pair_sums(residual(2 + 2 * m) + residual(3 + 2 * m)) for m in range(2)]
     for a in range(6):
         err_ref[pl.ds(16 * a, 16), :] = e1[pl.ds(32 * (a + 1) + 8, 16), :]
-    pay_ref[16:48, :] = err_ref[32:64, :]
+    piece = jnp.concatenate(low + [err_ref[32:64, :]], axis=0)
+    for i in range(pay_ref.shape[0] // 48):
+        pay_ref[pl.ds(48 * i, 48), :] = piece
 
 
 def solve_lines(target, weight, carry, link, middle, y, x_ref, offset):
@@ -585,26 +590,28 @@
     inputs = (right_side, value_guess, speed_liq, speed_ill, flag_liq, flag_ill)
     buffers = [pltpu.VMEM(x.shape, x.dtype) for x in inputs]
     sems = pltpu.SemaphoreType.DMA((6,))
-    lo, hi, up, down, copies = call(
+    lo, hi, up, down, low = call(
         pack_kernel,
         inputs,
-        [(576, LANES)] * 2 + [(1184, LANES)] * 2 + [(64 * lax.axis_size("liq"), LANES)],
+        [(576, LANES)] * 2 + [(1184, LANES)] * 2 + [(64, LANES)],
         buffers + [(1792, LANES), sems],
         places=[pltpu.HBM] * 6,
         limit=57,
     )
     ill_below, ill_above = neighbours(lo, hi, "ill")
     below, above = neighbours(down, up, "liq")
-    coefs = lax.all_to_all(copies, "liq", 0, 0, tiled=True)
     rates = jax.ShapeDtypeStruct((nz, nz), BF16)
     (own,) = call(
-        own_kernel, inputs, [(1792, LANES)], buffers + [sems], places=[pltpu.HBM] * 6, limit=57
+        own_kernel, inputs, [(1792, LANES)], buffers + [sems], places=[pltpu.HBM] * 6, limit=57,
+        flops=10**10,
     )
     jhi, jlo, out, own = call(
         rates_kernel, (jump_rates, own), [rates, rates, (TILE, LANES), own.shape]
     )
     up, down = call(corner_kernel, (ill_below, ill_above), [(720, LANES)] * 2)
     far_below, far_above = neighbours(down, up, "liq")
+    (copies,) = call(copies_kernel, (low, above), [(64 * lax.axis_size("liq"), LANES)])
+    coefs = lax.all_to_all(copies, "liq", 0, 0, tiled=True)
     pieces = (own, ill_below, ill_above, below, above, far_below, far_above)
     value, rhs_mid, lo, hi = call(
         fine_kernel,
@@ -621,11 +628,11 @@
     payload, err = call(
         mid_kernel,
         (rhs_mid, mid_below, mid_above, mid, jhi, jlo, out, middle),
-        [(48, LANES), (96, LANES)],
+        [(48 * lax.axis_size("liq"), LANES), (96, LANES)],
         [(256, LANES)] * 4,
         flops=dot_flops * 80,
     )
-    gathered = lax.all_gather(payload, "liq", axis=0, tiled=True)
+    gathered = lax.all_to_all(payload, "liq", 0, 0, tiled=True)
     e, lo, hi = call(
         first_solve_kernel, (gathered, fac, middle), [line, message, message], [line]
     )

time: 130 us -> 128 us (0.985)
  the two profiles are of different devices: /device:TPU:64 before, /device:TPU:128 now
where the time goes in v7:
time: 128 us; the launch traced here: 127 us
  starting transfers between devices  59.4 us (46%)
  waiting for transfers between devices  22.3 us (17%)
  blocking collectives  21.7 us (17%)
  Pallas kernels  17.8 us (14%)
  local copies, waits for them, and re-layouts  5.76 us (4%)
    ppermute x8, starting transfers between devices, neighbours(): below = lax.ppermute(hi, axis, [(i, i + 1) for i in range(count - 1)])  27.8 us
    ppermute x8, starting transfers between devices, neighbours(): above = lax.ppermute(lo, axis, [(i + 1, i) for i in range(count - 1)])  22.7 us
    all_to_all x1, blocking collectives, body(): gathered = lax.all_to_all(payload, 'liq', 0, 0, tiled=True)  21.7 us
    pallas_call x17, Pallas kernels, call(): pl.pallas_call(kernel, out_shape=outs, in_specs=[pl.BlockSpec(memory_spac...  17.8 us
    ppermute x8, waiting for transfers between devices, neighbours(): above = lax.ppermute(lo, axis, [(i + 1, i) for i in range(count - 1)])  12 us
    ppermute x8, waiting for transfers between devices, neighbours(): below = lax.ppermute(hi, axis, [(i, i + 1) for i in range(count - 1)])  10.3 us
    all_to_all x1, starting transfers between devices, body(): coefs = lax.all_to_all(copies, 'liq', 0, 0, tiled=True)  8.96 us
    unnamed x20, local copies, waits for them, and re-layouts  5.76 us
  transfers between devices with their start and end apart: 17, of which 11 were waited for; matrix products, arithmetic and copies ran while one was open for 0% of the time, Pallas kernels for 9%

profile of v7, /device:TPU:128, one launch (start us, length us, event | category | flops | bytes accessed | tf_op | source)
XLA Modules:
  0.0 127.3 jit_solution(17828273496635767708)
XLA Ops:
  0.0 2.6 %shard_map.75 = (f32[576,128]{1,0:T(8,128)}, f32[576,128]{1,0:T(8,128)}, f32[1184,128]{1,0:T(8,128)}, f32[1184,128]{1,0:T(8,128)}, f32[64,128]{1,0:T(8,128)}) custom-call(f32[8,8,512]{2,1,0:T(8,128)} %refs_0_.3, f32[8,8,512]{2,1,0:T(8,128)} %refs_1_.3, f32[8,8,512]{2,1,0:T(8,128)} %refs_2_.3, f32[8,8,512]{2,1,0:T(8,128)} %refs_3_.3, s32[8,8,512]{2,1,0:T(8,128)} %refs_4_.3, ...), custom_call_target="tpu_custom_call" | custom-call | bytes 2621440 | tf_op jit(solution)/shard_map/pallas_call | solution.py:569
  2.6 1.3 %collective-permute-start.3 = (f32[1184,128]{1,0:T(8,128)}, f32[1184,128]{1,0:T(8,128)S(1)}, u32[]{:S(2)}, u32[]{:S(2)}) collective-permute-start(f32[1184,128]{1,0:T(8,128)} %get-tuple-element.44), channel_id=1, source_target_pairs={{16,0},{32,16},{48,32},{64,48},{80,64},{96,80},{112,96},{128,112},... | collective-permute-start | bytes 1818632 | tf_op jit(solution)/shard_map/ppermute | solution.py:583
  3.9 3.8 %collective-permute-start = (f32[576,128]{1,0:T(8,128)}, f32[576,128]{1,0:T(8,128)S(1)}, u32[]{:S(2)}, u32[]{:S(2)}) collective-permute-start(f32[576,128]{1,0:T(8,128)} %get-tuple-element.41), channel_id=1, source_target_pairs={{0,1},{1,2},{2,3},{3,4},{4,5},{5,6},{6,7},{7,8},{8,9},{9,10},{10,1... | collective-permute-start | bytes 884744 | tf_op jit(solution)/shard_map/ppermute | solution.py:582
  7.7 3.2 %collective-permute-start.1 = (f32[576,128]{1,0:T(8,128)}, f32[576,128]{1,0:T(8,128)S(1)}, u32[]{:S(2)}, u32[]{:S(2)}) collective-permute-start(f32[576,128]{1,0:T(8,128)} %get-tuple-element.42), channel_id=1, source_target_pairs={{1,0},{2,1},{3,2},{4,3},{5,4},{6,5},{7,6},{8,7},{9,8},{10,9},{11,1... | collective-permute-start | bytes 884744 | tf_op jit(solution)/shard_map/ppermute | solution.py:583
  11.0 3.3 %collective-permute-start.2 = (f32[1184,128]{1,0:T(8,128)}, f32[1184,128]{1,0:T(8,128)}, u32[]{:S(2)}, u32[]{:S(2)}) collective-permute-start(f32[1184,128]{1,0:T(8,128)} %get-tuple-element.43), channel_id=1, source_target_pairs={{0,16},{16,32},{32,48},{48,64},{64,80},{80,96},{96,112},{112,128},... | collective-permute-start | bytes 1818632 | tf_op jit(solution)/shard_map/ppermute | solution.py:582
  14.3 2.7 %collective-permute-done.below.ill_below = f32[576,128]{1,0:T(8,128)S(1)} collective-permute-done((f32[576,128]{1,0:T(8,128)}, f32[576,128]{1,0:T(8,128)S(1)}, u32[]{:S(2)}, u32[]{:S(2)}) %collective-permute-start) | collective-permute-done | bytes 294944 | tf_op jit(solution)/shard_map/ppermute | solution.py:582
  16.9 2.7 %collective-permute-done.1.above.ill_above = f32[576,128]{1,0:T(8,128)S(1)} collective-permute-done((f32[576,128]{1,0:T(8,128)}, f32[576,128]{1,0:T(8,128)S(1)}, u32[]{:S(2)}, u32[]{:S(2)}) %collective-permute-start.1) | collective-permute-done | bytes 294944 | tf_op jit(solution)/shard_map/ppermute | solution.py:583
  19.7 0.9 shard_map.76
  20.6 2.8 %collective-permute-start.4 = (f32[720,128]{1,0:T(8,128)}, f32[720,128]{1,0:T(8,128)}, u32[]{:S(2)}, u32[]{:S(2)}) collective-permute-start(f32[720,128]{1,0:T(8,128)} %get-tuple-element.45), channel_id=1, source_target_pairs={{0,16},{16,32},{32,48},{48,64},{64,80},{80,96},{96,112},{112,128},... | collective-permute-start | bytes 1105928 | tf_op jit(solution)/shard_map/ppermute | solution.py:582
  23.4 1.3 %collective-permute-start.5 = (f32[720,128]{1,0:T(8,128)}, f32[720,128]{1,0:T(8,128)}, u32[]{:S(2)}, u32[]{:S(2)}) collective-permute-start(f32[720,128]{1,0:T(8,128)} %get-tuple-element.46), channel_id=1, source_target_pairs={{16,0},{32,16},{48,32},{64,48},{80,64},{96,80},{112,96},{128,112},... | collective-permute-start | bytes 1105928 | tf_op jit(solution)/shard_map/ppermute | solution.py:583
  24.6 0.0 collective-permute-done.3.above._
  24.7 0.0 copy-start.9
  24.7 0.7 copy-done.9
  25.4 1.1 shard_map.79
  26.5 9.0 %all-to-all-start = ((f32[32,64,128]{2,1,0:T(8,128)}), f32[32,64,128]{2,1,0:T(8,128)S(1)}, u32[]{:S(2)}, u32[]{:S(2)}) async-start(f32[32,64,128]{2,1,0:T(8,128)} %bitcast), calls=%async_computation | async-start | bytes 2097152 | tf_op jit(solution)/shard_map/all_to_all | solution.py:614
  35.5 0.0 copy-start.5
  35.5 2.4 %shard_map.73.own = f32[1792,128]{1,0:T(8,128)} custom-call(f32[8,8,512]{2,1,0:T(8,128)} %refs_0_.3, f32[8,8,512]{2,1,0:T(8,128)} %refs_1_.3, f32[8,8,512]{2,1,0:T(8,128)} %refs_2_.3, f32[8,8,512]{2,1,0:T(8,128)} %refs_3_.3, s32[8,8,512]{2,1,0:T(8,128)} %refs_4_.3, s32[8,8,512]{2,1,0:T(8,128)} %refs_5_.3), custom_call_target="tpu_custom_call" | custom-call | flops 10000000000 | bytes 1703936 | tf_op jit(solution)/shard_map/pallas_call | solution.py:569
  37.9 0.0 copy-done.5
  37.9 1.2 copy-done.6
  39.1 0.2 shard_map.74
  39.3 0.0 collective-permute-done.2.below
  39.3 0.0 collective-permute-done.4.far_below
  39.3 0.0 collective-permute-done.5.far_above
  39.4 4.2 %shard_map.77 = (f32[384,128]{1,0:T(8,128)S(1)}, f32[128,128]{1,0:T(8,128)S(1)}, f32[160,128]{1,0:T(8,128)}, f32[160,128]{1,0:T(8,128)}) custom-call(f32[1792,128]{1,0:T(8,128)S(1)} %get-tuple-element.40.own, f32[576,128]{1,0:T(8,128)S(1)} %collective-permute-done.below.ill_below, f32[576,128]{1,0:T(8,128)S(1)} %collective-permute-done.1.above.ill_above, ...), custom_call_target="tpu_custom_call" | custom-call | flops 1148190720 | bytes 4935680 | tf_op jit(solution)/shard_map/pallas_call | solution.py:569
  43.5 0.7 copy-done.7
  44.2 3.8 %collective-permute-start.6 = (f32[160,128]{1,0:T(8,128)}, f32[160,128]{1,0:T(8,128)S(1)}, u32[]{:S(2)}, u32[]{:S(2)}) collective-permute-start(f32[160,128]{1,0:T(8,128)} %get-tuple-element.51), channel_id=1, source_target_pairs={{0,1},{1,2},{2,3},{3,4},{4,5},{5,6},{6,7},{7,8},{8,9},{9,10},{10,1... | collective-permute-start | bytes 245768 | tf_op jit(solution)/shard_map/ppermute | solution.py:582
  48.0 3.2 %collective-permute-start.7 = (f32[160,128]{1,0:T(8,128)}, f32[160,128]{1,0:T(8,128)S(1)}, u32[]{:S(2)}, u32[]{:S(2)}) collective-permute-start(f32[160,128]{1,0:T(8,128)} %get-tuple-element.52), channel_id=1, source_target_pairs={{1,0},{2,1},{3,2},{4,3},{5,4},{6,5},{7,6},{8,7},{9,8},{10,9},{11,1... | collective-permute-start | bytes 245768 | tf_op jit(solution)/shard_map/ppermute | solution.py:583
  51.3 1.5 %shard_map.78 = (f32[6,576,128]{2,1,0:T(8,128)S(1)}, f32[5,256,128]{2,1,0:T(8,128)S(1)}) custom-call(f32[1792,128]{1,0:T(8,128)S(1)} %get-tuple-element.40.own, f32[576,128]{1,0:T(8,128)S(1)} %collective-permute-done.below.ill_below, f32[576,128]{1,0:T(8,128)S(1)} %collective-permute-done.1.above.ill_above, f32[1184,128]{1,0:T(8,128)} %collective-permute-done.2.below, ...), custom_call_target="tpu_custom_call" | custom-call | bytes 5885952 | tf_op jit(solution)/shard_map/pallas_call | solution.py:569
  52.7 0.0 copy-start
  52.8 0.8 copy-done
  53.6 1.2 copy-done.3
  54.8 0.0 all-to-all-done
  54.8 0.3 shard_map.80
  55.1 0.0 collective-permute-done.6.below
  55.2 0.7 collective-permute-done.7.above
  55.9 1.1 copy-done.1
  56.9 0.6 shard_map.81
  57.6 21.7 %all_to_all.22 = f32[32,48,128]{2,1,0:T(8,128)S(1)} all-to-all(f32[32,48,128]{2,1,0:T(8,128)S(1)} %bitcast.7), channel_id=1, replica_groups=mesh['liq'=32,'ill'=16] {'liq'}, dimensions={0} | all-to-all | bytes 1572864 | tf_op jit(solution)/shard_map/all_to_all | solution.py:635
  79.3 0.1 shard_map.82
  79.5 4.9 %collective-permute-start.8 = (f32[256,128]{1,0:T(8,128)S(1)}, f32[256,128]{1,0:T(8,128)S(1)}, u32[]{:S(2)}, u32[]{:S(2)}) collective-permute-start(f32[256,128]{1,0:T(8,128)S(1)} %get-tuple-element.62), channel_id=1, source_target_pairs={{0,1},{1,2},{2,3},{3,4},{4,5},{5,6},{6,7},{7,8},{8,9},{9,10},{10,1... | collective-permute-start | bytes 393224 | tf_op jit(solution)/shard_map/ppermute | solution.py:582
  84.3 2.2 %collective-permute-start.9 = (f32[256,128]{1,0:T(8,128)S(1)}, f32[256,128]{1,0:T(8,128)S(1)}, u32[]{:S(2)}, u32[]{:S(2)}) collective-permute-start(f32[256,128]{1,0:T(8,128)S(1)} %get-tuple-element.63), channel_id=1, source_target_pairs={{1,0},{2,1},{3,2},{4,3},{5,4},{6,5},{7,6},{8,7},{9,8},{10,9},{11,1... | collective-permute-start | bytes 393224 | tf_op jit(solution)/shard_map/ppermute | solution.py:583
  86.5 0.0 copy-done.8
  86.6 0.4 shard_map.83
  87.0 1.0 collective-permute-done.8.below
  87.9 3.6 %collective-permute-done.9.above = f32[256,128]{1,0:T(8,128)S(1)} collective-permute-done((f32[256,128]{1,0:T(8,128)S(1)}, f32[256,128]{1,0:T(8,128)S(1)}, u32[]{:S(2)}, u32[]{:S(2)}) %collective-permute-start.9) | collective-permute-done | bytes 131104 | tf_op jit(solution)/shard_map/ppermute | solution.py:583
  91.5 0.1 shard_map.84
  91.7 3.6 %collective-permute-start.10 = (f32[256,128]{1,0:T(8,128)S(1)}, f32[256,128]{1,0:T(8,128)S(1)}, u32[]{:S(2)}, u32[]{:S(2)}) collective-permute-start(f32[256,128]{1,0:T(8,128)S(1)} %get-tuple-element.66), channel_id=1, source_target_pairs={{0,1},{1,2},{2,3},{3,4},{4,5},{5,6},{6,7},{7,8},{8,9},{9,10},{10,1... | collective-permute-start | bytes 393224 | tf_op jit(solution)/shard_map/ppermute | solution.py:582
  95.3 3.4 %collective-permute-start.11 = (f32[256,128]{1,0:T(8,128)S(1)}, f32[256,128]{1,0:T(8,128)S(1)}, u32[]{:S(2)}, u32[]{:S(2)}) collective-permute-start(f32[256,128]{1,0:T(8,128)S(1)} %get-tuple-element.67), channel_id=1, source_target_pairs={{1,0},{2,1},{3,2},{4,3},{5,4},{6,5},{7,6},{8,7},{9,8},{10,9},{11,1... | collective-permute-start | bytes 393224 | tf_op jit(solution)/shard_map/ppermute | solution.py:583
  98.7 0.4 shard_map.85.t
  99.1 0.6 collective-permute-done.10.below
  99.7 2.4 %collective-permute-done.11.above = f32[256,128]{1,0:T(8,128)S(1)} collective-permute-done((f32[256,128]{1,0:T(8,128)S(1)}, f32[256,128]{1,0:T(8,128)S(1)}, u32[]{:S(2)}, u32[]{:S(2)}) %collective-permute-start.11) | collective-permute-done | bytes 131104 | tf_op jit(solution)/shard_map/ppermute | solution.py:583
  102.2 0.2 shard_map.86
  102.4 3.6 %collective-permute-start.12 = (f32[256,128]{1,0:T(8,128)S(1)}, f32[256,128]{1,0:T(8,128)S(1)}, u32[]{:S(2)}, u32[]{:S(2)}) collective-permute-start(f32[256,128]{1,0:T(8,128)S(1)} %get-tuple-element.69), channel_id=1, source_target_pairs={{0,1},{1,2},{2,3},{3,4},{4,5},{5,6},{6,7},{7,8},{8,9},{9,10},{10,1... | collective-permute-start | bytes 393224 | tf_op jit(solution)/shard_map/ppermute | solution.py:582
  106.0 3.4 %collective-permute-start.13 = (f32[256,128]{1,0:T(8,128)S(1)}, f32[256,128]{1,0:T(8,128)S(1)}, u32[]{:S(2)}, u32[]{:S(2)}) collective-permute-start(f32[256,128]{1,0:T(8,128)S(1)} %get-tuple-element.70), channel_id=1, source_target_pairs={{1,0},{2,1},{3,2},{4,3},{5,4},{6,5},{7,6},{8,7},{9,8},{10,9},{11,1... | collective-permute-start | bytes 393224 | tf_op jit(solution)/shard_map/ppermute | solution.py:583
  109.4 0.4 shard_map.87.t
  109.9 0.6 collective-permute-done.12.below
  110.4 2.4 %collective-permute-done.13.above = f32[256,128]{1,0:T(8,128)S(1)} collective-permute-done((f32[256,128]{1,0:T(8,128)S(1)}, f32[256,128]{1,0:T(8,128)S(1)}, u32[]{:S(2)}, u32[]{:S(2)}) %collective-permute-start.13) | collective-permute-done | bytes 131104 | tf_op jit(solution)/shard_map/ppermute | solution.py:583
  112.9 0.2 shard_map.88.own
  113.0 4.6 %collective-permute-start.15 = (f32[160,128]{1,0:T(8,128)S(1)}, f32[160,128]{1,0:T(8,128)S(1)}, u32[]{:S(2)}, u32[]{:S(2)}) collective-permute-start(f32[160,128]{1,0:T(8,128)S(1)} %shard_map.88.own), channel_id=1, source_target_pairs={{1,0},{2,1},{3,2},{4,3},{5,4},{6,5},{7,6},{8,7},{9,8},{10,9},{11,1... | collective-permute-start | bytes 245768 | tf_op jit(solution)/shard_map/ppermute | solution.py:583
  117.7 1.9 %collective-permute-start.14 = (f32[160,128]{1,0:T(8,128)S(1)}, f32[160,128]{1,0:T(8,128)S(1)}, u32[]{:S(2)}, u32[]{:S(2)}) collective-permute-start(f32[160,128]{1,0:T(8,128)S(1)} %shard_map.88.own), channel_id=1, source_target_pairs={{0,1},{1,2},{2,3},{3,4},{4,5},{5,6},{6,7},{7,8},{8,9},{9,10},{10,1... | collective-permute-start | bytes 245768 | tf_op jit(solution)/shard_map/ppermute | solution.py:582
  119.6 0.1 collective-permute-done.15.above
  119.7 5.5 %collective-permute-done.14.below = f32[160,128]{1,0:T(8,128)S(1)} collective-permute-done((f32[160,128]{1,0:T(8,128)S(1)}, f32[160,128]{1,0:T(8,128)S(1)}, u32[]{:S(2)}, u32[]{:S(2)}) %collective-permute-start.14) | collective-permute-done | bytes 81952 | tf_op jit(solution)/shard_map/ppermute | solution.py:582
  125.2 0.0 copy-done.4
  125.2 2.1 %shard_map.89 = f32[8,8,512]{2,1,0:T(8,128)} custom-call(f32[160,128]{1,0:T(8,128)S(1)} %shard_map.88.own, f32[160,128]{1,0:T(8,128)S(1)} %collective-permute-done.14.below, f32[160,128]{1,0:T(8,128)S(1)} %collective-permute-done.15.above, f32[5,256,128]{2,1,0:T(8,128)S(1)} %copy-done.2, f32[256,128]{1,0:T(8,128)S(1)} %get-tuple-element.72.rhs_mid, ...), custom_call_target="tpu_custom_call" | custom-call | flops 519045120 | bytes 4276224 | tf_op jit(solution)/shard_map/pallas_call | solution.py:569
  (8 shorter events, 0.0 us)
Async XLA Ops:
  2.6 22.0 %collective-permute-start.3 = (f32[1184,128]{1,0:T(8,128)}, f32[1184,128]{1,0:T(8,128)S(1)}, u32[]{:S(2)}, u32[]{:S(2)}) collective-permute-start(f32[1184,128]{1,0:T(8,128)} %get-tuple-element.44), channel_id=1, source_target_pairs={{16,0},{32,16},{48,32},{64,48},{80,64},{96,80},{112,96},{128,112},... | collective-permute-start | bytes 1818632 | tf_op jit(solution)/shard_map/ppermute | solution.py:583
  3.9 13.0 %collective-permute-start = (f32[576,128]{1,0:T(8,128)}, f32[576,128]{1,0:T(8,128)S(1)}, u32[]{:S(2)}, u32[]{:S(2)}) collective-permute-start(f32[576,128]{1,0:T(8,128)} %get-tuple-element.41), channel_id=1, source_target_pairs={{0,1},{1,2},{2,3},{3,4},{4,5},{5,6},{6,7},{7,8},{8,9},{9,10},{10,1... | collective-permute-start | bytes 884744 | tf_op jit(solution)/shard_map/ppermute | solution.py:582
  7.7 11.9 %collective-permute-start.1 = (f32[576,128]{1,0:T(8,128)}, f32[576,128]{1,0:T(8,128)S(1)}, u32[]{:S(2)}, u32[]{:S(2)}) collective-permute-start(f32[576,128]{1,0:T(8,128)} %get-tuple-element.42), channel_id=1, source_target_pairs={{1,0},{2,1},{3,2},{4,3},{5,4},{6,5},{7,6},{8,7},{9,8},{10,9},{11,1... | collective-permute-start | bytes 884744 | tf_op jit(solution)/shard_map/ppermute | solution.py:583
  11.0 28.4 %collective-permute-start.2 = (f32[1184,128]{1,0:T(8,128)}, f32[1184,128]{1,0:T(8,128)}, u32[]{:S(2)}, u32[]{:S(2)}) collective-permute-start(f32[1184,128]{1,0:T(8,128)} %get-tuple-element.43), channel_id=1, source_target_pairs={{0,16},{16,32},{32,48},{48,64},{64,80},{80,96},{96,112},{112,128},... | collective-permute-start | bytes 1818632 | tf_op jit(solution)/shard_map/ppermute | solution.py:582
  20.6 18.7 %collective-permute-start.4 = (f32[720,128]{1,0:T(8,128)}, f32[720,128]{1,0:T(8,128)}, u32[]{:S(2)}, u32[]{:S(2)}) collective-permute-start(f32[720,128]{1,0:T(8,128)} %get-tuple-element.45), channel_id=1, source_target_pairs={{0,16},{16,32},{32,48},{48,64},{64,80},{80,96},{96,112},{112,128},... | collective-permute-start | bytes 1105928 | tf_op jit(solution)/shard_map/ppermute | solution.py:582
  23.4 16.0 %collective-permute-start.5 = (f32[720,128]{1,0:T(8,128)}, f32[720,128]{1,0:T(8,128)}, u32[]{:S(2)}, u32[]{:S(2)}) collective-permute-start(f32[720,128]{1,0:T(8,128)} %get-tuple-element.46), channel_id=1, source_target_pairs={{16,0},{32,16},{48,32},{64,48},{80,64},{96,80},{112,96},{128,112},... | collective-permute-start | bytes 1105928 | tf_op jit(solution)/shard_map/ppermute | solution.py:583
  24.7 0.8 copy-start.9
  26.5 28.3 %all-to-all-start = ((f32[32,64,128]{2,1,0:T(8,128)}), f32[32,64,128]{2,1,0:T(8,128)S(1)}, u32[]{:S(2)}, u32[]{:S(2)}) async-start(f32[32,64,128]{2,1,0:T(8,128)} %bitcast), calls=%async_computation | async-start | bytes 2097152 | tf_op jit(solution)/shard_map/all_to_all | solution.py:614
  35.5 2.4 %copy-start.5 = (f32[512,512]{1,0:T(8,128)S(1)}, f32[512,512]{1,0:T(8,128)}, u32[]{:S(2)}) copy-start(f32[512,512]{1,0:T(8,128)} %j_ref.1) | copy-start | bytes 3145732
  37.9 1.2 copy-start.6
  43.5 0.7 copy-start.7
  44.2 10.9 %collective-permute-start.6 = (f32[160,128]{1,0:T(8,128)}, f32[160,128]{1,0:T(8,128)S(1)}, u32[]{:S(2)}, u32[]{:S(2)}) collective-permute-start(f32[160,128]{1,0:T(8,128)} %get-tuple-element.51), channel_id=1, source_target_pairs={{0,1},{1,2},{2,3},{3,4},{4,5},{5,6},{6,7},{7,8},{8,9},{9,10},{10,1... | collective-permute-start | bytes 245768 | tf_op jit(solution)/shard_map/ppermute | solution.py:582
  48.0 7.8 %collective-permute-start.7 = (f32[160,128]{1,0:T(8,128)}, f32[160,128]{1,0:T(8,128)S(1)}, u32[]{:S(2)}, u32[]{:S(2)}) collective-permute-start(f32[160,128]{1,0:T(8,128)} %get-tuple-element.52), channel_id=1, source_target_pairs={{1,0},{2,1},{3,2},{4,3},{5,4},{6,5},{7,6},{8,7},{9,8},{10,9},{11,1... | collective-permute-start | bytes 245768 | tf_op jit(solution)/shard_map/ppermute | solution.py:583
  52.7 0.8 copy-start
  53.6 1.2 copy-start.3
  55.9 1.1 copy-start.1
  57.6 29.0 %copy-start.8 = (f32[384,128]{1,0:T(8,128)S(1)}, f32[384,128]{1,0:T(8,128)}, u32[]{:S(2)}) copy-start(f32[384,128]{1,0:T(8,128)} %copy-done.7) | copy-start | bytes 589828
  79.5 8.4 %collective-permute-start.8 = (f32[256,128]{1,0:T(8,128)S(1)}, f32[256,128]{1,0:T(8,128)S(1)}, u32[]{:S(2)}, u32[]{:S(2)}) collective-permute-start(f32[256,128]{1,0:T(8,128)S(1)} %get-tuple-element.62), channel_id=1, source_target_pairs={{0,1},{1,2},{2,3},{3,4},{4,5},{5,6},{6,7},{7,8},{8,9},{9,10},{10,1... | collective-permute-start | bytes 393224 | tf_op jit(solution)/shard_map/ppermute | solution.py:582
  84.3 7.2 %collective-permute-start.9 = (f32[256,128]{1,0:T(8,128)S(1)}, f32[256,128]{1,0:T(8,128)S(1)}, u32[]{:S(2)}, u32[]{:S(2)}) collective-permute-start(f32[256,128]{1,0:T(8,128)S(1)} %get-tuple-element.63), channel_id=1, source_target_pairs={{1,0},{2,1},{3,2},{4,3},{5,4},{6,5},{7,6},{8,7},{9,8},{10,9},{11,1... | collective-permute-start | bytes 393224 | tf_op jit(solution)/shard_map/ppermute | solution.py:583
  91.7 8.1 %collective-permute-start.10 = (f32[256,128]{1,0:T(8,128)S(1)}, f32[256,128]{1,0:T(8,128)S(1)}, u32[]{:S(2)}, u32[]{:S(2)}) collective-permute-start(f32[256,128]{1,0:T(8,128)S(1)} %get-tuple-element.66), channel_id=1, source_target_pairs={{0,1},{1,2},{2,3},{3,4},{4,5},{5,6},{6,7},{7,8},{8,9},{9,10},{10,1... | collective-permute-start | bytes 393224 | tf_op jit(solution)/shard_map/ppermute | solution.py:582
  95.3 6.9 %collective-permute-start.11 = (f32[256,128]{1,0:T(8,128)S(1)}, f32[256,128]{1,0:T(8,128)S(1)}, u32[]{:S(2)}, u32[]{:S(2)}) collective-permute-start(f32[256,128]{1,0:T(8,128)S(1)} %get-tuple-element.67), channel_id=1, source_target_pairs={{1,0},{2,1},{3,2},{4,3},{5,4},{6,5},{7,6},{8,7},{9,8},{10,9},{11,1... | collective-permute-start | bytes 393224 | tf_op jit(solution)/shard_map/ppermute | solution.py:583
  102.4 8.1 %collective-permute-start.12 = (f32[256,128]{1,0:T(8,128)S(1)}, f32[256,128]{1,0:T(8,128)S(1)}, u32[]{:S(2)}, u32[]{:S(2)}) collective-permute-start(f32[256,128]{1,0:T(8,128)S(1)} %get-tuple-element.69), channel_id=1, source_target_pairs={{0,1},{1,2},{2,3},{3,4},{4,5},{5,6},{6,7},{7,8},{8,9},{9,10},{10,1... | collective-permute-start | bytes 393224 | tf_op jit(solution)/shard_map/ppermute | solution.py:582
  106.0 6.9 %collective-permute-start.13 = (f32[256,128]{1,0:T(8,128)S(1)}, f32[256,128]{1,0:T(8,128)S(1)}, u32[]{:S(2)}, u32[]{:S(2)}) collective-permute-start(f32[256,128]{1,0:T(8,128)S(1)} %get-tuple-element.70), channel_id=1, source_target_pairs={{1,0},{2,1},{3,2},{4,3},{5,4},{6,5},{7,6},{8,7},{9,8},{10,9},{11,1... | collective-permute-start | bytes 393224 | tf_op jit(solution)/shard_map/ppermute | solution.py:583
  109.4 15.8 %copy-start.4 = (f32[6,576,128]{2,1,0:T(8,128)S(1)}, f32[6,576,128]{2,1,0:T(8,128)}, u32[]{:S(2)}) copy-start(f32[6,576,128]{2,1,0:T(8,128)} %copy-done.3) | copy-start | bytes 5308420
  109.8 15.4 %copy-start.2 = (f32[5,256,128]{2,1,0:T(8,128)S(1)}, f32[5,256,128]{2,1,0:T(8,128)}, u32[]{:S(2)}) copy-start(f32[5,256,128]{2,1,0:T(8,128)} %copy-done) | copy-start | bytes 1966084
  113.0 6.7 %collective-permute-start.15 = (f32[160,128]{1,0:T(8,128)S(1)}, f32[160,128]{1,0:T(8,128)S(1)}, u32[]{:S(2)}, u32[]{:S(2)}) collective-permute-start(f32[160,128]{1,0:T(8,128)S(1)} %shard_map.88.own), channel_id=1, source_target_pairs={{1,0},{2,1},{3,2},{4,3},{5,4},{6,5},{7,6},{8,7},{9,8},{10,9},{11,1... | collective-permute-start | bytes 245768 | tf_op jit(solution)/shard_map/ppermute | solution.py:583
  117.7 7.5 %collective-permute-start.14 = (f32[160,128]{1,0:T(8,128)S(1)}, f32[160,128]{1,0:T(8,128)S(1)}, u32[]{:S(2)}, u32[]{:S(2)}) collective-permute-start(f32[160,128]{1,0:T(8,128)S(1)} %shard_map.88.own), channel_id=1, source_target_pairs={{0,1},{1,2},{2,3},{3,4},{4,5},{5,6},{6,7},{7,8},{8,9},{9,10},{10,1... | collective-permute-start | bytes 245768 | tf_op jit(solution)/shard_map/ppermute | solution.py:582

commit v8 on v5

--- a/solution.py
+++ b/solution.py
@@ -329,7 +329,7 @@
         wide_ref[pl.ds(48 * a + 40, 8), :] = ends[1]
 
 
-def mid_kernel(own, below, above, mid, jhi, jlo, out, pay_ref, err_ref, rhs_ref, e0, e1, inc):
+def mid_kernel(own, below, above, mid, jhi, jlo, out, coefs, pay_ref, err_ref, rhs_ref, e0, e1, inc):
     widen_rhs(own, below, above, rhs_ref)
     e0[...] = mid[4] * rhs_ref[...]
 
@@ -359,11 +359,12 @@
             diag = diag + mid[k, here, :]
         return (total - diag * center)[8:24]
 
-    for m in range(2):
-        pay_ref[pl.ds(8 * m, 8), :] = 0.25 * pair_sums(residual(2 + 2 * m) + residual(3 + 2 * m))
+    low = [0.25 * pair_sums(residual(2 + 2 * m) + residual(3 + 2 * m)) for m in range(2)]
     for a in range(6):
         err_ref[pl.ds(16 * a, 16), :] = e1[pl.ds(32 * (a + 1) + 8, 16), :]
-    pay_ref[16:48, :] = err_ref[32:64, :]
+    piece = jnp.concatenate(low + [err_ref[32:64, :], coefs[...]], axis=0)
+    for i in range(pay_ref.shape[0] // 112):
+        pay_ref[pl.ds(112 * i, 112), :] = piece
 
 
 def solve_lines(target, weight, carry, link, middle, y, x_ref, offset):
@@ -402,7 +403,7 @@
     count = fac_ref.shape[1] // TILE
 
     def part(k, a):
-        return gathered[pl.ds(64 * (a // 2) + 16 * k + 8 * (a % 2), TILE), :]
+        return gathered[pl.ds(112 * (a // 2) + 48 + 16 * k + 8 * (a % 2), TILE), :]
 
     outflow = DISCOUNT + out[...]
     gaps = [None, None]
@@ -427,7 +428,7 @@
 
 def first_solve_kernel(gathered, fac, middle, e_ref, lo_ref, hi_ref, y):
     solve_lines(
-        lambda a: gathered[pl.ds(48 * (a // 2) + 8 * (a % 2), TILE), :],
+        lambda a: gathered[pl.ds(112 * (a // 2) + 8 * (a % 2), TILE), :],
         lambda a: row(fac.at[2], a, TILE),
         lambda a: row(fac.at[3], a, TILE),
         lambda a: row(fac.at[4], a, TILE),
@@ -449,7 +450,7 @@
 ):
     blocks = e.shape[0] // (2 * TILE)
     for i in range(blocks):
-        rhs_ref[pl.ds(16 * i, 16), :] = gathered[pl.ds(48 * i, 16), :]
+        rhs_ref[pl.ds(16 * i, 16), :] = gathered[pl.ds(112 * i, 16), :]
     local_target(e, rhs_ref, fac, jhi, jlo, t_ref)
     widen_rhs(rhs_mid, below, above, rhs_wide_ref)
     widen_value(val, below, above, val_wide_ref)
@@ -457,7 +458,7 @@
     wide_ref[32:128, :] = err[...]
     for at, block, inside in ((0, here - 1, here > 0), (128, here + 1, here < blocks - 1)):
         block = jnp.minimum(jnp.maximum(block, 0), blocks - 1)
-        start = pl.multiple_of(block * 48 + 16, 16)
+        start = pl.multiple_of(block * 112 + 16, 16)
         piece = gathered[pl.ds(start, 32), :]
         wide_ref[pl.ds(at, 32), :] = jnp.where(inside, piece, jnp.zeros_like(piece))
 
@@ -593,7 +594,6 @@
     )
     ill_below, ill_above = neighbours(lo, hi, "ill")
     below, above = neighbours(down, up, "liq")
-    coefs = lax.all_gather(low, "liq", axis=0, tiled=True)
     rates = jax.ShapeDtypeStruct((nz, nz), BF16)
     (own,) = call(
         own_kernel, inputs, [(1792, LANES)], buffers + [sems], places=[pltpu.HBM] * 6, limit=57
@@ -615,15 +615,15 @@
     fine, mid = call(keep_kernel, (*pieces, out), [(6, 576, LANES), (5, 256, LANES)])
     payload, err = call(
         mid_kernel,
-        (rhs_mid, mid_below, mid_above, mid, jhi, jlo, out),
-        [(48, LANES), (96, LANES)],
+        (rhs_mid, mid_below, mid_above, mid, jhi, jlo, out, low),
+        [(112 * lax.axis_size("liq"), LANES), (96, LANES)],
         [(256, LANES)] * 4,
         flops=dot_flops * 80,
     )
-    gathered = lax.all_gather(payload, "liq", axis=0, tiled=True)
-    lines = gathered.shape[0] // 48 * 2 * TILE
+    gathered = lax.all_to_all(payload, "liq", 0, 0, tiled=True)
+    lines = gathered.shape[0] // 112 * 2 * TILE
     line, message = (lines, LANES), (lines // 2, LANES)
-    fac, middle = call(factor_kernel, (coefs, out), [(5, *line), (TILE, LANES)])
+    fac, middle = call(factor_kernel, (gathered, out), [(5, *line), (TILE, LANES)])
     e, lo, hi = call(
         first_solve_kernel, (gathered, fac, middle), [line, message, message], [line]
     )

time: 135 us -> 126 us (0.933)
  the two profiles are of different devices: /device:TPU:64 before, /device:TPU:128 now
where the time goes in v8:
time: 126 us; the launch traced here: 125 us
  starting transfers between devices  47 us (37%)
  blocking collectives  38.7 us (31%)
  waiting for transfers between devices  25.7 us (20%)
  Pallas kernels  12.6 us (10%)
    all_to_all x1, blocking collectives, body(): gathered = lax.all_to_all(payload, 'liq', 0, 0, tiled=True)  38.7 us
    ppermute x8, starting transfers between devices, neighbours(): below = lax.ppermute(hi, axis, [(i, i + 1) for i in range(count - 1)])  24.9 us
    ppermute x8, starting transfers between devices, neighbours(): above = lax.ppermute(lo, axis, [(i + 1, i) for i in range(count - 1)])  22.1 us
    ppermute x8, waiting for transfers between devices, neighbours(): above = lax.ppermute(lo, axis, [(i + 1, i) for i in range(count - 1)])  15.4 us
    pallas_call x16, Pallas kernels, call(): pl.pallas_call(kernel, out_shape=outs, in_specs=[pl.BlockSpec(memory_spac...  12.6 us
    ppermute x8, waiting for transfers between devices, neighbours(): below = lax.ppermute(hi, axis, [(i, i + 1) for i in range(count - 1)])  10.3 us
  transfers between devices with their start and end apart: 16, of which 13 were waited for; matrix products, arithmetic and copies ran while one was open for 0% of the time, Pallas kernels for 3%

profile of v8, /device:TPU:128, one launch (start us, length us, event | category | flops | bytes accessed | tf_op | source)
XLA Modules:
  0.0 125.4 jit_solution(16772770994857261895)
XLA Ops:
  0.0 0.0 copy-start.1
  0.0 2.7 %shard_map.75 = (f32[576,128]{1,0:T(8,128)}, f32[576,128]{1,0:T(8,128)}, f32[1184,128]{1,0:T(8,128)}, f32[1184,128]{1,0:T(8,128)}, f32[64,128]{1,0:T(8,128)}) custom-call(f32[8,8,512]{2,1,0:T(8,128)} %refs_0_.3, f32[8,8,512]{2,1,0:T(8,128)} %refs_1_.3, f32[8,8,512]{2,1,0:T(8,128)} %refs_2_.3, f32[8,8,512]{2,1,0:T(8,128)} %refs_3_.3, s32[8,8,512]{2,1,0:T(8,128)} %refs_4_.3, ...), custom_call_target="tpu_custom_call" | custom-call | bytes 2621440 | tf_op jit(solution)/shard_map/pallas_call | solution.py:563
  2.7 3.8 %collective-permute-start = (f32[576,128]{1,0:T(8,128)}, f32[576,128]{1,0:T(8,128)S(1)}, u32[]{:S(2)}, u32[]{:S(2)}) collective-permute-start(f32[576,128]{1,0:T(8,128)} %get-tuple-element.41), channel_id=1, source_target_pairs={{0,1},{1,2},{2,3},{3,4},{4,5},{5,6},{6,7},{7,8},{8,9},{9,10},{10,1... | collective-permute-start | bytes 884744 | tf_op jit(solution)/shard_map/ppermute | solution.py:576
  6.5 3.2 %collective-permute-start.1 = (f32[576,128]{1,0:T(8,128)}, f32[576,128]{1,0:T(8,128)S(1)}, u32[]{:S(2)}, u32[]{:S(2)}) collective-permute-start(f32[576,128]{1,0:T(8,128)} %get-tuple-element.42), channel_id=1, source_target_pairs={{1,0},{2,1},{3,2},{4,3},{5,4},{6,5},{7,6},{8,7},{9,8},{10,9},{11,1... | collective-permute-start | bytes 884744 | tf_op jit(solution)/shard_map/ppermute | solution.py:577
  9.7 1.3 %collective-permute-start.2 = (f32[1184,128]{1,0:T(8,128)}, f32[1184,128]{1,0:T(8,128)S(1)}, u32[]{:S(2)}, u32[]{:S(2)}) collective-permute-start(f32[1184,128]{1,0:T(8,128)} %get-tuple-element.43), channel_id=1, source_target_pairs={{0,16},{16,32},{32,48},{48,64},{64,80},{80,96},{96,112},{112,128},... | collective-permute-start | bytes 1818632 | tf_op jit(solution)/shard_map/ppermute | solution.py:576
  11.1 1.3 %collective-permute-start.3 = (f32[1184,128]{1,0:T(8,128)}, f32[1184,128]{1,0:T(8,128)S(1)}, u32[]{:S(2)}, u32[]{:S(2)}) collective-permute-start(f32[1184,128]{1,0:T(8,128)} %get-tuple-element.44), channel_id=1, source_target_pairs={{16,0},{32,16},{48,32},{64,48},{80,64},{96,80},{112,96},{128,112},... | collective-permute-start | bytes 1818632 | tf_op jit(solution)/shard_map/ppermute | solution.py:577
  12.4 2.4 %collective-permute-done.below.ill_below = f32[576,128]{1,0:T(8,128)S(1)} collective-permute-done((f32[576,128]{1,0:T(8,128)}, f32[576,128]{1,0:T(8,128)S(1)}, u32[]{:S(2)}, u32[]{:S(2)}) %collective-permute-start) | collective-permute-done | bytes 294944 | tf_op jit(solution)/shard_map/ppermute | solution.py:576
  14.7 2.5 %collective-permute-done.1.above.ill_above = f32[576,128]{1,0:T(8,128)S(1)} collective-permute-done((f32[576,128]{1,0:T(8,128)}, f32[576,128]{1,0:T(8,128)S(1)}, u32[]{:S(2)}, u32[]{:S(2)}) %collective-permute-start.1) | collective-permute-done | bytes 294944 | tf_op jit(solution)/shard_map/ppermute | solution.py:577
  17.3 1.3 %collective-permute-start.4 = (f32[720,128]{1,0:T(8,128)S(1)}, f32[720,128]{1,0:T(8,128)S(1)}, u32[]{:S(2)}, u32[]{:S(2)}) collective-permute-start(f32[720,128]{1,0:T(8,128)S(1)} %get-tuple-element.45), channel_id=1, source_target_pairs={{0,16},{16,32},{32,48},{48,64},{64,80},{80,96},{96,112},{112,128},... | collective-permute-start | bytes 1105928 | tf_op jit(solution)/shard_map/ppermute | solution.py:576
  18.6 1.3 %collective-permute-start.5 = (f32[720,128]{1,0:T(8,128)S(1)}, f32[720,128]{1,0:T(8,128)S(1)}, u32[]{:S(2)}, u32[]{:S(2)}) collective-permute-start(f32[720,128]{1,0:T(8,128)S(1)} %get-tuple-element.46), channel_id=1, source_target_pairs={{16,0},{32,16},{48,32},{64,48},{80,64},{96,80},{112,96},{128,112},... | collective-permute-start | bytes 1105928 | tf_op jit(solution)/shard_map/ppermute | solution.py:577
  19.9 2.3 %shard_map.73.own = f32[1792,128]{1,0:T(8,128)} custom-call(f32[8,8,512]{2,1,0:T(8,128)} %refs_0_.3, f32[8,8,512]{2,1,0:T(8,128)} %refs_1_.3, f32[8,8,512]{2,1,0:T(8,128)} %refs_2_.3, f32[8,8,512]{2,1,0:T(8,128)} %refs_3_.3, s32[8,8,512]{2,1,0:T(8,128)} %refs_4_.3, s32[8,8,512]{2,1,0:T(8,128)} %refs_5_.3), custom_call_target="tpu_custom_call" | custom-call | bytes 1703936 | tf_op jit(solution)/shard_map/pallas_call | solution.py:563
  22.2 0.0 copy-done.1
  22.2 0.0 copy-start
  22.2 1.2 copy-done
  23.4 0.2 shard_map.74
  23.7 0.0 collective-permute-done.2.below
  23.7 0.0 collective-permute-done.3.above
  23.7 0.0 collective-permute-done.4.far_below
  23.7 0.2 collective-permute-done.5.far_above
  23.9 2.2 %shard_map.77 = (f32[384,128]{1,0:T(8,128)S(1)}, f32[128,128]{1,0:T(8,128)S(1)}, f32[160,128]{1,0:T(8,128)S(1)}, f32[160,128]{1,0:T(8,128)S(1)}) custom-call(f32[1792,128]{1,0:T(8,128)S(1)} %get-tuple-element.40.own, f32[576,128]{1,0:T(8,128)S(1)} %collective-permute-done.below.ill_below, f32[576,128]{1,0:T(8,128)S(1)} %collective-permute-done.1.above.ill_above, ...), custom_call_target="tpu_custom_call" | custom-call | flops 1148190720 | bytes 4935680 | tf_op jit(solution)/shard_map/pallas_call | solution.py:563
  26.2 0.0 copy-start.2
  26.2 3.8 %collective-permute-start.6 = (f32[160,128]{1,0:T(8,128)S(1)}, f32[160,128]{1,0:T(8,128)S(1)}, u32[]{:S(2)}, u32[]{:S(2)}) collective-permute-start(f32[160,128]{1,0:T(8,128)S(1)} %get-tuple-element.51), channel_id=1, source_target_pairs={{0,1},{1,2},{2,3},{3,4},{4,5},{5,6},{6,7},{7,8},{8,9},{9,10},{10,1... | collective-permute-start | bytes 245768 | tf_op jit(solution)/shard_map/ppermute | solution.py:576
  30.0 3.2 %collective-permute-start.7 = (f32[160,128]{1,0:T(8,128)S(1)}, f32[160,128]{1,0:T(8,128)S(1)}, u32[]{:S(2)}, u32[]{:S(2)}) collective-permute-start(f32[160,128]{1,0:T(8,128)S(1)} %get-tuple-element.52), channel_id=1, source_target_pairs={{1,0},{2,1},{3,2},{4,3},{5,4},{6,5},{7,6},{8,7},{9,8},{10,9},{11,1... | collective-permute-start | bytes 245768 | tf_op jit(solution)/shard_map/ppermute | solution.py:577
  33.2 0.2 shard_map.78
  33.5 0.3 collective-permute-done.6.below
  33.7 3.7 %collective-permute-done.7.above = f32[160,128]{1,0:T(8,128)S(1)} collective-permute-done((f32[160,128]{1,0:T(8,128)S(1)}, f32[160,128]{1,0:T(8,128)S(1)}, u32[]{:S(2)}, u32[]{:S(2)}) %collective-permute-start.7) | collective-permute-done | bytes 81952 | tf_op jit(solution)/shard_map/ppermute | solution.py:577
  37.4 0.0 copy-done.2
  37.5 0.6 shard_map.79
  38.1 38.7 %all_to_all.11 = f32[32,112,128]{2,1,0:T(8,128)S(1)} all-to-all(f32[32,112,128]{2,1,0:T(8,128)S(1)} %bitcast.5), channel_id=1, replica_groups=mesh['liq'=32,'ill'=16] {'liq'}, dimensions={0} | all-to-all | bytes 3670016 | tf_op jit(solution)/shard_map/all_to_all | solution.py:623
  76.8 0.3 shard_map.80
  77.1 0.1 shard_map.81
  77.2 4.8 %collective-permute-start.8 = (f32[256,128]{1,0:T(8,128)S(1)}, f32[256,128]{1,0:T(8,128)S(1)}, u32[]{:S(2)}, u32[]{:S(2)}) collective-permute-start(f32[256,128]{1,0:T(8,128)S(1)} %get-tuple-element.62), channel_id=1, source_target_pairs={{0,1},{1,2},{2,3},{3,4},{4,5},{5,6},{6,7},{7,8},{8,9},{9,10},{10,1... | collective-permute-start | bytes 393224 | tf_op jit(solution)/shard_map/ppermute | solution.py:576
  82.1 2.2 %collective-permute-start.9 = (f32[256,128]{1,0:T(8,128)S(1)}, f32[256,128]{1,0:T(8,128)S(1)}, u32[]{:S(2)}, u32[]{:S(2)}) collective-permute-start(f32[256,128]{1,0:T(8,128)S(1)} %get-tuple-element.63), channel_id=1, source_target_pairs={{1,0},{2,1},{3,2},{4,3},{5,4},{6,5},{7,6},{8,7},{9,8},{10,9},{11,1... | collective-permute-start | bytes 393224 | tf_op jit(solution)/shard_map/ppermute | solution.py:577
  84.3 0.4 shard_map.82
  84.7 0.9 collective-permute-done.8.below
  85.7 3.4 %collective-permute-done.9.above = f32[256,128]{1,0:T(8,128)S(1)} collective-permute-done((f32[256,128]{1,0:T(8,128)S(1)}, f32[256,128]{1,0:T(8,128)S(1)}, u32[]{:S(2)}, u32[]{:S(2)}) %collective-permute-start.9) | collective-permute-done | bytes 131104 | tf_op jit(solution)/shard_map/ppermute | solution.py:577
  89.0 0.2 shard_map.83
  89.2 4.2 %collective-permute-start.10 = (f32[256,128]{1,0:T(8,128)S(1)}, f32[256,128]{1,0:T(8,128)S(1)}, u32[]{:S(2)}, u32[]{:S(2)}) collective-permute-start(f32[256,128]{1,0:T(8,128)S(1)} %get-tuple-element.66), channel_id=1, source_target_pairs={{0,1},{1,2},{2,3},{3,4},{4,5},{5,6},{6,7},{7,8},{8,9},{9,10},{10,1... | collective-permute-start | bytes 393224 | tf_op jit(solution)/shard_map/ppermute | solution.py:576
  93.4 2.8 %collective-permute-start.11 = (f32[256,128]{1,0:T(8,128)S(1)}, f32[256,128]{1,0:T(8,128)S(1)}, u32[]{:S(2)}, u32[]{:S(2)}) collective-permute-start(f32[256,128]{1,0:T(8,128)S(1)} %get-tuple-element.67), channel_id=1, source_target_pairs={{1,0},{2,1},{3,2},{4,3},{5,4},{6,5},{7,6},{8,7},{9,8},{10,9},{11,1... | collective-permute-start | bytes 393224 | tf_op jit(solution)/shard_map/ppermute | solution.py:577
  96.3 0.4 shard_map.84.t
  96.7 0.6 collective-permute-done.10.below
  97.3 3.0 %collective-permute-done.11.above = f32[256,128]{1,0:T(8,128)S(1)} collective-permute-done((f32[256,128]{1,0:T(8,128)S(1)}, f32[256,128]{1,0:T(8,128)S(1)}, u32[]{:S(2)}, u32[]{:S(2)}) %collective-permute-start.11) | collective-permute-done | bytes 131104 | tf_op jit(solution)/shard_map/ppermute | solution.py:577
  100.3 0.2 shard_map.85
  100.4 3.6 %collective-permute-start.12 = (f32[256,128]{1,0:T(8,128)S(1)}, f32[256,128]{1,0:T(8,128)S(1)}, u32[]{:S(2)}, u32[]{:S(2)}) collective-permute-start(f32[256,128]{1,0:T(8,128)S(1)} %get-tuple-element.69), channel_id=1, source_target_pairs={{0,1},{1,2},{2,3},{3,4},{4,5},{5,6},{6,7},{7,8},{8,9},{9,10},{10,1... | collective-permute-start | bytes 393224 | tf_op jit(solution)/shard_map/ppermute | solution.py:576
  104.1 3.4 %collective-permute-start.13 = (f32[256,128]{1,0:T(8,128)S(1)}, f32[256,128]{1,0:T(8,128)S(1)}, u32[]{:S(2)}, u32[]{:S(2)}) collective-permute-start(f32[256,128]{1,0:T(8,128)S(1)} %get-tuple-element.70), channel_id=1, source_target_pairs={{1,0},{2,1},{3,2},{4,3},{5,4},{6,5},{7,6},{8,7},{9,8},{10,9},{11,1... | collective-permute-start | bytes 393224 | tf_op jit(solution)/shard_map/ppermute | solution.py:577
  107.5 0.4 shard_map.86.t
  107.9 0.6 collective-permute-done.12.below
  108.5 2.4 %collective-permute-done.13.above = f32[256,128]{1,0:T(8,128)S(1)} collective-permute-done((f32[256,128]{1,0:T(8,128)S(1)}, f32[256,128]{1,0:T(8,128)S(1)}, u32[]{:S(2)}, u32[]{:S(2)}) %collective-permute-start.13) | collective-permute-done | bytes 131104 | tf_op jit(solution)/shard_map/ppermute | solution.py:577
  111.0 0.2 shard_map.87.own
  111.1 4.6 %collective-permute-start.15 = (f32[160,128]{1,0:T(8,128)S(1)}, f32[160,128]{1,0:T(8,128)S(1)}, u32[]{:S(2)}, u32[]{:S(2)}) collective-permute-start(f32[160,128]{1,0:T(8,128)S(1)} %shard_map.87.own), channel_id=1, source_target_pairs={{1,0},{2,1},{3,2},{4,3},{5,4},{6,5},{7,6},{8,7},{9,8},{10,9},{11,1... | collective-permute-start | bytes 245768 | tf_op jit(solution)/shard_map/ppermute | solution.py:577
  115.8 1.9 %collective-permute-start.14 = (f32[160,128]{1,0:T(8,128)S(1)}, f32[160,128]{1,0:T(8,128)S(1)}, u32[]{:S(2)}, u32[]{:S(2)}) collective-permute-start(f32[160,128]{1,0:T(8,128)S(1)} %shard_map.87.own), channel_id=1, source_target_pairs={{0,1},{1,2},{2,3},{3,4},{4,5},{5,6},{6,7},{7,8},{8,9},{9,10},{10,1... | collective-permute-start | bytes 245768 | tf_op jit(solution)/shard_map/ppermute | solution.py:576
  117.7 0.1 collective-permute-done.15.above
  117.8 5.5 %collective-permute-done.14.below = f32[160,128]{1,0:T(8,128)S(1)} collective-permute-done((f32[160,128]{1,0:T(8,128)S(1)}, f32[160,128]{1,0:T(8,128)S(1)}, u32[]{:S(2)}, u32[]{:S(2)}) %collective-permute-start.14) | collective-permute-done | bytes 81952 | tf_op jit(solution)/shard_map/ppermute | solution.py:576
  123.3 2.1 %shard_map.88 = f32[8,8,512]{2,1,0:T(8,128)} custom-call(f32[160,128]{1,0:T(8,128)S(1)} %shard_map.87.own, f32[160,128]{1,0:T(8,128)S(1)} %collective-permute-done.14.below, f32[160,128]{1,0:T(8,128)S(1)} %collective-permute-done.15.above, f32[5,256,128]{2,1,0:T(8,128)S(1)} %get-tuple-element.53.mid, f32[256,128]{1,0:T(8,128)S(1)} %get-tuple-element.72.rhs_mid, ...), custom_call_target="tpu_custom_call" | custom-call | flops 519045120 | bytes 4276224 | tf_op jit(solution)/shard_map/pallas_call | solution.py:563
  (1 shorter events, 0.0 us)
Async XLA Ops:
  0.0 22.2 %copy-start.1 = (f32[512,512]{1,0:T(8,128)S(1)}, f32[512,512]{1,0:T(8,128)}, u32[]{:S(2)}) copy-start(f32[512,512]{1,0:T(8,128)} %j_ref.1) | copy-start | bytes 3145732
  2.7 12.1 %collective-permute-start = (f32[576,128]{1,0:T(8,128)}, f32[576,128]{1,0:T(8,128)S(1)}, u32[]{:S(2)}, u32[]{:S(2)}) collective-permute-start(f32[576,128]{1,0:T(8,128)} %get-tuple-element.41), channel_id=1, source_target_pairs={{0,1},{1,2},{2,3},{3,4},{4,5},{5,6},{6,7},{7,8},{8,9},{9,10},{10,1... | collective-permute-start | bytes 884744 | tf_op jit(solution)/shard_map/ppermute | solution.py:576
  6.5 10.8 %collective-permute-start.1 = (f32[576,128]{1,0:T(8,128)}, f32[576,128]{1,0:T(8,128)S(1)}, u32[]{:S(2)}, u32[]{:S(2)}) collective-permute-start(f32[576,128]{1,0:T(8,128)} %get-tuple-element.42), channel_id=1, source_target_pairs={{1,0},{2,1},{3,2},{4,3},{5,4},{6,5},{7,6},{8,7},{9,8},{10,9},{11,1... | collective-permute-start | bytes 884744 | tf_op jit(solution)/shard_map/ppermute | solution.py:577
  9.7 13.9 %collective-permute-start.2 = (f32[1184,128]{1,0:T(8,128)}, f32[1184,128]{1,0:T(8,128)S(1)}, u32[]{:S(2)}, u32[]{:S(2)}) collective-permute-start(f32[1184,128]{1,0:T(8,128)} %get-tuple-element.43), channel_id=1, source_target_pairs={{0,16},{16,32},{32,48},{48,64},{64,80},{80,96},{96,112},{112,128},... | collective-permute-start | bytes 1818632 | tf_op jit(solution)/shard_map/ppermute | solution.py:576
  11.1 12.6 %collective-permute-start.3 = (f32[1184,128]{1,0:T(8,128)}, f32[1184,128]{1,0:T(8,128)S(1)}, u32[]{:S(2)}, u32[]{:S(2)}) collective-permute-start(f32[1184,128]{1,0:T(8,128)} %get-tuple-element.44), channel_id=1, source_target_pairs={{16,0},{32,16},{48,32},{64,48},{80,64},{96,80},{112,96},{128,112},... | collective-permute-start | bytes 1818632 | tf_op jit(solution)/shard_map/ppermute | solution.py:577
  17.3 6.4 %collective-permute-start.4 = (f32[720,128]{1,0:T(8,128)S(1)}, f32[720,128]{1,0:T(8,128)S(1)}, u32[]{:S(2)}, u32[]{:S(2)}) collective-permute-start(f32[720,128]{1,0:T(8,128)S(1)} %get-tuple-element.45), channel_id=1, source_target_pairs={{0,16},{16,32},{32,48},{48,64},{64,80},{80,96},{96,112},{112,128},... | collective-permute-start | bytes 1105928 | tf_op jit(solution)/shard_map/ppermute | solution.py:576
  18.6 5.3 %collective-permute-start.5 = (f32[720,128]{1,0:T(8,128)S(1)}, f32[720,128]{1,0:T(8,128)S(1)}, u32[]{:S(2)}, u32[]{:S(2)}) collective-permute-start(f32[720,128]{1,0:T(8,128)S(1)} %get-tuple-element.46), channel_id=1, source_target_pairs={{16,0},{32,16},{48,32},{64,48},{80,64},{96,80},{112,96},{128,112},... | collective-permute-start | bytes 1105928 | tf_op jit(solution)/shard_map/ppermute | solution.py:577
  22.2 1.2 copy-start
  26.2 11.3 %copy-start.2 = (f32[64,128]{1,0:T(8,128)S(1)}, f32[64,128]{1,0:T(8,128)}, u32[]{:S(2)}) copy-start(f32[64,128]{1,0:T(8,128)} %get-tuple-element.54.coefs) | copy-start | bytes 98308
  26.2 7.5 %collective-permute-start.6 = (f32[160,128]{1,0:T(8,128)S(1)}, f32[160,128]{1,0:T(8,128)S(1)}, u32[]{:S(2)}, u32[]{:S(2)}) collective-permute-start(f32[160,128]{1,0:T(8,128)S(1)} %get-tuple-element.51), channel_id=1, source_target_pairs={{0,1},{1,2},{2,3},{3,4},{4,5},{5,6},{6,7},{7,8},{8,9},{9,10},{10,1... | collective-permute-start | bytes 245768 | tf_op jit(solution)/shard_map/ppermute | solution.py:576
  30.0 7.4 %collective-permute-start.7 = (f32[160,128]{1,0:T(8,128)S(1)}, f32[160,128]{1,0:T(8,128)S(1)}, u32[]{:S(2)}, u32[]{:S(2)}) collective-permute-start(f32[160,128]{1,0:T(8,128)S(1)} %get-tuple-element.52), channel_id=1, source_target_pairs={{1,0},{2,1},{3,2},{4,3},{5,4},{6,5},{7,6},{8,7},{9,8},{10,9},{11,1... | collective-permute-start | bytes 245768 | tf_op jit(solution)/shard_map/ppermute | solution.py:577
  77.2 8.4 %collective-permute-start.8 = (f32[256,128]{1,0:T(8,128)S(1)}, f32[256,128]{1,0:T(8,128)S(1)}, u32[]{:S(2)}, u32[]{:S(2)}) collective-permute-start(f32[256,128]{1,0:T(8,128)S(1)} %get-tuple-element.62), channel_id=1, source_target_pairs={{0,1},{1,2},{2,3},{3,4},{4,5},{5,6},{6,7},{7,8},{8,9},{9,10},{10,1... | collective-permute-start | bytes 393224 | tf_op jit(solution)/shard_map/ppermute | solution.py:576
  82.1 6.9 %collective-permute-start.9 = (f32[256,128]{1,0:T(8,128)S(1)}, f32[256,128]{1,0:T(8,128)S(1)}, u32[]{:S(2)}, u32[]{:S(2)}) collective-permute-start(f32[256,128]{1,0:T(8,128)S(1)} %get-tuple-element.63), channel_id=1, source_target_pairs={{1,0},{2,1},{3,2},{4,3},{5,4},{6,5},{7,6},{8,7},{9,8},{10,9},{11,1... | collective-permute-start | bytes 393224 | tf_op jit(solution)/shard_map/ppermute | solution.py:577
  89.2 8.1 %collective-permute-start.10 = (f32[256,128]{1,0:T(8,128)S(1)}, f32[256,128]{1,0:T(8,128)S(1)}, u32[]{:S(2)}, u32[]{:S(2)}) collective-permute-start(f32[256,128]{1,0:T(8,128)S(1)} %get-tuple-element.66), channel_id=1, source_target_pairs={{0,1},{1,2},{2,3},{3,4},{4,5},{5,6},{6,7},{7,8},{8,9},{9,10},{10,1... | collective-permute-start | bytes 393224 | tf_op jit(solution)/shard_map/ppermute | solution.py:576
  93.4 6.9 %collective-permute-start.11 = (f32[256,128]{1,0:T(8,128)S(1)}, f32[256,128]{1,0:T(8,128)S(1)}, u32[]{:S(2)}, u32[]{:S(2)}) collective-permute-start(f32[256,128]{1,0:T(8,128)S(1)} %get-tuple-element.67), channel_id=1, source_target_pairs={{1,0},{2,1},{3,2},{4,3},{5,4},{6,5},{7,6},{8,7},{9,8},{10,9},{11,1... | collective-permute-start | bytes 393224 | tf_op jit(solution)/shard_map/ppermute | solution.py:577
  100.4 8.1 %collective-permute-start.12 = (f32[256,128]{1,0:T(8,128)S(1)}, f32[256,128]{1,0:T(8,128)S(1)}, u32[]{:S(2)}, u32[]{:S(2)}) collective-permute-start(f32[256,128]{1,0:T(8,128)S(1)} %get-tuple-element.69), channel_id=1, source_target_pairs={{0,1},{1,2},{2,3},{3,4},{4,5},{5,6},{6,7},{7,8},{8,9},{9,10},{10,1... | collective-permute-start | bytes 393224 | tf_op jit(solution)/shard_map/ppermute | solution.py:576
  104.1 6.9 %collective-permute-start.13 = (f32[256,128]{1,0:T(8,128)S(1)}, f32[256,128]{1,0:T(8,128)S(1)}, u32[]{:S(2)}, u32[]{:S(2)}) collective-permute-start(f32[256,128]{1,0:T(8,128)S(1)} %get-tuple-element.70), channel_id=1, source_target_pairs={{1,0},{2,1},{3,2},{4,3},{5,4},{6,5},{7,6},{8,7},{9,8},{10,9},{11,1... | collective-permute-start | bytes 393224 | tf_op jit(solution)/shard_map/ppermute | solution.py:577
  111.1 6.7 %collective-permute-start.15 = (f32[160,128]{1,0:T(8,128)S(1)}, f32[160,128]{1,0:T(8,128)S(1)}, u32[]{:S(2)}, u32[]{:S(2)}) collective-permute-start(f32[160,128]{1,0:T(8,128)S(1)} %shard_map.87.own), channel_id=1, source_target_pairs={{1,0},{2,1},{3,2},{4,3},{5,4},{6,5},{7,6},{8,7},{9,8},{10,9},{11,1... | collective-permute-start | bytes 245768 | tf_op jit(solution)/shard_map/ppermute | solution.py:577
  115.8 7.5 %collective-permute-start.14 = (f32[160,128]{1,0:T(8,128)S(1)}, f32[160,128]{1,0:T(8,128)S(1)}, u32[]{:S(2)}, u32[]{:S(2)}) collective-permute-start(f32[160,128]{1,0:T(8,128)S(1)} %shard_map.87.own), channel_id=1, source_target_pairs={{0,1},{1,2},{2,3},{3,4},{4,5},{5,6},{6,7},{7,8},{8,9},{9,10},{10,1... | collective-permute-start | bytes 245768 | tf_op jit(solution)/shard_map/ppermute | solution.py:576
